TPU v7x, 128 devices: a whole 4x4x4 slice. The times are simulated.
128 devices in a mesh: dir: 16 (over z_lo, y, core), freq: 8 (over z_hi, x).
Axes of the slice: x: 4, y: 4, z: 4 (z_hi: 2, z_lo: 2; z = z_hi * 2 + z_lo), core: 2. Of those that a mesh axis runs over, the one named last changes fastest.
Arguments:
- observed: float32 [512, 16, 2, 2, 512], P('dir', 'freq'), as said below
- flags: int32 [512, 2, 512], P('dir'), may hold values from 0 to 1, as said below
- screen: float32 [32, 512], P('dir'), may hold values from -6 to 6
- screen_kernel: float32 [512, 512], replicated
- station_uv: float32 [2, 2, 512], replicated, may hold values from -360 to 360
- source_lm: float32 [2, 6144], P(None, 'dir'), may hold values from -0.05 to 0.05
- source_flux: float32 [6144], P('dir')
- station_gain: bfloat16 [16, 2, 2, 512, 6144], P('freq', None, None, None, 'dir'), may hold values from -4.1875 to 4.1875
- source_direction: int32 [6144], P('dir'), may hold values from 0 to 1
- freq_ratio: float32 [16], P('freq')
Outputs:
- residual: float32 [512, 16, 2, 2, 512], P('dir', 'freq')
- updated_screen: float32 [32, 512], P('dir')
Inputs may be any that keep to these rules, and one draw needn't show every extreme that they name: observed is Hermitian in its stations: observed[p, f, t, 0, q] equals observed[q, f, t, 0, p] and observed[p, f, t, 1, q] equals minus observed[q, f, t, 1, p]. flags[p, t, q] equals flags[q, t, p].
All inputs are finite; a program needn't handle non-finite values.
Results may differ from a plain program's by a relative error of at most 0.0037.
Values may be sent and summed in bfloat16 or wider, within the bound.
No kernel may reach another device: no remote copies, remote signals or barrier semaphores. Data moves between devices by JAX's collectives and lax.ppermute only.
A program may use at most 128 MiB of HBM per device.

v0:
```python
import math

import jax
import jax.numpy as jnp
from jax import lax
from jax.sharding import PartitionSpec as P

step_size = 0.3
epsilon = 1e-06
highest = lax.Precision.HIGHEST


def body(
    observed,
    flags,
    screen,
    screen_kernel,
    station_uv,
    source_lm,
    source_flux,
    station_gain,
    source_direction,
    freq_ratio,
):
    dir_count = lax.axis_size("dir")
    stations = screen.shape[1]
    local_dirs = screen.shape[0]
    local_sources = source_flux.shape[0]
    local_rows = observed.shape[0]
    channels = freq_ratio.shape[0]
    times_count = station_uv.shape[0]
    matrices = channels * times_count
    scaling = 1.0 / math.sqrt(local_sources * dir_count)
    onehot_dirs = (
        source_direction[:, None] == jnp.arange(local_dirs, dtype=jnp.int32)[None, :]
    ).astype(jnp.float32)
    screen_src = jnp.einsum("dp,kd->pk", screen, onehot_dirs, precision=highest)
    freq_each = jnp.repeat(freq_ratio, times_count)
    uv_each = jnp.tile(station_uv, (channels, 1, 1))
    geometry = jnp.einsum("mcp,ck->pmk", uv_each, source_lm, precision=highest)
    phase_angle = (
        screen_src[:, None, :] / freq_each[None, :, None]
        + (2.0 * math.pi * freq_each)[None, :, None] * geometry
    )
    gain_all = station_gain.reshape(matrices, 2, stations, local_sources).astype(jnp.float32)
    gain_re = jnp.transpose(gain_all[:, 0], (1, 0, 2))
    gain_im = jnp.transpose(gain_all[:, 1], (1, 0, 2))
    cosine = jnp.cos(phase_angle)
    sine = jnp.sin(phase_angle)
    amplitude = jnp.sqrt(source_flux)[None, None, :]
    phasor_re = (amplitude * (gain_re * cosine - gain_im * sine)).astype(jnp.bfloat16)
    phasor_im = (amplitude * (gain_re * sine + gain_im * cosine)).astype(jnp.bfloat16)
    left_mat = jnp.concatenate([phasor_re, phasor_im], axis=2)
    skew_mat = jnp.concatenate([phasor_im, -phasor_re], axis=2)
    real_part = jnp.einsum("pmk,qmk->pmq", left_mat, left_mat, preferred_element_type=jnp.float32)
    imag_part = jnp.einsum("pmk,qmk->pmq", skew_mat, left_mat, preferred_element_type=jnp.float32)
    model_rows = lax.psum_scatter(
        jnp.stack([real_part, imag_part], axis=2) * scaling, "dir", scatter_dimension=0, tiled=True
    )
    row_ids = lax.axis_index("dir") * local_rows + jnp.arange(local_rows, dtype=jnp.int32)
    cross_baseline = (row_ids[:, None] != jnp.arange(stations, dtype=jnp.int32)[None, :]).astype(
        jnp.float32
    )
    baseline_keep = (
        jnp.tile(flags, (1, channels, 1)).astype(jnp.float32) * cross_baseline[:, None, :]
    )
    obs_rows = observed.reshape(local_rows, matrices, 2, stations)
    residual = baseline_keep[:, :, None, :] * (obs_rows - model_rows)
    resid_half = residual.astype(jnp.bfloat16)
    forward_mat = jnp.stack([left_mat, -skew_mat], axis=2)
    conj_mat = jnp.concatenate([phasor_re, -phasor_im], axis=2)
    dual_mat = jnp.concatenate([phasor_im, phasor_re], axis=2)
    adjoint_mat = jnp.stack([conj_mat, dual_mat], axis=2)
    rows_piece = lax.all_gather(resid_half, "dir", axis=0, tiled=True)
    row_part = jnp.einsum(
        "rmwq,qmwk->rmk", rows_piece, forward_mat, preferred_element_type=jnp.float32
    )
    col_total = jnp.einsum(
        "rmwp,rmwk->pmk", rows_piece, adjoint_mat, preferred_element_type=jnp.float32
    )
    weight_re = row_part[..., :local_sources] + col_total[..., :local_sources]
    weight_im = row_part[..., local_sources:] - col_total[..., local_sources:]
    source_grad = (
        phasor_im.astype(jnp.float32) * weight_re - phasor_re.astype(jnp.float32) * weight_im
    )
    source_grad = source_grad * (scaling / freq_each)[None, :, None]
    local_grad = jnp.einsum("pmk,kd->dp", source_grad, onehot_dirs, precision=highest)
    entry_count = local_dirs * dir_count * stations
    total_grad = lax.psum(local_grad, "freq")
    smooth = jnp.dot(total_grad, screen_kernel, precision=highest)
    total_sq = lax.psum(jnp.sum(smooth * smooth), "dir")
    updated = screen - step_size * smooth * lax.rsqrt(total_sq / entry_count + epsilon)
    return (residual.reshape(observed.shape), updated)


def solution(mesh):
    placed = (
        P("dir", "freq", None, None, None),
        P("dir", None, None),
        P("dir", None),
        P(),
        P(),
        P(None, "dir"),
        P("dir"),
        P("freq", None, None, None, "dir"),
        P("dir"),
        P("freq"),
    )
    return jax.shard_map(
        body,
        mesh=mesh,
        in_specs=placed,
        out_specs=(P("dir", "freq", None, None, None), P("dir", None)),
        check_vma=False,
    )
```

profile of v0, /device:TPU:0, one launch (start us, length us, event | category | flops | bytes accessed | tf_op | source)
XLA Modules:
  0.0 314.9 jit_solution(9520299736881047090)
XLA Ops:
  7.2 0.8 broadcast_in_dim.2
  8.1 0.7 sqrt.3
  8.8 5.5 %copy.25 = f32[2,2,2,512,384]{3,4,1,0,2:T(8,128)} copy(bf16[2,2,2,512,384]{4,3,2,1,0:T(8,128)(2,1)} %param.17) | data formatting | bytes 9437184 | tf_op jit(solution)/shard_map/convert_element_type | solution.py:45
  14.9 14.2 %fusion.44 = (f32[512,4,384]{0,2,1:T(8,128)S(1)}, f32[512,4,384]{0,2,1:T(8,128)S(1)}) fusion(f32[4,2,512]{2,1,0:T(2,128)S(1)} %bitcast.70, f32[2,384]{1,0:T(2,128)S(1)} %copy-done.10, f32[4]{0:T(128)S(1)} %get-tuple-element.20, f32[4]{0:T(128)S(1)} %div.26, f32[512,384]{0,1:T(8,128)S(1)} %convolution_bitcast_fusion.1), kind=kOutput, calls=%fused_computation.60 | convolution fusion | flops 21233664 | bytes 7097376 | tf_op jit(solution)/shard_map/mcp,ck->pmk/dot_general | solution.py:40
  29.1 3.1 negate_bitcast_fusion
  32.5 2.1 convolution_bitcast_fusion
  34.6 2.1 fusion.29
  36.7 4.3 %maximum_multiply_fusion = f32[512,4,2,512]{0,3,1,2:T(8,128)} fusion(f32[512,4,1,512]{0,3,1,2:T(8,128)S(1)} %fusion.29, f32[512,4,1,512]{0,3,1,2:T(8,128)S(1)} %convolution_bitcast_fusion), kind=kLoop, calls=%fused_computation | loop fusion | flops 4194304 | bytes 16777216 | tf_op jit(solution)/shard_map/mul | solution.py:58
  41.0 10.3 %copy.30 = f32[512,4,2,512]{3,1,2,0:T(4,128)} copy(f32[512,4,2,512]{0,3,1,2:T(8,128)} %maximum_multiply_fusion) | data formatting | bytes 16777216 | tf_op jit(solution)/shard_map/mul | solution.py:58
  51.5 0.6 copy-done.6
  52.5 0.6 dynamic-slice
  53.9 143.0 %all-reduce.3.cloned.1.call-done = f32[512,4,2,512]{3,1,2,0:T(4,128)} async-done(((f32[512,4,2,512]{3,1,2,0:T(4,128)}), f32[512,4,2,512]{3,1,2,0:T(4,128)}) %all-reduce.3.cloned.1.call-update) | async-done | bytes 8388624
  196.9 2.2 fusion.42
  199.1 4.4 %maximum_negate_fusion = bf16[512,4,1,768]{0,3,1,2:T(8,128)(2,1)} fusion(bf16[512,4,1,384]{0,3,1,2:T(8,128)(2,1)} %get-tuple-element.6, bf16[512,4,1,384]{0,3,1,2:T(8,128)(2,1)} %bitcast.67), kind=kLoop, calls=%fused_computation.29 | loop fusion | flops 7864320 | bytes 6291456 | tf_op jit(solution)/shard_map/neg | solution.py:70
  203.5 3.7 %fusion.30 = (bf16[512,4,1,768]{0,3,1,2:T(8,128)(2,1)}, bf16[512,4,1,768]{0,3,1,2:T(8,128)(2,1)}, bf16[512,4,1,768]{0,3,1,2:T(8,128)(2,1)}) fusion(bf16[512,4,384]{0,2,1:T(8,128)(2,1)S(1)} %copy-done.2, bf16[512,4,384]{0,2,1:T(8,128)(2,1)S(1)} %get-tuple-element.7, bf16[512,4,384]{0,2,1:T(8,128)(2,1)S(1)} %copy-done.4), kind=kLoop, calls=%fused_computation.36 | loop fusion | flops 17301504 | bytes 14155776 | tf_op jit(solution)/shard_map/stack | solution.py:70
  207.2 1.1 copy.45
  208.2 28.7 %all-gather.2.cloned.1.call-done = bf16[512,4,2,512]{3,1,2,0:T(4,128)(2,1)} async-done(((bf16[32,4,2,512]{3,1,2,0:T(4,128)(2,1)}), bf16[512,4,2,512]{3,1,2,0:T(4,128)(2,1)}) %all-gather.2.cloned.1.call-update) | async-done | bytes 4194320 | tf_op jit(solution)/shard_map/all_gather | solution.py:74
  236.9 7.7 %fusion.24 = f32[512,4,768]{0,2,1:T(8,128)S(1)} fusion(bf16[512,4,2,512]{3,1,2,0:T(4,128)(2,1)} %all-gather.2.cloned.1.call-done, bf16[512,4,1,768]{0,3,1,2:T(8,128)(2,1)} %maximum_negate_fusion, bf16[512,4,1,768]{0,3,1,2:T(8,128)(2,1)} %get-tuple-element.14), kind=kOutput, calls=%fused_computation.33 | convolution fusion | flops 3224371200 | bytes 16777216 | tf_op jit(solution)/shard_map/rmwq,qmwk->rmk/dot_general | solution.py:75
  244.7 6.8 %fusion.19 = f32[512,4,768]{0,2,1:T(8,128)S(1)} fusion(bf16[512,4,2,512]{3,1,2,0:T(4,128)(2,1)} %all-gather.2.cloned.1.call-done, bf16[512,4,1,768]{0,3,1,2:T(8,128)(2,1)S(1)} %copy-done.5, bf16[512,4,1,768]{0,3,1,2:T(8,128)(2,1)} %get-tuple-element.18), kind=kOutput, calls=%fused_computation.32 | convolution fusion | flops 3224371200 | bytes 16777216 | tf_op jit(solution)/shard_map/rmwp,rmwk->pmk/dot_general | solution.py:78
  251.5 1.9 fusion.16
  253.8 23.9 %psum.14 = f32[2,512]{1,0:T(2,128)S(1)} all-reduce(f32[2,512]{1,0:T(2,128)S(1)} %fusion.32), channel_id=1, replica_groups=mesh['dir'=16,'freq'=8] {'freq'}, use_global_device_ids=true, to_apply=%region_2.0 | all-reduce | flops 1024 | bytes 8192 | tf_op jit(solution)/shard_map/psum | solution.py:89
  277.8 1.2 multiply_reduce_fusion
  279.0 27.8 %psum.15 = f32[]{:T(128)} all-reduce(f32[]{:T(128)} %get-tuple-element.22), channel_id=1, replica_groups=mesh['dir'=16,'freq'=8] {'dir'}, use_global_device_ids=true, to_apply=%region_4.0 | all-reduce | flops 1 | bytes 8 | tf_op jit(solution)/shard_map/psum | solution.py:91
  307.4 0.6 multiply_subtract_fusion
  (44 shorter events, 2.2 us)
Async XLA Ops:
  7.2 270.6 %copy-start = (f32[512,512]{1,0:T(8,128)S(1)}, f32[512,512]{1,0:T(8,128)}, u32[]{:S(2)}) copy-start(f32[512,512]{1,0:T(8,128)} %param.13) | copy-start | bytes 3145732
  7.2 189.7 %all-reduce.3.cloned.1.call-start = ((), (), s32[]{:S(2)}) async-start(), calls=%async_computation.1 | async-start | bytes 16777216
  8.8 5.5 %copy-start.7 = (f32[2,512]{1,0:T(2,128)S(1)}, f32[2,512]{1,0:T(2,128)}, u32[]{:S(2)}) copy-start(f32[2,512]{1,0:T(2,128)} %param.12) | copy-start | bytes 12292
  8.8 5.5 %copy-start.8 = (s32[384]{0:T(512)S(1)}, s32[384]{0:T(512)}, u32[]{:S(2)}) copy-start(s32[384]{0:T(512)} %param.18) | copy-start | bytes 4612
  8.8 6.0 %copy-start.9 = (f32[2,2,512]{2,1,0:T(2,128)S(1)}, f32[2,2,512]{2,1,0:T(2,128)}, u32[]{:S(2)}) copy-start(f32[2,2,512]{2,1,0:T(2,128)} %param.14) | copy-start | bytes 24580
  8.8 6.0 %copy-start.10 = (f32[2,384]{1,0:T(2,128)S(1)}, f32[2,384]{1,0:T(2,128)}, u32[]{:S(2)}) copy-start(f32[2,384]{1,0:T(2,128)} %param.15) | copy-start | bytes 9220
  14.8 14.2 %slice-start = ((s8[6291456]{0:T(1024)(128)(4,1)}), s8[4194304]{0:T(1024)(128)(4,1)S(1)}, s32[]{:S(2)}) async-start(s8[6291456]{0:T(1024)(128)(4,1)} %bitcast.64), calls=%async_computation.2 | async-start | bytes 8388608
  14.9 14.2 %slice-start.1 = ((s8[6291456]{0:T(1024)(128)(4,1)}), s8[2097152]{0:T(1024)(128)(4,1)S(1)}, s32[]{:S(2)}) async-start(s8[6291456]{0:T(1024)(128)(4,1)} %bitcast.64), calls=%async_computation.3 | async-start | bytes 4194304
  32.2 2.4 copy-start.1
  51.2 0.9 copy-start.6
  51.3 1.3 copy-start.11
  51.3 185.7 %all-gather.2.cloned.1.call-start = ((), (), s32[]{:S(2)}) async-start(), calls=%async_computation | async-start | bytes 4456448 | tf_op jit(solution)/shard_map/all_gather | solution.py:74
  199.1 4.4 %copy-start.2 = (bf16[512,4,384]{0,2,1:T(8,128)(2,1)S(1)}, bf16[512,4,384]{0,2,1:T(8,128)(2,1)}, u32[]{:S(2)}) copy-start(bf16[512,4,384]{0,2,1:T(8,128)(2,1)} %copy-done.1) | copy-start | bytes 4718596
  199.1 4.4 %copy-start.4 = (bf16[512,4,384]{0,2,1:T(8,128)(2,1)S(1)}, bf16[512,4,384]{0,2,1:T(8,128)(2,1)}, u32[]{:S(2)}) copy-start(bf16[512,4,384]{0,2,1:T(8,128)(2,1)} %get-tuple-element.12) | copy-start | bytes 4718596
  236.9 7.7 %copy-start.5 = (bf16[512,4,1,768]{0,3,1,2:T(8,128)(2,1)S(1)}, bf16[512,4,1,768]{0,3,1,2:T(8,128)(2,1)}, u32[]{:S(2)}) copy-start(bf16[512,4,1,768]{0,3,1,2:T(8,128)(2,1)} %get-tuple-element.15) | copy-start | bytes 9437188
  244.7 6.8 %copy-start.3 = (bf16[512,4,384]{0,2,1:T(8,128)(2,1)S(1)}, bf16[512,4,384]{0,2,1:T(8,128)(2,1)}, u32[]{:S(2)}) copy-start(bf16[512,4,384]{0,2,1:T(8,128)(2,1)} %copy-done.1) | copy-start | bytes 4718596
Sparse Core Ops, SparseCore 0:
  51.4 145.4 all-reduce.2
  199.2 37.6 all-gather.1
where the time goes:
time: 316 us; the launch traced here: 315 us
  waiting for transfers between devices  172 us (54%)
  blocking collectives  51.7 us (16%)
  matrix products  35 us (11%)
  other arithmetic  20.5 us (6%)
  local copies, waits for them, and re-layouts  19.9 us (6%)
  between operations  15.6 us (5%)
    unnamed x3, waiting for transfers between devices  143 us
    all_gather x1, waiting for transfers between devices, body(): rows_piece = lax.all_gather(resid_half, 'dir', axis=0, tiled=True)  28.7 us
    psum x1, blocking collectives, body(): total_sq = lax.psum(jnp.sum(smooth * smooth), 'dir')  27.8 us
    psum x1, blocking collectives, body(): total_grad = lax.psum(local_grad, 'freq')  23.9 us
    dot_general x1, matrix products, body(): geometry = jnp.einsum('mcp,ck->pmk', uv_each, source_lm, precision=highest)  14.2 us
    mul x1, local copies, waits for them, and re-layouts, body(): jnp.stack([real_part, imag_part], axis=2) * scaling  10.3 us
    dot_general x1, matrix products, body(): jnp.einsum('rmwq,qmwk->rmk', rows_piece, forward_mat, preferred_element_t...  7.73 us
    dot_general x1, matrix products, body(): jnp.einsum('rmwp,rmwk->pmk', rows_piece, adjoint_mat, preferred_element_t...  6.79 us
  transfers between devices with their start and end apart: 2, of which 2 were waited for; matrix products, arithmetic and copies ran while one was open for 3% of the time, Pallas kernels for 0%

commit v1 on v0

v1 whole, which is shorter than its diff:
```python
import functools
import math

import jax
import jax.numpy as jnp
from jax import lax
from jax.experimental import pallas as pl
from jax.experimental.pallas import tpu as pltpu
from jax.sharding import PartitionSpec as P

step_size = 0.3
epsilon = 1e-06
highest = lax.Precision.HIGHEST
bf16 = jnp.bfloat16
f32 = jnp.float32

SIN_COEF = (4.44288292, -7.3082457, 3.60635441, -0.84611289, 0.10982699)
COS_COEF = (1.4142135, -6.97885099, 5.73946117, -1.88356299, 0.31069819)
ROUNDER = 12582912.0
CHUNK = 16
VMEM = 60 * 1024 * 1024
NT = (((1,), (1,)), ((), ()))


def y_partner(rel, y):
    if rel == 0:
        return y
    if rel == 1:
        return y + 1 - 2 * (y % 2)
    if rel == 2:
        return 3 - y
    return (y + 2) % 4


def dir_perm(rel, flip_z=False, flip_core=False):
    pairs = []
    for index in range(16):
        z, y, core = index // 8, (index // 2) % 4, index % 2
        z = 1 - z if flip_z else z
        core = 1 - core if flip_core else core
        pairs.append((index, z * 8 + y_partner(rel, y) * 2 + core))
    return pairs


def phasor_kernel(send, ids, freq, gain, cols, lanes, out):
    moment = pl.program_id(0)
    channel = 1 - ids[0] if send else ids[0]
    ratio = freq[channel]
    along = lanes[0:1, :] * ratio
    across = lanes[1:2, :] * ratio
    amp = jnp.sqrt(lanes[2:3, :])
    second = lanes[3:4, :] > 0.5
    per_turn = 1.0 / (2.0 * math.pi * ratio)
    stations = gain.shape[3]
    sources = gain.shape[4]

    def rows_of(step, carry):
        rows = pl.ds(pl.multiple_of(step * CHUNK, CHUNK), CHUNK)
        col = cols[rows, :]
        u = jnp.where(moment == 0, col[:, 0:1], col[:, 2:3])
        v = jnp.where(moment == 0, col[:, 1:2], col[:, 3:4])
        low = col[:, 4:5] * per_turn
        high = col[:, 5:6] * per_turn
        turns = u * along + v * across + jnp.where(second, high, low)
        turns = turns - ((turns + ROUNDER) - ROUNDER)
        z = turns * turns
        sin_half = SIN_COEF[4]
        cos_half = COS_COEF[4]
        for power in (3, 2, 1, 0):
            sin_half = sin_half * z + SIN_COEF[power]
            cos_half = cos_half * z + COS_COEF[power]
        sin_half = sin_half * turns
        sine = (sin_half * cos_half) * amp
        cosine = (1.0 - sin_half * sin_half) * amp
        gain_re = gain[0, 0, 0, rows, :].astype(f32)
        gain_im = gain[0, 0, 1, rows, :].astype(f32)
        out[0, rows, 0:sources] = (gain_re * cosine - gain_im * sine).astype(bf16)
        out[0, rows, sources : 2 * sources] = (gain_re * sine + gain_im * cosine).astype(bf16)
        return carry

    lax.fori_loop(0, stations // CHUNK, rows_of, 0, unroll=2)
    mask = jnp.broadcast_to(lanes[3:4, :], (16, sources)).astype(bf16)
    out[0, stations : stations + 16, 0:sources] = mask
    out[0, stations : stations + 16, sources : 2 * sources] = mask


def phasor(send, ids, freq, gain, cols, lanes):
    stations, sources = gain.shape[3], gain.shape[4]

    def gain_block(t, ids_ref):
        channel = 1 - ids_ref[0] if send else ids_ref[0]
        return (channel, t, 0, 0, 0)

    return pl.pallas_call(
        functools.partial(phasor_kernel, send),
        grid_spec=pltpu.PrefetchScalarGridSpec(
            num_scalar_prefetch=1,
            grid=(2,),
            in_specs=[
                pl.BlockSpec(memory_space=pltpu.SMEM),
                pl.BlockSpec((1, 1, 2, stations, sources), gain_block),
                pl.BlockSpec(cols.shape, lambda t, ids_ref: (0, 0)),
                pl.BlockSpec(lanes.shape, lambda t, ids_ref: (0, 0)),
            ],
            out_specs=pl.BlockSpec((1, stations + 16, 2 * sources), lambda t, ids_ref: (t, 0, 0)),
        ),
        out_shape=jax.ShapeDtypeStruct((2, stations + 16, 2 * sources), bf16),
        compiler_params=pltpu.CompilerParams(vmem_limit_bytes=VMEM),
        cost_estimate=pl.CostEstimate(
            flops=40 * 2 * stations * sources, bytes_accessed=3200000, transcendentals=0
        ),
        name="phasor_send" if send else "phasor_own",
    )(ids, freq, gain, cols, lanes)


def upper_mask():
    row = lax.broadcasted_iota(jnp.int32, (64, 64), 0)
    col = lax.broadcasted_iota(jnp.int32, (64, 64), 1)
    return row < col, row > col


def pack(re, im, odd, keep_re):
    re = jnp.where(odd, re[:, 64:384], re[:, 0:320])
    im = jnp.where(odd, im[:, 64:384], im[:, 0:320])
    upper, _ = upper_mask()
    own = jnp.where(upper, re[:, 0:64], im[:, 0:64])
    far = jnp.where(keep_re, re[:, 256:320], im[:, 256:320])
    return jnp.concatenate([own, re[:, 64:256], far, im[:, 64:256]], axis=1)


def skewed(q):
    half = q.shape[1] // 2
    return jnp.concatenate([q[:, half:], -q[:, :half]], axis=1)


def mm(a, b):
    return lax.dot_general(a, b, NT, preferred_element_type=f32)


def spread_wide(wide, part, value):
    wide[part, :, 0:512] = value
    wide[part, :, 512:768] = value[:, 0:256]


def block_of(wide, part, chip):
    start = pl.multiple_of((chip // 2) * 128, 128)
    return wide[part, pl.ds(pl.multiple_of(chip * 64, 64), 64), pl.ds(start, 384)]


def model_kernel(scaling, ids, own, other, out0, out1, out2, out3, wide):
    y, z = ids[1], ids[2]
    q_own = own[0, 0:512, :]
    q_other = other[0, 0:512, :]
    spread_wide(wide, 0, (mm(q_own, q_own) + mm(q_other, q_other)) * scaling)
    spread_wide(wide, 1, (mm(skewed(q_own), q_own) + mm(skewed(q_other), q_other)) * scaling)
    for rel, out in enumerate((out0, out1, out2, out3)):
        for flip in range(2):
            zz = 1 - z if flip else z
            chip = zz * 4 + y_partner(rel, y)
            out[flip, 0] = pack(
                block_of(wide, 0, chip), block_of(wide, 1, chip), chip % 2 == 1, zz == 0
            ).astype(out.dtype)


def model_parts(scaling, ids, own, other):
    rows, lanes = own.shape[1], own.shape[2]
    block = pl.BlockSpec((1, rows, lanes), lambda t, ids_ref: (t, 0, 0))
    out = pl.BlockSpec((2, 1, 64, 512), lambda t, ids_ref: (0, t, 0, 0))
    return pl.pallas_call(
        functools.partial(model_kernel, scaling),
        grid_spec=pltpu.PrefetchScalarGridSpec(
            num_scalar_prefetch=1,
            grid=(2,),
            in_specs=[block, block],
            out_specs=[out] * 4,
            scratch_shapes=[pltpu.VMEM((2, 512, 768), f32)],
        ),
        out_shape=[jax.ShapeDtypeStruct((2, 2, 64, 512), f32)]
        + [jax.ShapeDtypeStruct((2, 2, 64, 512), bf16)] * 3,
        compiler_params=pltpu.CompilerParams(vmem_limit_bytes=VMEM),
        cost_estimate=pl.CostEstimate(
            flops=2 * 2 * 4 * 512 * 512 * 768, bytes_accessed=5000000, transcendentals=0
        ),
        name="model_parts",
    )(ids, own, other)


def direction_kernel(ids, own, other, out, whole, first):
    core, y, z = ids[0], ids[1], ids[2]
    for source, core_of in ((own, core), (other, 1 - core)):
        q = source[0, 0:512, :]
        in_first = source[0, 512:513, :] < 0.5
        q_first = jnp.where(in_first, q, jnp.zeros_like(q))
        spread_wide(whole, 0, mm(q, q))
        spread_wide(whole, 1, mm(skewed(q), q))
        spread_wide(first, 0, mm(q_first, q))
        spread_wide(first, 1, mm(skewed(q_first), q))
        for rel in range(4):
            for flip in range(2):
                zz = 1 - z if flip else z
                chip = zz * 4 + y_partner(rel, y)
                re_first, im_first = block_of(first, 0, chip), block_of(first, 1, chip)
                re_rest = block_of(whole, 0, chip) - re_first
                im_rest = block_of(whole, 1, chip) - im_first
                odd = chip % 2 == 1
                out[core_of * 2, rel, flip, 0] = pack(im_first, -re_first, odd, zz == 0).astype(bf16)
                out[core_of * 2 + 1, rel, flip, 0] = pack(im_rest, -re_rest, odd, zz == 0).astype(bf16)


def direction_parts(ids, own, other):
    rows, lanes = own.shape[1], own.shape[2]
    block = pl.BlockSpec((1, rows, lanes), lambda t, ids_ref: (t, 0, 0))
    return pl.pallas_call(
        direction_kernel,
        grid_spec=pltpu.PrefetchScalarGridSpec(
            num_scalar_prefetch=1,
            grid=(2,),
            in_specs=[block, block],
            out_specs=pl.BlockSpec((4, 4, 2, 1, 64, 512), lambda t, ids_ref: (0, 0, 0, t, 0, 0)),
            scratch_shapes=[pltpu.VMEM((2, 512, 768), f32)] * 2,
        ),
        out_shape=jax.ShapeDtypeStruct((4, 4, 2, 2, 64, 512), bf16),
        compiler_params=pltpu.CompilerParams(vmem_limit_bytes=VMEM),
        cost_estimate=pl.CostEstimate(
            flops=2 * 2 * 8 * 512 * 512 * 768, bytes_accessed=8000000, transcendentals=0
        ),
        name="direction_parts",
    )(ids, own, other)


def observed_kernel(ids, own, other, obs_out, keep_out, wide):
    core, y, z = ids[0], ids[1], ids[2]
    for moment in range(2):
        for part in range(3):
            index = moment * 3 + part
            for rows, source in ((core, own), (1 - core, other)):
                place = pl.ds(pl.multiple_of(rows * 32, 32), 32)
                wide[part, place, 0:512] = source[index]
                wide[part, place, 512:768] = source[index, :, 0:256]
        chip = z * 4 + y
        start = pl.ds(pl.multiple_of((chip // 2) * 128, 128), 384)
        odd = chip % 2 == 1
        obs_out[moment] = pack(wide[0, :, start], wide[1, :, start], odd, z == 0)
        keep = pack(wide[2, :, start], wide[2, :, start], odd, z == 0)
        row = lax.broadcasted_iota(jnp.int32, (64, 512), 0)
        col = lax.broadcasted_iota(jnp.int32, (64, 512), 1)
        keep_out[moment] = jnp.where(row == col, 0.0, keep)


def observed_parts(ids, own, other):
    return pl.pallas_call(
        observed_kernel,
        in_specs=[
            pl.BlockSpec(memory_space=pltpu.SMEM),
            pl.BlockSpec(memory_space=pltpu.VMEM),
            pl.BlockSpec(memory_space=pltpu.VMEM),
        ],
        out_specs=[pl.BlockSpec(memory_space=pltpu.VMEM)] * 2,
        out_shape=[jax.ShapeDtypeStruct((2, 64, 512), f32)] * 2,
        scratch_shapes=[pltpu.VMEM((3, 64, 768), f32)],
        cost_estimate=pl.CostEstimate(flops=1000000, bytes_accessed=1500000, transcendentals=0),
        name="observed_parts",
    )(ids, own, other)


def gradient_kernel(scaling, ids, freq, here, one, two, three, parts, out, rows_sum, cols_sum, total):
    core, y, z = ids[0], ids[1], ids[2]
    which = pl.program_id(0)
    for rel, source in enumerate((here, one, two, three)):
        for flip in range(2):
            zz = 1 - z if flip else z
            chip = zz * 4 + y_partner(rel, y)
            product = source[flip, 0].astype(f32) * parts[0, rel, flip, 0].astype(f32)
            product += source[flip, 1].astype(f32) * parts[0, rel, flip, 1].astype(f32)
            rows_sum[pl.ds(pl.multiple_of(chip * 64, 64), 64), :] = (
                product[:, 0:128] + product[:, 128:256] + product[:, 256:384] + product[:, 384:512]
            )
            cols_sum[pl.ds(chip, 1), :] = jnp.sum(product, axis=0, keepdims=True)
    along_rows = jnp.sum(jnp.transpose(rows_sum[...]), axis=0, keepdims=True)
    low = cols_sum[:, 0:256]
    high = cols_sum[:, 256:512]
    near = lax.broadcasted_iota(jnp.int32, (8, 256), 1) < 64
    placed = jnp.concatenate(
        [low + jnp.where(near, 0.0, high), jnp.where(near, high, 0.0)], axis=1
    )
    along_cols = placed[0:1]
    for chip in range(1, 8):
        along_cols += pltpu.roll(placed[chip : chip + 1], 64 * chip, 1)
    grad = (along_rows - along_cols) * (2.0 * scaling / freq[core])
    for piece in range(4):
        total[pl.ds(which * 4 + piece, 1), :] = grad[:, piece * 128 : (piece + 1) * 128]

    @pl.when(which == 3)
    def _():
        value = total[...].astype(bf16)

        def copy(index, carry):
            out[index] = value
            return carry

        lax.fori_loop(0, out.shape[0], copy, 0, unroll=8)


def gradient_parts(scaling, devices, ids, freq, here, one, two, three, parts):
    resid = pl.BlockSpec((2, 2, 64, 512), lambda d, ids_ref: (0, 0, 0, 0))
    return pl.pallas_call(
        functools.partial(gradient_kernel, scaling),
        grid_spec=pltpu.PrefetchScalarGridSpec(
            num_scalar_prefetch=1,
            grid=(4,),
            in_specs=[pl.BlockSpec(memory_space=pltpu.SMEM)]
            + [resid] * 4
            + [pl.BlockSpec((1, 4, 2, 2, 64, 512), lambda d, ids_ref: (d, 0, 0, 0, 0, 0))],
            out_specs=pl.BlockSpec((devices, 16, 128), lambda d, ids_ref: (0, 0, 0)),
            scratch_shapes=[
                pltpu.VMEM((512, 128), f32),
                pltpu.VMEM((8, 512), f32),
                pltpu.VMEM((16, 128), f32),
            ],
        ),
        out_shape=jax.ShapeDtypeStruct((devices, 16, 128), bf16),
        compiler_params=pltpu.CompilerParams(vmem_limit_bytes=VMEM),
        cost_estimate=pl.CostEstimate(flops=10000000, bytes_accessed=6000000, transcendentals=0),
        name="gradient_parts",
    )(ids, freq, here, one, two, three, parts)


def rows_kernel(ids, resid, here, one, two, three, own_out, other_out, rolled):
    core, y, z = ids[0], ids[1], ids[2]
    chip = z * 4 + y
    upper, lower = upper_mask()
    even = y % 2 == 0
    flip5 = jnp.where(y < 3, 1, 0)
    flip6 = jnp.where(y < 2, 1, 0)
    flip7 = jnp.where(y < 1, 1, 0)
    for moment in range(2):
        own = resid[moment]
        near = own[:, 0:64]
        near_t = jnp.transpose(near)
        zero = jnp.zeros_like(near)
        near_re = jnp.where(upper, near, jnp.where(lower, near_t, zero))
        near_im = jnp.where(lower, near, jnp.where(upper, -near_t, zero))
        far = own[:, 256:320]
        far_t = jnp.transpose(here[1, moment][:, 256:320].astype(f32))
        far_re = jnp.where(z == 0, far, far_t)
        far_im = jnp.where(z == 0, -far_t, far)
        block5 = jnp.where(even, one[flip5, moment].astype(f32), two[flip5, moment].astype(f32))
        block6 = three[flip6, moment].astype(f32)
        block7 = jnp.where(even, two[flip7, moment].astype(f32), one[flip7, moment].astype(f32))
        re = [near_re, own[:, 64:256], far_re]
        im = [near_im, own[:, 320:512], far_im]
        for block, offset in ((block5, 3), (block6, 2), (block7, 1)):
            re.append(jnp.transpose(block[:, 64 * offset : 64 * offset + 64]))
            im.append(-jnp.transpose(block[:, 256 + 64 * offset : 320 + 64 * offset]))
        for part, pieces in enumerate((re, im)):
            index = moment * 2 + part
            rolled[index] = pltpu.roll(jnp.concatenate(pieces, axis=1), chip * 64, 1)
            own_out[index] = rolled[index, pl.ds(pl.multiple_of(core * 32, 32), 32), :]
            other_out[index] = rolled[index, pl.ds(pl.multiple_of((1 - core) * 32, 32), 32), :]


def whole_rows(ids, resid, here, one, two, three):
    return pl.pallas_call(
        rows_kernel,
        in_specs=[pl.BlockSpec(memory_space=pltpu.SMEM)]
        + [pl.BlockSpec(memory_space=pltpu.VMEM)] * 5,
        out_specs=[pl.BlockSpec(memory_space=pltpu.VMEM)] * 2,
        out_shape=[jax.ShapeDtypeStruct((4, 32, 512), f32)] * 2,
        scratch_shapes=[pltpu.VMEM((4, 64, 512), f32)],
        cost_estimate=pl.CostEstimate(flops=2000000, bytes_accessed=1500000, transcendentals=0),
        name="whole_rows",
    )(ids, resid, here, one, two, three)


def update_kernel(ids, grads, kernel, screen, out, total, smooth):
    per_chip = grads.shape[0] // 8
    for chip in range(8):
        total[chip * 16 : chip * 16 + 16, :] = jnp.sum(
            grads[chip * per_chip : (chip + 1) * per_chip].astype(f32), axis=0
        )
    gradient = jnp.concatenate(
        [total[pl.ds(piece, 32, stride=4), :] for piece in range(4)], axis=1
    )
    value = jnp.dot(gradient, kernel[...], precision=highest, preferred_element_type=f32)
    mean_sq = jnp.sum(value * value) / value.size
    smooth[...] = value * (step_size * lax.rsqrt(mean_sq + epsilon))
    row = (ids[2] * 4 + ids[1]) * 4 + ids[0] * 2
    for step in range(2):
        out[step : step + 1, :] = screen[step : step + 1, :] - smooth[pl.ds(row + step, 1), :]


def updated_rows(ids, grads, kernel, screen):
    return pl.pallas_call(
        update_kernel,
        in_specs=[pl.BlockSpec(memory_space=pltpu.SMEM)]
        + [pl.BlockSpec(memory_space=pltpu.VMEM)] * 3,
        out_specs=pl.BlockSpec(memory_space=pltpu.VMEM),
        out_shape=jax.ShapeDtypeStruct(screen.shape, f32),
        scratch_shapes=[pltpu.VMEM((128, 128), f32), pltpu.VMEM((32, 512), f32)],
        cost_estimate=pl.CostEstimate(flops=200000000, bytes_accessed=1500000, transcendentals=0),
        name="updated_rows",
    )(ids, grads, kernel, screen)


def body(
    observed,
    flags,
    screen,
    screen_kernel,
    station_uv,
    source_lm,
    source_flux,
    station_gain,
    source_direction,
    freq_ratio,
):
    devices = lax.axis_size("dir") * lax.axis_size("freq")
    stations = screen.shape[1]
    scaling = 1.0 / math.sqrt(source_flux.shape[0] * lax.axis_size("dir"))
    index = lax.axis_index("dir")
    core = index % 2
    y = (index // 2) % 4
    z = index // 8
    ids = jnp.stack([core, y, z]).astype(jnp.int32)
    cols = jnp.concatenate(
        [station_uv.reshape(4, stations), screen, jnp.zeros((2, stations), f32)], axis=0
    ).T
    lanes = jnp.concatenate(
        [source_lm, source_flux[None], source_direction.astype(f32)[None], jnp.zeros((4, source_flux.shape[0]), f32)],
        axis=0,
    )
    swap = functools.partial(lax.ppermute, axis_name="dir", perm=dir_perm(0, flip_core=True))

    sent = phasor(True, ids, freq_ratio, station_gain, cols, lanes)
    other = swap(sent)
    own = phasor(False, ids, freq_ratio, station_gain, cols, lanes)

    keep = flags.astype(f32)[:, None, :, None, :]
    keep = jnp.broadcast_to(keep, (32, 2, 2, 1, stations))
    rows = jnp.concatenate([observed, keep], axis=3)
    rows = jnp.transpose(rows, (1, 2, 3, 0, 4)).reshape(2, 6, 32, stations)
    rows_own = lax.dynamic_index_in_dim(rows, core, 0, keepdims=False)
    rows_sent = lax.dynamic_index_in_dim(rows, 1 - core, 0, keepdims=False)
    rows_other = swap(rows_sent)
    obs, kept = observed_parts(ids, rows_own, rows_other)

    part0, part1, part2, part3 = model_parts(scaling, ids, own, other)
    got = [
        lax.ppermute(part, "dir", dir_perm(rel)) for rel, part in ((3, part3), (2, part2), (1, part1))
    ]
    directions = direction_parts(ids, own, other)
    summed = part0 + got[0].astype(f32) + got[1].astype(f32) + got[2].astype(f32)
    last = lax.ppermute(summed[1].astype(bf16), "dir", dir_perm(0, flip_z=True))
    resid = kept * (obs - (summed[0] + last.astype(f32)))
    half = resid.astype(bf16)
    here = jnp.stack([half, lax.ppermute(half, "dir", dir_perm(0, flip_z=True))])
    three = lax.ppermute(here, "dir", dir_perm(3))
    two = lax.ppermute(here, "dir", dir_perm(2))
    one = lax.ppermute(here, "dir", dir_perm(1))

    grads = gradient_parts(scaling, devices, ids, freq_ratio, here, one, two, three, directions)
    own_rows, sent_rows = whole_rows(ids, resid, here, one, two, three)
    other_rows = swap(sent_rows)
    grads = lax.all_to_all(grads, ("dir", "freq"), 0, 0, tiled=True)
    updated = updated_rows(ids, grads, screen_kernel, screen)

    first = jnp.where(core == 0, own_rows, other_rows)
    second = jnp.where(core == 0, other_rows, own_rows)
    residual = jnp.stack([first, second]).reshape(2, 2, 2, 32, stations)
    return jnp.transpose(residual, (3, 0, 1, 2, 4)), updated


def solution(mesh):
    placed = (
        P("dir", "freq", None, None, None),
        P("dir", None, None),
        P("dir", None),
        P(),
        P(),
        P(None, "dir"),
        P("dir"),
        P("freq", None, None, None, "dir"),
        P("dir"),
        P("freq"),
    )
    return jax.shard_map(
        body,
        mesh=mesh,
        in_specs=placed,
        out_specs=(P("dir", "freq", None, None, None), P("dir", None)),
        check_vma=False,
    )
```

time: 316 us -> 130 us (0.41)
  waiting for transfers between devices: 172 us -> 36.3 us
  Pallas kernels: 0 us -> 56.4 us
  blocking collectives: 51.7 us -> 0 us
  matrix products: 35 us -> 0 us
  starting transfers between devices: 0.26 us -> 21.9 us
  between operations: 15.6 us -> 0.86 us
  other arithmetic: 20.5 us -> 6.6 us
  local copies, waits for them, and re-layouts: 19.9 us -> 7.59 us
    unnamed x3 -> x0, waiting for transfers between devices: 143 us -> none
    pallas_call x0 -> x8, Pallas kernels: none -> 56.4 us  [the longest x2 19.6 us: phasor(): pl.pallas_call(functools.partial(phasor_kernel, send), grid_spec=pltpu.Pr...]
    psum x2 -> x0, blocking collectives: 51.7 us -> none  [the longest x1 27.8 us: body(): total_sq = lax.psum(jnp.sum(smooth * smooth), 'dir')]
    dot_general x8 -> x0, matrix products: 35 us -> none  [the longest x1 14.2 us: body(): geometry = jnp.einsum('mcp,ck->pmk', uv_each, source_lm, precision=highest)]
    all_gather x1 -> x0, waiting for transfers between devices: 28.7 us -> none  [body(): rows_piece = lax.all_gather(resid_half, 'dir', axis=0, tiled=True)]
    ppermute x0 -> x11, waiting for transfers between devices: none -> 24.7 us  [the longest x3 11.2 us: body(): lax.ppermute(part, 'dir', dir_perm(rel))]
    ppermute x0 -> x11, starting transfers between devices: none -> 12.6 us  [the longest x3 4.33 us: body(): lax.ppermute(part, 'dir', dir_perm(rel))]
    all_to_all x0 -> x1, waiting for transfers between devices: none -> 11.6 us  [body(): grads = lax.all_to_all(grads, ('dir', 'freq'), 0, 0, tiled=True)]
  transfers between devices with their start and end apart: 2 -> 12, of which waited for: 2 -> 8; matrix products, arithmetic and copies ran while one was open for 3% -> 2% of each run, Pallas kernels for 0% -> 25%
where the time goes in v1:
time: 130 us
  Pallas kernels  56.4 us (43%)
  waiting for transfers between devices  36.3 us (28%)
  starting transfers between devices  21.9 us (17%)
  local copies, waits for them, and re-layouts  7.59 us (6%)
  other arithmetic  6.6 us (5%)
    pallas_call x2, Pallas kernels, phasor(): pl.pallas_call(functools.partial(phasor_kernel, send), grid_spec=pltpu.Pr...  19.6 us
    pallas_call x1, Pallas kernels, direction_parts(): pl.pallas_call(direction_kernel, grid_spec=pltpu.PrefetchScalarGridSpec(n...  14.6 us
    all_to_all x1, waiting for transfers between devices, body(): grads = lax.all_to_all(grads, ('dir', 'freq'), 0, 0, tiled=True)  11.6 us
    ppermute x3, waiting for transfers between devices, body(): lax.ppermute(part, 'dir', dir_perm(rel))  11.2 us
    all_to_all x1, starting transfers between devices, body(): grads = lax.all_to_all(grads, ('dir', 'freq'), 0, 0, tiled=True)  9.3 us
    pallas_call x1, Pallas kernels, model_parts(): pl.pallas_call(functools.partial(model_kernel, scaling), grid_spec=pltpu....  7.92 us
    pallas_call x1, Pallas kernels, gradient_parts(): pl.pallas_call(functools.partial(gradient_kernel, scaling), grid_spec=plt...  6.15 us
    ppermute x1, waiting for transfers between devices, body(): two = lax.ppermute(here, 'dir', dir_perm(2))  5.61 us
  transfers between devices with their start and end apart: 12, of which 8 were waited for; matrix products, arithmetic and copies ran while one was open for 2% of the time, Pallas kernels for 25%

profile of v1, /device:TPU:0, one launch (start us, length us, event | category | flops | bytes accessed | tf_op | source)
XLA Modules:
  0.0 129.7 jit_solution(12829763018440315247)
XLA Ops:
  5.1 1.3 %maximum_maximum_fusion.1.lanes = f32[8,384]{1,0:T(8,128)} fusion(f32[1,384]{1,0:T(1,128)S(1)} %broadcast_in_dim.21, f32[1,384]{1,0:T(1,128)S(1)} %broadcast_in_dim.20, f32[2,384]{1,0:T(2,128)} %param.15, f32[8]{0:T(128)S(1)} %pad.7.clone), kind=kLoop, calls=%fused_computation.15 | loop fusion | flops 9216 | bytes 18464 | tf_op jit(solution)/shard_map/concatenate | solution.py:428
  6.5 9.8 %phasor_send.1 = bf16[2,528,768]{2,1,0:T(8,128)(2,1)} custom-call(s32[3]{0:T(128)} %pad_add_fusion.ids, f32[2]{0:T(128)} %freq.5, bf16[2,2,2,512,384]{4,3,2,1,0:T(8,128)(2,1)} %gain.3, f32[512,8]{1,0:T(8,128)} %bitcast.29, f32[8,384]{1,0:T(8,128)} %maximum_maximum_fusion.1.lanes), custom_call_target="tpu_custom_call" | custom-call | flops 15728640 | bytes 3200000 | tf_op jit(solution)/shard_map/phasor_send/pallas_call | solution.py:94
  16.8 9.7 %phasor_own.1.own = bf16[2,528,768]{2,1,0:T(8,128)(2,1)} custom-call(s32[3]{0:T(128)} %pad_add_fusion.ids, f32[2]{0:T(128)} %freq.5, bf16[2,2,2,512,384]{4,3,2,1,0:T(8,128)(2,1)} %gain.3, f32[512,8]{1,0:T(8,128)} %bitcast.30, f32[8,384]{1,0:T(8,128)} %maximum_maximum_fusion.1.lanes), custom_call_target="tpu_custom_call" | custom-call | flops 15728640 | bytes 3200000 | tf_op jit(solution)/shard_map/phasor_own/pallas_call | solution.py:94
  26.5 1.2 copy-done.10
  27.7 7.9 %model_parts.1 = (f32[2,2,64,512]{3,2,1,0:T(8,128)}, bf16[2,2,64,512]{3,2,1,0:T(8,128)(2,1)}, bf16[2,2,64,512]{3,2,1,0:T(8,128)(2,1)}, bf16[2,2,64,512]{3,2,1,0:T(8,128)(2,1)}) custom-call(s32[3]{0:T(128)} %pad_add_fusion.ids, bf16[2,528,768]{2,1,0:T(8,128)(2,1)} %phasor_own.1.own, bf16[2,528,768]{2,1,0:T(8,128)(2,1)} %copy-done.10), custom_call_target="tpu_custom_call" | custom-call | flops 3221225472 | bytes 5000000 | tf_op jit(solution)/shard_map/model_parts/pallas_call | solution.py:169
  35.6 3.3 %collective-permute-start.2 = (bf16[2,2,64,512]{3,2,1,0:T(8,128)(2,1)}, bf16[2,2,64,512]{3,2,1,0:T(8,128)(2,1)S(1)}, u32[]{:S(2)}, u32[]{:S(2)}) collective-permute-start(bf16[2,2,64,512]{3,2,1,0:T(8,128)(2,1)} %get-tuple-element.13), channel_id=1, source_target_pairs={{0,32},{8,40},{16,48},{24,56},{32,0},{40,8},{48,16},{56,24},{64,96... | collective-permute-start | bytes 786440 | tf_op jit(solution)/shard_map/ppermute | solution.py:449
  40.9 5.6 %collective-permute-done.2 = bf16[2,2,64,512]{3,2,1,0:T(8,128)(2,1)S(1)} collective-permute-done((bf16[2,2,64,512]{3,2,1,0:T(8,128)(2,1)}, bf16[2,2,64,512]{3,2,1,0:T(8,128)(2,1)S(1)}, u32[]{:S(2)}, u32[]{:S(2)}) %collective-permute-start.2) | collective-permute-done | bytes 262176 | tf_op jit(solution)/shard_map/ppermute | solution.py:449
  46.5 5.2 %collective-permute-done.3 = bf16[2,2,64,512]{3,2,1,0:T(8,128)(2,1)S(1)} collective-permute-done((bf16[2,2,64,512]{3,2,1,0:T(8,128)(2,1)}, bf16[2,2,64,512]{3,2,1,0:T(8,128)(2,1)S(1)}, u32[]{:S(2)}, u32[]{:S(2)}) %collective-permute-start.3) | collective-permute-done | bytes 262176 | tf_op jit(solution)/shard_map/ppermute | solution.py:449
  52.3 2.0 %collective-permute-start.5 = (bf16[2,64,512]{2,1,0:T(8,128)(2,1)S(1)}, bf16[2,64,512]{2,1,0:T(8,128)(2,1)S(1)}, u32[]{:S(2)}, u32[]{:S(2)}) collective-permute-start(bf16[2,64,512]{2,1,0:T(8,128)(2,1)S(1)} %fusion.3), channel_id=1, source_target_pairs={{0,64},{8,72},{16,80},{24,88},{32,96},{40,104},{48,112},{56,120},{... | collective-permute-start | bytes 393224 | tf_op jit(solution)/shard_map/ppermute | solution.py:453
  55.0 2.5 %observed_parts.1 = (f32[2,64,512]{2,1,0:T(8,128)}, f32[2,64,512]{2,1,0:T(8,128)}) custom-call(s32[3]{0:T(128)} %pad_add_fusion.ids, f32[6,32,512]{2,1,0:T(8,128)} %get-tuple-element.21.own, f32[6,32,512]{2,1,0:T(8,128)} %copy-done.7), custom_call_target="tpu_custom_call" | custom-call | flops 1000000 | bytes 1500000 | tf_op jit(solution)/shard_map/observed_parts/pallas_call | solution.py:251
  57.7 1.8 %fusion.4 = (bf16[2,64,512]{2,1,0:T(8,128)(2,1)S(1)}, f32[2,64,512]{2,1,0:T(8,128)}) fusion(f32[2,64,512]{2,1,0:T(8,128)} %get-tuple-element.10, f32[2,64,512]{2,1,0:T(8,128)} %get-tuple-element.11, bf16[2,64,512]{2,1,0:T(8,128)(2,1)S(1)} %collective-permute-done.5, f32[2,2,64,512]{3,2,1,0:T(8,128)S(1)} %convert_add_fusion), kind=kLoop, calls=%fused_computation.17 | loop fusion | flops 327680 | bytes 1310720 | tf_op jit(solution)/shard_map/convert_element_type | solution.py:455
  59.5 1.7 %collective-permute-start.6 = (bf16[2,64,512]{2,1,0:T(8,128)(2,1)S(1)}, bf16[2,64,512]{2,1,0:T(8,128)(2,1)S(1)}, u32[]{:S(2)}, u32[]{:S(2)}) collective-permute-start(bf16[2,64,512]{2,1,0:T(8,128)(2,1)S(1)} %get-tuple-element.18), channel_id=1, source_target_pairs={{0,64},{8,72},{16,80},{24,88},{32,96},{40,104},{48,112},{56,120},{... | collective-permute-start | bytes 393224 | tf_op jit(solution)/shard_map/ppermute | solution.py:456
  61.2 3.2 %collective-permute-done.6 = bf16[2,64,512]{2,1,0:T(8,128)(2,1)S(1)} collective-permute-done((bf16[2,64,512]{2,1,0:T(8,128)(2,1)S(1)}, bf16[2,64,512]{2,1,0:T(8,128)(2,1)S(1)}, u32[]{:S(2)}, u32[]{:S(2)}) %collective-permute-start.6) | collective-permute-done | bytes 131104 | tf_op jit(solution)/shard_map/ppermute | solution.py:456
  64.5 1.6 %collective-permute-start.7 = (bf16[2,2,64,512]{3,2,1,0:T(8,128)(2,1)S(1)}, bf16[2,2,64,512]{3,2,1,0:T(8,128)(2,1)S(1)}, u32[]{:S(2)}, u32[]{:S(2)}) collective-permute-start(bf16[2,2,64,512]{3,2,1,0:T(8,128)(2,1)S(1)} %pad_maximum_fusion.1.here), channel_id=1, source_target_pairs={{0,16},{8,24},{16,0},{24,8},{32,48},{40,56},{48,32},{56,40},{64,80... | collective-permute-start | bytes 786440 | tf_op jit(solution)/shard_map/ppermute | solution.py:459
  66.1 1.5 %collective-permute-start.8 = (bf16[2,2,64,512]{3,2,1,0:T(8,128)(2,1)S(1)}, bf16[2,2,64,512]{3,2,1,0:T(8,128)(2,1)S(1)}, u32[]{:S(2)}, u32[]{:S(2)}) collective-permute-start(bf16[2,2,64,512]{3,2,1,0:T(8,128)(2,1)S(1)} %pad_maximum_fusion.1.here), channel_id=1, source_target_pairs={{0,48},{8,56},{16,32},{24,40},{32,16},{40,24},{48,0},{56,8},{64,11... | collective-permute-start | bytes 786440 | tf_op jit(solution)/shard_map/ppermute | solution.py:458
  67.6 1.4 %collective-permute-start.9 = (bf16[2,2,64,512]{3,2,1,0:T(8,128)(2,1)S(1)}, bf16[2,2,64,512]{3,2,1,0:T(8,128)(2,1)S(1)}, u32[]{:S(2)}, u32[]{:S(2)}) collective-permute-start(bf16[2,2,64,512]{3,2,1,0:T(8,128)(2,1)S(1)} %pad_maximum_fusion.1.here), channel_id=1, source_target_pairs={{0,32},{8,40},{16,48},{24,56},{32,0},{40,8},{48,16},{56,24},{64,96... | collective-permute-start | bytes 786440 | tf_op jit(solution)/shard_map/ppermute | solution.py:457
  69.0 4.6 %collective-permute-done.7.one = bf16[2,2,64,512]{3,2,1,0:T(8,128)(2,1)S(1)} collective-permute-done((bf16[2,2,64,512]{3,2,1,0:T(8,128)(2,1)S(1)}, bf16[2,2,64,512]{3,2,1,0:T(8,128)(2,1)S(1)}, u32[]{:S(2)}, u32[]{:S(2)}) %collective-permute-start.7) | collective-permute-done | bytes 262176 | tf_op jit(solution)/shard_map/ppermute | solution.py:459
  73.6 5.6 %collective-permute-done.8.two = bf16[2,2,64,512]{3,2,1,0:T(8,128)(2,1)S(1)} collective-permute-done((bf16[2,2,64,512]{3,2,1,0:T(8,128)(2,1)S(1)}, bf16[2,2,64,512]{3,2,1,0:T(8,128)(2,1)S(1)}, u32[]{:S(2)}, u32[]{:S(2)}) %collective-permute-start.8) | collective-permute-done | bytes 262176 | tf_op jit(solution)/shard_map/ppermute | solution.py:458
  80.0 2.8 %whole_rows.1 = (f32[4,32,512]{2,1,0:T(8,128)}, f32[4,32,512]{2,1,0:T(8,128)}) custom-call(s32[3]{0:T(128)} %pad_add_fusion.ids, f32[2,64,512]{2,1,0:T(8,128)} %get-tuple-element.19.resid, bf16[2,2,64,512]{3,2,1,0:T(8,128)(2,1)} %copy-done, bf16[2,2,64,512]{3,2,1,0:T(8,128)(2,1)} %copy-done.2, bf16[2,2,64,512]{3,2,1,0:T(8,128)(2,1)} %copy-done.3, ...), custom_call_target="tpu_custom_call" | custom-call | flops 2000000 | bytes 1500000 | tf_op jit(solution)/shard_map/whole_rows/pallas_call | solution.py:363
  82.8 14.6 %direction_parts.1.parts = bf16[4,4,2,2,64,512]{5,4,3,2,1,0:T(8,128)(2,1)} custom-call(s32[3]{0:T(128)} %pad_add_fusion.ids, bf16[2,528,768]{2,1,0:T(8,128)(2,1)} %phasor_own.1.own, bf16[2,528,768]{2,1,0:T(8,128)(2,1)} %copy-done.10), custom_call_target="tpu_custom_call" | custom-call | flops 6442450944 | bytes 8000000 | tf_op jit(solution)/shard_map/direction_parts/pallas_call | solution.py:213
  97.4 6.2 %gradient_parts.1 = bf16[128,16,128]{2,1,0:T(8,128)(2,1)} custom-call(s32[3]{0:T(128)} %pad_add_fusion.ids, f32[2]{0:T(128)} %freq.5, bf16[2,2,64,512]{3,2,1,0:T(8,128)(2,1)} %copy-done, bf16[2,2,64,512]{3,2,1,0:T(8,128)(2,1)} %copy-done.2, bf16[2,2,64,512]{3,2,1,0:T(8,128)(2,1)} %copy-done.3, bf16[2,2,64,512]{3,2,1,0:T(8,128)(2,1)} %copy-done.4, ...), custom_call_target="tpu_custom_call" | custom-call | flops 10000000 | bytes 6000000 | tf_op jit(solution)/shard_map/gradient_parts/pallas_call | solution.py:306
  103.5 9.3 %all-to-all-start = ((bf16[128,16,128]{2,1,0:T(8,128)(2,1)}), bf16[128,16,128]{2,1,0:T(8,128)(2,1)S(1)}, u32[]{:S(2)}, u32[]{:S(2)}) async-start(bf16[128,16,128]{2,1,0:T(8,128)(2,1)} %gradient_parts.1), calls=%async_computation | async-start | bytes 1048576 | tf_op jit(solution)/shard_map/all_to_all | solution.py:464
  114.4 11.6 %all-to-all-done.grads = bf16[128,16,128]{2,1,0:T(8,128)(2,1)S(1)} async-done(((bf16[128,16,128]{2,1,0:T(8,128)(2,1)}), bf16[128,16,128]{2,1,0:T(8,128)(2,1)S(1)}, u32[]{:S(2)}, u32[]{:S(2)}) %all-to-all-start) | async-done | bytes 524320 | tf_op jit(solution)/shard_map/all_to_all | solution.py:464
  126.8 2.9 %updated_rows.1 = f32[2,512]{1,0:T(2,128)} custom-call(s32[3]{0:T(128)} %pad_add_fusion.ids, bf16[128,16,128]{2,1,0:T(8,128)(2,1)} %copy-done.1, f32[512,512]{1,0:T(8,128)} %kernel.1, f32[2,512]{1,0:T(2,128)} %screen.1), custom_call_target="tpu_custom_call" | custom-call | flops 200000000 | bytes 1500000 | tf_op jit(solution)/shard_map/updated_rows/pallas_call | solution.py:393
  (56 shorter events, 11.5 us)
Async XLA Ops:
  6.5 9.9 %copy-start.9 = (s32[32,2,512]{2,1,0:T(2,128)S(1)}, s32[32,2,512]{2,1,0:T(2,128)}, u32[]{:S(2)}) copy-start(s32[32,2,512]{2,1,0:T(2,128)} %param.11) | copy-start | bytes 393220
  6.5 10.0 %copy-start.6 = (f32[32,2,2,2,512]{4,3,2,1,0:T(2,128)S(1)}, f32[32,2,2,2,512]{4,3,2,1,0:T(2,128)}, u32[]{:S(2)}) copy-start(f32[32,2,2,2,512]{4,3,2,1,0:T(2,128)} %param.10) | copy-start | bytes 1572868
  16.4 10.2 %collective-permute-start.1 = (bf16[2,528,768]{2,1,0:T(8,128)(2,1)}, bf16[2,528,768]{2,1,0:T(8,128)(2,1)S(1)}, u32[]{:S(2)}, u32[]{:S(2)}) collective-permute-start(bf16[2,528,768]{2,1,0:T(8,128)(2,1)} %phasor_send.1), channel_id=1, source_target_pairs={{0,8},{8,0},{16,24},{24,16},{32,40},{40,32},{48,56},{56,48},{64,72... | collective-permute-start | bytes 4866056 | tf_op jit(solution)/shard_map/ppermute | solution.py:435
  26.5 1.2 copy-start.10
  35.6 10.9 %collective-permute-start.2 = (bf16[2,2,64,512]{3,2,1,0:T(8,128)(2,1)}, bf16[2,2,64,512]{3,2,1,0:T(8,128)(2,1)S(1)}, u32[]{:S(2)}, u32[]{:S(2)}) collective-permute-start(bf16[2,2,64,512]{3,2,1,0:T(8,128)(2,1)} %get-tuple-element.13), channel_id=1, source_target_pairs={{0,32},{8,40},{16,48},{24,56},{32,0},{40,8},{48,16},{56,24},{64,96... | collective-permute-start | bytes 786440 | tf_op jit(solution)/shard_map/ppermute | solution.py:449
  38.9 12.8 %collective-permute-start.3 = (bf16[2,2,64,512]{3,2,1,0:T(8,128)(2,1)}, bf16[2,2,64,512]{3,2,1,0:T(8,128)(2,1)S(1)}, u32[]{:S(2)}, u32[]{:S(2)}) collective-permute-start(bf16[2,2,64,512]{3,2,1,0:T(8,128)(2,1)} %get-tuple-element.14), channel_id=1, source_target_pairs={{0,48},{8,56},{16,32},{24,40},{32,16},{40,24},{48,0},{56,8},{64,11... | collective-permute-start | bytes 786440 | tf_op jit(solution)/shard_map/ppermute | solution.py:449
  39.9 12.2 %collective-permute-start.4 = (bf16[2,2,64,512]{3,2,1,0:T(8,128)(2,1)}, bf16[2,2,64,512]{3,2,1,0:T(8,128)(2,1)S(1)}, u32[]{:S(2)}, u32[]{:S(2)}) collective-permute-start(bf16[2,2,64,512]{3,2,1,0:T(8,128)(2,1)} %get-tuple-element.15), channel_id=1, source_target_pairs={{0,16},{8,24},{16,0},{24,8},{32,48},{40,56},{48,32},{56,40},{64,80... | collective-permute-start | bytes 786440 | tf_op jit(solution)/shard_map/ppermute | solution.py:449
  40.0 12.1 %copy-start.5 = (f32[2,2,64,512]{3,2,1,0:T(8,128)S(1)}, f32[2,2,64,512]{3,2,1,0:T(8,128)}, u32[]{:S(2)}) copy-start(f32[2,2,64,512]{3,2,1,0:T(8,128)} %get-tuple-element.12) | copy-start | bytes 1572868
  40.9 13.4 %collective-permute-start = (f32[6,32,512]{2,1,0:T(8,128)S(1)}, f32[6,32,512]{2,1,0:T(8,128)S(1)}, u32[]{:S(2)}, u32[]{:S(2)}) collective-permute-start(f32[6,32,512]{2,1,0:T(8,128)S(1)} %get-tuple-element.20), channel_id=1, source_target_pairs={{0,8},{8,0},{16,24},{24,16},{32,40},{40,32},{48,56},{56,48},{64,72... | collective-permute-start | bytes 1179656 | tf_op jit(solution)/shard_map/ppermute | solution.py:444
  52.3 5.4 %collective-permute-start.5 = (bf16[2,64,512]{2,1,0:T(8,128)(2,1)S(1)}, bf16[2,64,512]{2,1,0:T(8,128)(2,1)S(1)}, u32[]{:S(2)}, u32[]{:S(2)}) collective-permute-start(bf16[2,64,512]{2,1,0:T(8,128)(2,1)S(1)} %fusion.3), channel_id=1, source_target_pairs={{0,64},{8,72},{16,80},{24,88},{32,96},{40,104},{48,112},{56,120},{... | collective-permute-start | bytes 393224 | tf_op jit(solution)/shard_map/ppermute | solution.py:453
  54.3 0.7 copy-start.7
  59.5 5.0 %collective-permute-start.6 = (bf16[2,64,512]{2,1,0:T(8,128)(2,1)S(1)}, bf16[2,64,512]{2,1,0:T(8,128)(2,1)S(1)}, u32[]{:S(2)}, u32[]{:S(2)}) collective-permute-start(bf16[2,64,512]{2,1,0:T(8,128)(2,1)S(1)} %get-tuple-element.18), channel_id=1, source_target_pairs={{0,64},{8,72},{16,80},{24,88},{32,96},{40,104},{48,112},{56,120},{... | collective-permute-start | bytes 393224 | tf_op jit(solution)/shard_map/ppermute | solution.py:456
  64.5 14.7 %copy-start = (bf16[2,2,64,512]{3,2,1,0:T(8,128)(2,1)}, bf16[2,2,64,512]{3,2,1,0:T(8,128)(2,1)S(1)}, u32[]{:S(2)}) copy-start(bf16[2,2,64,512]{3,2,1,0:T(8,128)(2,1)S(1)} %pad_maximum_fusion.1.here) | copy-start | bytes 786436
  64.5 9.1 %collective-permute-start.7 = (bf16[2,2,64,512]{3,2,1,0:T(8,128)(2,1)S(1)}, bf16[2,2,64,512]{3,2,1,0:T(8,128)(2,1)S(1)}, u32[]{:S(2)}, u32[]{:S(2)}) collective-permute-start(bf16[2,2,64,512]{3,2,1,0:T(8,128)(2,1)S(1)} %pad_maximum_fusion.1.here), channel_id=1, source_target_pairs={{0,16},{8,24},{16,0},{24,8},{32,48},{40,56},{48,32},{56,40},{64,80... | collective-permute-start | bytes 786440 | tf_op jit(solution)/shard_map/ppermute | solution.py:459
  66.1 13.1 %collective-permute-start.8 = (bf16[2,2,64,512]{3,2,1,0:T(8,128)(2,1)S(1)}, bf16[2,2,64,512]{3,2,1,0:T(8,128)(2,1)S(1)}, u32[]{:S(2)}, u32[]{:S(2)}) collective-permute-start(bf16[2,2,64,512]{3,2,1,0:T(8,128)(2,1)S(1)} %pad_maximum_fusion.1.here), channel_id=1, source_target_pairs={{0,48},{8,56},{16,32},{24,40},{32,16},{40,24},{48,0},{56,8},{64,11... | collective-permute-start | bytes 786440 | tf_op jit(solution)/shard_map/ppermute | solution.py:458
  67.6 11.6 %collective-permute-start.9 = (bf16[2,2,64,512]{3,2,1,0:T(8,128)(2,1)S(1)}, bf16[2,2,64,512]{3,2,1,0:T(8,128)(2,1)S(1)}, u32[]{:S(2)}, u32[]{:S(2)}) collective-permute-start(bf16[2,2,64,512]{3,2,1,0:T(8,128)(2,1)S(1)} %pad_maximum_fusion.1.here), channel_id=1, source_target_pairs={{0,32},{8,40},{16,48},{24,56},{32,0},{40,8},{48,16},{56,24},{64,96... | collective-permute-start | bytes 786440 | tf_op jit(solution)/shard_map/ppermute | solution.py:457
  73.6 5.6 %copy-start.2 = (bf16[2,2,64,512]{3,2,1,0:T(8,128)(2,1)}, bf16[2,2,64,512]{3,2,1,0:T(8,128)(2,1)S(1)}, u32[]{:S(2)}) copy-start(bf16[2,2,64,512]{3,2,1,0:T(8,128)(2,1)S(1)} %collective-permute-done.7.one) | copy-start | bytes 786436
  79.2 0.7 copy-start.3
  79.2 0.8 copy-start.4
  82.8 30.0 %collective-permute-start.10 = (f32[4,32,512]{2,1,0:T(8,128)}, f32[4,32,512]{2,1,0:T(8,128)S(1)}, u32[]{:S(2)}, u32[]{:S(2)}) collective-permute-start(f32[4,32,512]{2,1,0:T(8,128)} %get-tuple-element.17), channel_id=1, source_target_pairs={{0,8},{8,0},{16,24},{24,16},{32,40},{40,32},{48,56},{56,48},{64,72... | collective-permute-start | bytes 786440 | tf_op jit(solution)/shard_map/ppermute | solution.py:463
  97.4 15.5 %copy-start.8 = (f32[4,32,512]{2,1,0:T(8,128)S(1)}, f32[4,32,512]{2,1,0:T(8,128)}, u32[]{:S(2)}) copy-start(f32[4,32,512]{2,1,0:T(8,128)} %get-tuple-element.16) | copy-start | bytes 786436
  103.5 22.5 %all-to-all-start = ((bf16[128,16,128]{2,1,0:T(8,128)(2,1)}), bf16[128,16,128]{2,1,0:T(8,128)(2,1)S(1)}, u32[]{:S(2)}, u32[]{:S(2)}) async-start(bf16[128,16,128]{2,1,0:T(8,128)(2,1)} %gradient_parts.1), calls=%async_computation | async-start | bytes 1048576 | tf_op jit(solution)/shard_map/all_to_all | solution.py:464
  126.0 0.8 copy-start.1

commit v2 on v1

v2 whole, which is shorter than its diff:
```python
import functools
import math

import jax
import jax.numpy as jnp
from jax import lax
from jax.experimental import pallas as pl
from jax.experimental.pallas import tpu as pltpu
from jax.sharding import PartitionSpec as P

step_size = 0.3
epsilon = 1e-06
highest = lax.Precision.HIGHEST
bf16 = jnp.bfloat16
f32 = jnp.float32

SIN_COEF = (4.44288292, -7.3082457, 3.60635441, -0.84611289, 0.10982699)
COS_COEF = (1.4142135, -6.97885099, 5.73946117, -1.88356299, 0.31069819)
ROUNDER = 12582912.0
CHUNK = 32
MIB = 1024 * 1024
NT = (((1,), (1,)), ((), ()))


def y_partner(rel, y):
    if rel == 0:
        return y
    if rel == 1:
        return y + 1 - 2 * (y % 2)
    if rel == 2:
        return 3 - y
    return (y + 2) % 4


def dir_perm(rel, flip_z=False, flip_core=False):
    pairs = []
    for index in range(16):
        z, y, core = index // 8, (index // 2) % 4, index % 2
        z = 1 - z if flip_z else z
        core = 1 - core if flip_core else core
        pairs.append((index, z * 8 + y_partner(rel, y) * 2 + core))
    return pairs


ANY = pl.BlockSpec(memory_space=pl.ANY)
WHOLE = pl.BlockSpec(memory_space=pltpu.VMEM)
SCALARS = pl.BlockSpec(memory_space=pltpu.SMEM)


def position():
    index = lax.axis_index("dir")
    return index % 2, (index // 2) % 4, index // 8


def phasor_kernel(send, freq, gain, uv, screen, lm, flux, direction, out, held, sems):
    core, _, _ = position()
    channel = 1 - core if send else core
    stations, sources = gain.shape[3], gain.shape[4]
    half = stations // 2
    copies = []
    for moment in range(2):
        for part in range(2):
            rows = pl.ds(part * half, half)
            copies.append(
                pltpu.make_async_copy(
                    gain.at[channel, moment, :, rows, :],
                    held.at[moment, :, rows, :],
                    sems.at[moment * 2 + part],
                )
            )
    for copy in copies:
        copy.start()
    ratio = freq[channel]
    along = lm[0:1, :] * ratio
    across = lm[1:2, :] * ratio
    amp = jnp.sqrt(flux[...])
    second = direction[...] > 0
    per_turn = 1.0 / (2.0 * math.pi * ratio)
    by_station = jnp.concatenate(
        [uv[0], uv[1], screen[...] * per_turn, jnp.zeros((2, stations), f32)], axis=0
    )
    cols = jnp.transpose(by_station)
    mask = jnp.broadcast_to(jnp.where(second, 1.0, 0.0), (16, sources)).astype(bf16)
    for moment in range(2):
        for start in range(0, stations, CHUNK):
            if start % half == 0:
                copies[moment * 2 + start // half].wait()
            rows = slice(start, start + CHUNK)
            col = cols[rows]
            u = col[:, 2 * moment : 2 * moment + 1]
            v = col[:, 2 * moment + 1 : 2 * moment + 2]
            turns = u * along + v * across + jnp.where(second, col[:, 5:6], col[:, 4:5])
            turns = turns - ((turns + ROUNDER) - ROUNDER)
            z = turns * turns
            sin_half = SIN_COEF[4]
            cos_half = COS_COEF[4]
            for power in (3, 2, 1, 0):
                sin_half = sin_half * z + SIN_COEF[power]
                cos_half = cos_half * z + COS_COEF[power]
            sin_half = sin_half * turns
            sin_amp = sin_half * amp
            sine = sin_amp * cos_half
            cosine = amp - sin_amp * sin_half
            gain_re = held[moment, 0, rows, :].astype(f32)
            gain_im = held[moment, 1, rows, :].astype(f32)
            out[moment, rows, 0:sources] = (gain_re * cosine - gain_im * sine).astype(bf16)
            out[moment, rows, sources : 2 * sources] = (
                gain_re * sine + gain_im * cosine
            ).astype(bf16)
        out[moment, stations : stations + 16, 0:sources] = mask
        out[moment, stations : stations + 16, sources : 2 * sources] = mask


def phasor(send, freq, gain, uv, screen, lm, flux, direction):
    stations, sources = gain.shape[3], gain.shape[4]
    return pl.pallas_call(
        functools.partial(phasor_kernel, send),
        in_specs=[SCALARS, ANY] + [WHOLE] * 5,
        out_specs=WHOLE,
        out_shape=jax.ShapeDtypeStruct((2, stations + 16, 2 * sources), bf16),
        scratch_shapes=[
            pltpu.VMEM((2, 2, stations, sources), bf16),
            pltpu.SemaphoreType.DMA((4,)),
        ],
        compiler_params=pltpu.CompilerParams(vmem_limit_bytes=12 * MIB),
        cost_estimate=pl.CostEstimate(
            flops=40 * 2 * stations * sources, bytes_accessed=3200000, transcendentals=0
        ),
        name="phasor_send" if send else "phasor_own",
    )(freq, gain, uv, screen, lm, flux, direction)


def upper_mask():
    row = lax.broadcasted_iota(jnp.int32, (64, 64), 0)
    col = lax.broadcasted_iota(jnp.int32, (64, 64), 1)
    return row < col, row > col


def pack(re, im, odd, keep_re):
    re = jnp.where(odd, re[:, 64:384], re[:, 0:320])
    im = jnp.where(odd, im[:, 64:384], im[:, 0:320])
    upper, _ = upper_mask()
    own = jnp.where(upper, re[:, 0:64], im[:, 0:64])
    far = jnp.where(keep_re, re[:, 256:320], im[:, 256:320])
    return jnp.concatenate([own, re[:, 64:256], far, im[:, 64:256]], axis=1)


def skewed(q):
    half = q.shape[1] // 2
    return jnp.concatenate([q[:, half:], -q[:, :half]], axis=1)


def mm(a, b):
    return lax.dot_general(a, b, NT, preferred_element_type=f32)


def spread_wide(wide, part, value):
    wide[part, :, 0:512] = value
    wide[part, :, 512:768] = value[:, 0:256]


def block_of(wide, part, chip):
    start = pl.multiple_of((chip // 2) * 128, 128)
    return wide[part, pl.ds(pl.multiple_of(chip * 64, 64), 64), pl.ds(start, 384)]


def model_kernel(scaling, own, other, out0, out1, out2, out3, wide):
    _, y, z = position()
    for moment in range(2):
        q_own = own[moment, 0:512, :]
        q_other = other[moment, 0:512, :]
        spread_wide(wide, 0, (mm(q_own, q_own) + mm(q_other, q_other)) * scaling)
        spread_wide(wide, 1, (mm(skewed(q_own), q_own) + mm(skewed(q_other), q_other)) * scaling)
        for rel, out in enumerate((out0, out1, out2, out3)):
            for flip in range(2):
                zz = 1 - z if flip else z
                chip = zz * 4 + y_partner(rel, y)
                out[flip, moment] = pack(
                    block_of(wide, 0, chip), block_of(wide, 1, chip), chip % 2 == 1, zz == 0
                ).astype(out.dtype)


def model_parts(scaling, own, other):
    return pl.pallas_call(
        functools.partial(model_kernel, scaling),
        in_specs=[WHOLE] * 2,
        out_specs=[WHOLE] * 4,
        scratch_shapes=[pltpu.VMEM((2, 512, 768), f32)],
        out_shape=[jax.ShapeDtypeStruct((2, 2, 64, 512), f32)]
        + [jax.ShapeDtypeStruct((2, 2, 64, 512), bf16)] * 3,
        compiler_params=pltpu.CompilerParams(vmem_limit_bytes=16 * MIB),
        cost_estimate=pl.CostEstimate(
            flops=2 * 2 * 4 * 512 * 512 * 768, bytes_accessed=5000000, transcendentals=0
        ),
        name="model_parts",
    )(own, other)


def direction_kernel(moment, own, other, out, whole, first):
    core, y, z = position()
    for source, core_of in ((own, core), (other, 1 - core)):
        q = source[moment, 0:512, :]
        in_first = source[moment, 512:513, :] < 0.5
        q_first = jnp.where(in_first, q, jnp.zeros_like(q))
        spread_wide(whole, 0, mm(q, q))
        spread_wide(whole, 1, mm(skewed(q), q))
        spread_wide(first, 0, mm(q_first, q))
        spread_wide(first, 1, mm(skewed(q_first), q))
        for rel in range(4):
            for flip in range(2):
                zz = 1 - z if flip else z
                chip = zz * 4 + y_partner(rel, y)
                odd = chip % 2 == 1
                keep_im = zz == 0
                all_of = pack(block_of(whole, 1, chip), -block_of(whole, 0, chip), odd, keep_im)
                first_of = pack(block_of(first, 1, chip), -block_of(first, 0, chip), odd, keep_im)
                out[core_of * 2, rel, flip] = first_of.astype(bf16)
                out[core_of * 2 + 1, rel, flip] = (all_of - first_of).astype(bf16)


def direction_parts(moment, own, other):
    return pl.pallas_call(
        functools.partial(direction_kernel, moment),
        in_specs=[WHOLE] * 2,
        out_specs=WHOLE,
        scratch_shapes=[pltpu.VMEM((2, 512, 768), f32)] * 2,
        out_shape=jax.ShapeDtypeStruct((4, 4, 2, 64, 512), bf16),
        compiler_params=pltpu.CompilerParams(vmem_limit_bytes=18 * MIB),
        cost_estimate=pl.CostEstimate(
            flops=2 * 8 * 512 * 512 * 768, bytes_accessed=5000000, transcendentals=0
        ),
        name="direction_parts%d" % moment,
    )(own, other)


def sum_kernel(own, one, two, three, _, stay, send):
    for flip, out in ((0, stay), (1, send)):
        out[...] = (
            own[flip] + one[flip].astype(f32) + two[flip].astype(f32) + three[flip].astype(f32)
        ).astype(out.dtype)


def sum_parts(own, one, two, three, after):
    return pl.pallas_call(
        sum_kernel,
        in_specs=[WHOLE] * 4 + [ANY],
        out_specs=[WHOLE] * 2,
        out_shape=[
            jax.ShapeDtypeStruct(own.shape[1:], f32),
            jax.ShapeDtypeStruct(own.shape[1:], bf16),
        ],
        compiler_params=pltpu.CompilerParams(vmem_limit_bytes=4 * MIB),
        cost_estimate=pl.CostEstimate(flops=500000, bytes_accessed=2500000, transcendentals=0),
        name="sum_parts",
    )(own, one, two, three, after)


def observed_kernel(own, other, obs_out, keep_out, wide):
    core, y, z = position()
    for moment in range(2):
        for part in range(3):
            index = moment * 3 + part
            for rows, source in ((core, own), (1 - core, other)):
                place = pl.ds(pl.multiple_of(rows * 32, 32), 32)
                wide[part, place, 0:512] = source[index]
                wide[part, place, 512:768] = source[index, :, 0:256]
        chip = z * 4 + y
        start = pl.ds(pl.multiple_of((chip // 2) * 128, 128), 384)
        odd = chip % 2 == 1
        obs_out[moment] = pack(wide[0, :, start], wide[1, :, start], odd, z == 0)
        keep = pack(wide[2, :, start], wide[2, :, start], odd, z == 0)
        row = lax.broadcasted_iota(jnp.int32, (64, 512), 0)
        col = lax.broadcasted_iota(jnp.int32, (64, 512), 1)
        keep_out[moment] = jnp.where(row == col, 0.0, keep)


def observed_parts(own, other):
    return pl.pallas_call(
        observed_kernel,
        in_specs=[WHOLE] * 2,
        out_specs=[WHOLE] * 2,
        out_shape=[jax.ShapeDtypeStruct((2, 64, 512), f32)] * 2,
        scratch_shapes=[pltpu.VMEM((3, 64, 768), f32)],
        cost_estimate=pl.CostEstimate(flops=1000000, bytes_accessed=1500000, transcendentals=0),
        compiler_params=pltpu.CompilerParams(vmem_limit_bytes=4 * MIB),
        name="observed_parts",
    )(own, other)


def gradient_kernel(scaling, freq, here, one, two, three, parts0, parts1, out, rows_sum, cols_sum):
    core, y, z = position()
    for rel, source in enumerate((here, one, two, three)):
        for flip in range(2):
            zz = 1 - z if flip else z
            chip = zz * 4 + y_partner(rel, y)
            for start in range(0, 64, 32):
                rows = slice(start, start + 32)
                resid0 = source[flip, 0, rows, :].astype(f32)
                resid1 = source[flip, 1, rows, :].astype(f32)
                for which in range(4):
                    product = resid0 * parts0[which, rel, flip, rows, :].astype(f32)
                    product += resid1 * parts1[which, rel, flip, rows, :].astype(f32)
                    rows_sum[which, pl.ds(pl.multiple_of(chip * 64 + start, 32), 32), :] = (
                        product[:, 0:128] + product[:, 128:256]
                    ) + (product[:, 256:384] + product[:, 384:512])
                    column = (product[0:8] + product[8:16]) + (product[16:24] + product[24:32])
                    if start == 0:
                        cols_sum[which, chip] = column
                    else:
                        cols_sum[which, chip] += column
    near = lax.broadcasted_iota(jnp.int32, (8, 256), 1) < 64
    factor = 2.0 * scaling / freq[core]
    pieces = []
    for which in range(4):
        placed = []
        for odd in range(2):
            total = None
            for chip in range(odd, 8, 2):
                low = cols_sum[which, chip, :, 0:256]
                high = cols_sum[which, chip, :, 256:512]
                folded = [low + jnp.where(near, 0.0, high), jnp.where(near, high, 0.0)]
                quarters = [part[:, at : at + 128] for part in folded for at in (0, 128)]
                turn = (4 - chip // 2) % 4
                quarters = quarters[turn:] + quarters[:turn]
                total = quarters if total is None else [a + b for a, b in zip(total, quarters)]
            placed.append(jnp.concatenate(total, axis=1))
        columns = placed[0] + pltpu.roll(placed[1], 64, 1)
        along_rows = jnp.sum(jnp.transpose(rows_sum[which]), axis=0, keepdims=True)
        grad = (along_rows - jnp.sum(columns, axis=0, keepdims=True)) * factor
        pieces.extend(grad[:, at : at + 128] for at in range(0, 512, 128))
    value = jnp.concatenate(pieces, axis=0).astype(bf16)

    def copy(index, carry):
        out[index] = value
        return carry

    lax.fori_loop(0, out.shape[0], copy, 0, unroll=8)


def gradient_parts(scaling, devices, freq, here, one, two, three, parts0, parts1):
    return pl.pallas_call(
        functools.partial(gradient_kernel, scaling),
        in_specs=[SCALARS] + [WHOLE] * 6,
        out_specs=WHOLE,
        scratch_shapes=[pltpu.VMEM((4, 512, 128), f32), pltpu.VMEM((4, 8, 8, 512), f32)],
        out_shape=jax.ShapeDtypeStruct((devices, 16, 128), bf16),
        compiler_params=pltpu.CompilerParams(vmem_limit_bytes=12 * MIB),
        cost_estimate=pl.CostEstimate(flops=10000000, bytes_accessed=6000000, transcendentals=0),
        name="gradient_parts",
    )(freq, here, one, two, three, parts0, parts1)


def rows_kernel(resid, here, one, two, three, _, own_out, other_out, rolled):
    core, y, z = position()
    chip = z * 4 + y
    upper, lower = upper_mask()
    even = y % 2 == 0
    flip5 = jnp.where(y < 3, 1, 0)
    flip6 = jnp.where(y < 2, 1, 0)
    flip7 = jnp.where(y < 1, 1, 0)
    for moment in range(2):
        own = resid[moment]
        near = own[:, 0:64]
        near_t = jnp.transpose(near)
        zero = jnp.zeros_like(near)
        near_re = jnp.where(upper, near, jnp.where(lower, near_t, zero))
        near_im = jnp.where(lower, near, jnp.where(upper, -near_t, zero))
        far = own[:, 256:320]
        far_t = jnp.transpose(here[1, moment][:, 256:320].astype(f32))
        far_re = jnp.where(z == 0, far, far_t)
        far_im = jnp.where(z == 0, -far_t, far)
        block5 = jnp.where(even, one[flip5, moment].astype(f32), two[flip5, moment].astype(f32))
        block6 = three[flip6, moment].astype(f32)
        block7 = jnp.where(even, two[flip7, moment].astype(f32), one[flip7, moment].astype(f32))
        re = [near_re, own[:, 64:256], far_re]
        im = [near_im, own[:, 320:512], far_im]
        for block, offset in ((block5, 3), (block6, 2), (block7, 1)):
            re.append(jnp.transpose(block[:, 64 * offset : 64 * offset + 64]))
            im.append(-jnp.transpose(block[:, 256 + 64 * offset : 320 + 64 * offset]))
        for part, pieces in enumerate((re, im)):
            index = moment * 2 + part
            rolled[index] = pltpu.roll(jnp.concatenate(pieces, axis=1), chip * 64, 1)
            own_out[index] = rolled[index, pl.ds(pl.multiple_of(core * 32, 32), 32), :]
            other_out[index] = rolled[index, pl.ds(pl.multiple_of((1 - core) * 32, 32), 32), :]


def whole_rows(resid, here, one, two, three, after):
    return pl.pallas_call(
        rows_kernel,
        in_specs=[WHOLE] * 5 + [ANY],
        out_specs=[WHOLE] * 2,
        out_shape=[jax.ShapeDtypeStruct((4, 32, 512), f32)] * 2,
        scratch_shapes=[pltpu.VMEM((4, 64, 512), f32)],
        cost_estimate=pl.CostEstimate(flops=2000000, bytes_accessed=1500000, transcendentals=0),
        compiler_params=pltpu.CompilerParams(vmem_limit_bytes=6 * MIB),
        name="whole_rows",
    )(resid, here, one, two, three, after)


def halves(value):
    high = value.astype(bf16)
    return high, (value - high.astype(f32)).astype(bf16)


def update_kernel(grads, kernel, screen, out, total, smooth):
    core, y, z = position()
    per_chip = grads.shape[0] // 8
    for chip in range(8):
        total[chip * 16 : chip * 16 + 16, :] = jnp.sum(
            grads[chip * per_chip : (chip + 1) * per_chip].astype(f32), axis=0
        )
    gradient = jnp.concatenate(
        [total[pl.ds(piece, 32, stride=4), :] for piece in range(4)], axis=1
    )
    grad_high, grad_low = halves(gradient)
    kern_high, kern_low = halves(kernel[...])
    both = jnp.dot(
        jnp.concatenate([grad_high, grad_low], axis=0), kern_high, preferred_element_type=f32
    )
    value = both[0:32] + (
        both[32:64] + jnp.dot(grad_high, kern_low, preferred_element_type=f32)
    )
    mean_sq = jnp.sum(value * value) / value.size
    smooth[...] = value * (step_size * lax.rsqrt(mean_sq + epsilon))
    row = (z * 4 + y) * 4 + core * 2
    for step in range(2):
        out[step : step + 1, :] = screen[step : step + 1, :] - smooth[pl.ds(row + step, 1), :]


def updated_rows(grads, kernel, screen):
    return pl.pallas_call(
        update_kernel,
        in_specs=[WHOLE] * 3,
        out_specs=WHOLE,
        out_shape=jax.ShapeDtypeStruct(screen.shape, f32),
        scratch_shapes=[pltpu.VMEM((128, 128), f32), pltpu.VMEM((32, 512), f32)],
        compiler_params=pltpu.CompilerParams(vmem_limit_bytes=8 * MIB),
        cost_estimate=pl.CostEstimate(flops=200000000, bytes_accessed=1500000, transcendentals=0),
        name="updated_rows",
    )(grads, kernel, screen)


def body(
    observed,
    flags,
    screen,
    screen_kernel,
    station_uv,
    source_lm,
    source_flux,
    station_gain,
    source_direction,
    freq_ratio,
):
    devices = lax.axis_size("dir") * lax.axis_size("freq")
    stations = screen.shape[1]
    scaling = 1.0 / math.sqrt(source_flux.shape[0] * lax.axis_size("dir"))
    core = position()[0]
    swap = functools.partial(lax.ppermute, axis_name="dir", perm=dir_perm(0, flip_core=True))

    inputs = (
        freq_ratio,
        station_gain,
        station_uv,
        screen,
        source_lm,
        source_flux[None],
        source_direction[None],
    )
    sent = phasor(True, *inputs)
    other = swap(sent)
    own = phasor(False, *inputs)

    keep = flags.astype(f32)[:, None, :, None, :]
    keep = jnp.broadcast_to(keep, (32, 2, 2, 1, stations))
    rows = jnp.concatenate([observed, keep], axis=3)
    rows = jnp.transpose(rows, (1, 2, 3, 0, 4)).reshape(2, 6, 32, stations)
    rows_own = lax.dynamic_index_in_dim(rows, core, 0, keepdims=False)
    rows_sent = lax.dynamic_index_in_dim(rows, 1 - core, 0, keepdims=False)
    rows_other = swap(rows_sent)
    obs, kept = observed_parts(rows_own, rows_other)

    part0, part1, part2, part3 = model_parts(scaling, own, other)
    got = [
        lax.ppermute(part, "dir", dir_perm(rel)) for rel, part in ((1, part1), (2, part2), (3, part3))
    ]
    directions0 = direction_parts(0, own, other)
    stay, send = sum_parts(part0, *got, directions0)
    last = lax.ppermute(send, "dir", dir_perm(0, flip_z=True))
    resid = kept * (obs - (stay + last.astype(f32)))
    half = resid.astype(bf16)
    here = jnp.stack([half, lax.ppermute(half, "dir", dir_perm(0, flip_z=True))])
    three = lax.ppermute(here, "dir", dir_perm(3))
    two = lax.ppermute(here, "dir", dir_perm(2))
    one = lax.ppermute(here, "dir", dir_perm(1))
    directions1 = direction_parts(1, own, other)

    grads = gradient_parts(
        scaling, devices, freq_ratio, here, one, two, three, directions0, directions1
    )
    own_rows, sent_rows = whole_rows(resid, here, one, two, three, grads)
    other_rows = swap(sent_rows)
    grads = lax.all_to_all(grads, ("dir", "freq"), 0, 0, tiled=True)
    updated = updated_rows(grads, screen_kernel, screen)

    first = jnp.where(core == 0, own_rows, other_rows)
    second = jnp.where(core == 0, other_rows, own_rows)
    residual = jnp.stack([first, second]).reshape(2, 2, 2, 32, stations)
    return jnp.transpose(residual, (3, 0, 1, 2, 4)), updated


def solution(mesh):
    placed = (
        P("dir", "freq", None, None, None),
        P("dir", None, None),
        P("dir", None),
        P(),
        P(),
        P(None, "dir"),
        P("dir"),
        P("freq", None, None, None, "dir"),
        P("dir"),
        P("freq"),
    )
    return jax.shard_map(
        body,
        mesh=mesh,
        in_specs=placed,
        out_specs=(P("dir", "freq", None, None, None), P("dir", None)),
        check_vma=False,
    )
```

time: 130 us -> 92.3 us (0.71)
  Pallas kernels: 56.4 us -> 32.6 us
  waiting for transfers between devices: 36.3 us -> 23.8 us
  other arithmetic: 6.6 us -> 2.4 us
  starting transfers between devices: 21.9 us -> 23.2 us
    pallas_call x8 -> x10, Pallas kernels: 56.4 us -> 32.6 us  [the longest x2 13.2 us: direction_parts(): pl.pallas_call(functools.partial(direction_kernel, moment), in_specs=[WHO...]
    ppermute x3, waiting for transfers between devices: 11.2 us -> 5.29 us  [body(): lax.ppermute(part, 'dir', dir_perm(rel))]
    ppermute x1, waiting for transfers between devices: 5.61 us -> 0.01 us  [body(): two = lax.ppermute(here, 'dir', dir_perm(2))]
    ppermute x1, waiting for transfers between devices: 4.58 us -> 0.01 us  [body(): one = lax.ppermute(here, 'dir', dir_perm(1))]
    unnamed x23 -> x25, local copies, waits for them, and re-layouts: 3.87 us -> 6.95 us
    ppermute x1, waiting for transfers between devices: 0.09 us -> 2.39 us  [body(): last = lax.ppermute(send, 'dir', dir_perm(0, flip_z=True))]
    concatenate x2 -> x0, other arithmetic: 2.11 us -> none  [the longest x1 1.35 us: body(): jnp.concatenate([source_lm, source_flux[None], source_direction.astype(f3...]
    convert_element_type x1, other arithmetic: 1.81 us -> 0.09 us  [body(): half = resid.astype(bf16)]
  transfers between devices with their start and end apart: 12 -> 12, of which waited for: 8 -> 6; matrix products, arithmetic and copies ran while one was open for 2% -> 6% of each run, Pallas kernels for 25% -> 25%
where the time goes in v2:
time: 92.3 us; the launch traced here: 91.8 us
  Pallas kernels  32.6 us (35%)
  waiting for transfers between devices  23.8 us (26%)
  starting transfers between devices  23.2 us (25%)
  local copies, waits for them, and re-layouts  8.84 us (10%)
  other arithmetic  2.4 us (3%)
    pallas_call x2, Pallas kernels, direction_parts(): pl.pallas_call(functools.partial(direction_kernel, moment), in_specs=[WHO...  13.2 us
    all_to_all x1, waiting for transfers between devices, body(): grads = lax.all_to_all(grads, ('dir', 'freq'), 0, 0, tiled=True)  11.6 us
    all_to_all x1, starting transfers between devices, body(): grads = lax.all_to_all(grads, ('dir', 'freq'), 0, 0, tiled=True)  9.72 us
    pallas_call x2, Pallas kernels, phasor(): pl.pallas_call(functools.partial(phasor_kernel, send), in_specs=[SCALARS,...  8.19 us
    unnamed x25, local copies, waits for them, and re-layouts  6.95 us
    pallas_call x1, Pallas kernels, model_parts(): pl.pallas_call(functools.partial(model_kernel, scaling), in_specs=[WHOLE]...  5.71 us
    ppermute x3, waiting for transfers between devices, body(): lax.ppermute(part, 'dir', dir_perm(rel))  5.29 us
    ppermute x3, starting transfers between devices, body(): lax.ppermute(part, 'dir', dir_perm(rel))  4.62 us
  transfers between devices with their start and end apart: 12, of which 6 were waited for; matrix products, arithmetic and copies ran while one was open for 6% of the time, Pallas kernels for 25%

profile of v2, /device:TPU:0, one launch (start us, length us, event | category | flops | bytes accessed | tf_op | source)
XLA Modules:
  0.0 91.8 jit_solution(17457531540398688187)
XLA Ops:
  2.0 1.9 %copy-done = bf16[2,2,2,512,384]{4,3,2,1,0:T(8,128)(2,1)S(1)} copy-done((bf16[2,2,2,512,384]{4,3,2,1,0:T(8,128)(2,1)S(1)}, bf16[2,2,2,512,384]{4,3,2,1,0:T(8,128)(2,1)}, u32[]{:S(2)}) %copy-start) | copy-done | bytes 3145752
  6.6 4.7 %phasor_send.1 = bf16[2,528,768]{2,1,0:T(8,128)(2,1)} custom-call(f32[2]{0:T(128)S(1)} %copy-done.9, bf16[2,2,2,512,384]{4,3,2,1,0:T(8,128)(2,1)S(1)} %copy-done, f32[2,2,512]{2,1,0:T(2,128)S(1)} %copy-done.5, f32[2,512]{1,0:T(2,128)S(1)} %copy-done.3, f32[2,384]{1,0:T(2,128)S(1)} %copy-done.7, f32[1,384]{1,0:T(1,128)S(1)} %broadcast_in_dim.13.flux, ...), custom_call_target="tpu_custom_call" | custom-call | flops 15728640 | bytes 3200000 | tf_op jit(solution)/shard_map/phasor_send/pallas_call | solution.py:116
  11.6 2.3 %copy.17 = f32[32,2,2,2,512]{4,0,3,2,1:T(8,128)} copy(f32[32,2,2,2,512]{4,3,2,1,0:T(2,128)} %param.10) | data formatting | bytes 1048576 | tf_op args[0]
  13.9 1.1 %pad_maximum_fusion = f32[32,2,2,3,512]{4,0,3,2,1:T(8,128)S(1)} fusion(f32[32,2,2,1,512]{4,0,3,2,1:T(8,128)S(1)} %broadcast_in_dim.12, f32[32,2,2,2,512]{4,0,3,2,1:T(8,128)} %copy.17), kind=kLoop, calls=%fused_computation | loop fusion | flops 196608 | bytes 1572864 | tf_op jit(solution)/shard_map/concatenate | solution.py:476
  15.7 3.5 %phasor_own.1.own = bf16[2,528,768]{2,1,0:T(8,128)(2,1)S(1)} custom-call(f32[2]{0:T(128)S(1)} %copy-done.10, bf16[2,2,2,512,384]{4,3,2,1,0:T(8,128)(2,1)S(1)} %copy-done.1, f32[2,2,512]{2,1,0:T(2,128)S(1)} %copy-done.6, f32[2,512]{1,0:T(2,128)S(1)} %copy-done.4, f32[2,384]{1,0:T(2,128)S(1)} %copy-done.8, f32[1,384]{1,0:T(1,128)S(1)} %broadcast_in_dim.13.flux, ...), custom_call_target="tpu_custom_call" | custom-call | flops 15728640 | bytes 3200000 | tf_op jit(solution)/shard_map/phasor_own/pallas_call | solution.py:116
  19.2 5.7 %model_parts.1 = (f32[2,2,64,512]{3,2,1,0:T(8,128)S(1)}, bf16[2,2,64,512]{3,2,1,0:T(8,128)(2,1)S(1)}, bf16[2,2,64,512]{3,2,1,0:T(8,128)(2,1)S(1)}, bf16[2,2,64,512]{3,2,1,0:T(8,128)(2,1)S(1)}) custom-call(bf16[2,528,768]{2,1,0:T(8,128)(2,1)S(1)} %phasor_own.1.own, bf16[2,528,768]{2,1,0:T(8,128)(2,1)} %collective-permute-done.1.other), custom_call_target="tpu_custom_call" | custom-call | flops 3221225472 | bytes 5000000 | tf_op jit(solution)/shard_map/model_parts/pallas_call | solution.py:184
  24.9 1.7 %collective-permute-start.2 = (bf16[2,2,64,512]{3,2,1,0:T(8,128)(2,1)S(1)}, bf16[2,2,64,512]{3,2,1,0:T(8,128)(2,1)S(1)}, u32[]{:S(2)}, u32[]{:S(2)}) collective-permute-start(bf16[2,2,64,512]{3,2,1,0:T(8,128)(2,1)S(1)} %get-tuple-element.15), channel_id=1, source_target_pairs={{0,16},{8,24},{16,0},{24,8},{32,48},{40,56},{48,32},{56,40},{64,80... | collective-permute-start | bytes 786440 | tf_op jit(solution)/shard_map/ppermute | solution.py:485
  26.7 2.2 %collective-permute-start.3 = (bf16[2,2,64,512]{3,2,1,0:T(8,128)(2,1)S(1)}, bf16[2,2,64,512]{3,2,1,0:T(8,128)(2,1)S(1)}, u32[]{:S(2)}, u32[]{:S(2)}) collective-permute-start(bf16[2,2,64,512]{3,2,1,0:T(8,128)(2,1)S(1)} %get-tuple-element.16), channel_id=1, source_target_pairs={{0,48},{8,56},{16,32},{24,40},{32,16},{40,24},{48,0},{56,8},{64,11... | collective-permute-start | bytes 786440 | tf_op jit(solution)/shard_map/ppermute | solution.py:485
  29.6 6.6 %direction_parts0.1._.parts0 = bf16[4,4,2,64,512]{4,3,2,1,0:T(8,128)(2,1)S(1)} custom-call(bf16[2,528,768]{2,1,0:T(8,128)(2,1)S(1)} %phasor_own.1.own, bf16[2,528,768]{2,1,0:T(8,128)(2,1)} %collective-permute-done.1.other), custom_call_target="tpu_custom_call" | custom-call | flops 3221225472 | bytes 5000000 | tf_op jit(solution)/shard_map/direction_parts0/pallas_call | solution.py:222
  36.2 3.8 %collective-permute-done.3.two = bf16[2,2,64,512]{3,2,1,0:T(8,128)(2,1)S(1)} collective-permute-done((bf16[2,2,64,512]{3,2,1,0:T(8,128)(2,1)S(1)}, bf16[2,2,64,512]{3,2,1,0:T(8,128)(2,1)S(1)}, u32[]{:S(2)}, u32[]{:S(2)}) %collective-permute-start.3) | collective-permute-done | bytes 262176 | tf_op jit(solution)/shard_map/ppermute | solution.py:485
  39.9 1.5 %collective-permute-done.4.three = bf16[2,2,64,512]{3,2,1,0:T(8,128)(2,1)S(1)} collective-permute-done((bf16[2,2,64,512]{3,2,1,0:T(8,128)(2,1)S(1)}, bf16[2,2,64,512]{3,2,1,0:T(8,128)(2,1)S(1)}, u32[]{:S(2)}, u32[]{:S(2)}) %collective-permute-start.4) | collective-permute-done | bytes 262176 | tf_op jit(solution)/shard_map/ppermute | solution.py:485
  41.6 2.0 %collective-permute-start.5 = (bf16[2,64,512]{2,1,0:T(8,128)(2,1)S(1)}, bf16[2,64,512]{2,1,0:T(8,128)(2,1)S(1)}, u32[]{:S(2)}, u32[]{:S(2)}) collective-permute-start(bf16[2,64,512]{2,1,0:T(8,128)(2,1)S(1)} %get-tuple-element.19), channel_id=1, source_target_pairs={{0,64},{8,72},{16,80},{24,88},{32,96},{40,104},{48,112},{56,120},{... | collective-permute-start | bytes 393224 | tf_op jit(solution)/shard_map/ppermute | solution.py:489
  44.2 2.4 %collective-permute-done.5 = bf16[2,64,512]{2,1,0:T(8,128)(2,1)S(1)} collective-permute-done((bf16[2,64,512]{2,1,0:T(8,128)(2,1)S(1)}, bf16[2,64,512]{2,1,0:T(8,128)(2,1)S(1)}, u32[]{:S(2)}, u32[]{:S(2)}) %collective-permute-start.5) | collective-permute-done | bytes 131104 | tf_op jit(solution)/shard_map/ppermute | solution.py:489
  46.7 2.0 %collective-permute-start.6 = (bf16[2,64,512]{2,1,0:T(8,128)(2,1)S(1)}, bf16[2,64,512]{2,1,0:T(8,128)(2,1)S(1)}, u32[]{:S(2)}, u32[]{:S(2)}) collective-permute-start(bf16[2,64,512]{2,1,0:T(8,128)(2,1)S(1)} %get-tuple-element.22), channel_id=1, source_target_pairs={{0,64},{8,72},{16,80},{24,88},{32,96},{40,104},{48,112},{56,120},{... | collective-permute-start | bytes 393224 | tf_op jit(solution)/shard_map/ppermute | solution.py:492
  48.7 3.1 %collective-permute-done.6 = bf16[2,64,512]{2,1,0:T(8,128)(2,1)S(1)} collective-permute-done((bf16[2,64,512]{2,1,0:T(8,128)(2,1)S(1)}, bf16[2,64,512]{2,1,0:T(8,128)(2,1)S(1)}, u32[]{:S(2)}, u32[]{:S(2)}) %collective-permute-start.6) | collective-permute-done | bytes 131104 | tf_op jit(solution)/shard_map/ppermute | solution.py:492
  52.0 2.3 %collective-permute-start.8 = (bf16[2,2,64,512]{3,2,1,0:T(8,128)(2,1)S(1)}, bf16[2,2,64,512]{3,2,1,0:T(8,128)(2,1)S(1)}, u32[]{:S(2)}, u32[]{:S(2)}) collective-permute-start(bf16[2,2,64,512]{3,2,1,0:T(8,128)(2,1)S(1)} %pad_maximum_fusion.1.here), channel_id=1, source_target_pairs={{0,48},{8,56},{16,32},{24,40},{32,16},{40,24},{48,0},{56,8},{64,11... | collective-permute-start | bytes 786440 | tf_op jit(solution)/shard_map/ppermute | solution.py:494
  54.3 1.7 %collective-permute-start.9 = (bf16[2,2,64,512]{3,2,1,0:T(8,128)(2,1)S(1)}, bf16[2,2,64,512]{3,2,1,0:T(8,128)(2,1)S(1)}, u32[]{:S(2)}, u32[]{:S(2)}) collective-permute-start(bf16[2,2,64,512]{3,2,1,0:T(8,128)(2,1)S(1)} %pad_maximum_fusion.1.here), channel_id=1, source_target_pairs={{0,32},{8,40},{16,48},{24,56},{32,0},{40,8},{48,16},{56,24},{64,96... | collective-permute-start | bytes 786440 | tf_op jit(solution)/shard_map/ppermute | solution.py:493
  56.0 6.6 %direction_parts1.1.parts1 = bf16[4,4,2,64,512]{4,3,2,1,0:T(8,128)(2,1)S(1)} custom-call(bf16[2,528,768]{2,1,0:T(8,128)(2,1)S(1)} %phasor_own.1.own, bf16[2,528,768]{2,1,0:T(8,128)(2,1)} %collective-permute-done.1.other), custom_call_target="tpu_custom_call" | custom-call | flops 3221225472 | bytes 5000000 | tf_op jit(solution)/shard_map/direction_parts1/pallas_call | solution.py:222
  62.6 1.4 %collective-permute-done.9.three = bf16[2,2,64,512]{3,2,1,0:T(8,128)(2,1)S(1)} collective-permute-done((bf16[2,2,64,512]{3,2,1,0:T(8,128)(2,1)S(1)}, bf16[2,2,64,512]{3,2,1,0:T(8,128)(2,1)S(1)}, u32[]{:S(2)}, u32[]{:S(2)}) %collective-permute-start.9) | collective-permute-done | bytes 262176 | tf_op jit(solution)/shard_map/ppermute | solution.py:493
  64.1 2.9 %gradient_parts.1._ = bf16[128,16,128]{2,1,0:T(8,128)(2,1)} custom-call(f32[2]{0:T(128)S(1)} %copy-done.10, bf16[2,2,64,512]{3,2,1,0:T(8,128)(2,1)S(1)} %pad_maximum_fusion.1.here, bf16[2,2,64,512]{3,2,1,0:T(8,128)(2,1)S(1)} %collective-permute-done.7.one, bf16[2,2,64,512]{3,2,1,0:T(8,128)(2,1)S(1)} %collective-permute-done.8.two, ...), custom_call_target="tpu_custom_call" | custom-call | flops 10000000 | bytes 6000000 | tf_op jit(solution)/shard_map/gradient_parts/pallas_call | solution.py:341
  67.7 9.7 %all-to-all-start = ((bf16[128,16,128]{2,1,0:T(8,128)(2,1)}), bf16[128,16,128]{2,1,0:T(8,128)(2,1)S(1)}, u32[]{:S(2)}, u32[]{:S(2)}) async-start(bf16[128,16,128]{2,1,0:T(8,128)(2,1)} %gradient_parts.1._), calls=%async_computation | async-start | bytes 1048576 | tf_op jit(solution)/shard_map/all_to_all | solution.py:503
  78.0 1.1 %maximum_bitcast_fusion = f32[32,2,2,2,512]{4,3,2,1,0:T(2,128)} fusion(f32[1,2,2,32,512]{4,2,1,0,3:T(2,128)S(1)} %copy.19, f32[1,2,2,32,512]{4,2,1,0,3:T(2,128)S(1)} %copy.18), kind=kLoop, calls=%fused_computation.1 | loop fusion | flops 131072 | bytes 1048576 | tf_op jit(solution)/shard_map/transpose | solution.py:509
  79.0 11.6 %all-to-all-done.grads = bf16[128,16,128]{2,1,0:T(8,128)(2,1)S(1)} async-done(((bf16[128,16,128]{2,1,0:T(8,128)(2,1)}), bf16[128,16,128]{2,1,0:T(8,128)(2,1)S(1)}, u32[]{:S(2)}, u32[]{:S(2)}) %all-to-all-start) | async-done | bytes 524320 | tf_op jit(solution)/shard_map/all_to_all | solution.py:503
  90.6 1.2 %updated_rows.1 = f32[2,512]{1,0:T(2,128)} custom-call(bf16[128,16,128]{2,1,0:T(8,128)(2,1)S(1)} %all-to-all-done.grads, f32[512,512]{1,0:T(8,128)S(1)} %copy-done.2, f32[2,512]{1,0:T(2,128)S(1)} %copy-done.4), custom_call_target="tpu_custom_call" | custom-call | flops 200000000 | bytes 1500000 | tf_op jit(solution)/shard_map/updated_rows/pallas_call | solution.py:431
  (48 shorter events, 7.9 us)
Async XLA Ops:
  2.0 1.9 %copy-start = (bf16[2,2,2,512,384]{4,3,2,1,0:T(8,128)(2,1)S(1)}, bf16[2,2,2,512,384]{4,3,2,1,0:T(8,128)(2,1)}, u32[]{:S(2)}) copy-start(bf16[2,2,2,512,384]{4,3,2,1,0:T(8,128)(2,1)} %gain.3) | copy-start | bytes 9437188
  3.9 0.7 copy-start.3
  4.6 0.7 copy-start.5
  5.3 0.7 copy-start.7
  6.0 0.7 copy-start.9
  6.6 4.8 %copy-start.11 = (s32[32,2,512]{2,1,0:T(2,128)S(1)}, s32[32,2,512]{2,1,0:T(2,128)}, u32[]{:S(2)}) copy-start(s32[32,2,512]{2,1,0:T(2,128)} %param.11) | copy-start | bytes 393220
  11.3 7.9 %collective-permute-start.1 = (bf16[2,528,768]{2,1,0:T(8,128)(2,1)}, bf16[2,528,768]{2,1,0:T(8,128)(2,1)}, u32[]{:S(2)}, u32[]{:S(2)}) collective-permute-start(bf16[2,528,768]{2,1,0:T(8,128)(2,1)} %phasor_send.1), channel_id=1, source_target_pairs={{0,8},{8,0},{16,24},{24,16},{32,40},{40,32},{48,56},{56,48},{64,72... | collective-permute-start | bytes 4866056 | tf_op jit(solution)/shard_map/ppermute | solution.py:471
  11.5 4.2 %copy-start.1 = (bf16[2,2,2,512,384]{4,3,2,1,0:T(8,128)(2,1)S(1)}, bf16[2,2,2,512,384]{4,3,2,1,0:T(8,128)(2,1)}, u32[]{:S(2)}) copy-start(bf16[2,2,2,512,384]{4,3,2,1,0:T(8,128)(2,1)} %gain.3) | copy-start | bytes 9437188
  11.5 4.1 %copy-start.4 = (f32[2,512]{1,0:T(2,128)S(1)}, f32[2,512]{1,0:T(2,128)}, u32[]{:S(2)}) copy-start(f32[2,512]{1,0:T(2,128)} %screen.5) | copy-start | bytes 12292
  11.5 4.1 %copy-start.6 = (f32[2,2,512]{2,1,0:T(2,128)S(1)}, f32[2,2,512]{2,1,0:T(2,128)}, u32[]{:S(2)}) copy-start(f32[2,2,512]{2,1,0:T(2,128)} %uv.3) | copy-start | bytes 24580
  11.6 4.1 %copy-start.8 = (f32[2,384]{1,0:T(2,128)S(1)}, f32[2,384]{1,0:T(2,128)}, u32[]{:S(2)}) copy-start(f32[2,384]{1,0:T(2,128)} %lm.3) | copy-start | bytes 9220
  11.6 4.1 %copy-start.10 = (f32[2]{0:T(128)S(1)}, f32[2]{0:T(128)}, u32[]{:S(2)}) copy-start(f32[2]{0:T(128)} %freq.5) | copy-start | bytes 28
  15.1 28.5 %collective-permute-start = (f32[6,32,512]{2,1,0:T(8,128)S(1)}, f32[6,32,512]{2,1,0:T(8,128)S(1)}, u32[]{:S(2)}, u32[]{:S(2)}) collective-permute-start(f32[6,32,512]{2,1,0:T(8,128)S(1)} %get-tuple-element.24), channel_id=1, source_target_pairs={{0,8},{8,0},{16,24},{24,16},{32,40},{40,32},{48,56},{56,48},{64,72... | collective-permute-start | bytes 1179656 | tf_op jit(solution)/shard_map/ppermute | solution.py:480
  24.9 11.2 %collective-permute-start.2 = (bf16[2,2,64,512]{3,2,1,0:T(8,128)(2,1)S(1)}, bf16[2,2,64,512]{3,2,1,0:T(8,128)(2,1)S(1)}, u32[]{:S(2)}, u32[]{:S(2)}) collective-permute-start(bf16[2,2,64,512]{3,2,1,0:T(8,128)(2,1)S(1)} %get-tuple-element.15), channel_id=1, source_target_pairs={{0,16},{8,24},{16,0},{24,8},{32,48},{40,56},{48,32},{56,40},{64,80... | collective-permute-start | bytes 786440 | tf_op jit(solution)/shard_map/ppermute | solution.py:485
  26.7 13.3 %collective-permute-start.3 = (bf16[2,2,64,512]{3,2,1,0:T(8,128)(2,1)S(1)}, bf16[2,2,64,512]{3,2,1,0:T(8,128)(2,1)S(1)}, u32[]{:S(2)}, u32[]{:S(2)}) collective-permute-start(bf16[2,2,64,512]{3,2,1,0:T(8,128)(2,1)S(1)} %get-tuple-element.16), channel_id=1, source_target_pairs={{0,48},{8,56},{16,32},{24,40},{32,16},{40,24},{48,0},{56,8},{64,11... | collective-permute-start | bytes 786440 | tf_op jit(solution)/shard_map/ppermute | solution.py:485
  28.8 12.6 %collective-permute-start.4 = (bf16[2,2,64,512]{3,2,1,0:T(8,128)(2,1)S(1)}, bf16[2,2,64,512]{3,2,1,0:T(8,128)(2,1)S(1)}, u32[]{:S(2)}, u32[]{:S(2)}) collective-permute-start(bf16[2,2,64,512]{3,2,1,0:T(8,128)(2,1)S(1)} %get-tuple-element.17), channel_id=1, source_target_pairs={{0,32},{8,40},{16,48},{24,56},{32,0},{40,8},{48,16},{56,24},{64,96... | collective-permute-start | bytes 786440 | tf_op jit(solution)/shard_map/ppermute | solution.py:485
  41.6 5.0 %collective-permute-start.5 = (bf16[2,64,512]{2,1,0:T(8,128)(2,1)S(1)}, bf16[2,64,512]{2,1,0:T(8,128)(2,1)S(1)}, u32[]{:S(2)}, u32[]{:S(2)}) collective-permute-start(bf16[2,64,512]{2,1,0:T(8,128)(2,1)S(1)} %get-tuple-element.19), channel_id=1, source_target_pairs={{0,64},{8,72},{16,80},{24,88},{32,96},{40,104},{48,112},{56,120},{... | collective-permute-start | bytes 393224 | tf_op jit(solution)/shard_map/ppermute | solution.py:489
  46.7 5.0 %collective-permute-start.6 = (bf16[2,64,512]{2,1,0:T(8,128)(2,1)S(1)}, bf16[2,64,512]{2,1,0:T(8,128)(2,1)S(1)}, u32[]{:S(2)}, u32[]{:S(2)}) collective-permute-start(bf16[2,64,512]{2,1,0:T(8,128)(2,1)S(1)} %get-tuple-element.22), channel_id=1, source_target_pairs={{0,64},{8,72},{16,80},{24,88},{32,96},{40,104},{48,112},{56,120},{... | collective-permute-start | bytes 393224 | tf_op jit(solution)/shard_map/ppermute | solution.py:492
  51.8 10.8 %collective-permute-start.7 = (bf16[2,2,64,512]{3,2,1,0:T(8,128)(2,1)S(1)}, bf16[2,2,64,512]{3,2,1,0:T(8,128)(2,1)S(1)}, u32[]{:S(2)}, u32[]{:S(2)}) collective-permute-start(bf16[2,2,64,512]{3,2,1,0:T(8,128)(2,1)S(1)} %pad_maximum_fusion.1.here), channel_id=1, source_target_pairs={{0,16},{8,24},{16,0},{24,8},{32,48},{40,56},{48,32},{56,40},{64,80... | collective-permute-start | bytes 786440 | tf_op jit(solution)/shard_map/ppermute | solution.py:495
  52.0 10.7 %collective-permute-start.8 = (bf16[2,2,64,512]{3,2,1,0:T(8,128)(2,1)S(1)}, bf16[2,2,64,512]{3,2,1,0:T(8,128)(2,1)S(1)}, u32[]{:S(2)}, u32[]{:S(2)}) collective-permute-start(bf16[2,2,64,512]{3,2,1,0:T(8,128)(2,1)S(1)} %pad_maximum_fusion.1.here), channel_id=1, source_target_pairs={{0,48},{8,56},{16,32},{24,40},{32,16},{40,24},{48,0},{56,8},{64,11... | collective-permute-start | bytes 786440 | tf_op jit(solution)/shard_map/ppermute | solution.py:494
  54.3 9.8 %collective-permute-start.9 = (bf16[2,2,64,512]{3,2,1,0:T(8,128)(2,1)S(1)}, bf16[2,2,64,512]{3,2,1,0:T(8,128)(2,1)S(1)}, u32[]{:S(2)}, u32[]{:S(2)}) collective-permute-start(bf16[2,2,64,512]{3,2,1,0:T(8,128)(2,1)S(1)} %pad_maximum_fusion.1.here), channel_id=1, source_target_pairs={{0,32},{8,40},{16,48},{24,56},{32,0},{40,8},{48,16},{56,24},{64,96... | collective-permute-start | bytes 786440 | tf_op jit(solution)/shard_map/ppermute | solution.py:493
  67.6 23.0 %copy-start.2 = (f32[512,512]{1,0:T(8,128)S(1)}, f32[512,512]{1,0:T(8,128)}, u32[]{:S(2)}) copy-start(f32[512,512]{1,0:T(8,128)} %kernel.1) | copy-start | bytes 3145732
  67.6 9.8 %collective-permute-start.10 = (f32[4,32,512]{2,1,0:T(8,128)S(1)}, f32[4,32,512]{2,1,0:T(8,128)S(1)}, u32[]{:S(2)}, u32[]{:S(2)}) collective-permute-start(f32[4,32,512]{2,1,0:T(8,128)S(1)} %get-tuple-element.21), channel_id=1, source_target_pairs={{0,8},{8,0},{16,24},{24,16},{32,40},{40,32},{48,56},{56,48},{64,72... | collective-permute-start | bytes 786440 | tf_op jit(solution)/shard_map/ppermute | solution.py:502
  67.7 22.9 %all-to-all-start = ((bf16[128,16,128]{2,1,0:T(8,128)(2,1)}), bf16[128,16,128]{2,1,0:T(8,128)(2,1)S(1)}, u32[]{:S(2)}, u32[]{:S(2)}) async-start(bf16[128,16,128]{2,1,0:T(8,128)(2,1)} %gradient_parts.1._), calls=%async_computation | async-start | bytes 1048576 | tf_op jit(solution)/shard_map/all_to_all | solution.py:503

commit v3 on v2

--- a/solution.py
+++ b/solution.py
@@ -43,6 +43,7 @@
 
 
 ANY = pl.BlockSpec(memory_space=pl.ANY)
+HBM = pl.BlockSpec(memory_space=pltpu.HBM)
 WHOLE = pl.BlockSpec(memory_space=pltpu.VMEM)
 SCALARS = pl.BlockSpec(memory_space=pltpu.SMEM)
 
@@ -52,24 +53,8 @@
     return index % 2, (index // 2) % 4, index // 8
 
 
-def phasor_kernel(send, freq, gain, uv, screen, lm, flux, direction, out, held, sems):
-    core, _, _ = position()
-    channel = 1 - core if send else core
-    stations, sources = gain.shape[3], gain.shape[4]
-    half = stations // 2
-    copies = []
-    for moment in range(2):
-        for part in range(2):
-            rows = pl.ds(part * half, half)
-            copies.append(
-                pltpu.make_async_copy(
-                    gain.at[channel, moment, :, rows, :],
-                    held.at[moment, :, rows, :],
-                    sems.at[moment * 2 + part],
-                )
-            )
-    for copy in copies:
-        copy.start()
+def phasor_rows(channel, freq, gain_of, uv, screen, lm, flux, direction, out, ready):
+    stations, sources = screen.shape[1], lm.shape[1]
     ratio = freq[channel]
     along = lm[0:1, :] * ratio
     across = lm[1:2, :] * ratio
@@ -83,8 +68,7 @@
     mask = jnp.broadcast_to(jnp.where(second, 1.0, 0.0), (16, sources)).astype(bf16)
     for moment in range(2):
         for start in range(0, stations, CHUNK):
-            if start % half == 0:
-                copies[moment * 2 + start // half].wait()
+            ready(moment, start)
             rows = slice(start, start + CHUNK)
             col = cols[rows]
             u = col[:, 2 * moment : 2 * moment + 1]
@@ -101,8 +85,8 @@
             sin_amp = sin_half * amp
             sine = sin_amp * cos_half
             cosine = amp - sin_amp * sin_half
-            gain_re = held[moment, 0, rows, :].astype(f32)
-            gain_im = held[moment, 1, rows, :].astype(f32)
+            gain_re = gain_of(moment, 0, rows).astype(f32)
+            gain_im = gain_of(moment, 1, rows).astype(f32)
             out[moment, rows, 0:sources] = (gain_re * cosine - gain_im * sine).astype(bf16)
             out[moment, rows, sources : 2 * sources] = (
                 gain_re * sine + gain_im * cosine
@@ -111,23 +95,105 @@
         out[moment, stations : stations + 16, sources : 2 * sources] = mask
 
 
-def phasor(send, freq, gain, uv, screen, lm, flux, direction):
+def phasor_send_kernel(
+    freq, gain, uv, screen, lm, flux, direction, out, flux_held, direction_held, *rest
+):
+    held, freq_held, uv_held, screen_held, lm_held, sems = rest
+    core, _, _ = position()
+    channel = 1 - core
+    quarter = gain.shape[3] // 4
+    loads = [
+        pltpu.make_async_copy(source, target, sems.at[8 + index])
+        for index, (source, target) in enumerate(
+            (
+                (freq, freq_held),
+                (uv, uv_held),
+                (screen, screen_held),
+                (lm, lm_held),
+                (flux, flux_held.at[0]),
+                (direction, direction_held.at[0]),
+            )
+        )
+    ]
+    copies = []
+    for moment in range(2):
+        for part in range(4):
+            rows = pl.ds(part * quarter, quarter)
+            copies.append(
+                pltpu.make_async_copy(
+                    gain.at[channel, moment, :, rows, :],
+                    held.at[moment, :, rows, :],
+                    sems.at[moment * 4 + part],
+                )
+            )
+    for copy in loads + copies:
+        copy.start()
+    for load in loads:
+        load.wait()
+
+    def ready(moment, start):
+        if start % quarter == 0:
+            copies[moment * 4 + start // quarter].wait()
+
+    def gain_of(moment, part, rows):
+        return held[moment, part, rows, :]
+
+    phasor_rows(
+        channel, freq_held, gain_of, uv_held, screen_held, lm_held, flux_held, direction_held, out, ready
+    )
+
+
+def phasor_own_kernel(freq, gain, uv, screen, lm, flux, direction, out):
+    channel = position()[0]
+
+    def gain_of(moment, part, rows):
+        return gain[channel, moment, part, rows, :]
+
+    phasor_rows(
+        channel, freq, gain_of, uv, screen, lm, flux, direction, out, lambda moment, start: None
+    )
+
+
+def phasor_send(*inputs):
+    gain = inputs[1]
     stations, sources = gain.shape[3], gain.shape[4]
     return pl.pallas_call(
-        functools.partial(phasor_kernel, send),
-        in_specs=[SCALARS, ANY] + [WHOLE] * 5,
-        out_specs=WHOLE,
-        out_shape=jax.ShapeDtypeStruct((2, stations + 16, 2 * sources), bf16),
+        phasor_send_kernel,
+        in_specs=[HBM] * 7,
+        out_specs=[WHOLE] * 3,
+        out_shape=[
+            jax.ShapeDtypeStruct((2, stations + 16, 2 * sources), bf16),
+            jax.ShapeDtypeStruct((1, sources), f32),
+            jax.ShapeDtypeStruct((1, sources), jnp.int32),
+        ],
         scratch_shapes=[
             pltpu.VMEM((2, 2, stations, sources), bf16),
-            pltpu.SemaphoreType.DMA((4,)),
-        ],
-        compiler_params=pltpu.CompilerParams(vmem_limit_bytes=12 * MIB),
+            pltpu.SMEM(inputs[0].shape, f32),
+        ]
+        + [pltpu.VMEM(array.shape, f32) for array in inputs[2:5]]
+        + [pltpu.SemaphoreType.DMA((14,))],
+        compiler_params=pltpu.CompilerParams(vmem_limit_bytes=60 * MIB),
         cost_estimate=pl.CostEstimate(
             flops=40 * 2 * stations * sources, bytes_accessed=3200000, transcendentals=0
         ),
-        name="phasor_send" if send else "phasor_own",
-    )(freq, gain, uv, screen, lm, flux, direction)
+        name="phasor_send",
+    )(*inputs)
+
+
+def phasor_own(*inputs):
+    gain = inputs[1]
+    stations, sources = gain.shape[3], gain.shape[4]
+    return pl.pallas_call(
+        phasor_own_kernel,
+        in_specs=[SCALARS] + [WHOLE] * 6,
+        out_specs=WHOLE,
+        out_shape=jax.ShapeDtypeStruct((2, stations + 16, 2 * sources), bf16),
+        compiler_params=pltpu.CompilerParams(vmem_limit_bytes=16 * MIB),
+        cost_estimate=pl.CostEstimate(
+            flops=40 * 2 * stations * sources, bytes_accessed=3200000, transcendentals=0
+        ),
+        name="phasor_own",
+    )(*inputs)
 
 
 def upper_mask():
@@ -154,9 +220,18 @@
     return lax.dot_general(a, b, NT, preferred_element_type=f32)
 
 
-def spread_wide(wide, part, value):
-    wide[part, :, 0:512] = value
-    wide[part, :, 512:768] = value[:, 0:256]
+def fill_wide(wide, part, top, bottom):
+    wide[part, 0:256, 0:512] = top
+    wide[part, 256:512, 256:512] = bottom
+    corner = jnp.transpose(top[:, 256:512])
+    wide[part, 256:512, 512:768] = corner if part == 0 else -corner
+
+
+def fill_gram(wide, left, right):
+    for part, rows in ((0, left), (1, skewed(left))):
+        value = mm(rows, right)
+        wide[part, :, 0:512] = value
+        wide[part, :, 512:768] = value[:, 0:256]
 
 
 def block_of(wide, part, chip):
@@ -164,13 +239,28 @@
     return wide[part, pl.ds(pl.multiple_of(chip * 64, 64), 64), pl.ds(start, 384)]
 
 
-def model_kernel(scaling, own, other, out0, out1, out2, out3, wide):
+def model_kernel(scaling, own, other_hbm, out0, out1, out2, out3, wide, other, top, bottom, sems):
     _, y, z = position()
+    copies = [
+        pltpu.make_async_copy(other_hbm.at[moment], other.at[moment], sems.at[moment])
+        for moment in range(2)
+    ]
+    for copy in copies:
+        copy.start()
     for moment in range(2):
-        q_own = own[moment, 0:512, :]
-        q_other = other[moment, 0:512, :]
-        spread_wide(wide, 0, (mm(q_own, q_own) + mm(q_other, q_other)) * scaling)
-        spread_wide(wide, 1, (mm(skewed(q_own), q_own) + mm(skewed(q_other), q_other)) * scaling)
+        q = own[moment, 0:512, :]
+        for part, rows in ((0, q), (1, skewed(q))):
+            top[part] = mm(rows[0:256], q)
+            bottom[part] = mm(rows[256:512], q[256:512])
+        copies[moment].wait()
+        q = other[moment, 0:512, :]
+        for part, rows in ((0, q), (1, skewed(q))):
+            fill_wide(
+                wide,
+                part,
+                (top[part] + mm(rows[0:256], q)) * scaling,
+                (bottom[part] + mm(rows[256:512], q[256:512])) * scaling,
+            )
         for rel, out in enumerate((out0, out1, out2, out3)):
             for flip in range(2):
                 zz = 1 - z if flip else z
@@ -183,9 +273,15 @@
 def model_parts(scaling, own, other):
     return pl.pallas_call(
         functools.partial(model_kernel, scaling),
-        in_specs=[WHOLE] * 2,
+        in_specs=[WHOLE, HBM],
         out_specs=[WHOLE] * 4,
-        scratch_shapes=[pltpu.VMEM((2, 512, 768), f32)],
+        scratch_shapes=[
+            pltpu.VMEM((2, 512, 768), f32),
+            pltpu.VMEM(other.shape, bf16),
+            pltpu.VMEM((2, 256, 512), f32),
+            pltpu.VMEM((2, 256, 256), f32),
+            pltpu.SemaphoreType.DMA((2,)),
+        ],
         out_shape=[jax.ShapeDtypeStruct((2, 2, 64, 512), f32)]
         + [jax.ShapeDtypeStruct((2, 2, 64, 512), bf16)] * 3,
         compiler_params=pltpu.CompilerParams(vmem_limit_bytes=16 * MIB),
@@ -202,10 +298,8 @@
         q = source[moment, 0:512, :]
         in_first = source[moment, 512:513, :] < 0.5
         q_first = jnp.where(in_first, q, jnp.zeros_like(q))
-        spread_wide(whole, 0, mm(q, q))
-        spread_wide(whole, 1, mm(skewed(q), q))
-        spread_wide(first, 0, mm(q_first, q))
-        spread_wide(first, 1, mm(skewed(q_first), q))
+        fill_gram(whole, q, q)
+        fill_gram(first, q_first, q)
         for rel in range(4):
             for flip in range(2):
                 zz = 1 - z if flip else z
@@ -255,36 +349,43 @@
     )(own, one, two, three, after)
 
 
-def observed_kernel(own, other, obs_out, keep_out, wide):
+def observed_kernel(observed, flags, other, other_flags, obs_out, keep_out, own, wide, sem):
     core, y, z = position()
+    copy = pltpu.make_async_copy(observed.at[:, core], own, sem)
+    copy.start()
+    copy.wait()
+    chip = z * 4 + y
+    start = pl.ds(pl.multiple_of((chip // 2) * 128, 128), 384)
+    odd = chip % 2 == 1
+    row = lax.broadcasted_iota(jnp.int32, (64, 512), 0)
+    col = lax.broadcasted_iota(jnp.int32, (64, 512), 1)
     for moment in range(2):
-        for part in range(3):
-            index = moment * 3 + part
-            for rows, source in ((core, own), (1 - core, other)):
-                place = pl.ds(pl.multiple_of(rows * 32, 32), 32)
-                wide[part, place, 0:512] = source[index]
-                wide[part, place, 512:768] = source[index, :, 0:256]
-        chip = z * 4 + y
-        start = pl.ds(pl.multiple_of((chip // 2) * 128, 128), 384)
-        odd = chip % 2 == 1
+        for rows, source, kept in ((core, own, flags), (1 - core, other, other_flags)):
+            there = pl.ds(pl.multiple_of(rows * 32, 32), 32)
+            for part in range(3):
+                value = kept[:, moment, :].astype(f32) if part == 2 else source[:, moment, part, :]
+                wide[part, there, 0:512] = value
+                wide[part, there, 512:768] = value[:, 0:256]
         obs_out[moment] = pack(wide[0, :, start], wide[1, :, start], odd, z == 0)
         keep = pack(wide[2, :, start], wide[2, :, start], odd, z == 0)
-        row = lax.broadcasted_iota(jnp.int32, (64, 512), 0)
-        col = lax.broadcasted_iota(jnp.int32, (64, 512), 1)
         keep_out[moment] = jnp.where(row == col, 0.0, keep)
 
 
-def observed_parts(own, other):
+def observed_parts(observed, flags, other, other_flags):
     return pl.pallas_call(
         observed_kernel,
-        in_specs=[WHOLE] * 2,
+        in_specs=[HBM] + [WHOLE] * 3,
         out_specs=[WHOLE] * 2,
         out_shape=[jax.ShapeDtypeStruct((2, 64, 512), f32)] * 2,
-        scratch_shapes=[pltpu.VMEM((3, 64, 768), f32)],
+        scratch_shapes=[
+            pltpu.VMEM(other.shape, f32),
+            pltpu.VMEM((3, 64, 768), f32),
+            pltpu.SemaphoreType.DMA,
+        ],
         cost_estimate=pl.CostEstimate(flops=1000000, bytes_accessed=1500000, transcendentals=0),
-        compiler_params=pltpu.CompilerParams(vmem_limit_bytes=4 * MIB),
+        compiler_params=pltpu.CompilerParams(vmem_limit_bytes=6 * MIB),
         name="observed_parts",
-    )(own, other)
+    )(observed, flags, other, other_flags)
 
 
 def gradient_kernel(scaling, freq, here, one, two, three, parts0, parts1, out, rows_sum, cols_sum):
@@ -458,31 +559,18 @@
     core = position()[0]
     swap = functools.partial(lax.ppermute, axis_name="dir", perm=dir_perm(0, flip_core=True))
 
-    inputs = (
-        freq_ratio,
-        station_gain,
-        station_uv,
-        screen,
-        source_lm,
-        source_flux[None],
-        source_direction[None],
-    )
-    sent = phasor(True, *inputs)
+    inputs = (freq_ratio, station_gain, station_uv, screen, source_lm)
+    sent, flux_row, direction_row = phasor_send(*inputs, source_flux, source_direction)
     other = swap(sent)
-    own = phasor(False, *inputs)
-
-    keep = flags.astype(f32)[:, None, :, None, :]
-    keep = jnp.broadcast_to(keep, (32, 2, 2, 1, stations))
-    rows = jnp.concatenate([observed, keep], axis=3)
-    rows = jnp.transpose(rows, (1, 2, 3, 0, 4)).reshape(2, 6, 32, stations)
-    rows_own = lax.dynamic_index_in_dim(rows, core, 0, keepdims=False)
-    rows_sent = lax.dynamic_index_in_dim(rows, 1 - core, 0, keepdims=False)
-    rows_other = swap(rows_sent)
-    obs, kept = observed_parts(rows_own, rows_other)
+    own = phasor_own(*inputs, flux_row, direction_row)
+
+    other_flags = swap(flags)
+    other_observed = swap(lax.dynamic_index_in_dim(observed, 1 - core, 1, keepdims=False))
+    obs, kept = observed_parts(observed, flags, other_observed, other_flags)
 
     part0, part1, part2, part3 = model_parts(scaling, own, other)
     got = [
-        lax.ppermute(part, "dir", dir_perm(rel)) for rel, part in ((1, part1), (2, part2), (3, part3))
+        lax.ppermute(part, "dir", dir_perm(rel)) for rel, part in ((3, part3), (2, part2), (1, part1))
     ]
     directions0 = direction_parts(0, own, other)
     stay, send = sum_parts(part0, *got, directions0)

time: 92.3 us -> 85.6 us (0.927)
  local copies, waits for them, and re-layouts: 8.84 us -> 2.78 us
  waiting for transfers between devices: 23.8 us -> 26.2 us
  Pallas kernels: 32.6 us -> 31.3 us
  other arithmetic: 2.4 us -> 1.21 us
    unnamed x25 -> x20, local copies, waits for them, and re-layouts: 6.95 us -> 1.39 us
    ppermute x1, waiting for transfers between devices: 0.01 us -> 3.51 us  [body(): two = lax.ppermute(here, 'dir', dir_perm(2))]
    ppermute x1, starting transfers between devices: 0.14 us -> 1.65 us  [body(): one = lax.ppermute(here, 'dir', dir_perm(1))]
    ppermute x1, waiting for transfers between devices: 1.44 us -> 0.01 us  [body(): three = lax.ppermute(here, 'dir', dir_perm(3))]
    broadcast_in_dim x3 -> x0, local copies, waits for them, and re-layouts: 1.38 us -> none  [the longest x1 0.68 us: body(): source_flux[None]]
    pallas_call x4, Pallas kernels: 14.6 us -> 13.2 us  [the longest x1 5.13 us: phasor_send(): pl.pallas_call(phasor_send_kernel, in_specs=[HBM] * 7, out_specs=[WHOLE]...]
    concatenate x1 -> x0, other arithmetic: 1.14 us -> none  [body(): rows = jnp.concatenate([observed, keep], axis=3)]
  transfers between devices with their start and end apart: 12 -> 13, of which waited for: 6 -> 6; matrix products, arithmetic and copies ran while one was open for 6% -> 3% of each run, Pallas kernels for 25% -> 25%
where the time goes in v3:
time: 85.6 us; the launch traced here: 85.3 us
  Pallas kernels  31.3 us (37%)
  waiting for transfers between devices  26.2 us (31%)
  starting transfers between devices  22.9 us (27%)
  local copies, waits for them, and re-layouts  2.78 us (3%)
  other arithmetic  1.21 us (1%)
  between operations  0.9 us (1%)
    pallas_call x2, Pallas kernels, direction_parts(): pl.pallas_call(functools.partial(direction_kernel, moment), in_specs=[WHO...  13.3 us
    all_to_all x1, waiting for transfers between devices, body(): grads = lax.all_to_all(grads, ('dir', 'freq'), 0, 0, tiled=True)  11.6 us
    all_to_all x1, starting transfers between devices, body(): grads = lax.all_to_all(grads, ('dir', 'freq'), 0, 0, tiled=True)  9.34 us
    ppermute x3, waiting for transfers between devices, body(): lax.ppermute(part, 'dir', dir_perm(rel))  5.26 us
    pallas_call x1, Pallas kernels, phasor_send(): pl.pallas_call(phasor_send_kernel, in_specs=[HBM] * 7, out_specs=[WHOLE]...  5.13 us
    pallas_call x1, Pallas kernels, model_parts(): pl.pallas_call(functools.partial(model_kernel, scaling), in_specs=[WHOLE,...  4.46 us
    ppermute x3, starting transfers between devices, body(): lax.ppermute(part, 'dir', dir_perm(rel))  4.42 us
    ppermute x1, waiting for transfers between devices, body(): two = lax.ppermute(here, 'dir', dir_perm(2))  3.51 us
  transfers between devices with their start and end apart: 13, of which 6 were waited for; matrix products, arithmetic and copies ran while one was open for 3% of the time, Pallas kernels for 25%

profile of v3, /device:TPU:0, one launch (start us, length us, event | category | flops | bytes accessed | tf_op | source)
XLA Modules:
  0.0 85.3 jit_solution(7422982694641358784)
XLA Ops:
  0.7 5.1 %phasor_send.1 = (bf16[2,528,768]{2,1,0:T(8,128)(2,1)}, f32[1,384]{1,0:T(1,128)}, s32[1,384]{1,0:T(1,128)}) custom-call(f32[2]{0:T(128)} %freq.5, bf16[2,2,2,512,384]{4,3,2,1,0:T(8,128)(2,1)} %gain.3, f32[2,2,512]{2,1,0:T(2,128)} %uv.3, f32[2,512]{1,0:T(2,128)} %screen.5, f32[2,384]{1,0:T(2,128)} %lm.3, f32[384]{0:T(512)} %flux.1, s32[384]{0:T(512)} %direction.1), custom_call_target="tpu_custom_call" | custom-call | flops 15728640 | bytes 3200000 | tf_op jit(solution)/shard_map/phasor_send/pallas_call | solution.py:160
  5.9 1.0 %dynamic-slice_bitcast_fusion = f32[32,2,2,512]{3,2,1,0:T(2,128)S(1)} fusion(f32[32,2,2,2,512]{4,3,2,1,0:T(2,128)} %observed.1, s32[]{:T(128)S(6)} %select_n.25), kind=kLoop, calls=%fused_computation.3 | loop fusion | bytes 524292 | tf_op jit(solution)/shard_map/jit(dynamic_index_in_dim)/squeeze | solution.py:568
  8.3 0.7 copy-done.9
  9.0 2.9 %phasor_own.1.own = bf16[2,528,768]{2,1,0:T(8,128)(2,1)S(1)} custom-call(f32[2]{0:T(128)S(1)} %copy-done.7, bf16[2,2,2,512,384]{4,3,2,1,0:T(8,128)(2,1)S(1)} %copy-done, f32[2,2,512]{2,1,0:T(2,128)S(1)} %copy-done.5, f32[2,512]{1,0:T(2,128)S(1)} %copy-done.4, f32[2,384]{1,0:T(2,128)S(1)} %copy-done.6, f32[1,384]{1,0:T(1,128)S(1)} %copy-done.8, ...), custom_call_target="tpu_custom_call" | custom-call | flops 15728640 | bytes 3200000 | tf_op jit(solution)/shard_map/phasor_own/pallas_call | solution.py:186
  11.9 4.5 %model_parts.1 = (f32[2,2,64,512]{3,2,1,0:T(8,128)S(1)}, bf16[2,2,64,512]{3,2,1,0:T(8,128)(2,1)S(1)}, bf16[2,2,64,512]{3,2,1,0:T(8,128)(2,1)S(1)}, bf16[2,2,64,512]{3,2,1,0:T(8,128)(2,1)S(1)}) custom-call(bf16[2,528,768]{2,1,0:T(8,128)(2,1)S(1)} %phasor_own.1.own, bf16[2,528,768]{2,1,0:T(8,128)(2,1)} %collective-permute-done.2.other_hbm.other), custom_call_target="tpu_custom_call" | custom-call | flops 3221225472 | bytes 5000000 | tf_op jit(solution)/shard_map/model_parts/pallas_call | solution.py:274
  16.4 3.4 %collective-permute-start.3 = (bf16[2,2,64,512]{3,2,1,0:T(8,128)(2,1)S(1)}, bf16[2,2,64,512]{3,2,1,0:T(8,128)(2,1)S(1)}, u32[]{:S(2)}, u32[]{:S(2)}) collective-permute-start(bf16[2,2,64,512]{3,2,1,0:T(8,128)(2,1)S(1)} %get-tuple-element.21), channel_id=1, source_target_pairs={{0,32},{8,40},{16,48},{24,56},{32,0},{40,8},{48,16},{56,24},{64,96... | collective-permute-start | bytes 786440 | tf_op jit(solution)/shard_map/ppermute | solution.py:573
  19.7 1.0 %collective-permute-start.4 = (bf16[2,2,64,512]{3,2,1,0:T(8,128)(2,1)S(1)}, bf16[2,2,64,512]{3,2,1,0:T(8,128)(2,1)S(1)}, u32[]{:S(2)}, u32[]{:S(2)}) collective-permute-start(bf16[2,2,64,512]{3,2,1,0:T(8,128)(2,1)S(1)} %get-tuple-element.22), channel_id=1, source_target_pairs={{0,48},{8,56},{16,32},{24,40},{32,16},{40,24},{48,0},{56,8},{64,11... | collective-permute-start | bytes 786440 | tf_op jit(solution)/shard_map/ppermute | solution.py:573
  20.8 6.6 %direction_parts0.1._.parts0 = bf16[4,4,2,64,512]{4,3,2,1,0:T(8,128)(2,1)S(1)} custom-call(bf16[2,528,768]{2,1,0:T(8,128)(2,1)S(1)} %phasor_own.1.own, bf16[2,528,768]{2,1,0:T(8,128)(2,1)} %collective-permute-done.2.other_hbm.other), custom_call_target="tpu_custom_call" | custom-call | flops 3221225472 | bytes 5000000 | tf_op jit(solution)/shard_map/direction_parts0/pallas_call | solution.py:316
  27.4 4.8 %collective-permute-done.4.two = bf16[2,2,64,512]{3,2,1,0:T(8,128)(2,1)S(1)} collective-permute-done((bf16[2,2,64,512]{3,2,1,0:T(8,128)(2,1)S(1)}, bf16[2,2,64,512]{3,2,1,0:T(8,128)(2,1)S(1)}, u32[]{:S(2)}, u32[]{:S(2)}) %collective-permute-start.4) | collective-permute-done | bytes 262176 | tf_op jit(solution)/shard_map/ppermute | solution.py:573
  32.8 2.0 %collective-permute-start.6 = (bf16[2,64,512]{2,1,0:T(8,128)(2,1)S(1)}, bf16[2,64,512]{2,1,0:T(8,128)(2,1)S(1)}, u32[]{:S(2)}, u32[]{:S(2)}) collective-permute-start(bf16[2,64,512]{2,1,0:T(8,128)(2,1)S(1)} %get-tuple-element.25), channel_id=1, source_target_pairs={{0,64},{8,72},{16,80},{24,88},{32,96},{40,104},{48,112},{56,120},{... | collective-permute-start | bytes 393224 | tf_op jit(solution)/shard_map/ppermute | solution.py:577
  34.8 0.7 observed_parts.1
  35.5 2.6 %collective-permute-done.6 = bf16[2,64,512]{2,1,0:T(8,128)(2,1)S(1)} collective-permute-done((bf16[2,64,512]{2,1,0:T(8,128)(2,1)S(1)}, bf16[2,64,512]{2,1,0:T(8,128)(2,1)S(1)}, u32[]{:S(2)}, u32[]{:S(2)}) %collective-permute-start.6) | collective-permute-done | bytes 131104 | tf_op jit(solution)/shard_map/ppermute | solution.py:577
  38.2 1.8 %collective-permute-start.7 = (bf16[2,64,512]{2,1,0:T(8,128)(2,1)S(1)}, bf16[2,64,512]{2,1,0:T(8,128)(2,1)S(1)}, u32[]{:S(2)}, u32[]{:S(2)}) collective-permute-start(bf16[2,64,512]{2,1,0:T(8,128)(2,1)S(1)} %get-tuple-element.28), channel_id=1, source_target_pairs={{0,64},{8,72},{16,80},{24,88},{32,96},{40,104},{48,112},{56,120},{... | collective-permute-start | bytes 393224 | tf_op jit(solution)/shard_map/ppermute | solution.py:580
  40.0 3.2 %collective-permute-done.7 = bf16[2,64,512]{2,1,0:T(8,128)(2,1)S(1)} collective-permute-done((bf16[2,64,512]{2,1,0:T(8,128)(2,1)S(1)}, bf16[2,64,512]{2,1,0:T(8,128)(2,1)S(1)}, u32[]{:S(2)}, u32[]{:S(2)}) %collective-permute-start.7) | collective-permute-done | bytes 131104 | tf_op jit(solution)/shard_map/ppermute | solution.py:580
  43.3 1.7 %collective-permute-start.8 = (bf16[2,2,64,512]{3,2,1,0:T(8,128)(2,1)S(1)}, bf16[2,2,64,512]{3,2,1,0:T(8,128)(2,1)S(1)}, u32[]{:S(2)}, u32[]{:S(2)}) collective-permute-start(bf16[2,2,64,512]{3,2,1,0:T(8,128)(2,1)S(1)} %pad_maximum_fusion.here), channel_id=1, source_target_pairs={{0,16},{8,24},{16,0},{24,8},{32,48},{40,56},{48,32},{56,40},{64,80... | collective-permute-start | bytes 786440 | tf_op jit(solution)/shard_map/ppermute | solution.py:583
  44.9 1.5 %collective-permute-start.9 = (bf16[2,2,64,512]{3,2,1,0:T(8,128)(2,1)S(1)}, bf16[2,2,64,512]{3,2,1,0:T(8,128)(2,1)S(1)}, u32[]{:S(2)}, u32[]{:S(2)}) collective-permute-start(bf16[2,2,64,512]{3,2,1,0:T(8,128)(2,1)S(1)} %pad_maximum_fusion.here), channel_id=1, source_target_pairs={{0,48},{8,56},{16,32},{24,40},{32,16},{40,24},{48,0},{56,8},{64,11... | collective-permute-start | bytes 786440 | tf_op jit(solution)/shard_map/ppermute | solution.py:582
  46.5 1.4 %collective-permute-start.10 = (bf16[2,2,64,512]{3,2,1,0:T(8,128)(2,1)S(1)}, bf16[2,2,64,512]{3,2,1,0:T(8,128)(2,1)S(1)}, u32[]{:S(2)}, u32[]{:S(2)}) collective-permute-start(bf16[2,2,64,512]{3,2,1,0:T(8,128)(2,1)S(1)} %pad_maximum_fusion.here), channel_id=1, source_target_pairs={{0,32},{8,40},{16,48},{24,56},{32,0},{40,8},{48,16},{56,24},{64,96... | collective-permute-start | bytes 786440 | tf_op jit(solution)/shard_map/ppermute | solution.py:581
  47.8 6.6 %direction_parts1.1.parts1 = bf16[4,4,2,64,512]{4,3,2,1,0:T(8,128)(2,1)S(1)} custom-call(bf16[2,528,768]{2,1,0:T(8,128)(2,1)S(1)} %phasor_own.1.own, bf16[2,528,768]{2,1,0:T(8,128)(2,1)} %collective-permute-done.2.other_hbm.other), custom_call_target="tpu_custom_call" | custom-call | flops 3221225472 | bytes 5000000 | tf_op jit(solution)/shard_map/direction_parts1/pallas_call | solution.py:316
  54.5 3.5 %collective-permute-done.9.two = bf16[2,2,64,512]{3,2,1,0:T(8,128)(2,1)S(1)} collective-permute-done((bf16[2,2,64,512]{3,2,1,0:T(8,128)(2,1)S(1)}, bf16[2,2,64,512]{3,2,1,0:T(8,128)(2,1)S(1)}, u32[]{:S(2)}, u32[]{:S(2)}) %collective-permute-start.9) | collective-permute-done | bytes 262176 | tf_op jit(solution)/shard_map/ppermute | solution.py:582
  58.0 2.9 %gradient_parts.1._ = bf16[128,16,128]{2,1,0:T(8,128)(2,1)} custom-call(f32[2]{0:T(128)S(1)} %copy-done.7, bf16[2,2,64,512]{3,2,1,0:T(8,128)(2,1)S(1)} %pad_maximum_fusion.here, bf16[2,2,64,512]{3,2,1,0:T(8,128)(2,1)S(1)} %collective-permute-done.8.one, bf16[2,2,64,512]{3,2,1,0:T(8,128)(2,1)S(1)} %collective-permute-done.9.two, ...), custom_call_target="tpu_custom_call" | custom-call | flops 10000000 | bytes 6000000 | tf_op jit(solution)/shard_map/gradient_parts/pallas_call | solution.py:442
  61.7 9.3 %all-to-all-start = ((bf16[128,16,128]{2,1,0:T(8,128)(2,1)}), bf16[128,16,128]{2,1,0:T(8,128)(2,1)S(1)}, u32[]{:S(2)}, u32[]{:S(2)}) async-start(bf16[128,16,128]{2,1,0:T(8,128)(2,1)} %gradient_parts.1._), calls=%async_computation | async-start | bytes 1048576 | tf_op jit(solution)/shard_map/all_to_all | solution.py:591
  71.5 1.1 %maximum_bitcast_fusion = f32[32,2,2,2,512]{4,3,2,1,0:T(2,128)} fusion(f32[1,2,2,32,512]{4,2,1,0,3:T(2,128)S(1)} %copy.13, f32[1,2,2,32,512]{4,2,1,0,3:T(2,128)S(1)} %copy.12), kind=kLoop, calls=%fused_computation | loop fusion | flops 131072 | bytes 1048576 | tf_op jit(solution)/shard_map/transpose | solution.py:597
  72.5 11.6 %all-to-all-done.grads = bf16[128,16,128]{2,1,0:T(8,128)(2,1)S(1)} async-done(((bf16[128,16,128]{2,1,0:T(8,128)(2,1)}), bf16[128,16,128]{2,1,0:T(8,128)(2,1)S(1)}, u32[]{:S(2)}, u32[]{:S(2)}) %all-to-all-start) | async-done | bytes 524320 | tf_op jit(solution)/shard_map/all_to_all | solution.py:591
  84.2 1.2 %updated_rows.1 = f32[2,512]{1,0:T(2,128)} custom-call(bf16[128,16,128]{2,1,0:T(8,128)(2,1)S(1)} %all-to-all-done.grads, f32[512,512]{1,0:T(8,128)S(1)} %copy-done.2, f32[2,512]{1,0:T(2,128)S(1)} %copy-done.4), custom_call_target="tpu_custom_call" | custom-call | flops 200000000 | bytes 1500000 | tf_op jit(solution)/shard_map/updated_rows/pallas_call | solution.py:532
  (39 shorter events, 3.3 us)
Async XLA Ops:
  0.6 6.9 %copy-start.7 = (f32[2]{0:T(128)S(1)}, f32[2]{0:T(128)}, u32[]{:S(2)}) copy-start(f32[2]{0:T(128)} %freq.5) | copy-start | bytes 28
  0.6 6.9 %copy-start = (bf16[2,2,2,512,384]{4,3,2,1,0:T(8,128)(2,1)S(1)}, bf16[2,2,2,512,384]{4,3,2,1,0:T(8,128)(2,1)}, u32[]{:S(2)}) copy-start(bf16[2,2,2,512,384]{4,3,2,1,0:T(8,128)(2,1)} %gain.3) | copy-start | bytes 9437188
  0.7 6.9 %copy-start.5 = (f32[2,2,512]{2,1,0:T(2,128)S(1)}, f32[2,2,512]{2,1,0:T(2,128)}, u32[]{:S(2)}) copy-start(f32[2,2,512]{2,1,0:T(2,128)} %uv.3) | copy-start | bytes 24580
  0.7 6.9 %copy-start.4 = (f32[2,512]{1,0:T(2,128)S(1)}, f32[2,512]{1,0:T(2,128)}, u32[]{:S(2)}) copy-start(f32[2,512]{1,0:T(2,128)} %screen.5) | copy-start | bytes 12292
  0.7 6.9 %copy-start.6 = (f32[2,384]{1,0:T(2,128)S(1)}, f32[2,384]{1,0:T(2,128)}, u32[]{:S(2)}) copy-start(f32[2,384]{1,0:T(2,128)} %lm.3) | copy-start | bytes 9220
  0.7 6.8 %copy-start.3 = (s32[32,2,512]{2,1,0:T(2,128)S(1)}, s32[32,2,512]{2,1,0:T(2,128)}, u32[]{:S(2)}) copy-start(s32[32,2,512]{2,1,0:T(2,128)} %flags.1) | copy-start | bytes 393220
  5.8 6.0 %collective-permute-start.2 = (bf16[2,528,768]{2,1,0:T(8,128)(2,1)}, bf16[2,528,768]{2,1,0:T(8,128)(2,1)}, u32[]{:S(2)}, u32[]{:S(2)}) collective-permute-start(bf16[2,528,768]{2,1,0:T(8,128)(2,1)} %get-tuple-element.19), channel_id=1, source_target_pairs={{0,8},{8,0},{16,24},{24,16},{32,40},{40,32},{48,56},{56,48},{64,72... | collective-permute-start | bytes 4866056 | tf_op jit(solution)/shard_map/ppermute | solution.py:564
  6.9 27.9 %collective-permute-start = (f32[32,2,2,512]{3,2,1,0:T(2,128)S(1)}, f32[32,2,2,512]{3,2,1,0:T(2,128)S(1)}, u32[]{:S(2)}, u32[]{:S(2)}) collective-permute-start(f32[32,2,2,512]{3,2,1,0:T(2,128)S(1)} %dynamic-slice_bitcast_fusion), channel_id=1, source_target_pairs={{0,8},{8,0},{16,24},{24,16},{32,40},{40,32},{48,56},{56,48},{64,72... | collective-permute-start | bytes 786440 | tf_op jit(solution)/shard_map/ppermute | solution.py:568
  7.5 27.3 %collective-permute-start.1 = (s32[32,2,512]{2,1,0:T(2,128)S(1)}, s32[32,2,512]{2,1,0:T(2,128)S(1)}, u32[]{:S(2)}, u32[]{:S(2)}) collective-permute-start(s32[32,2,512]{2,1,0:T(2,128)S(1)} %copy-done.3), channel_id=1, source_target_pairs={{0,8},{8,0},{16,24},{24,16},{32,40},{40,32},{48,56},{56,48},{64,72... | collective-permute-start | bytes 393224 | tf_op jit(solution)/shard_map/ppermute | solution.py:567
  7.6 0.7 copy-start.8
  8.3 0.7 copy-start.9
  16.4 11.1 %collective-permute-start.3 = (bf16[2,2,64,512]{3,2,1,0:T(8,128)(2,1)S(1)}, bf16[2,2,64,512]{3,2,1,0:T(8,128)(2,1)S(1)}, u32[]{:S(2)}, u32[]{:S(2)}) collective-permute-start(bf16[2,2,64,512]{3,2,1,0:T(8,128)(2,1)S(1)} %get-tuple-element.21), channel_id=1, source_target_pairs={{0,32},{8,40},{16,48},{24,56},{32,0},{40,8},{48,16},{56,24},{64,96... | collective-permute-start | bytes 786440 | tf_op jit(solution)/shard_map/ppermute | solution.py:573
  19.7 12.5 %collective-permute-start.4 = (bf16[2,2,64,512]{3,2,1,0:T(8,128)(2,1)S(1)}, bf16[2,2,64,512]{3,2,1,0:T(8,128)(2,1)S(1)}, u32[]{:S(2)}, u32[]{:S(2)}) collective-permute-start(bf16[2,2,64,512]{3,2,1,0:T(8,128)(2,1)S(1)} %get-tuple-element.22), channel_id=1, source_target_pairs={{0,48},{8,56},{16,32},{24,40},{32,16},{40,24},{48,0},{56,8},{64,11... | collective-permute-start | bytes 786440 | tf_op jit(solution)/shard_map/ppermute | solution.py:573
  20.8 11.9 %collective-permute-start.5 = (bf16[2,2,64,512]{3,2,1,0:T(8,128)(2,1)S(1)}, bf16[2,2,64,512]{3,2,1,0:T(8,128)(2,1)S(1)}, u32[]{:S(2)}, u32[]{:S(2)}) collective-permute-start(bf16[2,2,64,512]{3,2,1,0:T(8,128)(2,1)S(1)} %get-tuple-element.23), channel_id=1, source_target_pairs={{0,16},{8,24},{16,0},{24,8},{32,48},{40,56},{48,32},{56,40},{64,80... | collective-permute-start | bytes 786440 | tf_op jit(solution)/shard_map/ppermute | solution.py:573
  27.4 7.4 %copy-start.1 = (f32[32,2,2,2,512]{4,3,2,1,0:T(2,128)S(1)}, f32[32,2,2,2,512]{4,3,2,1,0:T(2,128)}, u32[]{:S(2)}) copy-start(f32[32,2,2,2,512]{4,3,2,1,0:T(2,128)} %observed.1) | copy-start | bytes 1572868
  32.8 5.3 %collective-permute-start.6 = (bf16[2,64,512]{2,1,0:T(8,128)(2,1)S(1)}, bf16[2,64,512]{2,1,0:T(8,128)(2,1)S(1)}, u32[]{:S(2)}, u32[]{:S(2)}) collective-permute-start(bf16[2,64,512]{2,1,0:T(8,128)(2,1)S(1)} %get-tuple-element.25), channel_id=1, source_target_pairs={{0,64},{8,72},{16,80},{24,88},{32,96},{40,104},{48,112},{56,120},{... | collective-permute-start | bytes 393224 | tf_op jit(solution)/shard_map/ppermute | solution.py:577
  38.2 5.0 %collective-permute-start.7 = (bf16[2,64,512]{2,1,0:T(8,128)(2,1)S(1)}, bf16[2,64,512]{2,1,0:T(8,128)(2,1)S(1)}, u32[]{:S(2)}, u32[]{:S(2)}) collective-permute-start(bf16[2,64,512]{2,1,0:T(8,128)(2,1)S(1)} %get-tuple-element.28), channel_id=1, source_target_pairs={{0,64},{8,72},{16,80},{24,88},{32,96},{40,104},{48,112},{56,120},{... | collective-permute-start | bytes 393224 | tf_op jit(solution)/shard_map/ppermute | solution.py:580
  43.3 11.2 %collective-permute-start.8 = (bf16[2,2,64,512]{3,2,1,0:T(8,128)(2,1)S(1)}, bf16[2,2,64,512]{3,2,1,0:T(8,128)(2,1)S(1)}, u32[]{:S(2)}, u32[]{:S(2)}) collective-permute-start(bf16[2,2,64,512]{3,2,1,0:T(8,128)(2,1)S(1)} %pad_maximum_fusion.here), channel_id=1, source_target_pairs={{0,16},{8,24},{16,0},{24,8},{32,48},{40,56},{48,32},{56,40},{64,80... | collective-permute-start | bytes 786440 | tf_op jit(solution)/shard_map/ppermute | solution.py:583
  44.9 13.1 %collective-permute-start.9 = (bf16[2,2,64,512]{3,2,1,0:T(8,128)(2,1)S(1)}, bf16[2,2,64,512]{3,2,1,0:T(8,128)(2,1)S(1)}, u32[]{:S(2)}, u32[]{:S(2)}) collective-permute-start(bf16[2,2,64,512]{3,2,1,0:T(8,128)(2,1)S(1)} %pad_maximum_fusion.here), channel_id=1, source_target_pairs={{0,48},{8,56},{16,32},{24,40},{32,16},{40,24},{48,0},{56,8},{64,11... | collective-permute-start | bytes 786440 | tf_op jit(solution)/shard_map/ppermute | solution.py:582
  46.5 11.5 %collective-permute-start.10 = (bf16[2,2,64,512]{3,2,1,0:T(8,128)(2,1)S(1)}, bf16[2,2,64,512]{3,2,1,0:T(8,128)(2,1)S(1)}, u32[]{:S(2)}, u32[]{:S(2)}) collective-permute-start(bf16[2,2,64,512]{3,2,1,0:T(8,128)(2,1)S(1)} %pad_maximum_fusion.here), channel_id=1, source_target_pairs={{0,32},{8,40},{16,48},{24,56},{32,0},{40,8},{48,16},{56,24},{64,96... | collective-permute-start | bytes 786440 | tf_op jit(solution)/shard_map/ppermute | solution.py:581
  61.5 22.6 %copy-start.2 = (f32[512,512]{1,0:T(8,128)S(1)}, f32[512,512]{1,0:T(8,128)}, u32[]{:S(2)}) copy-start(f32[512,512]{1,0:T(8,128)} %kernel.1) | copy-start | bytes 3145732
  61.6 9.4 %collective-permute-start.11 = (f32[4,32,512]{2,1,0:T(8,128)S(1)}, f32[4,32,512]{2,1,0:T(8,128)S(1)}, u32[]{:S(2)}, u32[]{:S(2)}) collective-permute-start(f32[4,32,512]{2,1,0:T(8,128)S(1)} %get-tuple-element.27), channel_id=1, source_target_pairs={{0,8},{8,0},{16,24},{24,16},{32,40},{40,32},{48,56},{56,48},{64,72... | collective-permute-start | bytes 786440 | tf_op jit(solution)/shard_map/ppermute | solution.py:590
  61.7 22.5 %all-to-all-start = ((bf16[128,16,128]{2,1,0:T(8,128)(2,1)}), bf16[128,16,128]{2,1,0:T(8,128)(2,1)S(1)}, u32[]{:S(2)}, u32[]{:S(2)}) async-start(bf16[128,16,128]{2,1,0:T(8,128)(2,1)} %gradient_parts.1._), calls=%async_computation | async-start | bytes 1048576 | tf_op jit(solution)/shard_map/all_to_all | solution.py:591

commit v4 on v3

--- a/solution.py
+++ b/solution.py
@@ -42,6 +42,7 @@
     return pairs
 
 
+STEPS = ((1, 2), (2, 1))
 ANY = pl.BlockSpec(memory_space=pl.ANY)
 HBM = pl.BlockSpec(memory_space=pltpu.HBM)
 WHOLE = pl.BlockSpec(memory_space=pltpu.VMEM)
@@ -96,9 +97,9 @@
 
 
 def phasor_send_kernel(
-    freq, gain, uv, screen, lm, flux, direction, out, flux_held, direction_held, *rest
+    freq, gain, uv, screen, lm, flux, direction, out, *rest
 ):
-    held, freq_held, uv_held, screen_held, lm_held, sems = rest
+    held, freq_held, uv_held, screen_held, lm_held, flux_held, direction_held, sems = rest
     core, _, _ = position()
     channel = 1 - core
     quarter = gain.shape[3] // 4
@@ -143,14 +144,22 @@
     )
 
 
-def phasor_own_kernel(freq, gain, uv, screen, lm, flux, direction, out):
+def phasor_own_kernel(freq, gain, uv, screen, lm, flux, direction, out, flux_held, direction_held, sems):
     channel = position()[0]
+    loads = [
+        pltpu.make_async_copy(flux, flux_held.at[0], sems.at[0]),
+        pltpu.make_async_copy(direction, direction_held.at[0], sems.at[1]),
+    ]
+    for load in loads:
+        load.start()
+    for load in loads:
+        load.wait()
 
     def gain_of(moment, part, rows):
         return gain[channel, moment, part, rows, :]
 
     phasor_rows(
-        channel, freq, gain_of, uv, screen, lm, flux, direction, out, lambda moment, start: None
+        channel, freq, gain_of, uv, screen, lm, flux_held, direction_held, out, lambda moment, start: None
     )
 
 
@@ -160,17 +169,14 @@
     return pl.pallas_call(
         phasor_send_kernel,
         in_specs=[HBM] * 7,
-        out_specs=[WHOLE] * 3,
-        out_shape=[
-            jax.ShapeDtypeStruct((2, stations + 16, 2 * sources), bf16),
-            jax.ShapeDtypeStruct((1, sources), f32),
-            jax.ShapeDtypeStruct((1, sources), jnp.int32),
-        ],
+        out_specs=WHOLE,
+        out_shape=jax.ShapeDtypeStruct((2, stations + 16, 2 * sources), bf16),
         scratch_shapes=[
             pltpu.VMEM((2, 2, stations, sources), bf16),
             pltpu.SMEM(inputs[0].shape, f32),
         ]
         + [pltpu.VMEM(array.shape, f32) for array in inputs[2:5]]
+        + [pltpu.VMEM((1, sources), f32), pltpu.VMEM((1, sources), jnp.int32)]
         + [pltpu.SemaphoreType.DMA((14,))],
         compiler_params=pltpu.CompilerParams(vmem_limit_bytes=60 * MIB),
         cost_estimate=pl.CostEstimate(
@@ -185,15 +191,30 @@
     stations, sources = gain.shape[3], gain.shape[4]
     return pl.pallas_call(
         phasor_own_kernel,
-        in_specs=[SCALARS] + [WHOLE] * 6,
+        in_specs=[SCALARS] + [WHOLE] * 4 + [ANY] * 2,
         out_specs=WHOLE,
         out_shape=jax.ShapeDtypeStruct((2, stations + 16, 2 * sources), bf16),
+        scratch_shapes=[
+            pltpu.VMEM((1, sources), f32),
+            pltpu.VMEM((1, sources), jnp.int32),
+            pltpu.SemaphoreType.DMA((2,)),
+        ],
         compiler_params=pltpu.CompilerParams(vmem_limit_bytes=16 * MIB),
         cost_estimate=pl.CostEstimate(
             flops=40 * 2 * stations * sources, bytes_accessed=3200000, transcendentals=0
         ),
         name="phasor_own",
     )(*inputs)
+
+
+def resid_block(resids, moment, rel, flip):
+    here, near, far = resids[moment]
+    first, second = STEPS[moment]
+    if rel == 0:
+        return here.at[flip]
+    if rel == second:
+        return near.at[flip]
+    return far.at[0 if rel == first else 1, flip]
 
 
 def upper_mask():
@@ -239,7 +260,7 @@
     return wide[part, pl.ds(pl.multiple_of(chip * 64, 64), 64), pl.ds(start, 384)]
 
 
-def model_kernel(scaling, own, other_hbm, out0, out1, out2, out3, wide, other, top, bottom, sems):
+def model_kernel(scaling, own, other_hbm, stay, keep, send0, send1, wide, other, top, bottom, sems):
     _, y, z = position()
     copies = [
         pltpu.make_async_copy(other_hbm.at[moment], other.at[moment], sems.at[moment])
@@ -261,29 +282,37 @@
                 (top[part] + mm(rows[0:256], q)) * scaling,
                 (bottom[part] + mm(rows[256:512], q[256:512])) * scaling,
             )
-        for rel, out in enumerate((out0, out1, out2, out3)):
+        first, second = STEPS[moment]
+        for rel in range(4):
             for flip in range(2):
                 zz = 1 - z if flip else z
                 chip = zz * 4 + y_partner(rel, y)
-                out[flip, moment] = pack(
+                value = pack(
                     block_of(wide, 0, chip), block_of(wide, 1, chip), chip % 2 == 1, zz == 0
-                ).astype(out.dtype)
+                )
+                if rel == 0:
+                    stay[flip, moment] = value
+                elif rel == second:
+                    keep[moment, flip] = value
+                else:
+                    send = (send0, send1)[moment]
+                    send[0 if rel == first else 1, flip] = value.astype(bf16)
 
 
 def model_parts(scaling, own, other):
+    four = jax.ShapeDtypeStruct((2, 2, 64, 512), f32)
     return pl.pallas_call(
         functools.partial(model_kernel, scaling),
         in_specs=[WHOLE, HBM],
         out_specs=[WHOLE] * 4,
         scratch_shapes=[
             pltpu.VMEM((2, 512, 768), f32),
-            pltpu.VMEM(other.shape, bf16),
+            pltpu.VMEM(own.shape, bf16),
             pltpu.VMEM((2, 256, 512), f32),
             pltpu.VMEM((2, 256, 256), f32),
             pltpu.SemaphoreType.DMA((2,)),
         ],
-        out_shape=[jax.ShapeDtypeStruct((2, 2, 64, 512), f32)]
-        + [jax.ShapeDtypeStruct((2, 2, 64, 512), bf16)] * 3,
+        out_shape=[four, four] + [jax.ShapeDtypeStruct((2, 2, 64, 512), bf16)] * 2,
         compiler_params=pltpu.CompilerParams(vmem_limit_bytes=16 * MIB),
         cost_estimate=pl.CostEstimate(
             flops=2 * 2 * 4 * 512 * 512 * 768, bytes_accessed=5000000, transcendentals=0
@@ -327,17 +356,35 @@
     )(own, other)
 
 
-def sum_kernel(own, one, two, three, _, stay, send):
-    for flip, out in ((0, stay), (1, send)):
-        out[...] = (
-            own[flip] + one[flip].astype(f32) + two[flip].astype(f32) + three[flip].astype(f32)
-        ).astype(out.dtype)
-
-
-def sum_parts(own, one, two, three, after):
+def relay_kernel(keep, got0, got1, _, out0, out1):
+    for moment, (got, out) in enumerate(((got0, out0), (got1, out1))):
+        out[...] = (keep[moment] + got[1].astype(f32)).astype(bf16)
+
+
+def relay_parts(keep, got0, got1, after):
+    return pl.pallas_call(
+        relay_kernel,
+        in_specs=[WHOLE] * 3 + [ANY],
+        out_specs=[WHOLE] * 2,
+        out_shape=[jax.ShapeDtypeStruct(keep.shape[1:], bf16)] * 2,
+        compiler_params=pltpu.CompilerParams(vmem_limit_bytes=4 * MIB),
+        cost_estimate=pl.CostEstimate(flops=300000, bytes_accessed=1500000, transcendentals=0),
+        name="relay_parts",
+    )(keep, got0, got1, after)
+
+
+def sum_kernel(own, got0, got1, last0, last1, stay, send):
+    for moment, (got, last) in enumerate(((got0, last0), (got1, last1))):
+        for flip, out in ((0, stay), (1, send)):
+            out[moment] = (
+                own[flip, moment] + got[0, flip].astype(f32) + last[flip].astype(f32)
+            ).astype(out.dtype)
+
+
+def sum_parts(own, *parts):
     return pl.pallas_call(
         sum_kernel,
-        in_specs=[WHOLE] * 4 + [ANY],
+        in_specs=[WHOLE] * 5,
         out_specs=[WHOLE] * 2,
         out_shape=[
             jax.ShapeDtypeStruct(own.shape[1:], f32),
@@ -346,10 +393,35 @@
         compiler_params=pltpu.CompilerParams(vmem_limit_bytes=4 * MIB),
         cost_estimate=pl.CostEstimate(flops=500000, bytes_accessed=2500000, transcendentals=0),
         name="sum_parts",
-    )(own, one, two, three, after)
-
-
-def observed_kernel(observed, flags, other, other_flags, obs_out, keep_out, own, wide, sem):
+    )(own, *parts)
+
+
+def observed_send_kernel(observed, flags, _, out, sem):
+    core, _, _ = position()
+    copy = pltpu.make_async_copy(observed.at[:, 1 - core], out.at[:, :, 0:2, :], sem)
+    copy.start()
+    for moment in range(2):
+        keep = flags[:, moment, :].astype(f32)
+        out[:, moment, 2, :] = keep
+        out[:, moment, 3, :] = keep
+    copy.wait()
+
+
+def observed_send(observed, flags, after):
+    rows, _, _, _, stations = observed.shape
+    return pl.pallas_call(
+        observed_send_kernel,
+        in_specs=[HBM, WHOLE, ANY],
+        out_specs=WHOLE,
+        out_shape=jax.ShapeDtypeStruct((rows, 2, 4, stations), f32),
+        scratch_shapes=[pltpu.SemaphoreType.DMA],
+        cost_estimate=pl.CostEstimate(flops=100000, bytes_accessed=700000, transcendentals=0),
+        compiler_params=pltpu.CompilerParams(vmem_limit_bytes=4 * MIB),
+        name="observed_send",
+    )(observed, flags, after)
+
+
+def observed_kernel(observed, flags, other, obs_out, keep_out, own, wide, sem):
     core, y, z = position()
     copy = pltpu.make_async_copy(observed.at[:, core], own, sem)
     copy.start()
@@ -360,10 +432,15 @@
     row = lax.broadcasted_iota(jnp.int32, (64, 512), 0)
     col = lax.broadcasted_iota(jnp.int32, (64, 512), 1)
     for moment in range(2):
-        for rows, source, kept in ((core, own, flags), (1 - core, other, other_flags)):
+        for rows, mine in ((core, True), (1 - core, False)):
             there = pl.ds(pl.multiple_of(rows * 32, 32), 32)
             for part in range(3):
-                value = kept[:, moment, :].astype(f32) if part == 2 else source[:, moment, part, :]
+                if not mine:
+                    value = other[:, moment, part, :]
+                elif part == 2:
+                    value = flags[:, moment, :].astype(f32)
+                else:
+                    value = own[:, moment, part, :]
                 wide[part, there, 0:512] = value
                 wide[part, there, 512:768] = value[:, 0:256]
         obs_out[moment] = pack(wide[0, :, start], wide[1, :, start], odd, z == 0)
@@ -371,33 +448,38 @@
         keep_out[moment] = jnp.where(row == col, 0.0, keep)
 
 
-def observed_parts(observed, flags, other, other_flags):
+def observed_parts(observed, flags, other):
+    rows, _, _, _, stations = observed.shape
     return pl.pallas_call(
         observed_kernel,
-        in_specs=[HBM] + [WHOLE] * 3,
+        in_specs=[HBM] + [WHOLE] * 2,
         out_specs=[WHOLE] * 2,
         out_shape=[jax.ShapeDtypeStruct((2, 64, 512), f32)] * 2,
         scratch_shapes=[
-            pltpu.VMEM(other.shape, f32),
+            pltpu.VMEM((rows, 2, 2, stations), f32),
             pltpu.VMEM((3, 64, 768), f32),
             pltpu.SemaphoreType.DMA,
         ],
         cost_estimate=pl.CostEstimate(flops=1000000, bytes_accessed=1500000, transcendentals=0),
         compiler_params=pltpu.CompilerParams(vmem_limit_bytes=6 * MIB),
         name="observed_parts",
-    )(observed, flags, other, other_flags)
-
-
-def gradient_kernel(scaling, freq, here, one, two, three, parts0, parts1, out, rows_sum, cols_sum):
+    )(observed, flags, other)
+
+
+def gradient_kernel(scaling, freq, *refs):
+    resids = refs[0:3], refs[3:6]
+    parts0, parts1, out, rows_sum, cols_sum = refs[6:]
     core, y, z = position()
-    for rel, source in enumerate((here, one, two, three)):
+    for rel in range(4):
         for flip in range(2):
             zz = 1 - z if flip else z
             chip = zz * 4 + y_partner(rel, y)
+            first = resid_block(resids, 0, rel, flip)
+            second = resid_block(resids, 1, rel, flip)
             for start in range(0, 64, 32):
                 rows = slice(start, start + 32)
-                resid0 = source[flip, 0, rows, :].astype(f32)
-                resid1 = source[flip, 1, rows, :].astype(f32)
+                resid0 = first[rows, :].astype(f32)
+                resid1 = second[rows, :].astype(f32)
                 for which in range(4):
                     product = resid0 * parts0[which, rel, flip, rows, :].astype(f32)
                     product += resid1 * parts1[which, rel, flip, rows, :].astype(f32)
@@ -438,20 +520,22 @@
     lax.fori_loop(0, out.shape[0], copy, 0, unroll=8)
 
 
-def gradient_parts(scaling, devices, freq, here, one, two, three, parts0, parts1):
+def gradient_parts(scaling, devices, freq, resids, parts0, parts1):
     return pl.pallas_call(
         functools.partial(gradient_kernel, scaling),
-        in_specs=[SCALARS] + [WHOLE] * 6,
+        in_specs=[SCALARS] + [WHOLE] * 8,
         out_specs=WHOLE,
         scratch_shapes=[pltpu.VMEM((4, 512, 128), f32), pltpu.VMEM((4, 8, 8, 512), f32)],
         out_shape=jax.ShapeDtypeStruct((devices, 16, 128), bf16),
         compiler_params=pltpu.CompilerParams(vmem_limit_bytes=12 * MIB),
         cost_estimate=pl.CostEstimate(flops=10000000, bytes_accessed=6000000, transcendentals=0),
         name="gradient_parts",
-    )(freq, here, one, two, three, parts0, parts1)
-
-
-def rows_kernel(resid, here, one, two, three, _, own_out, other_out, rolled):
+    )(freq, *resids, parts0, parts1)
+
+
+def rows_kernel(resid, *refs):
+    resids = refs[0:3], refs[3:6]
+    _, own_out, other_out, rolled = refs[6:]
     core, y, z = position()
     chip = z * 4 + y
     upper, lower = upper_mask()
@@ -467,12 +551,15 @@
         near_re = jnp.where(upper, near, jnp.where(lower, near_t, zero))
         near_im = jnp.where(lower, near, jnp.where(upper, -near_t, zero))
         far = own[:, 256:320]
-        far_t = jnp.transpose(here[1, moment][:, 256:320].astype(f32))
+        far_t = jnp.transpose(resid_block(resids, moment, 0, 1)[:, 256:320].astype(f32))
         far_re = jnp.where(z == 0, far, far_t)
         far_im = jnp.where(z == 0, -far_t, far)
-        block5 = jnp.where(even, one[flip5, moment].astype(f32), two[flip5, moment].astype(f32))
-        block6 = three[flip6, moment].astype(f32)
-        block7 = jnp.where(even, two[flip7, moment].astype(f32), one[flip7, moment].astype(f32))
+        one5, two5, block6, one7, two7 = (
+            resid_block(resids, moment, rel, flip)[...].astype(f32)
+            for rel, flip in ((1, flip5), (2, flip5), (3, flip6), (1, flip7), (2, flip7))
+        )
+        block5 = jnp.where(even, one5, two5)
+        block7 = jnp.where(even, two7, one7)
         re = [near_re, own[:, 64:256], far_re]
         im = [near_im, own[:, 320:512], far_im]
         for block, offset in ((block5, 3), (block6, 2), (block7, 1)):
@@ -485,17 +572,17 @@
             other_out[index] = rolled[index, pl.ds(pl.multiple_of((1 - core) * 32, 32), 32), :]
 
 
-def whole_rows(resid, here, one, two, three, after):
+def whole_rows(resid, resids, after):
     return pl.pallas_call(
         rows_kernel,
-        in_specs=[WHOLE] * 5 + [ANY],
+        in_specs=[WHOLE] * 7 + [ANY],
         out_specs=[WHOLE] * 2,
         out_shape=[jax.ShapeDtypeStruct((4, 32, 512), f32)] * 2,
         scratch_shapes=[pltpu.VMEM((4, 64, 512), f32)],
-        cost_estimate=pl.CostEstimate(flops=2000000, bytes_accessed=1500000, transcendentals=0),
+        cost_estimate=pl.CostEstimate(flops=0, bytes_accessed=0, transcendentals=0),
         compiler_params=pltpu.CompilerParams(vmem_limit_bytes=6 * MIB),
         name="whole_rows",
-    )(resid, here, one, two, three, after)
+    )(resid, *resids, after)
 
 
 def halves(value):
@@ -559,34 +646,36 @@
     core = position()[0]
     swap = functools.partial(lax.ppermute, axis_name="dir", perm=dir_perm(0, flip_core=True))
 
-    inputs = (freq_ratio, station_gain, station_uv, screen, source_lm)
-    sent, flux_row, direction_row = phasor_send(*inputs, source_flux, source_direction)
-    other = swap(sent)
-    own = phasor_own(*inputs, flux_row, direction_row)
-
-    other_flags = swap(flags)
-    other_observed = swap(lax.dynamic_index_in_dim(observed, 1 - core, 1, keepdims=False))
-    obs, kept = observed_parts(observed, flags, other_observed, other_flags)
-
-    part0, part1, part2, part3 = model_parts(scaling, own, other)
-    got = [
-        lax.ppermute(part, "dir", dir_perm(rel)) for rel, part in ((3, part3), (2, part2), (1, part1))
-    ]
+    inputs = (freq_ratio, station_gain, station_uv, screen, source_lm, source_flux, source_direction)
+    other = swap(phasor_send(*inputs))
+    own = phasor_own(*inputs)
+
+    def across(rel, array):
+        return lax.ppermute(array, "dir", dir_perm(rel))
+
+    def across_z(array):
+        return lax.ppermute(array, "dir", dir_perm(0, flip_z=True))
+
+    kept0, keep, send0, send1 = model_parts(scaling, own, other)
+    other_observed = swap(observed_send(observed, flags, send0))
+    obs, kept = observed_parts(observed, flags, other_observed)
+    got0, got1 = across(1, send0), across(2, send1)
     directions0 = direction_parts(0, own, other)
-    stay, send = sum_parts(part0, *got, directions0)
-    last = lax.ppermute(send, "dir", dir_perm(0, flip_z=True))
-    resid = kept * (obs - (stay + last.astype(f32)))
+    relay0, relay1 = relay_parts(keep, got0, got1, directions0)
+    last0, last1 = across(2, relay0), across(1, relay1)
+    stay, send = sum_parts(kept0, got0, got1, last0, last1)
+    resid = kept * (obs - (stay + across_z(send).astype(f32)))
     half = resid.astype(bf16)
-    here = jnp.stack([half, lax.ppermute(half, "dir", dir_perm(0, flip_z=True))])
-    three = lax.ppermute(here, "dir", dir_perm(3))
-    two = lax.ppermute(here, "dir", dir_perm(2))
-    one = lax.ppermute(here, "dir", dir_perm(1))
+    half_z = across_z(half)
     directions1 = direction_parts(1, own, other)
-
-    grads = gradient_parts(
-        scaling, devices, freq_ratio, here, one, two, three, directions0, directions1
-    )
-    own_rows, sent_rows = whole_rows(resid, here, one, two, three, grads)
+    resids = []
+    for moment, (first, second) in enumerate(STEPS):
+        here = jnp.stack([half[moment], half_z[moment]])
+        near = across(second, here)
+        resids.extend([here, near, across(first, jnp.stack([here, near]))])
+
+    grads = gradient_parts(scaling, devices, freq_ratio, resids, directions0, directions1)
+    own_rows, sent_rows = whole_rows(resid, resids, grads)
     other_rows = swap(sent_rows)
     grads = lax.all_to_all(grads, ("dir", "freq"), 0, 0, tiled=True)
     updated = updated_rows(grads, screen_kernel, screen)

time: 85.6 us -> 86.7 us (1.013)
  waiting for transfers between devices: 26.2 us -> 31.6 us
  Pallas kernels: 31.3 us -> 28.5 us
  local copies, waits for them, and re-layouts: 2.78 us -> 0.48 us
    ppermute x11 -> x12, waiting for transfers between devices: 14.6 us -> 20 us  [the longest x8 14.1 us: across(): return lax.ppermute(array, 'dir', dir_perm(rel))]
    pallas_call x2, Pallas kernels: 13.3 us -> 10.5 us  [direction_parts(): pl.pallas_call(functools.partial(direction_kernel, moment), in_specs=[WHO...]
    unnamed x20, local copies, waits for them, and re-layouts: 1.39 us -> 0.05 us
    squeeze x1 -> x0, local copies, waits for them, and re-layouts: 0.98 us -> none  [body(): lax.dynamic_index_in_dim(observed, 1 - core, 1, keepdims=False)]
    ppermute x11 -> x12, starting transfers between devices: 13.5 us -> 14.1 us  [the longest x8 9.84 us: across(): return lax.ppermute(array, 'dir', dir_perm(rel))]
    pallas_call x5 -> x7, Pallas kernels: 9.53 us -> 9.7 us  [the longest x1 5.1 us: phasor_send(): pl.pallas_call(phasor_send_kernel, in_specs=[HBM] * 7, out_specs=WHOLE, o...]
  transfers between devices with their start and end apart: 13 -> 14, of which waited for: 6 -> 10; matrix products, arithmetic and copies ran while one was open for 3% -> 2% of each run, Pallas kernels for 25% -> 17%
where the time goes in v4:
time: 86.7 us; the launch traced here: 86.6 us
  waiting for transfers between devices  31.6 us (36%)
  Pallas kernels  28.5 us (33%)
  starting transfers between devices  23.7 us (27%)
  other arithmetic  1.28 us (1%)
  between operations  0.98 us (1%)
    ppermute x8, waiting for transfers between devices, across(): return lax.ppermute(array, 'dir', dir_perm(rel))  14.1 us
    all_to_all x1, waiting for transfers between devices, body(): grads = lax.all_to_all(grads, ('dir', 'freq'), 0, 0, tiled=True)  11.6 us
    pallas_call x2, Pallas kernels, direction_parts(): pl.pallas_call(functools.partial(direction_kernel, moment), in_specs=[WHO...  10.5 us
    ppermute x8, starting transfers between devices, across(): return lax.ppermute(array, 'dir', dir_perm(rel))  9.84 us
    all_to_all x1, starting transfers between devices, body(): grads = lax.all_to_all(grads, ('dir', 'freq'), 0, 0, tiled=True)  9.55 us
    ppermute x2, waiting for transfers between devices, across_z(): return lax.ppermute(array, 'dir', dir_perm(0, flip_z=True))  5.28 us
    pallas_call x1, Pallas kernels, phasor_send(): pl.pallas_call(phasor_send_kernel, in_specs=[HBM] * 7, out_specs=WHOLE, o...  5.1 us
    pallas_call x1, Pallas kernels, model_parts(): pl.pallas_call(functools.partial(model_kernel, scaling), in_specs=[WHOLE,...  4.32 us
  transfers between devices with their start and end apart: 14, of which 10 were waited for; matrix products, arithmetic and copies ran while one was open for 2% of the time, Pallas kernels for 17%

profile of v4, /device:TPU:0, one launch (start us, length us, event | category | flops | bytes accessed | tf_op | source)
XLA Modules:
  0.0 86.6 jit_solution(8038887246685885213)
XLA Ops:
  0.7 5.1 %phasor_send.1 = bf16[2,528,768]{2,1,0:T(8,128)(2,1)} custom-call(f32[2]{0:T(128)} %freq.5, bf16[2,2,2,512,384]{4,3,2,1,0:T(8,128)(2,1)} %gain.3, f32[2,2,512]{2,1,0:T(2,128)} %uv.3, f32[2,512]{1,0:T(2,128)} %screen.5, f32[2,384]{1,0:T(2,128)} %lm.3, f32[384]{0:T(512)} %flux.3, s32[384]{0:T(512)} %direction.3), custom_call_target="tpu_custom_call" | custom-call | flops 15728640 | bytes 3200000 | tf_op jit(solution)/shard_map/phasor_send/pallas_call | solution.py:169
  6.0 2.9 %phasor_own.1.own = bf16[2,528,768]{2,1,0:T(8,128)(2,1)S(1)} custom-call(f32[2]{0:T(128)S(1)} %copy-done.9, bf16[2,2,2,512,384]{4,3,2,1,0:T(8,128)(2,1)S(1)} %copy-done, f32[2,2,512]{2,1,0:T(2,128)S(1)} %copy-done.5, f32[2,512]{1,0:T(2,128)S(1)} %copy-done.4, f32[2,384]{1,0:T(2,128)S(1)} %copy-done.6, f32[384]{0:T(512)S(1)} %copy-done.7, s32[384]{0:T(512)S(1)} %copy-done.8), custom_call_target="tpu_custom_call" | custom-call | flops 15728640 | bytes 3200000 | tf_op jit(solution)/shard_map/phasor_own/pallas_call | solution.py:192
  9.6 4.3 %model_parts.1 = (f32[2,2,64,512]{3,2,1,0:T(8,128)S(1)}, f32[2,2,64,512]{3,2,1,0:T(8,128)S(1)}, bf16[2,2,64,512]{3,2,1,0:T(8,128)(2,1)S(1)}, bf16[2,2,64,512]{3,2,1,0:T(8,128)(2,1)S(1)}) custom-call(bf16[2,528,768]{2,1,0:T(8,128)(2,1)S(1)} %phasor_own.1.own, bf16[2,528,768]{2,1,0:T(8,128)(2,1)S(1)} %collective-permute-done.other_hbm.other), custom_call_target="tpu_custom_call" | custom-call | flops 3221225472 | bytes 5000000 | tf_op jit(solution)/shard_map/model_parts/pallas_call | solution.py:304
  13.9 1.7 %collective-permute-start.2 = (bf16[2,2,64,512]{3,2,1,0:T(8,128)(2,1)S(1)}, bf16[2,2,64,512]{3,2,1,0:T(8,128)(2,1)S(1)}, u32[]{:S(2)}, u32[]{:S(2)}) collective-permute-start(bf16[2,2,64,512]{3,2,1,0:T(8,128)(2,1)S(1)} %get-tuple-element.14._), channel_id=1, source_target_pairs={{0,16},{8,24},{16,0},{24,8},{32,48},{40,56},{48,32},{56,40},{64,80... | collective-permute-start | bytes 786440 | tf_op jit(solution)/shard_map/ppermute | solution.py:654
  15.9 2.4 %collective-permute-start.3 = (bf16[2,2,64,512]{3,2,1,0:T(8,128)(2,1)S(1)}, bf16[2,2,64,512]{3,2,1,0:T(8,128)(2,1)S(1)}, u32[]{:S(2)}, u32[]{:S(2)}) collective-permute-start(bf16[2,2,64,512]{3,2,1,0:T(8,128)(2,1)S(1)} %get-tuple-element.18), channel_id=1, source_target_pairs={{0,48},{8,56},{16,32},{24,40},{32,16},{40,24},{48,0},{56,8},{64,11... | collective-permute-start | bytes 786440 | tf_op jit(solution)/shard_map/ppermute | solution.py:654
  18.3 5.2 %direction_parts0.1._.refs_6_ = bf16[4,4,2,64,512]{4,3,2,1,0:T(8,128)(2,1)S(1)} custom-call(bf16[2,528,768]{2,1,0:T(8,128)(2,1)S(1)} %phasor_own.1.own, bf16[2,528,768]{2,1,0:T(8,128)(2,1)S(1)} %collective-permute-done.other_hbm.other), custom_call_target="tpu_custom_call" | custom-call | flops 3221225472 | bytes 5000000 | tf_op jit(solution)/shard_map/direction_parts0/pallas_call | solution.py:345
  23.6 2.2 %collective-permute-done.3.got1 = bf16[2,2,64,512]{3,2,1,0:T(8,128)(2,1)S(1)} collective-permute-done((bf16[2,2,64,512]{3,2,1,0:T(8,128)(2,1)S(1)}, bf16[2,2,64,512]{3,2,1,0:T(8,128)(2,1)S(1)}, u32[]{:S(2)}, u32[]{:S(2)}) %collective-permute-start.3) | collective-permute-done | bytes 262176 | tf_op jit(solution)/shard_map/ppermute | solution.py:654
  25.9 2.3 %collective-permute-start.4 = (bf16[2,64,512]{2,1,0:T(8,128)(2,1)S(1)}, bf16[2,64,512]{2,1,0:T(8,128)(2,1)S(1)}, u32[]{:S(2)}, u32[]{:S(2)}) collective-permute-start(bf16[2,64,512]{2,1,0:T(8,128)(2,1)S(1)} %get-tuple-element.20), channel_id=1, source_target_pairs={{0,48},{8,56},{16,32},{24,40},{32,16},{40,24},{48,0},{56,8},{64,11... | collective-permute-start | bytes 393224 | tf_op jit(solution)/shard_map/ppermute | solution.py:654
  28.1 4.0 %collective-permute-done.4.last0 = bf16[2,64,512]{2,1,0:T(8,128)(2,1)S(1)} collective-permute-done((bf16[2,64,512]{2,1,0:T(8,128)(2,1)S(1)}, bf16[2,64,512]{2,1,0:T(8,128)(2,1)S(1)}, u32[]{:S(2)}, u32[]{:S(2)}) %collective-permute-start.4) | collective-permute-done | bytes 131104 | tf_op jit(solution)/shard_map/ppermute | solution.py:654
  32.1 1.0 %collective-permute-done.5.last1 = bf16[2,64,512]{2,1,0:T(8,128)(2,1)S(1)} collective-permute-done((bf16[2,64,512]{2,1,0:T(8,128)(2,1)S(1)}, bf16[2,64,512]{2,1,0:T(8,128)(2,1)S(1)}, u32[]{:S(2)}, u32[]{:S(2)}) %collective-permute-start.5) | collective-permute-done | bytes 131104 | tf_op jit(solution)/shard_map/ppermute | solution.py:654
  33.2 2.0 %collective-permute-start.6 = (bf16[2,64,512]{2,1,0:T(8,128)(2,1)S(1)}, bf16[2,64,512]{2,1,0:T(8,128)(2,1)S(1)}, u32[]{:S(2)}, u32[]{:S(2)}) collective-permute-start(bf16[2,64,512]{2,1,0:T(8,128)(2,1)S(1)} %get-tuple-element.23), channel_id=1, source_target_pairs={{0,64},{8,72},{16,80},{24,88},{32,96},{40,104},{48,112},{56,120},{... | collective-permute-start | bytes 393224 | tf_op jit(solution)/shard_map/ppermute | solution.py:657
  35.2 0.7 observed_parts.1
  35.9 2.3 %collective-permute-done.6 = bf16[2,64,512]{2,1,0:T(8,128)(2,1)S(1)} collective-permute-done((bf16[2,64,512]{2,1,0:T(8,128)(2,1)S(1)}, bf16[2,64,512]{2,1,0:T(8,128)(2,1)S(1)}, u32[]{:S(2)}, u32[]{:S(2)}) %collective-permute-start.6) | collective-permute-done | bytes 131104 | tf_op jit(solution)/shard_map/ppermute | solution.py:657
  38.3 2.1 %collective-permute-start.7 = (bf16[2,64,512]{2,1,0:T(8,128)(2,1)S(1)}, bf16[2,64,512]{2,1,0:T(8,128)(2,1)S(1)}, u32[]{:S(2)}, u32[]{:S(2)}) collective-permute-start(bf16[2,64,512]{2,1,0:T(8,128)(2,1)S(1)} %get-tuple-element.26), channel_id=1, source_target_pairs={{0,64},{8,72},{16,80},{24,88},{32,96},{40,104},{48,112},{56,120},{... | collective-permute-start | bytes 393224 | tf_op jit(solution)/shard_map/ppermute | solution.py:657
  40.4 3.0 %collective-permute-done.7 = bf16[2,64,512]{2,1,0:T(8,128)(2,1)S(1)} collective-permute-done((bf16[2,64,512]{2,1,0:T(8,128)(2,1)S(1)}, bf16[2,64,512]{2,1,0:T(8,128)(2,1)S(1)}, u32[]{:S(2)}, u32[]{:S(2)}) %collective-permute-start.7) | collective-permute-done | bytes 131104 | tf_op jit(solution)/shard_map/ppermute | solution.py:657
  43.4 1.3 %collective-permute-start.8 = (bf16[2,64,512]{2,1,0:T(8,128)(2,1)S(1)}, bf16[2,64,512]{2,1,0:T(8,128)(2,1)S(1)}, u32[]{:S(2)}, u32[]{:S(2)}) collective-permute-start(bf16[2,64,512]{2,1,0:T(8,128)(2,1)S(1)} %get-tuple-element.37.refs_0_), channel_id=1, source_target_pairs={{0,48},{8,56},{16,32},{24,40},{32,16},{40,24},{48,0},{56,8},{64,11... | collective-permute-start | bytes 393224 | tf_op jit(solution)/shard_map/ppermute | solution.py:654
  44.8 5.6 %collective-permute-done.8.refs_1_ = bf16[2,64,512]{2,1,0:T(8,128)(2,1)S(1)} collective-permute-done((bf16[2,64,512]{2,1,0:T(8,128)(2,1)S(1)}, bf16[2,64,512]{2,1,0:T(8,128)(2,1)S(1)}, u32[]{:S(2)}, u32[]{:S(2)}) %collective-permute-start.8) | collective-permute-done | bytes 131104 | tf_op jit(solution)/shard_map/ppermute | solution.py:654
  51.2 1.9 %collective-permute-start.11 = (bf16[2,2,64,512]{3,2,1,0:T(8,128)(2,1)S(1)}, bf16[2,2,64,512]{3,2,1,0:T(8,128)(2,1)S(1)}, u32[]{:S(2)}, u32[]{:S(2)}) collective-permute-start(bf16[2,2,64,512]{3,2,1,0:T(8,128)(2,1)S(1)} %pad_maximum_fusion.1), channel_id=1, source_target_pairs={{0,48},{8,56},{16,32},{24,40},{32,16},{40,24},{48,0},{56,8},{64,11... | collective-permute-start | bytes 786440 | tf_op jit(solution)/shard_map/ppermute | solution.py:654
  53.2 5.2 %direction_parts1.1.refs_7_ = bf16[4,4,2,64,512]{4,3,2,1,0:T(8,128)(2,1)S(1)} custom-call(bf16[2,528,768]{2,1,0:T(8,128)(2,1)S(1)} %phasor_own.1.own, bf16[2,528,768]{2,1,0:T(8,128)(2,1)S(1)} %collective-permute-done.other_hbm.other), custom_call_target="tpu_custom_call" | custom-call | flops 3221225472 | bytes 5000000 | tf_op jit(solution)/shard_map/direction_parts1/pallas_call | solution.py:345
  59.1 2.9 %gradient_parts.1.refs_6_ = bf16[128,16,128]{2,1,0:T(8,128)(2,1)} custom-call(f32[2]{0:T(128)S(1)} %copy-done.9, bf16[2,64,512]{2,1,0:T(8,128)(2,1)S(1)} %get-tuple-element.37.refs_0_, bf16[2,64,512]{2,1,0:T(8,128)(2,1)S(1)} %collective-permute-done.8.refs_1_, bf16[2,2,64,512]{3,2,1,0:T(8,128)(2,1)S(1)} %collective-permute-done.9.refs_2_, ...), custom_call_target="tpu_custom_call" | custom-call | flops 10000000 | bytes 6000000 | tf_op jit(solution)/shard_map/gradient_parts/pallas_call | solution.py:524
  62.7 9.5 %all-to-all-start = ((bf16[128,16,128]{2,1,0:T(8,128)(2,1)}), bf16[128,16,128]{2,1,0:T(8,128)(2,1)S(1)}, u32[]{:S(2)}, u32[]{:S(2)}) async-start(bf16[128,16,128]{2,1,0:T(8,128)(2,1)} %gradient_parts.1.refs_6_), calls=%async_computation | async-start | bytes 1048576 | tf_op jit(solution)/shard_map/all_to_all | solution.py:680
  72.8 1.1 %maximum_bitcast_fusion = f32[32,2,2,2,512]{4,3,2,1,0:T(2,128)} fusion(f32[1,2,2,32,512]{4,2,1,0,3:T(2,128)S(1)} %copy.13, f32[1,2,2,32,512]{4,2,1,0,3:T(2,128)S(1)} %copy.12), kind=kLoop, calls=%fused_computation | loop fusion | flops 131072 | bytes 1048576 | tf_op jit(solution)/shard_map/transpose | solution.py:686
  73.8 11.6 %all-to-all-done.grads = bf16[128,16,128]{2,1,0:T(8,128)(2,1)S(1)} async-done(((bf16[128,16,128]{2,1,0:T(8,128)(2,1)}), bf16[128,16,128]{2,1,0:T(8,128)(2,1)S(1)}, u32[]{:S(2)}, u32[]{:S(2)}) %all-to-all-start) | async-done | bytes 524320 | tf_op jit(solution)/shard_map/all_to_all | solution.py:680
  85.4 1.2 %updated_rows.1 = f32[2,512]{1,0:T(2,128)} custom-call(bf16[128,16,128]{2,1,0:T(8,128)(2,1)S(1)} %all-to-all-done.grads, f32[512,512]{1,0:T(8,128)S(1)} %copy-done.2, f32[2,512]{1,0:T(2,128)S(1)} %copy-done.4), custom_call_target="tpu_custom_call" | custom-call | flops 200000000 | bytes 1500000 | tf_op jit(solution)/shard_map/updated_rows/pallas_call | solution.py:619
  (47 shorter events, 4.0 us)
Async XLA Ops:
  0.6 5.3 %copy-start.9 = (f32[2]{0:T(128)S(1)}, f32[2]{0:T(128)}, u32[]{:S(2)}) copy-start(f32[2]{0:T(128)} %freq.5) | copy-start | bytes 28
  0.6 5.3 %copy-start = (bf16[2,2,2,512,384]{4,3,2,1,0:T(8,128)(2,1)S(1)}, bf16[2,2,2,512,384]{4,3,2,1,0:T(8,128)(2,1)}, u32[]{:S(2)}) copy-start(bf16[2,2,2,512,384]{4,3,2,1,0:T(8,128)(2,1)} %gain.3) | copy-start | bytes 9437188
  0.7 5.3 %copy-start.5 = (f32[2,2,512]{2,1,0:T(2,128)S(1)}, f32[2,2,512]{2,1,0:T(2,128)}, u32[]{:S(2)}) copy-start(f32[2,2,512]{2,1,0:T(2,128)} %uv.3) | copy-start | bytes 24580
  0.7 5.3 %copy-start.4 = (f32[2,512]{1,0:T(2,128)S(1)}, f32[2,512]{1,0:T(2,128)}, u32[]{:S(2)}) copy-start(f32[2,512]{1,0:T(2,128)} %screen.5) | copy-start | bytes 12292
  0.7 5.3 %copy-start.6 = (f32[2,384]{1,0:T(2,128)S(1)}, f32[2,384]{1,0:T(2,128)}, u32[]{:S(2)}) copy-start(f32[2,384]{1,0:T(2,128)} %lm.3) | copy-start | bytes 9220
  0.7 5.3 %copy-start.7 = (f32[384]{0:T(512)S(1)}, f32[384]{0:T(512)}, u32[]{:S(2)}) copy-start(f32[384]{0:T(512)} %flux.3) | copy-start | bytes 4612
  0.7 5.3 %copy-start.8 = (s32[384]{0:T(512)S(1)}, s32[384]{0:T(512)}, u32[]{:S(2)}) copy-start(s32[384]{0:T(512)} %direction.3) | copy-start | bytes 4612
  5.8 3.8 %collective-permute-start = (bf16[2,528,768]{2,1,0:T(8,128)(2,1)}, bf16[2,528,768]{2,1,0:T(8,128)(2,1)S(1)}, u32[]{:S(2)}, u32[]{:S(2)}) collective-permute-start(bf16[2,528,768]{2,1,0:T(8,128)(2,1)} %phasor_send.1), channel_id=1, source_target_pairs={{0,8},{8,0},{16,24},{24,16},{32,40},{40,32},{48,56},{56,48},{64,72... | collective-permute-start | bytes 4866056 | tf_op jit(solution)/shard_map/ppermute | solution.py:650
  8.9 6.7 %copy-start.1 = (f32[32,2,2,2,512]{4,3,2,1,0:T(2,128)S(1)}, f32[32,2,2,2,512]{4,3,2,1,0:T(2,128)}, u32[]{:S(2)}) copy-start(f32[32,2,2,2,512]{4,3,2,1,0:T(2,128)} %observed.3) | copy-start | bytes 1572868
  8.9 6.7 %copy-start.3 = (s32[32,2,512]{2,1,0:T(2,128)S(1)}, s32[32,2,512]{2,1,0:T(2,128)}, u32[]{:S(2)}) copy-start(s32[32,2,512]{2,1,0:T(2,128)} %flags.3) | copy-start | bytes 393220
  13.9 9.7 %collective-permute-start.2 = (bf16[2,2,64,512]{3,2,1,0:T(8,128)(2,1)S(1)}, bf16[2,2,64,512]{3,2,1,0:T(8,128)(2,1)S(1)}, u32[]{:S(2)}, u32[]{:S(2)}) collective-permute-start(bf16[2,2,64,512]{3,2,1,0:T(8,128)(2,1)S(1)} %get-tuple-element.14._), channel_id=1, source_target_pairs={{0,16},{8,24},{16,0},{24,8},{32,48},{40,56},{48,32},{56,40},{64,80... | collective-permute-start | bytes 786440 | tf_op jit(solution)/shard_map/ppermute | solution.py:654
  15.8 19.4 %collective-permute-start.1 = (f32[32,2,4,512]{3,2,1,0:T(4,128)S(1)}, f32[32,2,4,512]{3,2,1,0:T(4,128)S(1)}, u32[]{:S(2)}, u32[]{:S(2)}) collective-permute-start(f32[32,2,4,512]{3,2,1,0:T(4,128)S(1)} %observed_send.1), channel_id=1, source_target_pairs={{0,8},{8,0},{16,24},{24,16},{32,40},{40,32},{48,56},{56,48},{64,72... | collective-permute-start | bytes 1572872 | tf_op jit(solution)/shard_map/ppermute | solution.py:660
  15.9 9.9 %collective-permute-start.3 = (bf16[2,2,64,512]{3,2,1,0:T(8,128)(2,1)S(1)}, bf16[2,2,64,512]{3,2,1,0:T(8,128)(2,1)S(1)}, u32[]{:S(2)}, u32[]{:S(2)}) collective-permute-start(bf16[2,2,64,512]{3,2,1,0:T(8,128)(2,1)S(1)} %get-tuple-element.18), channel_id=1, source_target_pairs={{0,48},{8,56},{16,32},{24,40},{32,16},{40,24},{48,0},{56,8},{64,11... | collective-permute-start | bytes 786440 | tf_op jit(solution)/shard_map/ppermute | solution.py:654
  25.9 6.3 %collective-permute-start.4 = (bf16[2,64,512]{2,1,0:T(8,128)(2,1)S(1)}, bf16[2,64,512]{2,1,0:T(8,128)(2,1)S(1)}, u32[]{:S(2)}, u32[]{:S(2)}) collective-permute-start(bf16[2,64,512]{2,1,0:T(8,128)(2,1)S(1)} %get-tuple-element.20), channel_id=1, source_target_pairs={{0,48},{8,56},{16,32},{24,40},{32,16},{40,24},{48,0},{56,8},{64,11... | collective-permute-start | bytes 393224 | tf_op jit(solution)/shard_map/ppermute | solution.py:654
  28.1 5.0 %collective-permute-start.5 = (bf16[2,64,512]{2,1,0:T(8,128)(2,1)S(1)}, bf16[2,64,512]{2,1,0:T(8,128)(2,1)S(1)}, u32[]{:S(2)}, u32[]{:S(2)}) collective-permute-start(bf16[2,64,512]{2,1,0:T(8,128)(2,1)S(1)} %get-tuple-element.21), channel_id=1, source_target_pairs={{0,16},{8,24},{16,0},{24,8},{32,48},{40,56},{48,32},{56,40},{64,80... | collective-permute-start | bytes 393224 | tf_op jit(solution)/shard_map/ppermute | solution.py:654
  33.2 5.0 %collective-permute-start.6 = (bf16[2,64,512]{2,1,0:T(8,128)(2,1)S(1)}, bf16[2,64,512]{2,1,0:T(8,128)(2,1)S(1)}, u32[]{:S(2)}, u32[]{:S(2)}) collective-permute-start(bf16[2,64,512]{2,1,0:T(8,128)(2,1)S(1)} %get-tuple-element.23), channel_id=1, source_target_pairs={{0,64},{8,72},{16,80},{24,88},{32,96},{40,104},{48,112},{56,120},{... | collective-permute-start | bytes 393224 | tf_op jit(solution)/shard_map/ppermute | solution.py:657
  38.3 5.0 %collective-permute-start.7 = (bf16[2,64,512]{2,1,0:T(8,128)(2,1)S(1)}, bf16[2,64,512]{2,1,0:T(8,128)(2,1)S(1)}, u32[]{:S(2)}, u32[]{:S(2)}) collective-permute-start(bf16[2,64,512]{2,1,0:T(8,128)(2,1)S(1)} %get-tuple-element.26), channel_id=1, source_target_pairs={{0,64},{8,72},{16,80},{24,88},{32,96},{40,104},{48,112},{56,120},{... | collective-permute-start | bytes 393224 | tf_op jit(solution)/shard_map/ppermute | solution.py:657
  43.4 7.0 %collective-permute-start.8 = (bf16[2,64,512]{2,1,0:T(8,128)(2,1)S(1)}, bf16[2,64,512]{2,1,0:T(8,128)(2,1)S(1)}, u32[]{:S(2)}, u32[]{:S(2)}) collective-permute-start(bf16[2,64,512]{2,1,0:T(8,128)(2,1)S(1)} %get-tuple-element.37.refs_0_), channel_id=1, source_target_pairs={{0,48},{8,56},{16,32},{24,40},{32,16},{40,24},{48,0},{56,8},{64,11... | collective-permute-start | bytes 393224 | tf_op jit(solution)/shard_map/ppermute | solution.py:654
  44.7 6.4 %collective-permute-start.10 = (bf16[2,64,512]{2,1,0:T(8,128)(2,1)S(1)}, bf16[2,64,512]{2,1,0:T(8,128)(2,1)S(1)}, u32[]{:S(2)}, u32[]{:S(2)}) collective-permute-start(bf16[2,64,512]{2,1,0:T(8,128)(2,1)S(1)} %get-tuple-element.31.refs_3_), channel_id=1, source_target_pairs={{0,16},{8,24},{16,0},{24,8},{32,48},{40,56},{48,32},{56,40},{64,80... | collective-permute-start | bytes 393224 | tf_op jit(solution)/shard_map/ppermute | solution.py:654
  50.5 7.9 %collective-permute-start.9 = (bf16[2,2,64,512]{3,2,1,0:T(8,128)(2,1)S(1)}, bf16[2,2,64,512]{3,2,1,0:T(8,128)(2,1)S(1)}, u32[]{:S(2)}, u32[]{:S(2)}) collective-permute-start(bf16[2,2,64,512]{3,2,1,0:T(8,128)(2,1)S(1)} %pad_maximum_fusion), channel_id=1, source_target_pairs={{0,16},{8,24},{16,0},{24,8},{32,48},{40,56},{48,32},{56,40},{64,80... | collective-permute-start | bytes 786440 | tf_op jit(solution)/shard_map/ppermute | solution.py:654
  51.2 7.9 %collective-permute-start.11 = (bf16[2,2,64,512]{3,2,1,0:T(8,128)(2,1)S(1)}, bf16[2,2,64,512]{3,2,1,0:T(8,128)(2,1)S(1)}, u32[]{:S(2)}, u32[]{:S(2)}) collective-permute-start(bf16[2,2,64,512]{3,2,1,0:T(8,128)(2,1)S(1)} %pad_maximum_fusion.1), channel_id=1, source_target_pairs={{0,48},{8,56},{16,32},{24,40},{32,16},{40,24},{48,0},{56,8},{64,11... | collective-permute-start | bytes 786440 | tf_op jit(solution)/shard_map/ppermute | solution.py:654
  62.6 22.8 %copy-start.2 = (f32[512,512]{1,0:T(8,128)S(1)}, f32[512,512]{1,0:T(8,128)}, u32[]{:S(2)}) copy-start(f32[512,512]{1,0:T(8,128)} %kernel.1) | copy-start | bytes 3145732
  62.6 9.7 %collective-permute-start.12 = (f32[4,32,512]{2,1,0:T(8,128)S(1)}, f32[4,32,512]{2,1,0:T(8,128)S(1)}, u32[]{:S(2)}, u32[]{:S(2)}) collective-permute-start(f32[4,32,512]{2,1,0:T(8,128)S(1)} %get-tuple-element.25), channel_id=1, source_target_pairs={{0,8},{8,0},{16,24},{24,16},{32,40},{40,32},{48,56},{56,48},{64,72... | collective-permute-start | bytes 786440 | tf_op jit(solution)/shard_map/ppermute | solution.py:679
  62.7 22.7 %all-to-all-start = ((bf16[128,16,128]{2,1,0:T(8,128)(2,1)}), bf16[128,16,128]{2,1,0:T(8,128)(2,1)S(1)}, u32[]{:S(2)}, u32[]{:S(2)}) async-start(bf16[128,16,128]{2,1,0:T(8,128)(2,1)} %gradient_parts.1.refs_6_), calls=%async_computation | async-start | bytes 1048576 | tf_op jit(solution)/shard_map/all_to_all | solution.py:680

commit v5 on v4

--- a/solution.py
+++ b/solution.py
@@ -42,7 +42,6 @@
     return pairs
 
 
-STEPS = ((1, 2), (2, 1))
 ANY = pl.BlockSpec(memory_space=pl.ANY)
 HBM = pl.BlockSpec(memory_space=pltpu.HBM)
 WHOLE = pl.BlockSpec(memory_space=pltpu.VMEM)
@@ -207,16 +206,6 @@
     )(*inputs)
 
 
-def resid_block(resids, moment, rel, flip):
-    here, near, far = resids[moment]
-    first, second = STEPS[moment]
-    if rel == 0:
-        return here.at[flip]
-    if rel == second:
-        return near.at[flip]
-    return far.at[0 if rel == first else 1, flip]
-
-
 def upper_mask():
     row = lax.broadcasted_iota(jnp.int32, (64, 64), 0)
     col = lax.broadcasted_iota(jnp.int32, (64, 64), 1)
@@ -260,7 +249,7 @@
     return wide[part, pl.ds(pl.multiple_of(chip * 64, 64), 64), pl.ds(start, 384)]
 
 
-def model_kernel(scaling, own, other_hbm, stay, keep, send0, send1, wide, other, top, bottom, sems):
+def model_kernel(scaling, own, other_hbm, stay, out11, out21, out31, out10, out20, out30, wide, other, top, bottom, sems):
     _, y, z = position()
     copies = [
         pltpu.make_async_copy(other_hbm.at[moment], other.at[moment], sems.at[moment])
@@ -282,9 +271,8 @@
                 (top[part] + mm(rows[0:256], q)) * scaling,
                 (bottom[part] + mm(rows[256:512], q[256:512])) * scaling,
             )
-        first, second = STEPS[moment]
-        for rel in range(4):
-            for flip in range(2):
+        for flip, outs in ((1, (out11, out21, out31)), (0, (out10, out20, out30))):
+            for rel in range(4):
                 zz = 1 - z if flip else z
                 chip = zz * 4 + y_partner(rel, y)
                 value = pack(
@@ -292,19 +280,15 @@
                 )
                 if rel == 0:
                     stay[flip, moment] = value
-                elif rel == second:
-                    keep[moment, flip] = value
                 else:
-                    send = (send0, send1)[moment]
-                    send[0 if rel == first else 1, flip] = value.astype(bf16)
+                    outs[rel - 1][moment] = value.astype(bf16)
 
 
 def model_parts(scaling, own, other):
-    four = jax.ShapeDtypeStruct((2, 2, 64, 512), f32)
     return pl.pallas_call(
         functools.partial(model_kernel, scaling),
         in_specs=[WHOLE, HBM],
-        out_specs=[WHOLE] * 4,
+        out_specs=[WHOLE] * 7,
         scratch_shapes=[
             pltpu.VMEM((2, 512, 768), f32),
             pltpu.VMEM(own.shape, bf16),
@@ -312,7 +296,8 @@
             pltpu.VMEM((2, 256, 256), f32),
             pltpu.SemaphoreType.DMA((2,)),
         ],
-        out_shape=[four, four] + [jax.ShapeDtypeStruct((2, 2, 64, 512), bf16)] * 2,
+        out_shape=[jax.ShapeDtypeStruct((2, 2, 64, 512), f32)]
+        + [jax.ShapeDtypeStruct((2, 64, 512), bf16)] * 6,
         compiler_params=pltpu.CompilerParams(vmem_limit_bytes=16 * MIB),
         cost_estimate=pl.CostEstimate(
             flops=2 * 2 * 4 * 512 * 512 * 768, bytes_accessed=5000000, transcendentals=0
@@ -356,35 +341,35 @@
     )(own, other)
 
 
-def relay_kernel(keep, got0, got1, _, out0, out1):
-    for moment, (got, out) in enumerate(((got0, out0), (got1, out1))):
-        out[...] = (keep[moment] + got[1].astype(f32)).astype(bf16)
-
-
-def relay_parts(keep, got0, got1, after):
-    return pl.pallas_call(
-        relay_kernel,
-        in_specs=[WHOLE] * 3 + [ANY],
-        out_specs=[WHOLE] * 2,
-        out_shape=[jax.ShapeDtypeStruct(keep.shape[1:], bf16)] * 2,
+def send_kernel(own, one, two, three, send):
+    send[...] = (
+        own[1] + one[...].astype(f32) + two[...].astype(f32) + three[...].astype(f32)
+    ).astype(bf16)
+
+
+def send_parts(own, *parts):
+    return pl.pallas_call(
+        send_kernel,
+        in_specs=[WHOLE] * 4,
+        out_specs=WHOLE,
+        out_shape=jax.ShapeDtypeStruct(own.shape[1:], bf16),
         compiler_params=pltpu.CompilerParams(vmem_limit_bytes=4 * MIB),
         cost_estimate=pl.CostEstimate(flops=300000, bytes_accessed=1500000, transcendentals=0),
-        name="relay_parts",
-    )(keep, got0, got1, after)
-
-
-def sum_kernel(own, got0, got1, last0, last1, stay, send):
-    for moment, (got, last) in enumerate(((got0, last0), (got1, last1))):
-        for flip, out in ((0, stay), (1, send)):
-            out[moment] = (
-                own[flip, moment] + got[0, flip].astype(f32) + last[flip].astype(f32)
-            ).astype(out.dtype)
-
-
-def sum_parts(own, *parts):
-    return pl.pallas_call(
-        sum_kernel,
-        in_specs=[WHOLE] * 5,
+        name="send_parts",
+    )(own, *parts)
+
+
+def residual_kernel(own, one, two, three, last, obs, kept, _, resid, half):
+    total = own[0] + one[...].astype(f32) + two[...].astype(f32) + three[...].astype(f32)
+    value = kept[...] * (obs[...] - (total + last[...].astype(f32)))
+    resid[...] = value
+    half[...] = value.astype(bf16)
+
+
+def residual_parts(own, *parts):
+    return pl.pallas_call(
+        residual_kernel,
+        in_specs=[WHOLE] * 7 + [ANY],
         out_specs=[WHOLE] * 2,
         out_shape=[
             jax.ShapeDtypeStruct(own.shape[1:], f32),
@@ -392,7 +377,7 @@
         ],
         compiler_params=pltpu.CompilerParams(vmem_limit_bytes=4 * MIB),
         cost_estimate=pl.CostEstimate(flops=500000, bytes_accessed=2500000, transcendentals=0),
-        name="sum_parts",
+        name="residual_parts",
     )(own, *parts)
 
 
@@ -467,19 +452,18 @@
 
 
 def gradient_kernel(scaling, freq, *refs):
-    resids = refs[0:3], refs[3:6]
-    parts0, parts1, out, rows_sum, cols_sum = refs[6:]
+    resids = refs[0:8]
+    parts0, parts1, out, rows_sum, cols_sum = refs[8:]
     core, y, z = position()
     for rel in range(4):
         for flip in range(2):
             zz = 1 - z if flip else z
             chip = zz * 4 + y_partner(rel, y)
-            first = resid_block(resids, 0, rel, flip)
-            second = resid_block(resids, 1, rel, flip)
+            source = resids[flip * 4 + rel]
             for start in range(0, 64, 32):
                 rows = slice(start, start + 32)
-                resid0 = first[rows, :].astype(f32)
-                resid1 = second[rows, :].astype(f32)
+                resid0 = source[0, rows, :].astype(f32)
+                resid1 = source[1, rows, :].astype(f32)
                 for which in range(4):
                     product = resid0 * parts0[which, rel, flip, rows, :].astype(f32)
                     product += resid1 * parts1[which, rel, flip, rows, :].astype(f32)
@@ -523,7 +507,7 @@
 def gradient_parts(scaling, devices, freq, resids, parts0, parts1):
     return pl.pallas_call(
         functools.partial(gradient_kernel, scaling),
-        in_specs=[SCALARS] + [WHOLE] * 8,
+        in_specs=[SCALARS] + [WHOLE] * 10,
         out_specs=WHOLE,
         scratch_shapes=[pltpu.VMEM((4, 512, 128), f32), pltpu.VMEM((4, 8, 8, 512), f32)],
         out_shape=jax.ShapeDtypeStruct((devices, 16, 128), bf16),
@@ -534,8 +518,8 @@
 
 
 def rows_kernel(resid, *refs):
-    resids = refs[0:3], refs[3:6]
-    _, own_out, other_out, rolled = refs[6:]
+    resids = refs[0:8]
+    _, own_out, other_out, rolled = refs[8:]
     core, y, z = position()
     chip = z * 4 + y
     upper, lower = upper_mask()
@@ -551,11 +535,11 @@
         near_re = jnp.where(upper, near, jnp.where(lower, near_t, zero))
         near_im = jnp.where(lower, near, jnp.where(upper, -near_t, zero))
         far = own[:, 256:320]
-        far_t = jnp.transpose(resid_block(resids, moment, 0, 1)[:, 256:320].astype(f32))
+        far_t = jnp.transpose(resids[4][moment][:, 256:320].astype(f32))
         far_re = jnp.where(z == 0, far, far_t)
         far_im = jnp.where(z == 0, -far_t, far)
         one5, two5, block6, one7, two7 = (
-            resid_block(resids, moment, rel, flip)[...].astype(f32)
+            jnp.where(flip == 1, resids[4 + rel][moment], resids[rel][moment]).astype(f32)
             for rel, flip in ((1, flip5), (2, flip5), (3, flip6), (1, flip7), (2, flip7))
         )
         block5 = jnp.where(even, one5, two5)
@@ -575,7 +559,7 @@
 def whole_rows(resid, resids, after):
     return pl.pallas_call(
         rows_kernel,
-        in_specs=[WHOLE] * 7 + [ANY],
+        in_specs=[WHOLE] * 9 + [ANY],
         out_specs=[WHOLE] * 2,
         out_shape=[jax.ShapeDtypeStruct((4, 32, 512), f32)] * 2,
         scratch_shapes=[pltpu.VMEM((4, 64, 512), f32)],
@@ -656,23 +640,19 @@
     def across_z(array):
         return lax.ppermute(array, "dir", dir_perm(0, flip_z=True))
 
-    kept0, keep, send0, send1 = model_parts(scaling, own, other)
-    other_observed = swap(observed_send(observed, flags, send0))
+    parts = model_parts(scaling, own, other)
+    far = [across(rel, parts[rel]) for rel in (3, 2, 1)]
+    near = [across(rel, parts[rel + 3]) for rel in (3, 2, 1)]
+    other_observed = swap(observed_send(observed, flags, parts[6]))
     obs, kept = observed_parts(observed, flags, other_observed)
-    got0, got1 = across(1, send0), across(2, send1)
     directions0 = direction_parts(0, own, other)
-    relay0, relay1 = relay_parts(keep, got0, got1, directions0)
-    last0, last1 = across(2, relay0), across(1, relay1)
-    stay, send = sum_parts(kept0, got0, got1, last0, last1)
-    resid = kept * (obs - (stay + across_z(send).astype(f32)))
-    half = resid.astype(bf16)
+    last = across_z(send_parts(parts[0], *far))
+    resid, half = residual_parts(parts[0], *near, last, obs, kept, directions0)
     half_z = across_z(half)
     directions1 = direction_parts(1, own, other)
-    resids = []
-    for moment, (first, second) in enumerate(STEPS):
-        here = jnp.stack([half[moment], half_z[moment]])
-        near = across(second, here)
-        resids.extend([here, near, across(first, jnp.stack([here, near]))])
+    resids = [
+        array if rel == 0 else across(rel, array) for array in (half, half_z) for rel in range(4)
+    ]
 
     grads = gradient_parts(scaling, devices, freq_ratio, resids, directions0, directions1)
     own_rows, sent_rows = whole_rows(resid, resids, grads)

time: 86.7 us -> 78.8 us (0.909)
  waiting for transfers between devices: 31.6 us -> 14.9 us
  starting transfers between devices: 23.7 us -> 32.7 us
    ppermute x8 -> x12, waiting for transfers between devices: 14.1 us -> 1.28 us  [across(): return lax.ppermute(array, 'dir', dir_perm(rel))]
    ppermute x8 -> x12, starting transfers between devices: 9.84 us -> 19.4 us  [across(): return lax.ppermute(array, 'dir', dir_perm(rel))]
    ppermute x2, waiting for transfers between devices: 5.28 us -> 1.38 us  [across_z(): return lax.ppermute(array, 'dir', dir_perm(0, flip_z=True))]
    ppermute x2, starting transfers between devices: 4.08 us -> 2.37 us  [across_z(): return lax.ppermute(array, 'dir', dir_perm(0, flip_z=True))]
    all_to_all x1, starting transfers between devices: 9.55 us -> 10.6 us  [body(): grads = lax.all_to_all(grads, ('dir', 'freq'), 0, 0, tiled=True)]
  transfers between devices with their start and end apart: 14 -> 18, of which waited for: 10 -> 5; matrix products, arithmetic and copies ran while one was open for 2% -> 2% of each run, Pallas kernels for 17% -> 18%
where the time goes in v5:
time: 78.8 us; the launch traced here: 78.6 us
  starting transfers between devices  32.7 us (41%)
  Pallas kernels  28.4 us (36%)
  waiting for transfers between devices  14.9 us (19%)
  other arithmetic  1.1 us (1%)
  between operations  0.99 us (1%)
    ppermute x12, starting transfers between devices, across(): return lax.ppermute(array, 'dir', dir_perm(rel))  19.4 us
    all_to_all x1, waiting for transfers between devices, body(): grads = lax.all_to_all(grads, ('dir', 'freq'), 0, 0, tiled=True)  11.6 us
    all_to_all x1, starting transfers between devices, body(): grads = lax.all_to_all(grads, ('dir', 'freq'), 0, 0, tiled=True)  10.6 us
    pallas_call x2, Pallas kernels, direction_parts(): pl.pallas_call(functools.partial(direction_kernel, moment), in_specs=[WHO...  10.5 us
    pallas_call x1, Pallas kernels, phasor_send(): pl.pallas_call(phasor_send_kernel, in_specs=[HBM] * 7, out_specs=WHOLE, o...  5.1 us
    pallas_call x1, Pallas kernels, model_parts(): pl.pallas_call(functools.partial(model_kernel, scaling), in_specs=[WHOLE,...  4.17 us
    pallas_call x1, Pallas kernels, phasor_own(): pl.pallas_call(phasor_own_kernel, in_specs=[SCALARS] + [WHOLE] * 4 + [ANY...  2.93 us
    pallas_call x1, Pallas kernels, gradient_parts(): pl.pallas_call(functools.partial(gradient_kernel, scaling), in_specs=[SCA...  2.86 us
  transfers between devices with their start and end apart: 18, of which 5 were waited for; matrix products, arithmetic and copies ran while one was open for 2% of the time, Pallas kernels for 18%

profile of v5, /device:TPU:0, one launch (start us, length us, event | category | flops | bytes accessed | tf_op | source)
XLA Modules:
  0.0 78.6 jit_solution(3138181172026057388)
XLA Ops:
  0.7 5.1 %phasor_send.1 = bf16[2,528,768]{2,1,0:T(8,128)(2,1)} custom-call(f32[2]{0:T(128)} %freq.5, bf16[2,2,2,512,384]{4,3,2,1,0:T(8,128)(2,1)} %gain.3, f32[2,2,512]{2,1,0:T(2,128)} %uv.3, f32[2,512]{1,0:T(2,128)} %screen.5, f32[2,384]{1,0:T(2,128)} %lm.3, f32[384]{0:T(512)} %flux.3, s32[384]{0:T(512)} %direction.3), custom_call_target="tpu_custom_call" | custom-call | flops 15728640 | bytes 3200000 | tf_op jit(solution)/shard_map/phasor_send/pallas_call | solution.py:168
  6.0 2.9 %phasor_own.1.own = bf16[2,528,768]{2,1,0:T(8,128)(2,1)S(1)} custom-call(f32[2]{0:T(128)S(1)} %copy-done.9, bf16[2,2,2,512,384]{4,3,2,1,0:T(8,128)(2,1)S(1)} %copy-done, f32[2,2,512]{2,1,0:T(2,128)S(1)} %copy-done.5, f32[2,512]{1,0:T(2,128)S(1)} %copy-done.4, f32[2,384]{1,0:T(2,128)S(1)} %copy-done.6, f32[384]{0:T(512)S(1)} %copy-done.7, s32[384]{0:T(512)S(1)} %copy-done.8), custom_call_target="tpu_custom_call" | custom-call | flops 15728640 | bytes 3200000 | tf_op jit(solution)/shard_map/phasor_own/pallas_call | solution.py:191
  8.9 0.6 collective-permute-done.other_hbm.other
  9.6 4.2 %model_parts.1 = (f32[2,2,64,512]{3,2,1,0:T(8,128)S(1)}, bf16[2,64,512]{2,1,0:T(8,128)(2,1)S(1)}, bf16[2,64,512]{2,1,0:T(8,128)(2,1)S(1)}, bf16[2,64,512]{2,1,0:...) custom-call(bf16[2,528,768]{2,1,0:T(8,128)(2,1)S(1)} %phasor_own.1.o, ...), custom_call_target="tpu_custom_call" | custom-call | flops 3221225472 | bytes 5000000 | tf_op jit(solution)/shard_map/model_parts/pallas_call | solution.py:288
  14.2 3.3 %collective-permute-start.4 = (bf16[2,64,512]{2,1,0:T(8,128)(2,1)S(1)}, bf16[2,64,512]{2,1,0:T(8,128)(2,1)S(1)}, u32[]{:S(2)}, u32[]{:S(2)}) collective-permute-start(bf16[2,64,512]{2,1,0:T(8,128)(2,1)S(1)} %get-tuple-element.19), channel_id=1, source_target_pairs={{0,32},{8,40},{16,48},{24,56},{32,0},{40,8},{48,16},{56,24},{64,96... | collective-permute-start | bytes 393224 | tf_op jit(solution)/shard_map/ppermute | solution.py:638
  17.4 1.1 %collective-permute-start.5 = (bf16[2,64,512]{2,1,0:T(8,128)(2,1)S(1)}, bf16[2,64,512]{2,1,0:T(8,128)(2,1)S(1)}, u32[]{:S(2)}, u32[]{:S(2)}) collective-permute-start(bf16[2,64,512]{2,1,0:T(8,128)(2,1)S(1)} %get-tuple-element.20), channel_id=1, source_target_pairs={{0,48},{8,56},{16,32},{24,40},{32,16},{40,24},{48,0},{56,8},{64,11... | collective-permute-start | bytes 393224 | tf_op jit(solution)/shard_map/ppermute | solution.py:638
  18.5 3.6 %collective-permute-start.1 = (bf16[2,64,512]{2,1,0:T(8,128)(2,1)S(1)}, bf16[2,64,512]{2,1,0:T(8,128)(2,1)S(1)}, u32[]{:S(2)}, u32[]{:S(2)}) collective-permute-start(bf16[2,64,512]{2,1,0:T(8,128)(2,1)S(1)} %get-tuple-element.16._), channel_id=1, source_target_pairs={{0,32},{8,40},{16,48},{24,56},{32,0},{40,8},{48,16},{56,24},{64,96... | collective-permute-start | bytes 393224 | tf_op jit(solution)/shard_map/ppermute | solution.py:638
  22.1 2.9 %collective-permute-start.2 = (bf16[2,64,512]{2,1,0:T(8,128)(2,1)S(1)}, bf16[2,64,512]{2,1,0:T(8,128)(2,1)S(1)}, u32[]{:S(2)}, u32[]{:S(2)}) collective-permute-start(bf16[2,64,512]{2,1,0:T(8,128)(2,1)S(1)} %get-tuple-element.17), channel_id=1, source_target_pairs={{0,48},{8,56},{16,32},{24,40},{32,16},{40,24},{48,0},{56,8},{64,11... | collective-permute-start | bytes 393224 | tf_op jit(solution)/shard_map/ppermute | solution.py:638
  25.1 1.5 %collective-permute-start.3 = (bf16[2,64,512]{2,1,0:T(8,128)(2,1)S(1)}, bf16[2,64,512]{2,1,0:T(8,128)(2,1)S(1)}, u32[]{:S(2)}, u32[]{:S(2)}) collective-permute-start(bf16[2,64,512]{2,1,0:T(8,128)(2,1)S(1)} %get-tuple-element.18), channel_id=1, source_target_pairs={{0,16},{8,24},{16,0},{24,8},{32,48},{40,56},{48,32},{56,40},{64,80... | collective-permute-start | bytes 393224 | tf_op jit(solution)/shard_map/ppermute | solution.py:638
  26.6 2.2 %collective-permute-start.7 = (bf16[2,64,512]{2,1,0:T(8,128)(2,1)S(1)}, bf16[2,64,512]{2,1,0:T(8,128)(2,1)S(1)}, u32[]{:S(2)}, u32[]{:S(2)}) collective-permute-start(bf16[2,64,512]{2,1,0:T(8,128)(2,1)S(1)} %send_parts.1), channel_id=1, source_target_pairs={{0,64},{8,72},{16,80},{24,88},{32,96},{40,104},{48,112},{56,120},{... | collective-permute-start | bytes 393224 | tf_op jit(solution)/shard_map/ppermute | solution.py:641
  28.8 5.2 %direction_parts0.1._.refs_8_ = bf16[4,4,2,64,512]{4,3,2,1,0:T(8,128)(2,1)S(1)} custom-call(bf16[2,528,768]{2,1,0:T(8,128)(2,1)S(1)} %phasor_own.1.own, bf16[2,528,768]{2,1,0:T(8,128)(2,1)S(1)} %collective-permute-done.other_hbm.other), custom_call_target="tpu_custom_call" | custom-call | flops 3221225472 | bytes 5000000 | tf_op jit(solution)/shard_map/direction_parts0/pallas_call | solution.py:330
  34.1 0.7 observed_parts.1
  35.1 2.8 %collective-permute-start.11 = (bf16[2,64,512]{2,1,0:T(8,128)(2,1)S(1)}, bf16[2,64,512]{2,1,0:T(8,128)(2,1)S(1)}, u32[]{:S(2)}, u32[]{:S(2)}) collective-permute-start(bf16[2,64,512]{2,1,0:T(8,128)(2,1)S(1)} %get-tuple-element.25.refs_0_), channel_id=1, source_target_pairs={{0,32},{8,40},{16,48},{24,56},{32,0},{40,8},{48,16},{56,24},{64,96... | collective-permute-start | bytes 393224 | tf_op jit(solution)/shard_map/ppermute | solution.py:638
  37.9 0.4 collective-permute-start.10
  38.6 1.4 %collective-permute-done.12.refs_4_ = bf16[2,64,512]{2,1,0:T(8,128)(2,1)S(1)} collective-permute-done((bf16[2,64,512]{2,1,0:T(8,128)(2,1)S(1)}, bf16[2,64,512]{2,1,0:T(8,128)(2,1)S(1)}, u32[]{:S(2)}, u32[]{:S(2)}) %collective-permute-start.12) | collective-permute-done | bytes 131104 | tf_op jit(solution)/shard_map/ppermute | solution.py:641
  40.0 2.8 %collective-permute-start.15 = (bf16[2,64,512]{2,1,0:T(8,128)(2,1)S(1)}, bf16[2,64,512]{2,1,0:T(8,128)(2,1)S(1)}, u32[]{:S(2)}, u32[]{:S(2)}) collective-permute-start(bf16[2,64,512]{2,1,0:T(8,128)(2,1)S(1)} %collective-permute-done.12.refs_4_), channel_id=1, source_target_pairs={{0,32},{8,40},{16,48},{24,56},{32,0},{40,8},{48,16},{56,24},{64,96... | collective-permute-start | bytes 393224 | tf_op jit(solution)/shard_map/ppermute | solution.py:638
  43.5 5.3 %direction_parts1.1.refs_9_ = bf16[4,4,2,64,512]{4,3,2,1,0:T(8,128)(2,1)S(1)} custom-call(bf16[2,528,768]{2,1,0:T(8,128)(2,1)S(1)} %phasor_own.1.own, bf16[2,528,768]{2,1,0:T(8,128)(2,1)S(1)} %collective-permute-done.other_hbm.other), custom_call_target="tpu_custom_call" | custom-call | flops 3221225472 | bytes 5000000 | tf_op jit(solution)/shard_map/direction_parts1/pallas_call | solution.py:330
  49.2 0.9 %collective-permute-done.14.refs_6_ = bf16[2,64,512]{2,1,0:T(8,128)(2,1)S(1)} collective-permute-done((bf16[2,64,512]{2,1,0:T(8,128)(2,1)S(1)}, bf16[2,64,512]{2,1,0:T(8,128)(2,1)S(1)}, u32[]{:S(2)}, u32[]{:S(2)}) %collective-permute-start.14) | collective-permute-done | bytes 131104 | tf_op jit(solution)/shard_map/ppermute | solution.py:638
  50.0 2.9 %gradient_parts.1.refs_8_ = bf16[128,16,128]{2,1,0:T(8,128)(2,1)} custom-call(f32[2]{0:T(128)S(1)} %copy-done.9, bf16[2,64,512]{2,1,0:T(8,128)(2,1)S(1)} %get-tuple-element.25.refs_0_, bf16[2,64,512]{2,1,0:T(8,128)(2,1)S(1)} %collective-permute-done.9.refs_1_, bf16[2,64,512]{2,1,0:T(8,128)(2,1)S(1)} %collective-permute-done.10.refs_2_, ...), custom_call_target="tpu_custom_call" | custom-call | flops 10000000 | bytes 6000000 | tf_op jit(solution)/shard_map/gradient_parts/pallas_call | solution.py:508
  52.9 0.7 whole_rows.1
  53.7 10.6 %all-to-all-start = ((bf16[128,16,128]{2,1,0:T(8,128)(2,1)}), bf16[128,16,128]{2,1,0:T(8,128)(2,1)S(1)}, u32[]{:S(2)}, u32[]{:S(2)}) async-start(bf16[128,16,128]{2,1,0:T(8,128)(2,1)} %gradient_parts.1.refs_8_), calls=%async_computation | async-start | bytes 1048576 | tf_op jit(solution)/shard_map/all_to_all | solution.py:660
  64.8 1.1 %maximum_bitcast_fusion = f32[32,2,2,2,512]{4,3,2,1,0:T(2,128)} fusion(f32[1,2,2,32,512]{4,2,1,0,3:T(2,128)S(1)} %copy.13, f32[1,2,2,32,512]{4,2,1,0,3:T(2,128)S(1)} %copy.12), kind=kLoop, calls=%fused_computation | loop fusion | flops 131072 | bytes 1048576 | tf_op jit(solution)/shard_map/transpose | solution.py:666
  65.9 11.6 %all-to-all-done.grads = bf16[128,16,128]{2,1,0:T(8,128)(2,1)S(1)} async-done(((bf16[128,16,128]{2,1,0:T(8,128)(2,1)}), bf16[128,16,128]{2,1,0:T(8,128)(2,1)S(1)}, u32[]{:S(2)}, u32[]{:S(2)}) %all-to-all-start) | async-done | bytes 524320 | tf_op jit(solution)/shard_map/all_to_all | solution.py:660
  77.5 1.2 %updated_rows.1 = f32[2,512]{1,0:T(2,128)} custom-call(bf16[128,16,128]{2,1,0:T(8,128)(2,1)S(1)} %all-to-all-done.grads, f32[512,512]{1,0:T(8,128)S(1)} %copy-done.2, f32[2,512]{1,0:T(2,128)S(1)} %copy-done.4), custom_call_target="tpu_custom_call" | custom-call | flops 200000000 | bytes 1500000 | tf_op jit(solution)/shard_map/updated_rows/pallas_call | solution.py:603
  (48 shorter events, 2.7 us)
Async XLA Ops:
  0.6 5.3 %copy-start.9 = (f32[2]{0:T(128)S(1)}, f32[2]{0:T(128)}, u32[]{:S(2)}) copy-start(f32[2]{0:T(128)} %freq.5) | copy-start | bytes 28
  0.6 5.3 %copy-start.4 = (f32[2,512]{1,0:T(2,128)S(1)}, f32[2,512]{1,0:T(2,128)}, u32[]{:S(2)}) copy-start(f32[2,512]{1,0:T(2,128)} %screen.5) | copy-start | bytes 12292
  0.7 5.3 %copy-start.8 = (s32[384]{0:T(512)S(1)}, s32[384]{0:T(512)}, u32[]{:S(2)}) copy-start(s32[384]{0:T(512)} %direction.3) | copy-start | bytes 4612
  0.7 5.3 %copy-start = (bf16[2,2,2,512,384]{4,3,2,1,0:T(8,128)(2,1)S(1)}, bf16[2,2,2,512,384]{4,3,2,1,0:T(8,128)(2,1)}, u32[]{:S(2)}) copy-start(bf16[2,2,2,512,384]{4,3,2,1,0:T(8,128)(2,1)} %gain.3) | copy-start | bytes 9437188
  0.7 5.3 %copy-start.7 = (f32[384]{0:T(512)S(1)}, f32[384]{0:T(512)}, u32[]{:S(2)}) copy-start(f32[384]{0:T(512)} %flux.3) | copy-start | bytes 4612
  5.8 3.8 %collective-permute-start = (bf16[2,528,768]{2,1,0:T(8,128)(2,1)}, bf16[2,528,768]{2,1,0:T(8,128)(2,1)S(1)}, u32[]{:S(2)}, u32[]{:S(2)}) collective-permute-start(bf16[2,528,768]{2,1,0:T(8,128)(2,1)} %phasor_send.1), channel_id=1, source_target_pairs={{0,8},{8,0},{16,24},{24,16},{32,40},{40,32},{48,56},{56,48},{64,72... | collective-permute-start | bytes 4866056 | tf_op jit(solution)/shard_map/ppermute | solution.py:634
  14.0 20.1 %collective-permute-start.8 = (f32[32,2,4,512]{3,2,1,0:T(4,128)S(1)}, f32[32,2,4,512]{3,2,1,0:T(4,128)S(1)}, u32[]{:S(2)}, u32[]{:S(2)}) collective-permute-start(f32[32,2,4,512]{3,2,1,0:T(4,128)S(1)} %observed_send.1), channel_id=1, source_target_pairs={{0,8},{8,0},{16,24},{24,16},{32,40},{40,32},{48,56},{56,48},{64,72... | collective-permute-start | bytes 1572872 | tf_op jit(solution)/shard_map/ppermute | solution.py:646
  14.2 8.0 %collective-permute-start.4 = (bf16[2,64,512]{2,1,0:T(8,128)(2,1)S(1)}, bf16[2,64,512]{2,1,0:T(8,128)(2,1)S(1)}, u32[]{:S(2)}, u32[]{:S(2)}) collective-permute-start(bf16[2,64,512]{2,1,0:T(8,128)(2,1)S(1)} %get-tuple-element.19), channel_id=1, source_target_pairs={{0,32},{8,40},{16,48},{24,56},{32,0},{40,8},{48,16},{56,24},{64,96... | collective-permute-start | bytes 393224 | tf_op jit(solution)/shard_map/ppermute | solution.py:638
  17.4 7.7 %collective-permute-start.5 = (bf16[2,64,512]{2,1,0:T(8,128)(2,1)S(1)}, bf16[2,64,512]{2,1,0:T(8,128)(2,1)S(1)}, u32[]{:S(2)}, u32[]{:S(2)}) collective-permute-start(bf16[2,64,512]{2,1,0:T(8,128)(2,1)S(1)} %get-tuple-element.20), channel_id=1, source_target_pairs={{0,48},{8,56},{16,32},{24,40},{32,16},{40,24},{48,0},{56,8},{64,11... | collective-permute-start | bytes 393224 | tf_op jit(solution)/shard_map/ppermute | solution.py:638
  18.5 8.0 %collective-permute-start.6 = (bf16[2,64,512]{2,1,0:T(8,128)(2,1)S(1)}, bf16[2,64,512]{2,1,0:T(8,128)(2,1)S(1)}, u32[]{:S(2)}, u32[]{:S(2)}) collective-permute-start(bf16[2,64,512]{2,1,0:T(8,128)(2,1)S(1)} %get-tuple-element.21), channel_id=1, source_target_pairs={{0,16},{8,24},{16,0},{24,8},{32,48},{40,56},{48,32},{56,40},{64,80... | collective-permute-start | bytes 393224 | tf_op jit(solution)/shard_map/ppermute | solution.py:638
  18.5 16.3 %collective-permute-start.1 = (bf16[2,64,512]{2,1,0:T(8,128)(2,1)S(1)}, bf16[2,64,512]{2,1,0:T(8,128)(2,1)S(1)}, u32[]{:S(2)}, u32[]{:S(2)}) collective-permute-start(bf16[2,64,512]{2,1,0:T(8,128)(2,1)S(1)} %get-tuple-element.16._), channel_id=1, source_target_pairs={{0,32},{8,40},{16,48},{24,56},{32,0},{40,8},{48,16},{56,24},{64,96... | collective-permute-start | bytes 393224 | tf_op jit(solution)/shard_map/ppermute | solution.py:638
  22.1 12.7 %collective-permute-start.2 = (bf16[2,64,512]{2,1,0:T(8,128)(2,1)S(1)}, bf16[2,64,512]{2,1,0:T(8,128)(2,1)S(1)}, u32[]{:S(2)}, u32[]{:S(2)}) collective-permute-start(bf16[2,64,512]{2,1,0:T(8,128)(2,1)S(1)} %get-tuple-element.17), channel_id=1, source_target_pairs={{0,48},{8,56},{16,32},{24,40},{32,16},{40,24},{48,0},{56,8},{64,11... | collective-permute-start | bytes 393224 | tf_op jit(solution)/shard_map/ppermute | solution.py:638
  25.1 9.7 %collective-permute-start.3 = (bf16[2,64,512]{2,1,0:T(8,128)(2,1)S(1)}, bf16[2,64,512]{2,1,0:T(8,128)(2,1)S(1)}, u32[]{:S(2)}, u32[]{:S(2)}) collective-permute-start(bf16[2,64,512]{2,1,0:T(8,128)(2,1)S(1)} %get-tuple-element.18), channel_id=1, source_target_pairs={{0,16},{8,24},{16,0},{24,8},{32,48},{40,56},{48,32},{56,40},{64,80... | collective-permute-start | bytes 393224 | tf_op jit(solution)/shard_map/ppermute | solution.py:638
  26.6 8.2 %collective-permute-start.7 = (bf16[2,64,512]{2,1,0:T(8,128)(2,1)S(1)}, bf16[2,64,512]{2,1,0:T(8,128)(2,1)S(1)}, u32[]{:S(2)}, u32[]{:S(2)}) collective-permute-start(bf16[2,64,512]{2,1,0:T(8,128)(2,1)S(1)} %send_parts.1), channel_id=1, source_target_pairs={{0,64},{8,72},{16,80},{24,88},{32,96},{40,104},{48,112},{56,120},{... | collective-permute-start | bytes 393224 | tf_op jit(solution)/shard_map/ppermute | solution.py:641
  35.0 5.0 %collective-permute-start.12 = (bf16[2,64,512]{2,1,0:T(8,128)(2,1)S(1)}, bf16[2,64,512]{2,1,0:T(8,128)(2,1)S(1)}, u32[]{:S(2)}, u32[]{:S(2)}) collective-permute-start(bf16[2,64,512]{2,1,0:T(8,128)(2,1)S(1)} %get-tuple-element.25.refs_0_), channel_id=1, source_target_pairs={{0,64},{8,72},{16,80},{24,88},{32,96},{40,104},{48,112},{56,120},{... | collective-permute-start | bytes 393224 | tf_op jit(solution)/shard_map/ppermute | solution.py:641
  35.1 8.1 %collective-permute-start.11 = (bf16[2,64,512]{2,1,0:T(8,128)(2,1)S(1)}, bf16[2,64,512]{2,1,0:T(8,128)(2,1)S(1)}, u32[]{:S(2)}, u32[]{:S(2)}) collective-permute-start(bf16[2,64,512]{2,1,0:T(8,128)(2,1)S(1)} %get-tuple-element.25.refs_0_), channel_id=1, source_target_pairs={{0,32},{8,40},{16,48},{24,56},{32,0},{40,8},{48,16},{56,24},{64,96... | collective-permute-start | bytes 393224 | tf_op jit(solution)/shard_map/ppermute | solution.py:638
  37.9 10.8 %collective-permute-start.10 = (bf16[2,64,512]{2,1,0:T(8,128)(2,1)S(1)}, bf16[2,64,512]{2,1,0:T(8,128)(2,1)S(1)}, u32[]{:S(2)}, u32[]{:S(2)}) collective-permute-start(bf16[2,64,512]{2,1,0:T(8,128)(2,1)S(1)} %get-tuple-element.25.refs_0_), channel_id=1, source_target_pairs={{0,48},{8,56},{16,32},{24,40},{32,16},{40,24},{48,0},{56,8},{64,11... | collective-permute-start | bytes 393224 | tf_op jit(solution)/shard_map/ppermute | solution.py:638
  38.4 10.4 %collective-permute-start.9 = (bf16[2,64,512]{2,1,0:T(8,128)(2,1)S(1)}, bf16[2,64,512]{2,1,0:T(8,128)(2,1)S(1)}, u32[]{:S(2)}, u32[]{:S(2)}) collective-permute-start(bf16[2,64,512]{2,1,0:T(8,128)(2,1)S(1)} %get-tuple-element.25.refs_0_), channel_id=1, source_target_pairs={{0,16},{8,24},{16,0},{24,8},{32,48},{40,56},{48,32},{56,40},{64,80... | collective-permute-start | bytes 393224 | tf_op jit(solution)/shard_map/ppermute | solution.py:638
  40.0 9.2 %collective-permute-start.15 = (bf16[2,64,512]{2,1,0:T(8,128)(2,1)S(1)}, bf16[2,64,512]{2,1,0:T(8,128)(2,1)S(1)}, u32[]{:S(2)}, u32[]{:S(2)}) collective-permute-start(bf16[2,64,512]{2,1,0:T(8,128)(2,1)S(1)} %collective-permute-done.12.refs_4_), channel_id=1, source_target_pairs={{0,32},{8,40},{16,48},{24,56},{32,0},{40,8},{48,16},{56,24},{64,96... | collective-permute-start | bytes 393224 | tf_op jit(solution)/shard_map/ppermute | solution.py:638
  42.8 7.2 %collective-permute-start.14 = (bf16[2,64,512]{2,1,0:T(8,128)(2,1)S(1)}, bf16[2,64,512]{2,1,0:T(8,128)(2,1)S(1)}, u32[]{:S(2)}, u32[]{:S(2)}) collective-permute-start(bf16[2,64,512]{2,1,0:T(8,128)(2,1)S(1)} %collective-permute-done.12.refs_4_), channel_id=1, source_target_pairs={{0,48},{8,56},{16,32},{24,40},{32,16},{40,24},{48,0},{56,8},{64,11... | collective-permute-start | bytes 393224 | tf_op jit(solution)/shard_map/ppermute | solution.py:638
  43.3 6.8 %collective-permute-start.13 = (bf16[2,64,512]{2,1,0:T(8,128)(2,1)S(1)}, bf16[2,64,512]{2,1,0:T(8,128)(2,1)S(1)}, u32[]{:S(2)}, u32[]{:S(2)}) collective-permute-start(bf16[2,64,512]{2,1,0:T(8,128)(2,1)S(1)} %collective-permute-done.12.refs_4_), channel_id=1, source_target_pairs={{0,16},{8,24},{16,0},{24,8},{32,48},{40,56},{48,32},{56,40},{64,80... | collective-permute-start | bytes 393224 | tf_op jit(solution)/shard_map/ppermute | solution.py:638
  53.6 23.9 %copy-start.2 = (f32[512,512]{1,0:T(8,128)S(1)}, f32[512,512]{1,0:T(8,128)}, u32[]{:S(2)}) copy-start(f32[512,512]{1,0:T(8,128)} %kernel.1) | copy-start | bytes 3145732
  53.6 10.7 %collective-permute-start.16 = (f32[4,32,512]{2,1,0:T(8,128)S(1)}, f32[4,32,512]{2,1,0:T(8,128)S(1)}, u32[]{:S(2)}, u32[]{:S(2)}) collective-permute-start(f32[4,32,512]{2,1,0:T(8,128)S(1)} %get-tuple-element.27), channel_id=1, source_target_pairs={{0,8},{8,0},{16,24},{24,16},{32,40},{40,32},{48,56},{56,48},{64,72... | collective-permute-start | bytes 786440 | tf_op jit(solution)/shard_map/ppermute | solution.py:659
  53.7 23.8 %all-to-all-start = ((bf16[128,16,128]{2,1,0:T(8,128)(2,1)}), bf16[128,16,128]{2,1,0:T(8,128)(2,1)S(1)}, u32[]{:S(2)}, u32[]{:S(2)}) async-start(bf16[128,16,128]{2,1,0:T(8,128)(2,1)} %gradient_parts.1.refs_8_), calls=%async_computation | async-start | bytes 1048576 | tf_op jit(solution)/shard_map/all_to_all | solution.py:660
  (4 other events, 20.3 us)

commit v6 on v5

--- a/solution.py
+++ b/solution.py
@@ -96,9 +96,9 @@
 
 
 def phasor_send_kernel(
-    freq, gain, uv, screen, lm, flux, direction, out, *rest
+    freq, gain, uv, screen, lm, flux, direction, out_hbm, *rest
 ):
-    held, freq_held, uv_held, screen_held, lm_held, flux_held, direction_held, sems = rest
+    out, out_sems, held, freq_held, uv_held, screen_held, lm_held, flux_held, direction_held, sems = rest
     core, _, _ = position()
     channel = 1 - core
     quarter = gain.shape[3] // 4
@@ -131,9 +131,25 @@
     for load in loads:
         load.wait()
 
+    half = gain.shape[3] // 2
+    writes = []
+
+    def write(moment, start, size):
+        rows = pl.ds(start, size)
+        writes.append(
+            pltpu.make_async_copy(
+                out.at[moment, rows, :], out_hbm.at[moment, rows, :], out_sems.at[len(writes)]
+            )
+        )
+        writes[-1].start()
+
     def ready(moment, start):
         if start % quarter == 0:
             copies[moment * 4 + start // quarter].wait()
+        if start == half:
+            write(moment, 0, half)
+        if start == 0 and moment == 1:
+            write(0, half, half + 16)
 
     def gain_of(moment, part, rows):
         return held[moment, part, rows, :]
@@ -141,6 +157,9 @@
     phasor_rows(
         channel, freq_held, gain_of, uv_held, screen_held, lm_held, flux_held, direction_held, out, ready
     )
+    write(1, half, half + 16)
+    for copy in writes:
+        copy.wait()
 
 
 def phasor_own_kernel(freq, gain, uv, screen, lm, flux, direction, out, flux_held, direction_held, sems):
@@ -168,9 +187,11 @@
     return pl.pallas_call(
         phasor_send_kernel,
         in_specs=[HBM] * 7,
-        out_specs=WHOLE,
+        out_specs=HBM,
         out_shape=jax.ShapeDtypeStruct((2, stations + 16, 2 * sources), bf16),
         scratch_shapes=[
+            pltpu.VMEM((2, stations + 16, 2 * sources), bf16),
+            pltpu.SemaphoreType.DMA((4,)),
             pltpu.VMEM((2, 2, stations, sources), bf16),
             pltpu.SMEM(inputs[0].shape, f32),
         ]
@@ -213,12 +234,21 @@
 
 
 def pack(re, im, odd, keep_re):
-    re = jnp.where(odd, re[:, 64:384], re[:, 0:320])
-    im = jnp.where(odd, im[:, 64:384], im[:, 0:320])
-    upper, _ = upper_mask()
-    own = jnp.where(upper, re[:, 0:64], im[:, 0:64])
-    far = jnp.where(keep_re, re[:, 256:320], im[:, 256:320])
-    return jnp.concatenate([own, re[:, 64:256], far, im[:, 64:256]], axis=1)
+    re = jnp.where(odd, pltpu.roll(re, 320, 1), re)
+    im = jnp.where(odd, pltpu.roll(im, 320, 1), im)
+    row = lax.broadcasted_iota(jnp.int32, (64, 128), 0)
+    col = lax.broadcasted_iota(jnp.int32, (64, 128), 1)
+    near = col < 64
+    far = jnp.where(keep_re, re[:, 256:384], im[:, 256:384])
+    return jnp.concatenate(
+        [
+            jnp.where(near & (row >= col), im[:, 0:128], re[:, 0:128]),
+            re[:, 128:256],
+            jnp.where(near, far, im[:, 0:128]),
+            im[:, 128:256],
+        ],
+        axis=1,
+    )
 
 
 def skewed(q):
@@ -237,9 +267,9 @@
     wide[part, 256:512, 512:768] = corner if part == 0 else -corner
 
 
-def fill_gram(wide, left, right):
+def fill_gram(wide, left, right, scaling):
     for part, rows in ((0, left), (1, skewed(left))):
-        value = mm(rows, right)
+        value = mm(rows, right) * scaling
         wide[part, :, 0:512] = value
         wide[part, :, 512:768] = value[:, 0:256]
 
@@ -249,7 +279,7 @@
     return wide[part, pl.ds(pl.multiple_of(chip * 64, 64), 64), pl.ds(start, 384)]
 
 
-def model_kernel(scaling, own, other_hbm, stay, out11, out21, out31, out10, out20, out30, wide, other, top, bottom, sems):
+def model_kernel(scaling, own, other_hbm, stay, out11, out21, out31, out10, out20, out30, wides, tops, bottoms, other, sems):
     _, y, z = position()
     copies = [
         pltpu.make_async_copy(other_hbm.at[moment], other.at[moment], sems.at[moment])
@@ -258,18 +288,19 @@
     for copy in copies:
         copy.start()
     for moment in range(2):
+        wide, top, bottom = wides.at[moment], tops.at[moment], bottoms.at[moment]
         q = own[moment, 0:512, :]
         for part, rows in ((0, q), (1, skewed(q))):
-            top[part] = mm(rows[0:256], q)
-            bottom[part] = mm(rows[256:512], q[256:512])
+            top[part] = mm(rows[0:256], q) * scaling
+            bottom[part] = mm(rows[256:512], q[256:512]) * scaling
         copies[moment].wait()
         q = other[moment, 0:512, :]
         for part, rows in ((0, q), (1, skewed(q))):
             fill_wide(
                 wide,
                 part,
-                (top[part] + mm(rows[0:256], q)) * scaling,
-                (bottom[part] + mm(rows[256:512], q[256:512])) * scaling,
+                top[part] + mm(rows[0:256], q) * scaling,
+                bottom[part] + mm(rows[256:512], q[256:512]) * scaling,
             )
         for flip, outs in ((1, (out11, out21, out31)), (0, (out10, out20, out30))):
             for rel in range(4):
@@ -288,17 +319,16 @@
     return pl.pallas_call(
         functools.partial(model_kernel, scaling),
         in_specs=[WHOLE, HBM],
-        out_specs=[WHOLE] * 7,
-        scratch_shapes=[
-            pltpu.VMEM((2, 512, 768), f32),
-            pltpu.VMEM(own.shape, bf16),
-            pltpu.VMEM((2, 256, 512), f32),
-            pltpu.VMEM((2, 256, 256), f32),
-            pltpu.SemaphoreType.DMA((2,)),
+        out_specs=[WHOLE] * 10,
+        scratch_shapes=[pltpu.VMEM(own.shape, bf16), pltpu.SemaphoreType.DMA((2,))],
+        out_shape=[jax.ShapeDtypeStruct((2, 2, 64, 512), f32)]
+        + [jax.ShapeDtypeStruct((2, 64, 512), bf16)] * 6
+        + [
+            jax.ShapeDtypeStruct((2, 2, 512, 768), f32),
+            jax.ShapeDtypeStruct((2, 2, 256, 512), f32),
+            jax.ShapeDtypeStruct((2, 2, 256, 256), f32),
         ],
-        out_shape=[jax.ShapeDtypeStruct((2, 2, 64, 512), f32)]
-        + [jax.ShapeDtypeStruct((2, 64, 512), bf16)] * 6,
-        compiler_params=pltpu.CompilerParams(vmem_limit_bytes=16 * MIB),
+        compiler_params=pltpu.CompilerParams(vmem_limit_bytes=20 * MIB),
         cost_estimate=pl.CostEstimate(
             flops=2 * 2 * 4 * 512 * 512 * 768, bytes_accessed=5000000, transcendentals=0
         ),
@@ -306,39 +336,42 @@
     )(own, other)
 
 
-def direction_kernel(moment, own, other, out, whole, first):
+def direction_kernel(moment, scaling, own, other, totals, tops, bottoms, out, mine, first_own, first_other):
     core, y, z = position()
-    for source, core_of in ((own, core), (other, 1 - core)):
+    total = totals.at[moment]
+    for part in range(2):
+        fill_wide(mine, part, tops[moment, part], bottoms[moment, part])
+    for source, first in ((own, first_own), (other, first_other)):
         q = source[moment, 0:512, :]
         in_first = source[moment, 512:513, :] < 0.5
-        q_first = jnp.where(in_first, q, jnp.zeros_like(q))
-        fill_gram(whole, q, q)
-        fill_gram(first, q_first, q)
-        for rel in range(4):
-            for flip in range(2):
-                zz = 1 - z if flip else z
-                chip = zz * 4 + y_partner(rel, y)
-                odd = chip % 2 == 1
-                keep_im = zz == 0
-                all_of = pack(block_of(whole, 1, chip), -block_of(whole, 0, chip), odd, keep_im)
-                first_of = pack(block_of(first, 1, chip), -block_of(first, 0, chip), odd, keep_im)
-                out[core_of * 2, rel, flip] = first_of.astype(bf16)
-                out[core_of * 2 + 1, rel, flip] = (all_of - first_of).astype(bf16)
-
-
-def direction_parts(moment, own, other):
-    return pl.pallas_call(
-        functools.partial(direction_kernel, moment),
-        in_specs=[WHOLE] * 2,
+        fill_gram(first, jnp.where(in_first, q, jnp.zeros_like(q)), q, scaling)
+    for rel in range(4):
+        for flip in range(2):
+            zz = 1 - z if flip else z
+            chip = zz * 4 + y_partner(rel, y)
+            whole, own_all, own_first, other_first = (
+                pack(block_of(wide, 1, chip), -block_of(wide, 0, chip), chip % 2 == 1, zz == 0)
+                for wide in (total, mine, first_own, first_other)
+            )
+            out[core * 2, rel, flip] = own_first.astype(bf16)
+            out[core * 2 + 1, rel, flip] = (own_all - own_first).astype(bf16)
+            out[2 - core * 2, rel, flip] = other_first.astype(bf16)
+            out[3 - core * 2, rel, flip] = ((whole - own_all) - other_first).astype(bf16)
+
+
+def direction_parts(moment, scaling, *arrays):
+    return pl.pallas_call(
+        functools.partial(direction_kernel, moment, scaling),
+        in_specs=[WHOLE] * 5,
         out_specs=WHOLE,
-        scratch_shapes=[pltpu.VMEM((2, 512, 768), f32)] * 2,
+        scratch_shapes=[pltpu.VMEM((2, 512, 768), f32)] * 3,
         out_shape=jax.ShapeDtypeStruct((4, 4, 2, 64, 512), bf16),
         compiler_params=pltpu.CompilerParams(vmem_limit_bytes=18 * MIB),
         cost_estimate=pl.CostEstimate(
-            flops=2 * 8 * 512 * 512 * 768, bytes_accessed=5000000, transcendentals=0
+            flops=2 * 4 * 512 * 512 * 768, bytes_accessed=5000000, transcendentals=0
         ),
         name="direction_parts%d" % moment,
-    )(own, other)
+    )(*arrays)
 
 
 def send_kernel(own, one, two, three, send):
@@ -451,7 +484,7 @@
     )(observed, flags, other)
 
 
-def gradient_kernel(scaling, freq, *refs):
+def gradient_kernel(freq, *refs):
     resids = refs[0:8]
     parts0, parts1, out, rows_sum, cols_sum = refs[8:]
     core, y, z = position()
@@ -462,11 +495,11 @@
             source = resids[flip * 4 + rel]
             for start in range(0, 64, 32):
                 rows = slice(start, start + 32)
-                resid0 = source[0, rows, :].astype(f32)
-                resid1 = source[1, rows, :].astype(f32)
+                resid0 = source[0, rows, :]
+                resid1 = source[1, rows, :]
                 for which in range(4):
-                    product = resid0 * parts0[which, rel, flip, rows, :].astype(f32)
-                    product += resid1 * parts1[which, rel, flip, rows, :].astype(f32)
+                    product = (resid0 * parts0[which, rel, flip, rows, :]).astype(f32)
+                    product += (resid1 * parts1[which, rel, flip, rows, :]).astype(f32)
                     rows_sum[which, pl.ds(pl.multiple_of(chip * 64 + start, 32), 32), :] = (
                         product[:, 0:128] + product[:, 128:256]
                     ) + (product[:, 256:384] + product[:, 384:512])
@@ -476,7 +509,7 @@
                     else:
                         cols_sum[which, chip] += column
     near = lax.broadcasted_iota(jnp.int32, (8, 256), 1) < 64
-    factor = 2.0 * scaling / freq[core]
+    factor = 2.0 / freq[core]
     pieces = []
     for which in range(4):
         placed = []
@@ -504,9 +537,9 @@
     lax.fori_loop(0, out.shape[0], copy, 0, unroll=8)
 
 
-def gradient_parts(scaling, devices, freq, resids, parts0, parts1):
-    return pl.pallas_call(
-        functools.partial(gradient_kernel, scaling),
+def gradient_parts(devices, freq, resids, parts0, parts1):
+    return pl.pallas_call(
+        gradient_kernel,
         in_specs=[SCALARS] + [WHOLE] * 10,
         out_specs=WHOLE,
         scratch_shapes=[pltpu.VMEM((4, 512, 128), f32), pltpu.VMEM((4, 8, 8, 512), f32)],
@@ -645,16 +678,16 @@
     near = [across(rel, parts[rel + 3]) for rel in (3, 2, 1)]
     other_observed = swap(observed_send(observed, flags, parts[6]))
     obs, kept = observed_parts(observed, flags, other_observed)
-    directions0 = direction_parts(0, own, other)
+    directions0 = direction_parts(0, scaling, own, other, *parts[7:])
     last = across_z(send_parts(parts[0], *far))
     resid, half = residual_parts(parts[0], *near, last, obs, kept, directions0)
     half_z = across_z(half)
-    directions1 = direction_parts(1, own, other)
+    directions1 = direction_parts(1, scaling, own, other, *parts[7:])
     resids = [
         array if rel == 0 else across(rel, array) for array in (half, half_z) for rel in range(4)
     ]
 
-    grads = gradient_parts(scaling, devices, freq_ratio, resids, directions0, directions1)
+    grads = gradient_parts(devices, freq_ratio, resids, directions0, directions1)
     own_rows, sent_rows = whole_rows(resid, resids, grads)
     other_rows = swap(sent_rows)
     grads = lax.all_to_all(grads, ("dir", "freq"), 0, 0, tiled=True)

time: 78.8 us -> 75.7 us (0.961)
  Pallas kernels: 28.4 us -> 23.1 us
  starting transfers between devices: 32.7 us -> 34.9 us
    pallas_call x4, Pallas kernels: 18.5 us -> 13.6 us  [the longest x2 6.28 us: direction_parts(): pl.pallas_call(functools.partial(direction_kernel, moment, scaling), in_s...]
    ppermute x12, starting transfers between devices: 19.4 us -> 21.6 us  [across(): return lax.ppermute(array, 'dir', dir_perm(rel))]
    ppermute x12, waiting for transfers between devices: 1.28 us -> 2.76 us  [across(): return lax.ppermute(array, 'dir', dir_perm(rel))]
    ppermute x2, waiting for transfers between devices: 1.38 us -> 0.01 us  [across_z(): return lax.ppermute(array, 'dir', dir_perm(0, flip_z=True))]
    all_to_all x1, starting transfers between devices: 10.6 us -> 9.26 us  [body(): grads = lax.all_to_all(grads, ('dir', 'freq'), 0, 0, tiled=True)]
    ppermute x2, starting transfers between devices: 2.37 us -> 3.61 us  [across_z(): return lax.ppermute(array, 'dir', dir_perm(0, flip_z=True))]
  transfers between devices with their start and end apart: 18 -> 18, of which waited for: 5 -> 3; matrix products, arithmetic and copies ran while one was open for 2% -> 2% of each run, Pallas kernels for 18% -> 13%
where the time goes in v6:
time: 75.7 us; the launch traced here: 75.5 us
  starting transfers between devices  34.9 us (46%)
  Pallas kernels  23.1 us (31%)
  waiting for transfers between devices  15 us (20%)
  other arithmetic  1.1 us (1%)
  between operations  1 us (1%)
    ppermute x12, starting transfers between devices, across(): return lax.ppermute(array, 'dir', dir_perm(rel))  21.6 us
    all_to_all x1, waiting for transfers between devices, body(): grads = lax.all_to_all(grads, ('dir', 'freq'), 0, 0, tiled=True)  11.6 us
    all_to_all x1, starting transfers between devices, body(): grads = lax.all_to_all(grads, ('dir', 'freq'), 0, 0, tiled=True)  9.26 us
    pallas_call x2, Pallas kernels, direction_parts(): pl.pallas_call(functools.partial(direction_kernel, moment, scaling), in_s...  6.28 us
    pallas_call x1, Pallas kernels, phasor_send(): pl.pallas_call(phasor_send_kernel, in_specs=[HBM] * 7, out_specs=HBM, out...  4.67 us
    pallas_call x1, Pallas kernels, model_parts(): pl.pallas_call(functools.partial(model_kernel, scaling), in_specs=[WHOLE,...  3.96 us
    ppermute x2, starting transfers between devices, across_z(): return lax.ppermute(array, 'dir', dir_perm(0, flip_z=True))  3.61 us
    pallas_call x1, Pallas kernels, phasor_own(): pl.pallas_call(phasor_own_kernel, in_specs=[SCALARS] + [WHOLE] * 4 + [ANY...  2.94 us
  transfers between devices with their start and end apart: 18, of which 3 were waited for; matrix products, arithmetic and copies ran while one was open for 2% of the time, Pallas kernels for 13%

profile of v6, /device:TPU:0, one launch (start us, length us, event | category | flops | bytes accessed | tf_op | source)
XLA Modules:
  0.0 75.5 jit_solution(5459866960133664826)
XLA Ops:
  0.7 4.7 %phasor_send.1 = bf16[2,528,768]{2,1,0:T(8,128)(2,1)} custom-call(f32[2]{0:T(128)} %freq.5, bf16[2,2,2,512,384]{4,3,2,1,0:T(8,128)(2,1)} %gain.3, f32[2,2,512]{2,1,0:T(2,128)} %uv.3, f32[2,512]{1,0:T(2,128)} %screen.5, f32[2,384]{1,0:T(2,128)} %lm.3, f32[384]{0:T(512)} %flux.3, s32[384]{0:T(512)} %direction.3), custom_call_target="tpu_custom_call" | custom-call | flops 15728640 | bytes 3200000 | tf_op jit(solution)/shard_map/phasor_send/pallas_call | solution.py:187
  5.5 2.9 %phasor_own.1.own = bf16[2,528,768]{2,1,0:T(8,128)(2,1)S(1)} custom-call(f32[2]{0:T(128)S(1)} %copy-done.9, bf16[2,2,2,512,384]{4,3,2,1,0:T(8,128)(2,1)S(1)} %copy-done, f32[2,2,512]{2,1,0:T(2,128)S(1)} %copy-done.5, f32[2,512]{1,0:T(2,128)S(1)} %copy-done.4, f32[2,384]{1,0:T(2,128)S(1)} %copy-done.6, f32[384]{0:T(512)S(1)} %copy-done.7, s32[384]{0:T(512)S(1)} %copy-done.8), custom_call_target="tpu_custom_call" | custom-call | flops 15728640 | bytes 3200000 | tf_op jit(solution)/shard_map/phasor_own/pallas_call | solution.py:212
  8.5 0.6 collective-permute-done.other_hbm.other
  9.2 4.0 %model_parts.1 = (f32[2,2,64,512]{3,2,1,0:T(8,128)S(1)}, bf16[2,64,512]{2,1,0:T(8,128)(2,1)S(1)}, bf16[2,64,512]{2,1,0:T(8,128)(2,1)S(1)}, bf16[2,64,512]{2,1,0:...) custom-call(bf16[2,528,768]{2,1,0:T(8,128)(2,1)S(1)} %phasor_own.1.o, ...), custom_call_target="tpu_custom_call" | custom-call | flops 3221225472 | bytes 5000000 | tf_op jit(solution)/shard_map/model_parts/pallas_call | solution.py:319
  13.5 3.3 %collective-permute-start.4 = (bf16[2,64,512]{2,1,0:T(8,128)(2,1)S(1)}, bf16[2,64,512]{2,1,0:T(8,128)(2,1)S(1)}, u32[]{:S(2)}, u32[]{:S(2)}) collective-permute-start(bf16[2,64,512]{2,1,0:T(8,128)(2,1)S(1)} %get-tuple-element.22), channel_id=1, source_target_pairs={{0,32},{8,40},{16,48},{24,56},{32,0},{40,8},{48,16},{56,24},{64,96... | collective-permute-start | bytes 393224 | tf_op jit(solution)/shard_map/ppermute | solution.py:671
  16.8 1.0 %collective-permute-start.5 = (bf16[2,64,512]{2,1,0:T(8,128)(2,1)S(1)}, bf16[2,64,512]{2,1,0:T(8,128)(2,1)S(1)}, u32[]{:S(2)}, u32[]{:S(2)}) collective-permute-start(bf16[2,64,512]{2,1,0:T(8,128)(2,1)S(1)} %get-tuple-element.23), channel_id=1, source_target_pairs={{0,48},{8,56},{16,32},{24,40},{32,16},{40,24},{48,0},{56,8},{64,11... | collective-permute-start | bytes 393224 | tf_op jit(solution)/shard_map/ppermute | solution.py:671
  17.9 3.6 %collective-permute-start.1 = (bf16[2,64,512]{2,1,0:T(8,128)(2,1)S(1)}, bf16[2,64,512]{2,1,0:T(8,128)(2,1)S(1)}, u32[]{:S(2)}, u32[]{:S(2)}) collective-permute-start(bf16[2,64,512]{2,1,0:T(8,128)(2,1)S(1)} %get-tuple-element.19._), channel_id=1, source_target_pairs={{0,32},{8,40},{16,48},{24,56},{32,0},{40,8},{48,16},{56,24},{64,96... | collective-permute-start | bytes 393224 | tf_op jit(solution)/shard_map/ppermute | solution.py:671
  21.5 2.9 %collective-permute-start.2 = (bf16[2,64,512]{2,1,0:T(8,128)(2,1)S(1)}, bf16[2,64,512]{2,1,0:T(8,128)(2,1)S(1)}, u32[]{:S(2)}, u32[]{:S(2)}) collective-permute-start(bf16[2,64,512]{2,1,0:T(8,128)(2,1)S(1)} %get-tuple-element.20), channel_id=1, source_target_pairs={{0,48},{8,56},{16,32},{24,40},{32,16},{40,24},{48,0},{56,8},{64,11... | collective-permute-start | bytes 393224 | tf_op jit(solution)/shard_map/ppermute | solution.py:671
  24.5 1.4 %collective-permute-start.3 = (bf16[2,64,512]{2,1,0:T(8,128)(2,1)S(1)}, bf16[2,64,512]{2,1,0:T(8,128)(2,1)S(1)}, u32[]{:S(2)}, u32[]{:S(2)}) collective-permute-start(bf16[2,64,512]{2,1,0:T(8,128)(2,1)S(1)} %get-tuple-element.21), channel_id=1, source_target_pairs={{0,16},{8,24},{16,0},{24,8},{32,48},{40,56},{48,32},{56,40},{64,80... | collective-permute-start | bytes 393224 | tf_op jit(solution)/shard_map/ppermute | solution.py:671
  26.0 2.2 %collective-permute-start.7 = (bf16[2,64,512]{2,1,0:T(8,128)(2,1)S(1)}, bf16[2,64,512]{2,1,0:T(8,128)(2,1)S(1)}, u32[]{:S(2)}, u32[]{:S(2)}) collective-permute-start(bf16[2,64,512]{2,1,0:T(8,128)(2,1)S(1)} %send_parts.1), channel_id=1, source_target_pairs={{0,64},{8,72},{16,80},{24,88},{32,96},{40,104},{48,112},{56,120},{... | collective-permute-start | bytes 393224 | tf_op jit(solution)/shard_map/ppermute | solution.py:674
  28.2 3.1 %direction_parts0.1._.refs_8_ = bf16[4,4,2,64,512]{4,3,2,1,0:T(8,128)(2,1)S(1)} custom-call(bf16[2,528,768]{2,1,0:T(8,128)(2,1)S(1)} %phasor_own.1.own, bf16[2,528,768]{2,1,0:T(8,128)(2,1)S(1)} %collective-permute-done.other_hbm.other, f32[2,2,512,768]{3,2,1,0:T(8,128)S(1)} %get-tuple-element.27.totals, f32[2,2,256,512]{3,2,1,0:T(8,128)S(1)} %get-tuple-element.28.tops, ...), custom_call_target="tpu_custom_call" | custom-call | flops 1610612736 | bytes 5000000 | tf_op jit(solution)/shard_map/direction_parts0/pallas_call | solution.py:363
  31.9 1.4 %collective-permute-start.12 = (bf16[2,64,512]{2,1,0:T(8,128)(2,1)S(1)}, bf16[2,64,512]{2,1,0:T(8,128)(2,1)S(1)}, u32[]{:S(2)}, u32[]{:S(2)}) collective-permute-start(bf16[2,64,512]{2,1,0:T(8,128)(2,1)S(1)} %get-tuple-element.31.refs_0_), channel_id=1, source_target_pairs={{0,64},{8,72},{16,80},{24,88},{32,96},{40,104},{48,112},{56,120},{... | collective-permute-start | bytes 393224 | tf_op jit(solution)/shard_map/ppermute | solution.py:674
  33.9 2.9 %collective-permute-start.10 = (bf16[2,64,512]{2,1,0:T(8,128)(2,1)S(1)}, bf16[2,64,512]{2,1,0:T(8,128)(2,1)S(1)}, u32[]{:S(2)}, u32[]{:S(2)}) collective-permute-start(bf16[2,64,512]{2,1,0:T(8,128)(2,1)S(1)} %get-tuple-element.31.refs_0_), channel_id=1, source_target_pairs={{0,48},{8,56},{16,32},{24,40},{32,16},{40,24},{48,0},{56,8},{64,11... | collective-permute-start | bytes 393224 | tf_op jit(solution)/shard_map/ppermute | solution.py:671
  36.8 0.6 collective-permute-start.11
  38.0 2.9 %collective-permute-start.14 = (bf16[2,64,512]{2,1,0:T(8,128)(2,1)S(1)}, bf16[2,64,512]{2,1,0:T(8,128)(2,1)S(1)}, u32[]{:S(2)}, u32[]{:S(2)}) collective-permute-start(bf16[2,64,512]{2,1,0:T(8,128)(2,1)S(1)} %collective-permute-done.12.refs_4_), channel_id=1, source_target_pairs={{0,48},{8,56},{16,32},{24,40},{32,16},{40,24},{48,0},{56,8},{64,11... | collective-permute-start | bytes 393224 | tf_op jit(solution)/shard_map/ppermute | solution.py:671
  40.9 1.7 %collective-permute-start.15 = (bf16[2,64,512]{2,1,0:T(8,128)(2,1)S(1)}, bf16[2,64,512]{2,1,0:T(8,128)(2,1)S(1)}, u32[]{:S(2)}, u32[]{:S(2)}) collective-permute-start(bf16[2,64,512]{2,1,0:T(8,128)(2,1)S(1)} %collective-permute-done.12.refs_4_), channel_id=1, source_target_pairs={{0,32},{8,40},{16,48},{24,56},{32,0},{40,8},{48,16},{56,24},{64,96... | collective-permute-start | bytes 393224 | tf_op jit(solution)/shard_map/ppermute | solution.py:671
  42.6 3.1 %direction_parts1.1.refs_9_ = bf16[4,4,2,64,512]{4,3,2,1,0:T(8,128)(2,1)S(1)} custom-call(bf16[2,528,768]{2,1,0:T(8,128)(2,1)S(1)} %phasor_own.1.own, bf16[2,528,768]{2,1,0:T(8,128)(2,1)S(1)} %collective-permute-done.other_hbm.other, f32[2,2,512,768]{3,2,1,0:T(8,128)S(1)} %get-tuple-element.27.totals, f32[2,2,256,512]{3,2,1,0:T(8,128)S(1)} %get-tuple-element.28.tops, ...), custom_call_target="tpu_custom_call" | custom-call | flops 1610612736 | bytes 5000000 | tf_op jit(solution)/shard_map/direction_parts1/pallas_call | solution.py:363
  45.8 2.7 %collective-permute-done.14.refs_6_ = bf16[2,64,512]{2,1,0:T(8,128)(2,1)S(1)} collective-permute-done((bf16[2,64,512]{2,1,0:T(8,128)(2,1)S(1)}, bf16[2,64,512]{2,1,0:T(8,128)(2,1)S(1)}, u32[]{:S(2)}, u32[]{:S(2)}) %collective-permute-start.14) | collective-permute-done | bytes 131104 | tf_op jit(solution)/shard_map/ppermute | solution.py:671
  48.5 2.7 %gradient_parts.1.refs_8_ = bf16[128,16,128]{2,1,0:T(8,128)(2,1)} custom-call(f32[2]{0:T(128)S(1)} %copy-done.9, bf16[2,64,512]{2,1,0:T(8,128)(2,1)S(1)} %get-tuple-element.31.refs_0_, bf16[2,64,512]{2,1,0:T(8,128)(2,1)S(1)} %collective-permute-done.9.refs_1_, bf16[2,64,512]{2,1,0:T(8,128)(2,1)S(1)} %collective-permute-done.10.refs_2_, ...), custom_call_target="tpu_custom_call" | custom-call | flops 10000000 | bytes 6000000 | tf_op jit(solution)/shard_map/gradient_parts/pallas_call | solution.py:541
  51.2 0.7 whole_rows.1
  52.0 9.3 %all-to-all-start = ((bf16[128,16,128]{2,1,0:T(8,128)(2,1)}), bf16[128,16,128]{2,1,0:T(8,128)(2,1)S(1)}, u32[]{:S(2)}, u32[]{:S(2)}) async-start(bf16[128,16,128]{2,1,0:T(8,128)(2,1)} %gradient_parts.1.refs_8_), calls=%async_computation | async-start | bytes 1048576 | tf_op jit(solution)/shard_map/all_to_all | solution.py:693
  61.7 1.1 %maximum_bitcast_fusion = f32[32,2,2,2,512]{4,3,2,1,0:T(2,128)} fusion(f32[1,2,2,32,512]{4,2,1,0,3:T(2,128)S(1)} %copy.13, f32[1,2,2,32,512]{4,2,1,0,3:T(2,128)S(1)} %copy.12), kind=kLoop, calls=%fused_computation | loop fusion | flops 131072 | bytes 1048576 | tf_op jit(solution)/shard_map/transpose | solution.py:699
  62.8 11.6 %all-to-all-done.grads = bf16[128,16,128]{2,1,0:T(8,128)(2,1)S(1)} async-done(((bf16[128,16,128]{2,1,0:T(8,128)(2,1)}), bf16[128,16,128]{2,1,0:T(8,128)(2,1)S(1)}, u32[]{:S(2)}, u32[]{:S(2)}) %all-to-all-start) | async-done | bytes 524320 | tf_op jit(solution)/shard_map/all_to_all | solution.py:693
  74.4 1.2 %updated_rows.1 = f32[2,512]{1,0:T(2,128)} custom-call(bf16[128,16,128]{2,1,0:T(8,128)(2,1)S(1)} %all-to-all-done.grads, f32[512,512]{1,0:T(8,128)S(1)} %copy-done.2, f32[2,512]{1,0:T(2,128)S(1)} %copy-done.4), custom_call_target="tpu_custom_call" | custom-call | flops 200000000 | bytes 1500000 | tf_op jit(solution)/shard_map/updated_rows/pallas_call | solution.py:636
  (48 shorter events, 2.8 us)
Async XLA Ops:
  0.6 4.8 %copy-start.9 = (f32[2]{0:T(128)S(1)}, f32[2]{0:T(128)}, u32[]{:S(2)}) copy-start(f32[2]{0:T(128)} %freq.5) | copy-start | bytes 28
  0.6 4.8 %copy-start = (bf16[2,2,2,512,384]{4,3,2,1,0:T(8,128)(2,1)S(1)}, bf16[2,2,2,512,384]{4,3,2,1,0:T(8,128)(2,1)}, u32[]{:S(2)}) copy-start(bf16[2,2,2,512,384]{4,3,2,1,0:T(8,128)(2,1)} %gain.3) | copy-start | bytes 9437188
  0.7 4.8 %copy-start.5 = (f32[2,2,512]{2,1,0:T(2,128)S(1)}, f32[2,2,512]{2,1,0:T(2,128)}, u32[]{:S(2)}) copy-start(f32[2,2,512]{2,1,0:T(2,128)} %uv.3) | copy-start | bytes 24580
  0.7 4.8 %copy-start.4 = (f32[2,512]{1,0:T(2,128)S(1)}, f32[2,512]{1,0:T(2,128)}, u32[]{:S(2)}) copy-start(f32[2,512]{1,0:T(2,128)} %screen.5) | copy-start | bytes 12292
  0.7 4.8 %copy-start.6 = (f32[2,384]{1,0:T(2,128)S(1)}, f32[2,384]{1,0:T(2,128)}, u32[]{:S(2)}) copy-start(f32[2,384]{1,0:T(2,128)} %lm.3) | copy-start | bytes 9220
  5.4 3.8 %collective-permute-start = (bf16[2,528,768]{2,1,0:T(8,128)(2,1)}, bf16[2,528,768]{2,1,0:T(8,128)(2,1)S(1)}, u32[]{:S(2)}, u32[]{:S(2)}) collective-permute-start(bf16[2,528,768]{2,1,0:T(8,128)(2,1)} %phasor_send.1), channel_id=1, source_target_pairs={{0,8},{8,0},{16,24},{24,16},{32,40},{40,32},{48,56},{56,48},{64,72... | collective-permute-start | bytes 4866056 | tf_op jit(solution)/shard_map/ppermute | solution.py:667
  13.3 18.0 %collective-permute-start.8 = (f32[32,2,4,512]{3,2,1,0:T(4,128)S(1)}, f32[32,2,4,512]{3,2,1,0:T(4,128)S(1)}, u32[]{:S(2)}, u32[]{:S(2)}) collective-permute-start(f32[32,2,4,512]{3,2,1,0:T(4,128)S(1)} %observed_send.1), channel_id=1, source_target_pairs={{0,8},{8,0},{16,24},{24,16},{32,40},{40,32},{48,56},{56,48},{64,72... | collective-permute-start | bytes 1572872 | tf_op jit(solution)/shard_map/ppermute | solution.py:679
  13.5 8.0 %collective-permute-start.4 = (bf16[2,64,512]{2,1,0:T(8,128)(2,1)S(1)}, bf16[2,64,512]{2,1,0:T(8,128)(2,1)S(1)}, u32[]{:S(2)}, u32[]{:S(2)}) collective-permute-start(bf16[2,64,512]{2,1,0:T(8,128)(2,1)S(1)} %get-tuple-element.22), channel_id=1, source_target_pairs={{0,32},{8,40},{16,48},{24,56},{32,0},{40,8},{48,16},{56,24},{64,96... | collective-permute-start | bytes 393224 | tf_op jit(solution)/shard_map/ppermute | solution.py:671
  16.8 7.7 %collective-permute-start.5 = (bf16[2,64,512]{2,1,0:T(8,128)(2,1)S(1)}, bf16[2,64,512]{2,1,0:T(8,128)(2,1)S(1)}, u32[]{:S(2)}, u32[]{:S(2)}) collective-permute-start(bf16[2,64,512]{2,1,0:T(8,128)(2,1)S(1)} %get-tuple-element.23), channel_id=1, source_target_pairs={{0,48},{8,56},{16,32},{24,40},{32,16},{40,24},{48,0},{56,8},{64,11... | collective-permute-start | bytes 393224 | tf_op jit(solution)/shard_map/ppermute | solution.py:671
  17.9 8.1 %collective-permute-start.6 = (bf16[2,64,512]{2,1,0:T(8,128)(2,1)S(1)}, bf16[2,64,512]{2,1,0:T(8,128)(2,1)S(1)}, u32[]{:S(2)}, u32[]{:S(2)}) collective-permute-start(bf16[2,64,512]{2,1,0:T(8,128)(2,1)S(1)} %get-tuple-element.24), channel_id=1, source_target_pairs={{0,16},{8,24},{16,0},{24,8},{32,48},{40,56},{48,32},{56,40},{64,80... | collective-permute-start | bytes 393224 | tf_op jit(solution)/shard_map/ppermute | solution.py:671
  17.9 13.9 %collective-permute-start.1 = (bf16[2,64,512]{2,1,0:T(8,128)(2,1)S(1)}, bf16[2,64,512]{2,1,0:T(8,128)(2,1)S(1)}, u32[]{:S(2)}, u32[]{:S(2)}) collective-permute-start(bf16[2,64,512]{2,1,0:T(8,128)(2,1)S(1)} %get-tuple-element.19._), channel_id=1, source_target_pairs={{0,32},{8,40},{16,48},{24,56},{32,0},{40,8},{48,16},{56,24},{64,96... | collective-permute-start | bytes 393224 | tf_op jit(solution)/shard_map/ppermute | solution.py:671
  21.5 10.2 %collective-permute-start.2 = (bf16[2,64,512]{2,1,0:T(8,128)(2,1)S(1)}, bf16[2,64,512]{2,1,0:T(8,128)(2,1)S(1)}, u32[]{:S(2)}, u32[]{:S(2)}) collective-permute-start(bf16[2,64,512]{2,1,0:T(8,128)(2,1)S(1)} %get-tuple-element.20), channel_id=1, source_target_pairs={{0,48},{8,56},{16,32},{24,40},{32,16},{40,24},{48,0},{56,8},{64,11... | collective-permute-start | bytes 393224 | tf_op jit(solution)/shard_map/ppermute | solution.py:671
  24.5 7.3 %collective-permute-start.3 = (bf16[2,64,512]{2,1,0:T(8,128)(2,1)S(1)}, bf16[2,64,512]{2,1,0:T(8,128)(2,1)S(1)}, u32[]{:S(2)}, u32[]{:S(2)}) collective-permute-start(bf16[2,64,512]{2,1,0:T(8,128)(2,1)S(1)} %get-tuple-element.21), channel_id=1, source_target_pairs={{0,16},{8,24},{16,0},{24,8},{32,48},{40,56},{48,32},{56,40},{64,80... | collective-permute-start | bytes 393224 | tf_op jit(solution)/shard_map/ppermute | solution.py:671
  26.0 5.8 %collective-permute-start.7 = (bf16[2,64,512]{2,1,0:T(8,128)(2,1)S(1)}, bf16[2,64,512]{2,1,0:T(8,128)(2,1)S(1)}, u32[]{:S(2)}, u32[]{:S(2)}) collective-permute-start(bf16[2,64,512]{2,1,0:T(8,128)(2,1)S(1)} %send_parts.1), channel_id=1, source_target_pairs={{0,64},{8,72},{16,80},{24,88},{32,96},{40,104},{48,112},{56,120},{... | collective-permute-start | bytes 393224 | tf_op jit(solution)/shard_map/ppermute | solution.py:674
  31.9 5.5 %collective-permute-start.12 = (bf16[2,64,512]{2,1,0:T(8,128)(2,1)S(1)}, bf16[2,64,512]{2,1,0:T(8,128)(2,1)S(1)}, u32[]{:S(2)}, u32[]{:S(2)}) collective-permute-start(bf16[2,64,512]{2,1,0:T(8,128)(2,1)S(1)} %get-tuple-element.31.refs_0_), channel_id=1, source_target_pairs={{0,64},{8,72},{16,80},{24,88},{32,96},{40,104},{48,112},{56,120},{... | collective-permute-start | bytes 393224 | tf_op jit(solution)/shard_map/ppermute | solution.py:674
  33.3 7.6 %collective-permute-start.9 = (bf16[2,64,512]{2,1,0:T(8,128)(2,1)S(1)}, bf16[2,64,512]{2,1,0:T(8,128)(2,1)S(1)}, u32[]{:S(2)}, u32[]{:S(2)}) collective-permute-start(bf16[2,64,512]{2,1,0:T(8,128)(2,1)S(1)} %get-tuple-element.31.refs_0_), channel_id=1, source_target_pairs={{0,16},{8,24},{16,0},{24,8},{32,48},{40,56},{48,32},{56,40},{64,80... | collective-permute-start | bytes 393224 | tf_op jit(solution)/shard_map/ppermute | solution.py:671
  33.9 11.8 %collective-permute-start.10 = (bf16[2,64,512]{2,1,0:T(8,128)(2,1)S(1)}, bf16[2,64,512]{2,1,0:T(8,128)(2,1)S(1)}, u32[]{:S(2)}, u32[]{:S(2)}) collective-permute-start(bf16[2,64,512]{2,1,0:T(8,128)(2,1)S(1)} %get-tuple-element.31.refs_0_), channel_id=1, source_target_pairs={{0,48},{8,56},{16,32},{24,40},{32,16},{40,24},{48,0},{56,8},{64,11... | collective-permute-start | bytes 393224 | tf_op jit(solution)/shard_map/ppermute | solution.py:671
  36.8 9.0 %collective-permute-start.11 = (bf16[2,64,512]{2,1,0:T(8,128)(2,1)S(1)}, bf16[2,64,512]{2,1,0:T(8,128)(2,1)S(1)}, u32[]{:S(2)}, u32[]{:S(2)}) collective-permute-start(bf16[2,64,512]{2,1,0:T(8,128)(2,1)S(1)} %get-tuple-element.31.refs_0_), channel_id=1, source_target_pairs={{0,32},{8,40},{16,48},{24,56},{32,0},{40,8},{48,16},{56,24},{64,96... | collective-permute-start | bytes 393224 | tf_op jit(solution)/shard_map/ppermute | solution.py:671
  37.4 8.3 %collective-permute-start.13 = (bf16[2,64,512]{2,1,0:T(8,128)(2,1)S(1)}, bf16[2,64,512]{2,1,0:T(8,128)(2,1)S(1)}, u32[]{:S(2)}, u32[]{:S(2)}) collective-permute-start(bf16[2,64,512]{2,1,0:T(8,128)(2,1)S(1)} %collective-permute-done.12.refs_4_), channel_id=1, source_target_pairs={{0,16},{8,24},{16,0},{24,8},{32,48},{40,56},{48,32},{56,40},{64,80... | collective-permute-start | bytes 393224 | tf_op jit(solution)/shard_map/ppermute | solution.py:671
  38.0 10.5 %collective-permute-start.14 = (bf16[2,64,512]{2,1,0:T(8,128)(2,1)S(1)}, bf16[2,64,512]{2,1,0:T(8,128)(2,1)S(1)}, u32[]{:S(2)}, u32[]{:S(2)}) collective-permute-start(bf16[2,64,512]{2,1,0:T(8,128)(2,1)S(1)} %collective-permute-done.12.refs_4_), channel_id=1, source_target_pairs={{0,48},{8,56},{16,32},{24,40},{32,16},{40,24},{48,0},{56,8},{64,11... | collective-permute-start | bytes 393224 | tf_op jit(solution)/shard_map/ppermute | solution.py:671
  40.9 7.6 %collective-permute-start.15 = (bf16[2,64,512]{2,1,0:T(8,128)(2,1)S(1)}, bf16[2,64,512]{2,1,0:T(8,128)(2,1)S(1)}, u32[]{:S(2)}, u32[]{:S(2)}) collective-permute-start(bf16[2,64,512]{2,1,0:T(8,128)(2,1)S(1)} %collective-permute-done.12.refs_4_), channel_id=1, source_target_pairs={{0,32},{8,40},{16,48},{24,56},{32,0},{40,8},{48,16},{56,24},{64,96... | collective-permute-start | bytes 393224 | tf_op jit(solution)/shard_map/ppermute | solution.py:671
  51.9 22.5 %copy-start.2 = (f32[512,512]{1,0:T(8,128)S(1)}, f32[512,512]{1,0:T(8,128)}, u32[]{:S(2)}) copy-start(f32[512,512]{1,0:T(8,128)} %kernel.1) | copy-start | bytes 3145732
  51.9 9.4 %collective-permute-start.16 = (f32[4,32,512]{2,1,0:T(8,128)S(1)}, f32[4,32,512]{2,1,0:T(8,128)S(1)}, u32[]{:S(2)}, u32[]{:S(2)}) collective-permute-start(f32[4,32,512]{2,1,0:T(8,128)S(1)} %get-tuple-element.33), channel_id=1, source_target_pairs={{0,8},{8,0},{16,24},{24,16},{32,40},{40,32},{48,56},{56,48},{64,72... | collective-permute-start | bytes 786440 | tf_op jit(solution)/shard_map/ppermute | solution.py:692
  52.0 22.4 %all-to-all-start = ((bf16[128,16,128]{2,1,0:T(8,128)(2,1)}), bf16[128,16,128]{2,1,0:T(8,128)(2,1)S(1)}, u32[]{:S(2)}, u32[]{:S(2)}) async-start(bf16[128,16,128]{2,1,0:T(8,128)(2,1)} %gradient_parts.1.refs_8_), calls=%async_computation | async-start | bytes 1048576 | tf_op jit(solution)/shard_map/all_to_all | solution.py:693
  (4 other events, 18.9 us)

commit v7 on v6

--- a/solution.py
+++ b/solution.py
@@ -484,30 +484,29 @@
     )(observed, flags, other)
 
 
-def gradient_kernel(freq, *refs):
-    resids = refs[0:8]
-    parts0, parts1, out, rows_sum, cols_sum = refs[8:]
+def gradient_kernel(flip, freq, *refs):
+    sources = refs[0:4]
+    parts0, parts1 = refs[4:6]
+    out, rows_sum, cols_sum = refs[-3:]
     core, y, z = position()
-    for rel in range(4):
-        for flip in range(2):
-            zz = 1 - z if flip else z
-            chip = zz * 4 + y_partner(rel, y)
-            source = resids[flip * 4 + rel]
-            for start in range(0, 64, 32):
-                rows = slice(start, start + 32)
-                resid0 = source[0, rows, :]
-                resid1 = source[1, rows, :]
-                for which in range(4):
-                    product = (resid0 * parts0[which, rel, flip, rows, :]).astype(f32)
-                    product += (resid1 * parts1[which, rel, flip, rows, :]).astype(f32)
-                    rows_sum[which, pl.ds(pl.multiple_of(chip * 64 + start, 32), 32), :] = (
-                        product[:, 0:128] + product[:, 128:256]
-                    ) + (product[:, 256:384] + product[:, 384:512])
-                    column = (product[0:8] + product[8:16]) + (product[16:24] + product[24:32])
-                    if start == 0:
-                        cols_sum[which, chip] = column
-                    else:
-                        cols_sum[which, chip] += column
+    zz = 1 - z if flip else z
+    for rel, source in enumerate(sources):
+        chip = y_partner(rel, y)
+        for start in range(0, 64, 32):
+            rows = slice(start, start + 32)
+            resid0 = source[0, rows, :]
+            resid1 = source[1, rows, :]
+            for which in range(4):
+                product = (resid0 * parts0[which, rel, flip, rows, :]).astype(f32)
+                product += (resid1 * parts1[which, rel, flip, rows, :]).astype(f32)
+                rows_sum[which, pl.ds(pl.multiple_of(chip * 64 + start, 32), 32), :] = (
+                    product[:, 0:128] + product[:, 128:256]
+                ) + (product[:, 256:384] + product[:, 384:512])
+                column = (product[0:8] + product[8:16]) + (product[16:24] + product[24:32])
+                if start == 0:
+                    cols_sum[which, chip] = column
+                else:
+                    cols_sum[which, chip] += column
     near = lax.broadcasted_iota(jnp.int32, (8, 256), 1) < 64
     factor = 2.0 / freq[core]
     pieces = []
@@ -515,7 +514,7 @@
         placed = []
         for odd in range(2):
             total = None
-            for chip in range(odd, 8, 2):
+            for chip in range(odd, 4, 2):
                 low = cols_sum[which, chip, :, 0:256]
                 high = cols_sum[which, chip, :, 256:512]
                 folded = [low + jnp.where(near, 0.0, high), jnp.where(near, high, 0.0)]
@@ -524,30 +523,40 @@
                 quarters = quarters[turn:] + quarters[:turn]
                 total = quarters if total is None else [a + b for a, b in zip(total, quarters)]
             placed.append(jnp.concatenate(total, axis=1))
-        columns = placed[0] + pltpu.roll(placed[1], 64, 1)
+        columns = jnp.sum(placed[0] + pltpu.roll(placed[1], 64, 1), axis=0, keepdims=True)
         along_rows = jnp.sum(jnp.transpose(rows_sum[which]), axis=0, keepdims=True)
-        grad = (along_rows - jnp.sum(columns, axis=0, keepdims=True)) * factor
-        pieces.extend(grad[:, at : at + 128] for at in range(0, 512, 128))
-    value = jnp.concatenate(pieces, axis=0).astype(bf16)
-
-    def copy(index, carry):
-        out[index] = value
-        return carry
-
-    lax.fori_loop(0, out.shape[0], copy, 0, unroll=8)
-
-
-def gradient_parts(devices, freq, resids, parts0, parts1):
-    return pl.pallas_call(
-        gradient_kernel,
-        in_specs=[SCALARS] + [WHOLE] * 10,
+        first = (along_rows - columns[:, 0:256]) * factor
+        second = -columns[:, 256:512] * factor
+        low = jnp.where(zz == 0, first, second)
+        high = jnp.where(zz == 0, second, first)
+        pieces.extend([low[:, 0:128], low[:, 128:256], high[:, 0:128], high[:, 128:256]])
+    value = jnp.concatenate(pieces, axis=0)
+    if flip == 0:
+        out[...] = value
+    else:
+        value = (value + refs[6][...]).astype(bf16)
+
+        def copy(index, carry):
+            out[index] = value
+            return carry
+
+        lax.fori_loop(0, out.shape[0], copy, 0, unroll=8)
+
+
+def gradient_parts(flip, devices, freq, *arrays):
+    out = jax.ShapeDtypeStruct((16, 128), f32)
+    if flip:
+        out = jax.ShapeDtypeStruct((devices, 16, 128), bf16)
+    return pl.pallas_call(
+        functools.partial(gradient_kernel, flip),
+        in_specs=[SCALARS] + [WHOLE] * len(arrays),
         out_specs=WHOLE,
-        scratch_shapes=[pltpu.VMEM((4, 512, 128), f32), pltpu.VMEM((4, 8, 8, 512), f32)],
-        out_shape=jax.ShapeDtypeStruct((devices, 16, 128), bf16),
-        compiler_params=pltpu.CompilerParams(vmem_limit_bytes=12 * MIB),
-        cost_estimate=pl.CostEstimate(flops=10000000, bytes_accessed=6000000, transcendentals=0),
-        name="gradient_parts",
-    )(freq, *resids, parts0, parts1)
+        scratch_shapes=[pltpu.VMEM((4, 256, 128), f32), pltpu.VMEM((4, 4, 8, 512), f32)],
+        out_shape=out,
+        compiler_params=pltpu.CompilerParams(vmem_limit_bytes=10 * MIB),
+        cost_estimate=pl.CostEstimate(flops=5000000, bytes_accessed=3000000, transcendentals=0),
+        name="gradient_parts%d" % flip,
+    )(freq, *arrays)
 
 
 def rows_kernel(resid, *refs):
@@ -683,11 +692,12 @@
     resid, half = residual_parts(parts[0], *near, last, obs, kept, directions0)
     half_z = across_z(half)
     directions1 = direction_parts(1, scaling, own, other, *parts[7:])
-    resids = [
-        array if rel == 0 else across(rel, array) for array in (half, half_z) for rel in range(4)
-    ]
-
-    grads = gradient_parts(devices, freq_ratio, resids, directions0, directions1)
+    one, two = across(1, half), across(2, half)
+    one_z, two_z = across(1, half_z), across(2, half_z)
+    resids = [half, one, two, across(2, one), half_z, one_z, two_z, across(1, two_z)]
+
+    grads = gradient_parts(0, devices, freq_ratio, *resids[:4], directions0, directions1)
+    grads = gradient_parts(1, devices, freq_ratio, *resids[4:], directions0, directions1, grads)
     own_rows, sent_rows = whole_rows(resid, resids, grads)
     other_rows = swap(sent_rows)
     grads = lax.all_to_all(grads, ("dir", "freq"), 0, 0, tiled=True)

time: 75.7 us -> 77 us (1.017)
  waiting for transfers between devices: 15 us -> 18 us
  starting transfers between devices: 34.9 us -> 32.5 us
    ppermute x12, starting transfers between devices: 21.6 us -> 18.4 us  [across(): return lax.ppermute(array, 'dir', dir_perm(rel))]
    ppermute x2, waiting for transfers between devices: 0.01 us -> 3.04 us  [across_z(): return lax.ppermute(array, 'dir', dir_perm(0, flip_z=True))]
    all_to_all x1, starting transfers between devices: 9.26 us -> 10.1 us  [body(): grads = lax.all_to_all(grads, ('dir', 'freq'), 0, 0, tiled=True)]
    pallas_call x1 -> x2, Pallas kernels: 2.66 us -> 3.3 us  [gradient_parts(): pl.pallas_call(functools.partial(gradient_kernel, flip), in_specs=[SCALAR...]
  transfers between devices with their start and end apart: 18 -> 18, of which waited for: 3 -> 5; matrix products, arithmetic and copies ran while one was open for 2% -> 2% of each run, Pallas kernels for 13% -> 14%
where the time goes in v7:
time: 77 us; the launch traced here: 76.8 us
  starting transfers between devices  32.5 us (42%)
  Pallas kernels  23.8 us (31%)
  waiting for transfers between devices  18 us (23%)
  other arithmetic  1.1 us (1%)
  between operations  1 us (1%)
    ppermute x12, starting transfers between devices, across(): return lax.ppermute(array, 'dir', dir_perm(rel))  18.4 us
    all_to_all x1, waiting for transfers between devices, body(): grads = lax.all_to_all(grads, ('dir', 'freq'), 0, 0, tiled=True)  11.6 us
    all_to_all x1, starting transfers between devices, body(): grads = lax.all_to_all(grads, ('dir', 'freq'), 0, 0, tiled=True)  10.1 us
    pallas_call x2, Pallas kernels, direction_parts(): pl.pallas_call(functools.partial(direction_kernel, moment, scaling), in_s...  6.29 us
    pallas_call x1, Pallas kernels, phasor_send(): pl.pallas_call(phasor_send_kernel, in_specs=[HBM] * 7, out_specs=HBM, out...  4.71 us
    pallas_call x1, Pallas kernels, model_parts(): pl.pallas_call(functools.partial(model_kernel, scaling), in_specs=[WHOLE,...  3.96 us
    ppermute x2, starting transfers between devices, across_z(): return lax.ppermute(array, 'dir', dir_perm(0, flip_z=True))  3.61 us
    pallas_call x2, Pallas kernels, gradient_parts(): pl.pallas_call(functools.partial(gradient_kernel, flip), in_specs=[SCALAR...  3.3 us
  transfers between devices with their start and end apart: 18, of which 5 were waited for; matrix products, arithmetic and copies ran while one was open for 2% of the time, Pallas kernels for 14%

profile of v7, /device:TPU:0, one launch (start us, length us, event | category | flops | bytes accessed | tf_op | source)
XLA Modules:
  0.0 76.8 jit_solution(3287143837010067262)
XLA Ops:
  0.7 4.7 %phasor_send.1 = bf16[2,528,768]{2,1,0:T(8,128)(2,1)} custom-call(f32[2]{0:T(128)} %freq.7, bf16[2,2,2,512,384]{4,3,2,1,0:T(8,128)(2,1)} %gain.3, f32[2,2,512]{2,1,0:T(2,128)} %uv.3, f32[2,512]{1,0:T(2,128)} %screen.5, f32[2,384]{1,0:T(2,128)} %lm.3, f32[384]{0:T(512)} %flux.3, s32[384]{0:T(512)} %direction.3), custom_call_target="tpu_custom_call" | custom-call | flops 15728640 | bytes 3200000 | tf_op jit(solution)/shard_map/phasor_send/pallas_call | solution.py:187
  5.6 2.9 %phasor_own.1.own = bf16[2,528,768]{2,1,0:T(8,128)(2,1)S(1)} custom-call(f32[2]{0:T(128)S(1)} %copy-done.9, bf16[2,2,2,512,384]{4,3,2,1,0:T(8,128)(2,1)S(1)} %copy-done, f32[2,2,512]{2,1,0:T(2,128)S(1)} %copy-done.5, f32[2,512]{1,0:T(2,128)S(1)} %copy-done.4, f32[2,384]{1,0:T(2,128)S(1)} %copy-done.6, f32[384]{0:T(512)S(1)} %copy-done.7, s32[384]{0:T(512)S(1)} %copy-done.8), custom_call_target="tpu_custom_call" | custom-call | flops 15728640 | bytes 3200000 | tf_op jit(solution)/shard_map/phasor_own/pallas_call | solution.py:212
  9.2 4.0 %model_parts.1 = (f32[2,2,64,512]{3,2,1,0:T(8,128)S(1)}, bf16[2,64,512]{2,1,0:T(8,128)(2,1)S(1)}, bf16[2,64,512]{2,1,0:T(8,128)(2,1)S(1)}, bf16[2,64,512]{2,1,0:...) custom-call(bf16[2,528,768]{2,1,0:T(8,128)(2,1)S(1)} %phasor_own.1.o, ...), custom_call_target="tpu_custom_call" | custom-call | flops 3221225472 | bytes 5000000 | tf_op jit(solution)/shard_map/model_parts/pallas_call | solution.py:319
  13.6 3.3 %collective-permute-start.4 = (bf16[2,64,512]{2,1,0:T(8,128)(2,1)S(1)}, bf16[2,64,512]{2,1,0:T(8,128)(2,1)S(1)}, u32[]{:S(2)}, u32[]{:S(2)}) collective-permute-start(bf16[2,64,512]{2,1,0:T(8,128)(2,1)S(1)} %get-tuple-element.22), channel_id=1, source_target_pairs={{0,32},{8,40},{16,48},{24,56},{32,0},{40,8},{48,16},{56,24},{64,96... | collective-permute-start | bytes 393224 | tf_op jit(solution)/shard_map/ppermute | solution.py:680
  16.9 1.0 %collective-permute-start.5 = (bf16[2,64,512]{2,1,0:T(8,128)(2,1)S(1)}, bf16[2,64,512]{2,1,0:T(8,128)(2,1)S(1)}, u32[]{:S(2)}, u32[]{:S(2)}) collective-permute-start(bf16[2,64,512]{2,1,0:T(8,128)(2,1)S(1)} %get-tuple-element.23), channel_id=1, source_target_pairs={{0,48},{8,56},{16,32},{24,40},{32,16},{40,24},{48,0},{56,8},{64,11... | collective-permute-start | bytes 393224 | tf_op jit(solution)/shard_map/ppermute | solution.py:680
  17.9 3.7 %collective-permute-start.1 = (bf16[2,64,512]{2,1,0:T(8,128)(2,1)S(1)}, bf16[2,64,512]{2,1,0:T(8,128)(2,1)S(1)}, u32[]{:S(2)}, u32[]{:S(2)}) collective-permute-start(bf16[2,64,512]{2,1,0:T(8,128)(2,1)S(1)} %get-tuple-element.19._), channel_id=1, source_target_pairs={{0,32},{8,40},{16,48},{24,56},{32,0},{40,8},{48,16},{56,24},{64,96... | collective-permute-start | bytes 393224 | tf_op jit(solution)/shard_map/ppermute | solution.py:680
  21.6 3.0 %collective-permute-start.2 = (bf16[2,64,512]{2,1,0:T(8,128)(2,1)S(1)}, bf16[2,64,512]{2,1,0:T(8,128)(2,1)S(1)}, u32[]{:S(2)}, u32[]{:S(2)}) collective-permute-start(bf16[2,64,512]{2,1,0:T(8,128)(2,1)S(1)} %get-tuple-element.20), channel_id=1, source_target_pairs={{0,48},{8,56},{16,32},{24,40},{32,16},{40,24},{48,0},{56,8},{64,11... | collective-permute-start | bytes 393224 | tf_op jit(solution)/shard_map/ppermute | solution.py:680
  24.5 1.4 %collective-permute-start.3 = (bf16[2,64,512]{2,1,0:T(8,128)(2,1)S(1)}, bf16[2,64,512]{2,1,0:T(8,128)(2,1)S(1)}, u32[]{:S(2)}, u32[]{:S(2)}) collective-permute-start(bf16[2,64,512]{2,1,0:T(8,128)(2,1)S(1)} %get-tuple-element.21), channel_id=1, source_target_pairs={{0,16},{8,24},{16,0},{24,8},{32,48},{40,56},{48,32},{56,40},{64,80... | collective-permute-start | bytes 393224 | tf_op jit(solution)/shard_map/ppermute | solution.py:680
  26.0 2.2 %collective-permute-start.7 = (bf16[2,64,512]{2,1,0:T(8,128)(2,1)S(1)}, bf16[2,64,512]{2,1,0:T(8,128)(2,1)S(1)}, u32[]{:S(2)}, u32[]{:S(2)}) collective-permute-start(bf16[2,64,512]{2,1,0:T(8,128)(2,1)S(1)} %send_parts.1), channel_id=1, source_target_pairs={{0,64},{8,72},{16,80},{24,88},{32,96},{40,104},{48,112},{56,120},{... | collective-permute-start | bytes 393224 | tf_op jit(solution)/shard_map/ppermute | solution.py:683
  28.2 3.1 %direction_parts0.1._.refs_4_ = bf16[4,4,2,64,512]{4,3,2,1,0:T(8,128)(2,1)S(1)} custom-call(bf16[2,528,768]{2,1,0:T(8,128)(2,1)S(1)} %phasor_own.1.own, bf16[2,528,768]{2,1,0:T(8,128)(2,1)S(1)} %collective-permute-done.other_hbm.other, f32[2,2,512,768]{3,2,1,0:T(8,128)S(1)} %get-tuple-element.27.totals, f32[2,2,256,512]{3,2,1,0:T(8,128)S(1)} %get-tuple-element.28.tops, ...), custom_call_target="tpu_custom_call" | custom-call | flops 1610612736 | bytes 5000000 | tf_op jit(solution)/shard_map/direction_parts0/pallas_call | solution.py:363
  31.9 1.4 %collective-permute-start.12 = (bf16[2,64,512]{2,1,0:T(8,128)(2,1)S(1)}, bf16[2,64,512]{2,1,0:T(8,128)(2,1)S(1)}, u32[]{:S(2)}, u32[]{:S(2)}) collective-permute-start(bf16[2,64,512]{2,1,0:T(8,128)(2,1)S(1)} %get-tuple-element.31.refs_0_), channel_id=1, source_target_pairs={{0,64},{8,72},{16,80},{24,88},{32,96},{40,104},{48,112},{56,120},{... | collective-permute-start | bytes 393224 | tf_op jit(solution)/shard_map/ppermute | solution.py:683
  33.9 3.0 %collective-permute-done.12.refs_0_.refs_4_ = bf16[2,64,512]{2,1,0:T(8,128)(2,1)S(1)} collective-permute-done((bf16[2,64,512]{2,1,0:T(8,128)(2,1)S(1)}, bf16[2,64,512]{2,1,0:T(8,128)(2,1)S(1)}, u32[]{:S(2)}, u32[]{:S(2)}) %collective-permute-start.12) | collective-permute-done | bytes 131104 | tf_op jit(solution)/shard_map/ppermute | solution.py:683
  37.0 1.5 %collective-permute-start.14 = (bf16[2,64,512]{2,1,0:T(8,128)(2,1)S(1)}, bf16[2,64,512]{2,1,0:T(8,128)(2,1)S(1)}, u32[]{:S(2)}, u32[]{:S(2)}) collective-permute-start(bf16[2,64,512]{2,1,0:T(8,128)(2,1)S(1)} %collective-permute-done.12.refs_0_.refs_4_), channel_id=1, source_target_pairs={{0,48},{8,56},{16,32},{24,40},{32,16},{40,24},{48,0},{56,8},{64,11... | collective-permute-start | bytes 393224 | tf_op jit(solution)/shard_map/ppermute | solution.py:680
  38.5 1.8 %collective-permute-start.10 = (bf16[2,64,512]{2,1,0:T(8,128)(2,1)S(1)}, bf16[2,64,512]{2,1,0:T(8,128)(2,1)S(1)}, u32[]{:S(2)}, u32[]{:S(2)}) collective-permute-start(bf16[2,64,512]{2,1,0:T(8,128)(2,1)S(1)} %get-tuple-element.31.refs_0_), channel_id=1, source_target_pairs={{0,48},{8,56},{16,32},{24,40},{32,16},{40,24},{48,0},{56,8},{64,11... | collective-permute-start | bytes 393224 | tf_op jit(solution)/shard_map/ppermute | solution.py:680
  40.2 2.2 %collective-permute-start.11 = (bf16[2,64,512]{2,1,0:T(8,128)(2,1)S(1)}, bf16[2,64,512]{2,1,0:T(8,128)(2,1)S(1)}, u32[]{:S(2)}, u32[]{:S(2)}) collective-permute-start(bf16[2,64,512]{2,1,0:T(8,128)(2,1)S(1)} %collective-permute-done.9.refs_1_), channel_id=1, source_target_pairs={{0,48},{8,56},{16,32},{24,40},{32,16},{40,24},{48,0},{56,8},{64,11... | collective-permute-start | bytes 393224 | tf_op jit(solution)/shard_map/ppermute | solution.py:680
  42.4 2.2 %collective-permute-done.14.refs_2_.refs_6_ = bf16[2,64,512]{2,1,0:T(8,128)(2,1)S(1)} collective-permute-done((bf16[2,64,512]{2,1,0:T(8,128)(2,1)S(1)}, bf16[2,64,512]{2,1,0:T(8,128)(2,1)S(1)}, u32[]{:S(2)}, u32[]{:S(2)}) %collective-permute-start.14) | collective-permute-done | bytes 131104 | tf_op jit(solution)/shard_map/ppermute | solution.py:680
  44.6 3.1 %direction_parts1.1.refs_5_ = bf16[4,4,2,64,512]{4,3,2,1,0:T(8,128)(2,1)S(1)} custom-call(bf16[2,528,768]{2,1,0:T(8,128)(2,1)S(1)} %phasor_own.1.own, bf16[2,528,768]{2,1,0:T(8,128)(2,1)S(1)} %collective-permute-done.other_hbm.other, f32[2,2,512,768]{3,2,1,0:T(8,128)S(1)} %get-tuple-element.27.totals, f32[2,2,256,512]{3,2,1,0:T(8,128)S(1)} %get-tuple-element.28.tops, ...), custom_call_target="tpu_custom_call" | custom-call | flops 1610612736 | bytes 5000000 | tf_op jit(solution)/shard_map/direction_parts1/pallas_call | solution.py:363
  47.8 1.2 %gradient_parts0.1.refs_6_ = f32[16,128]{1,0:T(8,128)S(1)} custom-call(f32[2]{0:T(128)S(1)} %copy-done.9, bf16[2,64,512]{2,1,0:T(8,128)(2,1)S(1)} %get-tuple-element.31.refs_0_, bf16[2,64,512]{2,1,0:T(8,128)(2,1)S(1)} %collective-permute-done.9.refs_1_, bf16[2,64,512]{2,1,0:T(8,128)(2,1)S(1)} %collective-permute-done.10.refs_2_, ...), custom_call_target="tpu_custom_call" | custom-call | flops 5000000 | bytes 3000000 | tf_op jit(solution)/shard_map/gradient_parts0/pallas_call | solution.py:550
  49.5 2.1 %gradient_parts1.1.refs_8_ = bf16[128,16,128]{2,1,0:T(8,128)(2,1)} custom-call(f32[2]{0:T(128)S(1)} %copy-done.9, bf16[2,64,512]{2,1,0:T(8,128)(2,1)S(1)} %collective-permute-done.12.refs_0_.refs_4_, bf16[2,64,512]{2,1,0:T(8,128)(2,1)S(1)} %collective-permute-done.13.refs_1_.refs_5_, bf16[2,64,512]{2,1,0:T(8,128)(2,1)S(1)} %collective-permute-done.14.refs_2_.refs_6_, ...), custom_call_target="tpu_custom_call" | custom-call | flops 5000000 | bytes 3000000 | tf_op jit(solution)/shard_map/gradient_parts1/pallas_call | solution.py:550
  51.6 0.7 whole_rows.1
  52.4 10.1 %all-to-all-start = ((bf16[128,16,128]{2,1,0:T(8,128)(2,1)}), bf16[128,16,128]{2,1,0:T(8,128)(2,1)S(1)}, u32[]{:S(2)}, u32[]{:S(2)}) async-start(bf16[128,16,128]{2,1,0:T(8,128)(2,1)} %gradient_parts1.1.refs_8_), calls=%async_computation | async-start | bytes 1048576 | tf_op jit(solution)/shard_map/all_to_all | solution.py:703
  63.0 1.1 %maximum_bitcast_fusion = f32[32,2,2,2,512]{4,3,2,1,0:T(2,128)} fusion(f32[1,2,2,32,512]{4,2,1,0,3:T(2,128)S(1)} %copy.13, f32[1,2,2,32,512]{4,2,1,0,3:T(2,128)S(1)} %copy.12), kind=kLoop, calls=%fused_computation | loop fusion | flops 131072 | bytes 1048576 | tf_op jit(solution)/shard_map/transpose | solution.py:709
  64.1 11.6 %all-to-all-done.grads = bf16[128,16,128]{2,1,0:T(8,128)(2,1)S(1)} async-done(((bf16[128,16,128]{2,1,0:T(8,128)(2,1)}), bf16[128,16,128]{2,1,0:T(8,128)(2,1)S(1)}, u32[]{:S(2)}, u32[]{:S(2)}) %all-to-all-start) | async-done | bytes 524320 | tf_op jit(solution)/shard_map/all_to_all | solution.py:703
  75.7 1.2 %updated_rows.1 = f32[2,512]{1,0:T(2,128)} custom-call(bf16[128,16,128]{2,1,0:T(8,128)(2,1)S(1)} %all-to-all-done.grads, f32[512,512]{1,0:T(8,128)S(1)} %copy-done.2, f32[2,512]{1,0:T(2,128)S(1)} %copy-done.4), custom_call_target="tpu_custom_call" | custom-call | flops 200000000 | bytes 1500000 | tf_op jit(solution)/shard_map/updated_rows/pallas_call | solution.py:645
  (49 shorter events, 3.4 us)
Async XLA Ops:
  0.6 4.9 %copy-start.4 = (f32[2,512]{1,0:T(2,128)S(1)}, f32[2,512]{1,0:T(2,128)}, u32[]{:S(2)}) copy-start(f32[2,512]{1,0:T(2,128)} %screen.5) | copy-start | bytes 12292
  0.6 4.9 %copy-start.5 = (f32[2,2,512]{2,1,0:T(2,128)S(1)}, f32[2,2,512]{2,1,0:T(2,128)}, u32[]{:S(2)}) copy-start(f32[2,2,512]{2,1,0:T(2,128)} %uv.3) | copy-start | bytes 24580
  0.7 4.9 %copy-start.6 = (f32[2,384]{1,0:T(2,128)S(1)}, f32[2,384]{1,0:T(2,128)}, u32[]{:S(2)}) copy-start(f32[2,384]{1,0:T(2,128)} %lm.3) | copy-start | bytes 9220
  0.7 4.9 %copy-start.7 = (f32[384]{0:T(512)S(1)}, f32[384]{0:T(512)}, u32[]{:S(2)}) copy-start(f32[384]{0:T(512)} %flux.3) | copy-start | bytes 4612
  0.7 4.9 %copy-start = (bf16[2,2,2,512,384]{4,3,2,1,0:T(8,128)(2,1)S(1)}, bf16[2,2,2,512,384]{4,3,2,1,0:T(8,128)(2,1)}, u32[]{:S(2)}) copy-start(bf16[2,2,2,512,384]{4,3,2,1,0:T(8,128)(2,1)} %gain.3) | copy-start | bytes 9437188
  5.4 3.8 %collective-permute-start = (bf16[2,528,768]{2,1,0:T(8,128)(2,1)}, bf16[2,528,768]{2,1,0:T(8,128)(2,1)S(1)}, u32[]{:S(2)}, u32[]{:S(2)}) collective-permute-start(bf16[2,528,768]{2,1,0:T(8,128)(2,1)} %phasor_send.1), channel_id=1, source_target_pairs={{0,8},{8,0},{16,24},{24,16},{32,40},{40,32},{48,56},{56,48},{64,72... | collective-permute-start | bytes 4866056 | tf_op jit(solution)/shard_map/ppermute | solution.py:676
  13.4 18.0 %collective-permute-start.8 = (f32[32,2,4,512]{3,2,1,0:T(4,128)S(1)}, f32[32,2,4,512]{3,2,1,0:T(4,128)S(1)}, u32[]{:S(2)}, u32[]{:S(2)}) collective-permute-start(f32[32,2,4,512]{3,2,1,0:T(4,128)S(1)} %observed_send.1), channel_id=1, source_target_pairs={{0,8},{8,0},{16,24},{24,16},{32,40},{40,32},{48,56},{56,48},{64,72... | collective-permute-start | bytes 1572872 | tf_op jit(solution)/shard_map/ppermute | solution.py:688
  13.6 8.0 %collective-permute-start.4 = (bf16[2,64,512]{2,1,0:T(8,128)(2,1)S(1)}, bf16[2,64,512]{2,1,0:T(8,128)(2,1)S(1)}, u32[]{:S(2)}, u32[]{:S(2)}) collective-permute-start(bf16[2,64,512]{2,1,0:T(8,128)(2,1)S(1)} %get-tuple-element.22), channel_id=1, source_target_pairs={{0,32},{8,40},{16,48},{24,56},{32,0},{40,8},{48,16},{56,24},{64,96... | collective-permute-start | bytes 393224 | tf_op jit(solution)/shard_map/ppermute | solution.py:680
  16.9 7.7 %collective-permute-start.5 = (bf16[2,64,512]{2,1,0:T(8,128)(2,1)S(1)}, bf16[2,64,512]{2,1,0:T(8,128)(2,1)S(1)}, u32[]{:S(2)}, u32[]{:S(2)}) collective-permute-start(bf16[2,64,512]{2,1,0:T(8,128)(2,1)S(1)} %get-tuple-element.23), channel_id=1, source_target_pairs={{0,48},{8,56},{16,32},{24,40},{32,16},{40,24},{48,0},{56,8},{64,11... | collective-permute-start | bytes 393224 | tf_op jit(solution)/shard_map/ppermute | solution.py:680
  17.9 8.1 %collective-permute-start.6 = (bf16[2,64,512]{2,1,0:T(8,128)(2,1)S(1)}, bf16[2,64,512]{2,1,0:T(8,128)(2,1)S(1)}, u32[]{:S(2)}, u32[]{:S(2)}) collective-permute-start(bf16[2,64,512]{2,1,0:T(8,128)(2,1)S(1)} %get-tuple-element.24), channel_id=1, source_target_pairs={{0,16},{8,24},{16,0},{24,8},{32,48},{40,56},{48,32},{56,40},{64,80... | collective-permute-start | bytes 393224 | tf_op jit(solution)/shard_map/ppermute | solution.py:680
  17.9 13.9 %collective-permute-start.1 = (bf16[2,64,512]{2,1,0:T(8,128)(2,1)S(1)}, bf16[2,64,512]{2,1,0:T(8,128)(2,1)S(1)}, u32[]{:S(2)}, u32[]{:S(2)}) collective-permute-start(bf16[2,64,512]{2,1,0:T(8,128)(2,1)S(1)} %get-tuple-element.19._), channel_id=1, source_target_pairs={{0,32},{8,40},{16,48},{24,56},{32,0},{40,8},{48,16},{56,24},{64,96... | collective-permute-start | bytes 393224 | tf_op jit(solution)/shard_map/ppermute | solution.py:680
  21.6 10.2 %collective-permute-start.2 = (bf16[2,64,512]{2,1,0:T(8,128)(2,1)S(1)}, bf16[2,64,512]{2,1,0:T(8,128)(2,1)S(1)}, u32[]{:S(2)}, u32[]{:S(2)}) collective-permute-start(bf16[2,64,512]{2,1,0:T(8,128)(2,1)S(1)} %get-tuple-element.20), channel_id=1, source_target_pairs={{0,48},{8,56},{16,32},{24,40},{32,16},{40,24},{48,0},{56,8},{64,11... | collective-permute-start | bytes 393224 | tf_op jit(solution)/shard_map/ppermute | solution.py:680
  24.5 7.3 %collective-permute-start.3 = (bf16[2,64,512]{2,1,0:T(8,128)(2,1)S(1)}, bf16[2,64,512]{2,1,0:T(8,128)(2,1)S(1)}, u32[]{:S(2)}, u32[]{:S(2)}) collective-permute-start(bf16[2,64,512]{2,1,0:T(8,128)(2,1)S(1)} %get-tuple-element.21), channel_id=1, source_target_pairs={{0,16},{8,24},{16,0},{24,8},{32,48},{40,56},{48,32},{56,40},{64,80... | collective-permute-start | bytes 393224 | tf_op jit(solution)/shard_map/ppermute | solution.py:680
  26.0 5.8 %collective-permute-start.7 = (bf16[2,64,512]{2,1,0:T(8,128)(2,1)S(1)}, bf16[2,64,512]{2,1,0:T(8,128)(2,1)S(1)}, u32[]{:S(2)}, u32[]{:S(2)}) collective-permute-start(bf16[2,64,512]{2,1,0:T(8,128)(2,1)S(1)} %send_parts.1), channel_id=1, source_target_pairs={{0,64},{8,72},{16,80},{24,88},{32,96},{40,104},{48,112},{56,120},{... | collective-permute-start | bytes 393224 | tf_op jit(solution)/shard_map/ppermute | solution.py:683
  31.9 5.0 %collective-permute-start.12 = (bf16[2,64,512]{2,1,0:T(8,128)(2,1)S(1)}, bf16[2,64,512]{2,1,0:T(8,128)(2,1)S(1)}, u32[]{:S(2)}, u32[]{:S(2)}) collective-permute-start(bf16[2,64,512]{2,1,0:T(8,128)(2,1)S(1)} %get-tuple-element.31.refs_0_), channel_id=1, source_target_pairs={{0,64},{8,72},{16,80},{24,88},{32,96},{40,104},{48,112},{56,120},{... | collective-permute-start | bytes 393224 | tf_op jit(solution)/shard_map/ppermute | solution.py:683
  33.4 6.9 %collective-permute-start.9 = (bf16[2,64,512]{2,1,0:T(8,128)(2,1)S(1)}, bf16[2,64,512]{2,1,0:T(8,128)(2,1)S(1)}, u32[]{:S(2)}, u32[]{:S(2)}) collective-permute-start(bf16[2,64,512]{2,1,0:T(8,128)(2,1)S(1)} %get-tuple-element.31.refs_0_), channel_id=1, source_target_pairs={{0,16},{8,24},{16,0},{24,8},{32,48},{40,56},{48,32},{56,40},{64,80... | collective-permute-start | bytes 393224 | tf_op jit(solution)/shard_map/ppermute | solution.py:680
  37.0 7.6 %collective-permute-start.14 = (bf16[2,64,512]{2,1,0:T(8,128)(2,1)S(1)}, bf16[2,64,512]{2,1,0:T(8,128)(2,1)S(1)}, u32[]{:S(2)}, u32[]{:S(2)}) collective-permute-start(bf16[2,64,512]{2,1,0:T(8,128)(2,1)S(1)} %collective-permute-done.12.refs_0_.refs_4_), channel_id=1, source_target_pairs={{0,48},{8,56},{16,32},{24,40},{32,16},{40,24},{48,0},{56,8},{64,11... | collective-permute-start | bytes 393224 | tf_op jit(solution)/shard_map/ppermute | solution.py:680
  38.5 9.3 %collective-permute-start.10 = (bf16[2,64,512]{2,1,0:T(8,128)(2,1)S(1)}, bf16[2,64,512]{2,1,0:T(8,128)(2,1)S(1)}, u32[]{:S(2)}, u32[]{:S(2)}) collective-permute-start(bf16[2,64,512]{2,1,0:T(8,128)(2,1)S(1)} %get-tuple-element.31.refs_0_), channel_id=1, source_target_pairs={{0,48},{8,56},{16,32},{24,40},{32,16},{40,24},{48,0},{56,8},{64,11... | collective-permute-start | bytes 393224 | tf_op jit(solution)/shard_map/ppermute | solution.py:680
  40.2 8.8 %collective-permute-start.13 = (bf16[2,64,512]{2,1,0:T(8,128)(2,1)S(1)}, bf16[2,64,512]{2,1,0:T(8,128)(2,1)S(1)}, u32[]{:S(2)}, u32[]{:S(2)}) collective-permute-start(bf16[2,64,512]{2,1,0:T(8,128)(2,1)S(1)} %collective-permute-done.12.refs_0_.refs_4_), channel_id=1, source_target_pairs={{0,16},{8,24},{16,0},{24,8},{32,48},{40,56},{48,32},{56,40},{64,80... | collective-permute-start | bytes 393224 | tf_op jit(solution)/shard_map/ppermute | solution.py:680
  40.2 7.5 %collective-permute-start.11 = (bf16[2,64,512]{2,1,0:T(8,128)(2,1)S(1)}, bf16[2,64,512]{2,1,0:T(8,128)(2,1)S(1)}, u32[]{:S(2)}, u32[]{:S(2)}) collective-permute-start(bf16[2,64,512]{2,1,0:T(8,128)(2,1)S(1)} %collective-permute-done.9.refs_1_), channel_id=1, source_target_pairs={{0,48},{8,56},{16,32},{24,40},{32,16},{40,24},{48,0},{56,8},{64,11... | collective-permute-start | bytes 393224 | tf_op jit(solution)/shard_map/ppermute | solution.py:680
  44.6 5.0 %collective-permute-start.15 = (bf16[2,64,512]{2,1,0:T(8,128)(2,1)S(1)}, bf16[2,64,512]{2,1,0:T(8,128)(2,1)S(1)}, u32[]{:S(2)}, u32[]{:S(2)}) collective-permute-start(bf16[2,64,512]{2,1,0:T(8,128)(2,1)S(1)} %collective-permute-done.14.refs_2_.refs_6_), channel_id=1, source_target_pairs={{0,16},{8,24},{16,0},{24,8},{32,48},{40,56},{48,32},{56,40},{64,80... | collective-permute-start | bytes 393224 | tf_op jit(solution)/shard_map/ppermute | solution.py:680
  52.3 23.4 %copy-start.2 = (f32[512,512]{1,0:T(8,128)S(1)}, f32[512,512]{1,0:T(8,128)}, u32[]{:S(2)}) copy-start(f32[512,512]{1,0:T(8,128)} %kernel.1) | copy-start | bytes 3145732
  52.3 10.2 %collective-permute-start.16 = (f32[4,32,512]{2,1,0:T(8,128)S(1)}, f32[4,32,512]{2,1,0:T(8,128)S(1)}, u32[]{:S(2)}, u32[]{:S(2)}) collective-permute-start(f32[4,32,512]{2,1,0:T(8,128)S(1)} %get-tuple-element.33), channel_id=1, source_target_pairs={{0,8},{8,0},{16,24},{24,16},{32,40},{40,32},{48,56},{56,48},{64,72... | collective-permute-start | bytes 786440 | tf_op jit(solution)/shard_map/ppermute | solution.py:702
  52.4 23.3 %all-to-all-start = ((bf16[128,16,128]{2,1,0:T(8,128)(2,1)}), bf16[128,16,128]{2,1,0:T(8,128)(2,1)S(1)}, u32[]{:S(2)}, u32[]{:S(2)}) async-start(bf16[128,16,128]{2,1,0:T(8,128)(2,1)} %gradient_parts1.1.refs_8_), calls=%async_computation | async-start | bytes 1048576 | tf_op jit(solution)/shard_map/all_to_all | solution.py:703
  (4 other events, 19.0 us)

commit v8 on v7

--- a/solution.py
+++ b/solution.py
@@ -611,6 +611,26 @@
     )(resid, *resids, after)
 
 
+def assemble_kernel(own, other, out):
+    core = position()[0]
+    for channel, source in ((core, own), (1 - core, other)):
+        for moment in range(2):
+            for part in range(2):
+                out[:, channel, moment, part, :] = source[moment * 2 + part]
+
+
+def assemble(own, other, like):
+    return pl.pallas_call(
+        assemble_kernel,
+        in_specs=[WHOLE] * 2,
+        out_specs=WHOLE,
+        out_shape=jax.ShapeDtypeStruct(like.shape, f32),
+        compiler_params=pltpu.CompilerParams(vmem_limit_bytes=4 * MIB),
+        cost_estimate=pl.CostEstimate(flops=0, bytes_accessed=0, transcendentals=0),
+        name="assemble",
+    )(own, other)
+
+
 def halves(value):
     high = value.astype(bf16)
     return high, (value - high.astype(f32)).astype(bf16)
@@ -692,9 +712,9 @@
     resid, half = residual_parts(parts[0], *near, last, obs, kept, directions0)
     half_z = across_z(half)
     directions1 = direction_parts(1, scaling, own, other, *parts[7:])
-    one, two = across(1, half), across(2, half)
-    one_z, two_z = across(1, half_z), across(2, half_z)
-    resids = [half, one, two, across(2, one), half_z, one_z, two_z, across(1, two_z)]
+    resids = [
+        array if rel == 0 else across(rel, array) for array in (half, half_z) for rel in range(4)
+    ]
 
     grads = gradient_parts(0, devices, freq_ratio, *resids[:4], directions0, directions1)
     grads = gradient_parts(1, devices, freq_ratio, *resids[4:], directions0, directions1, grads)
@@ -703,10 +723,7 @@
     grads = lax.all_to_all(grads, ("dir", "freq"), 0, 0, tiled=True)
     updated = updated_rows(grads, screen_kernel, screen)
 
-    first = jnp.where(core == 0, own_rows, other_rows)
-    second = jnp.where(core == 0, other_rows, own_rows)
-    residual = jnp.stack([first, second]).reshape(2, 2, 2, 32, stations)
-    return jnp.transpose(residual, (3, 0, 1, 2, 4)), updated
+    return assemble(own_rows, other_rows, observed), updated
 
 
 def solution(mesh):

time: 77 us -> 75.2 us (0.977)
  waiting for transfers between devices: 18 us -> 16.7 us
  other arithmetic: 1.1 us -> 0 us
    ppermute x2, waiting for transfers between devices: 3.04 us -> 0.01 us  [across_z(): return lax.ppermute(array, 'dir', dir_perm(0, flip_z=True))]
    ppermute x12, waiting for transfers between devices: 2.75 us -> 4.59 us  [across(): return lax.ppermute(array, 'dir', dir_perm(rel))]
    all_to_all x1, waiting for transfers between devices: 11.6 us -> 9.94 us  [body(): grads = lax.all_to_all(grads, ('dir', 'freq'), 0, 0, tiled=True)]
    ppermute x12, starting transfers between devices: 18.4 us -> 19.9 us  [across(): return lax.ppermute(array, 'dir', dir_perm(rel))]
    ppermute x1, waiting for transfers between devices: 0.01 us -> 1.52 us  [body(): other_rows = swap(sent_rows)]
    all_to_all x1, starting transfers between devices: 10.1 us -> 8.83 us  [body(): grads = lax.all_to_all(grads, ('dir', 'freq'), 0, 0, tiled=True)]
    transpose x1 -> x0, other arithmetic: 1.05 us -> none  [body(): return (jnp.transpose(residual, (3, 0, 1, 2, 4)), updated)]
    pallas_call x0 -> x1, Pallas kernels: none -> 0.9 us  [assemble(): pl.pallas_call(assemble_kernel, in_specs=[WHOLE] * 2, out_specs=WHOLE, ou...]
  transfers between devices with their start and end apart: 18 -> 18, of which waited for: 5 -> 5; matrix products, arithmetic and copies ran while one was open for 2% -> 0% of each run, Pallas kernels for 14% -> 17%
where the time goes in v8:
time: 75.2 us; the launch traced here: 75 us
  starting transfers between devices  32.8 us (44%)
  Pallas kernels  24.5 us (33%)
  waiting for transfers between devices  16.7 us (22%)
  between operations  0.97 us (1%)
    ppermute x12, starting transfers between devices, across(): return lax.ppermute(array, 'dir', dir_perm(rel))  19.9 us
    all_to_all x1, waiting for transfers between devices, body(): grads = lax.all_to_all(grads, ('dir', 'freq'), 0, 0, tiled=True)  9.94 us
    all_to_all x1, starting transfers between devices, body(): grads = lax.all_to_all(grads, ('dir', 'freq'), 0, 0, tiled=True)  8.83 us
    pallas_call x2, Pallas kernels, direction_parts(): pl.pallas_call(functools.partial(direction_kernel, moment, scaling), in_s...  6.27 us
    pallas_call x1, Pallas kernels, phasor_send(): pl.pallas_call(phasor_send_kernel, in_specs=[HBM] * 7, out_specs=HBM, out...  4.72 us
    ppermute x12, waiting for transfers between devices, across(): return lax.ppermute(array, 'dir', dir_perm(rel))  4.59 us
    pallas_call x1, Pallas kernels, model_parts(): pl.pallas_call(functools.partial(model_kernel, scaling), in_specs=[WHOLE,...  3.9 us
    ppermute x2, starting transfers between devices, across_z(): return lax.ppermute(array, 'dir', dir_perm(0, flip_z=True))  3.62 us
  transfers between devices with their start and end apart: 18, of which 5 were waited for; matrix products, arithmetic and copies ran while one was open for 0% of the time, Pallas kernels for 17%

profile of v8, /device:TPU:0, one launch (start us, length us, event | category | flops | bytes accessed | tf_op | source)
XLA Modules:
  0.0 75.0 jit_solution(2000592544143872769)
XLA Ops:
  0.7 4.7 %phasor_send.1 = bf16[2,528,768]{2,1,0:T(8,128)(2,1)} custom-call(f32[2]{0:T(128)} %freq.7, bf16[2,2,2,512,384]{4,3,2,1,0:T(8,128)(2,1)} %gain.3, f32[2,2,512]{2,1,0:T(2,128)} %uv.3, f32[2,512]{1,0:T(2,128)} %screen.5, f32[2,384]{1,0:T(2,128)} %lm.3, f32[384]{0:T(512)} %flux.3, s32[384]{0:T(512)} %direction.3), custom_call_target="tpu_custom_call" | custom-call | flops 15728640 | bytes 3200000 | tf_op jit(solution)/shard_map/phasor_send/pallas_call | solution.py:187
  5.6 2.9 %phasor_own.1.own = bf16[2,528,768]{2,1,0:T(8,128)(2,1)S(1)} custom-call(f32[2]{0:T(128)S(1)} %copy-done.9, bf16[2,2,2,512,384]{4,3,2,1,0:T(8,128)(2,1)S(1)} %copy-done, f32[2,2,512]{2,1,0:T(2,128)S(1)} %copy-done.5, f32[2,512]{1,0:T(2,128)S(1)} %copy-done.4, f32[2,384]{1,0:T(2,128)S(1)} %copy-done.6, f32[384]{0:T(512)S(1)} %copy-done.7, s32[384]{0:T(512)S(1)} %copy-done.8), custom_call_target="tpu_custom_call" | custom-call | flops 15728640 | bytes 3200000 | tf_op jit(solution)/shard_map/phasor_own/pallas_call | solution.py:212
  9.2 3.9 %model_parts.1 = (f32[2,2,64,512]{3,2,1,0:T(8,128)S(1)}, bf16[2,64,512]{2,1,0:T(8,128)(2,1)S(1)}, bf16[2,64,512]{2,1,0:T(8,128)(2,1)S(1)}, bf16[2,64,512]{2,1,0:...) custom-call(bf16[2,528,768]{2,1,0:T(8,128)(2,1)S(1)} %phasor_own.1.o, ...), custom_call_target="tpu_custom_call" | custom-call | flops 3221225472 | bytes 5000000 | tf_op jit(solution)/shard_map/model_parts/pallas_call | solution.py:319
  13.5 3.3 %collective-permute-start.4 = (bf16[2,64,512]{2,1,0:T(8,128)(2,1)S(1)}, bf16[2,64,512]{2,1,0:T(8,128)(2,1)S(1)}, u32[]{:S(2)}, u32[]{:S(2)}) collective-permute-start(bf16[2,64,512]{2,1,0:T(8,128)(2,1)S(1)} %get-tuple-element.22), channel_id=1, source_target_pairs={{0,32},{8,40},{16,48},{24,56},{32,0},{40,8},{48,16},{56,24},{64,96... | collective-permute-start | bytes 393224 | tf_op jit(solution)/shard_map/ppermute | solution.py:700
  16.8 1.1 %collective-permute-start.5 = (bf16[2,64,512]{2,1,0:T(8,128)(2,1)S(1)}, bf16[2,64,512]{2,1,0:T(8,128)(2,1)S(1)}, u32[]{:S(2)}, u32[]{:S(2)}) collective-permute-start(bf16[2,64,512]{2,1,0:T(8,128)(2,1)S(1)} %get-tuple-element.23), channel_id=1, source_target_pairs={{0,48},{8,56},{16,32},{24,40},{32,16},{40,24},{48,0},{56,8},{64,11... | collective-permute-start | bytes 393224 | tf_op jit(solution)/shard_map/ppermute | solution.py:700
  17.9 3.6 %collective-permute-start.1 = (bf16[2,64,512]{2,1,0:T(8,128)(2,1)S(1)}, bf16[2,64,512]{2,1,0:T(8,128)(2,1)S(1)}, u32[]{:S(2)}, u32[]{:S(2)}) collective-permute-start(bf16[2,64,512]{2,1,0:T(8,128)(2,1)S(1)} %get-tuple-element.19._), channel_id=1, source_target_pairs={{0,32},{8,40},{16,48},{24,56},{32,0},{40,8},{48,16},{56,24},{64,96... | collective-permute-start | bytes 393224 | tf_op jit(solution)/shard_map/ppermute | solution.py:700
  21.5 2.9 %collective-permute-start.2 = (bf16[2,64,512]{2,1,0:T(8,128)(2,1)S(1)}, bf16[2,64,512]{2,1,0:T(8,128)(2,1)S(1)}, u32[]{:S(2)}, u32[]{:S(2)}) collective-permute-start(bf16[2,64,512]{2,1,0:T(8,128)(2,1)S(1)} %get-tuple-element.20), channel_id=1, source_target_pairs={{0,48},{8,56},{16,32},{24,40},{32,16},{40,24},{48,0},{56,8},{64,11... | collective-permute-start | bytes 393224 | tf_op jit(solution)/shard_map/ppermute | solution.py:700
  24.5 1.4 %collective-permute-start.3 = (bf16[2,64,512]{2,1,0:T(8,128)(2,1)S(1)}, bf16[2,64,512]{2,1,0:T(8,128)(2,1)S(1)}, u32[]{:S(2)}, u32[]{:S(2)}) collective-permute-start(bf16[2,64,512]{2,1,0:T(8,128)(2,1)S(1)} %get-tuple-element.21), channel_id=1, source_target_pairs={{0,16},{8,24},{16,0},{24,8},{32,48},{40,56},{48,32},{56,40},{64,80... | collective-permute-start | bytes 393224 | tf_op jit(solution)/shard_map/ppermute | solution.py:700
  26.0 2.2 %collective-permute-start.7 = (bf16[2,64,512]{2,1,0:T(8,128)(2,1)S(1)}, bf16[2,64,512]{2,1,0:T(8,128)(2,1)S(1)}, u32[]{:S(2)}, u32[]{:S(2)}) collective-permute-start(bf16[2,64,512]{2,1,0:T(8,128)(2,1)S(1)} %send_parts.1), channel_id=1, source_target_pairs={{0,64},{8,72},{16,80},{24,88},{32,96},{40,104},{48,112},{56,120},{... | collective-permute-start | bytes 393224 | tf_op jit(solution)/shard_map/ppermute | solution.py:703
  28.2 3.1 %direction_parts0.1._.refs_4_ = bf16[4,4,2,64,512]{4,3,2,1,0:T(8,128)(2,1)S(1)} custom-call(bf16[2,528,768]{2,1,0:T(8,128)(2,1)S(1)} %phasor_own.1.own, bf16[2,528,768]{2,1,0:T(8,128)(2,1)S(1)} %collective-permute-done.other_hbm.other, f32[2,2,512,768]{3,2,1,0:T(8,128)S(1)} %get-tuple-element.27.totals, f32[2,2,256,512]{3,2,1,0:T(8,128)S(1)} %get-tuple-element.28.tops, ...), custom_call_target="tpu_custom_call" | custom-call | flops 1610612736 | bytes 5000000 | tf_op jit(solution)/shard_map/direction_parts0/pallas_call | solution.py:363
  31.9 1.4 %collective-permute-start.12 = (bf16[2,64,512]{2,1,0:T(8,128)(2,1)S(1)}, bf16[2,64,512]{2,1,0:T(8,128)(2,1)S(1)}, u32[]{:S(2)}, u32[]{:S(2)}) collective-permute-start(bf16[2,64,512]{2,1,0:T(8,128)(2,1)S(1)} %get-tuple-element.31.refs_0_), channel_id=1, source_target_pairs={{0,64},{8,72},{16,80},{24,88},{32,96},{40,104},{48,112},{56,120},{... | collective-permute-start | bytes 393224 | tf_op jit(solution)/shard_map/ppermute | solution.py:703
  33.3 1.7 %collective-permute-start.10 = (bf16[2,64,512]{2,1,0:T(8,128)(2,1)S(1)}, bf16[2,64,512]{2,1,0:T(8,128)(2,1)S(1)}, u32[]{:S(2)}, u32[]{:S(2)}) collective-permute-start(bf16[2,64,512]{2,1,0:T(8,128)(2,1)S(1)} %get-tuple-element.31.refs_0_), channel_id=1, source_target_pairs={{0,48},{8,56},{16,32},{24,40},{32,16},{40,24},{48,0},{56,8},{64,11... | collective-permute-start | bytes 393224 | tf_op jit(solution)/shard_map/ppermute | solution.py:700
  35.0 1.2 %collective-permute-start.11 = (bf16[2,64,512]{2,1,0:T(8,128)(2,1)S(1)}, bf16[2,64,512]{2,1,0:T(8,128)(2,1)S(1)}, u32[]{:S(2)}, u32[]{:S(2)}) collective-permute-start(bf16[2,64,512]{2,1,0:T(8,128)(2,1)S(1)} %get-tuple-element.31.refs_0_), channel_id=1, source_target_pairs={{0,32},{8,40},{16,48},{24,56},{32,0},{40,8},{48,16},{56,24},{64,96... | collective-permute-start | bytes 393224 | tf_op jit(solution)/shard_map/ppermute | solution.py:700
  36.2 1.2 %collective-permute-start.9 = (bf16[2,64,512]{2,1,0:T(8,128)(2,1)S(1)}, bf16[2,64,512]{2,1,0:T(8,128)(2,1)S(1)}, u32[]{:S(2)}, u32[]{:S(2)}) collective-permute-start(bf16[2,64,512]{2,1,0:T(8,128)(2,1)S(1)} %get-tuple-element.31.refs_0_), channel_id=1, source_target_pairs={{0,16},{8,24},{16,0},{24,8},{32,48},{40,56},{48,32},{56,40},{64,80... | collective-permute-start | bytes 393224 | tf_op jit(solution)/shard_map/ppermute | solution.py:700
  38.2 2.6 %collective-permute-start.14 = (bf16[2,64,512]{2,1,0:T(8,128)(2,1)S(1)}, bf16[2,64,512]{2,1,0:T(8,128)(2,1)S(1)}, u32[]{:S(2)}, u32[]{:S(2)}) collective-permute-start(bf16[2,64,512]{2,1,0:T(8,128)(2,1)S(1)} %collective-permute-done.12.refs_0_.refs_4_), channel_id=1, source_target_pairs={{0,48},{8,56},{16,32},{24,40},{32,16},{40,24},{48,0},{56,8},{64,11... | collective-permute-start | bytes 393224 | tf_op jit(solution)/shard_map/ppermute | solution.py:700
  40.9 2.5 %collective-permute-done.10.refs_2_ = bf16[2,64,512]{2,1,0:T(8,128)(2,1)S(1)} collective-permute-done((bf16[2,64,512]{2,1,0:T(8,128)(2,1)S(1)}, bf16[2,64,512]{2,1,0:T(8,128)(2,1)S(1)}, u32[]{:S(2)}, u32[]{:S(2)}) %collective-permute-start.10) | collective-permute-done | bytes 131104 | tf_op jit(solution)/shard_map/ppermute | solution.py:700
  43.3 3.1 %direction_parts1.1.refs_5_ = bf16[4,4,2,64,512]{4,3,2,1,0:T(8,128)(2,1)S(1)} custom-call(bf16[2,528,768]{2,1,0:T(8,128)(2,1)S(1)} %phasor_own.1.own, bf16[2,528,768]{2,1,0:T(8,128)(2,1)S(1)} %collective-permute-done.other_hbm.other, f32[2,2,512,768]{3,2,1,0:T(8,128)S(1)} %get-tuple-element.27.totals, f32[2,2,256,512]{3,2,1,0:T(8,128)S(1)} %get-tuple-element.28.tops, ...), custom_call_target="tpu_custom_call" | custom-call | flops 1610612736 | bytes 5000000 | tf_op jit(solution)/shard_map/direction_parts1/pallas_call | solution.py:363
  46.5 1.2 %gradient_parts0.1.refs_6_ = f32[16,128]{1,0:T(8,128)S(1)} custom-call(f32[2]{0:T(128)S(1)} %copy-done.9, bf16[2,64,512]{2,1,0:T(8,128)(2,1)S(1)} %get-tuple-element.31.refs_0_, bf16[2,64,512]{2,1,0:T(8,128)(2,1)S(1)} %collective-permute-done.9.refs_1_, bf16[2,64,512]{2,1,0:T(8,128)(2,1)S(1)} %collective-permute-done.10.refs_2_, ...), custom_call_target="tpu_custom_call" | custom-call | flops 5000000 | bytes 3000000 | tf_op jit(solution)/shard_map/gradient_parts0/pallas_call | solution.py:550
  47.7 2.1 %collective-permute-done.15.refs_3_.refs_7_ = bf16[2,64,512]{2,1,0:T(8,128)(2,1)S(1)} collective-permute-done((bf16[2,64,512]{2,1,0:T(8,128)(2,1)S(1)}, bf16[2,64,512]{2,1,0:T(8,128)(2,1)S(1)}, u32[]{:S(2)}, u32[]{:S(2)}) %collective-permute-start.15) | collective-permute-done | bytes 131104 | tf_op jit(solution)/shard_map/ppermute | solution.py:700
  49.8 2.1 %gradient_parts1.1.refs_8_ = bf16[128,16,128]{2,1,0:T(8,128)(2,1)} custom-call(f32[2]{0:T(128)S(1)} %copy-done.9, bf16[2,64,512]{2,1,0:T(8,128)(2,1)S(1)} %collective-permute-done.12.refs_0_.refs_4_, bf16[2,64,512]{2,1,0:T(8,128)(2,1)S(1)} %collective-permute-done.13.refs_1_.refs_5_, bf16[2,64,512]{2,1,0:T(8,128)(2,1)S(1)} %collective-permute-done.14.refs_2_.refs_6_, ...), custom_call_target="tpu_custom_call" | custom-call | flops 5000000 | bytes 3000000 | tf_op jit(solution)/shard_map/gradient_parts1/pallas_call | solution.py:550
  51.9 8.8 %all-to-all-start = ((bf16[128,16,128]{2,1,0:T(8,128)(2,1)}), bf16[128,16,128]{2,1,0:T(8,128)(2,1)S(1)}, u32[]{:S(2)}, u32[]{:S(2)}) async-start(bf16[128,16,128]{2,1,0:T(8,128)(2,1)} %gradient_parts1.1.refs_8_), calls=%async_computation | async-start | bytes 1048576 | tf_op jit(solution)/shard_map/all_to_all | solution.py:723
  61.5 1.5 %collective-permute-done.16.other = f32[4,32,512]{2,1,0:T(8,128)S(1)} collective-permute-done((f32[4,32,512]{2,1,0:T(8,128)S(1)}, f32[4,32,512]{2,1,0:T(8,128)S(1)}, u32[]{:S(2)}, u32[]{:S(2)}) %collective-permute-start.16) | collective-permute-done | bytes 262176 | tf_op jit(solution)/shard_map/ppermute | solution.py:722
  63.9 9.9 %all-to-all-done.grads = bf16[128,16,128]{2,1,0:T(8,128)(2,1)S(1)} async-done(((bf16[128,16,128]{2,1,0:T(8,128)(2,1)}), bf16[128,16,128]{2,1,0:T(8,128)(2,1)S(1)}, u32[]{:S(2)}, u32[]{:S(2)}) %all-to-all-start) | async-done | bytes 524320 | tf_op jit(solution)/shard_map/all_to_all | solution.py:723
  73.9 1.1 %updated_rows.1 = f32[2,512]{1,0:T(2,128)} custom-call(bf16[128,16,128]{2,1,0:T(8,128)(2,1)S(1)} %all-to-all-done.grads, f32[512,512]{1,0:T(8,128)S(1)} %copy-done.2, f32[2,512]{1,0:T(2,128)S(1)} %copy-done.4), custom_call_target="tpu_custom_call" | custom-call | flops 200000000 | bytes 1500000 | tf_op jit(solution)/shard_map/updated_rows/pallas_call | solution.py:665
  (46 shorter events, 4.2 us)
Async XLA Ops:
  0.6 4.9 %copy-start.4 = (f32[2,512]{1,0:T(2,128)S(1)}, f32[2,512]{1,0:T(2,128)}, u32[]{:S(2)}) copy-start(f32[2,512]{1,0:T(2,128)} %screen.5) | copy-start | bytes 12292
  0.6 4.9 %copy-start.5 = (f32[2,2,512]{2,1,0:T(2,128)S(1)}, f32[2,2,512]{2,1,0:T(2,128)}, u32[]{:S(2)}) copy-start(f32[2,2,512]{2,1,0:T(2,128)} %uv.3) | copy-start | bytes 24580
  0.7 4.9 %copy-start.6 = (f32[2,384]{1,0:T(2,128)S(1)}, f32[2,384]{1,0:T(2,128)}, u32[]{:S(2)}) copy-start(f32[2,384]{1,0:T(2,128)} %lm.3) | copy-start | bytes 9220
  0.7 4.9 %copy-start.7 = (f32[384]{0:T(512)S(1)}, f32[384]{0:T(512)}, u32[]{:S(2)}) copy-start(f32[384]{0:T(512)} %flux.3) | copy-start | bytes 4612
  0.7 4.9 %copy-start = (bf16[2,2,2,512,384]{4,3,2,1,0:T(8,128)(2,1)S(1)}, bf16[2,2,2,512,384]{4,3,2,1,0:T(8,128)(2,1)}, u32[]{:S(2)}) copy-start(bf16[2,2,2,512,384]{4,3,2,1,0:T(8,128)(2,1)} %gain.3) | copy-start | bytes 9437188
  5.4 3.8 %collective-permute-start = (bf16[2,528,768]{2,1,0:T(8,128)(2,1)}, bf16[2,528,768]{2,1,0:T(8,128)(2,1)S(1)}, u32[]{:S(2)}, u32[]{:S(2)}) collective-permute-start(bf16[2,528,768]{2,1,0:T(8,128)(2,1)} %phasor_send.1), channel_id=1, source_target_pairs={{0,8},{8,0},{16,24},{24,16},{32,40},{40,32},{48,56},{56,48},{64,72... | collective-permute-start | bytes 4866056 | tf_op jit(solution)/shard_map/ppermute | solution.py:696
  13.3 18.0 %collective-permute-start.8 = (f32[32,2,4,512]{3,2,1,0:T(4,128)S(1)}, f32[32,2,4,512]{3,2,1,0:T(4,128)S(1)}, u32[]{:S(2)}, u32[]{:S(2)}) collective-permute-start(f32[32,2,4,512]{3,2,1,0:T(4,128)S(1)} %observed_send.1), channel_id=1, source_target_pairs={{0,8},{8,0},{16,24},{24,16},{32,40},{40,32},{48,56},{56,48},{64,72... | collective-permute-start | bytes 1572872 | tf_op jit(solution)/shard_map/ppermute | solution.py:708
  13.5 8.0 %collective-permute-start.4 = (bf16[2,64,512]{2,1,0:T(8,128)(2,1)S(1)}, bf16[2,64,512]{2,1,0:T(8,128)(2,1)S(1)}, u32[]{:S(2)}, u32[]{:S(2)}) collective-permute-start(bf16[2,64,512]{2,1,0:T(8,128)(2,1)S(1)} %get-tuple-element.22), channel_id=1, source_target_pairs={{0,32},{8,40},{16,48},{24,56},{32,0},{40,8},{48,16},{56,24},{64,96... | collective-permute-start | bytes 393224 | tf_op jit(solution)/shard_map/ppermute | solution.py:700
  16.8 7.7 %collective-permute-start.5 = (bf16[2,64,512]{2,1,0:T(8,128)(2,1)S(1)}, bf16[2,64,512]{2,1,0:T(8,128)(2,1)S(1)}, u32[]{:S(2)}, u32[]{:S(2)}) collective-permute-start(bf16[2,64,512]{2,1,0:T(8,128)(2,1)S(1)} %get-tuple-element.23), channel_id=1, source_target_pairs={{0,48},{8,56},{16,32},{24,40},{32,16},{40,24},{48,0},{56,8},{64,11... | collective-permute-start | bytes 393224 | tf_op jit(solution)/shard_map/ppermute | solution.py:700
  17.9 8.0 %collective-permute-start.6 = (bf16[2,64,512]{2,1,0:T(8,128)(2,1)S(1)}, bf16[2,64,512]{2,1,0:T(8,128)(2,1)S(1)}, u32[]{:S(2)}, u32[]{:S(2)}) collective-permute-start(bf16[2,64,512]{2,1,0:T(8,128)(2,1)S(1)} %get-tuple-element.24), channel_id=1, source_target_pairs={{0,16},{8,24},{16,0},{24,8},{32,48},{40,56},{48,32},{56,40},{64,80... | collective-permute-start | bytes 393224 | tf_op jit(solution)/shard_map/ppermute | solution.py:700
  17.9 13.8 %collective-permute-start.1 = (bf16[2,64,512]{2,1,0:T(8,128)(2,1)S(1)}, bf16[2,64,512]{2,1,0:T(8,128)(2,1)S(1)}, u32[]{:S(2)}, u32[]{:S(2)}) collective-permute-start(bf16[2,64,512]{2,1,0:T(8,128)(2,1)S(1)} %get-tuple-element.19._), channel_id=1, source_target_pairs={{0,32},{8,40},{16,48},{24,56},{32,0},{40,8},{48,16},{56,24},{64,96... | collective-permute-start | bytes 393224 | tf_op jit(solution)/shard_map/ppermute | solution.py:700
  21.5 10.2 %collective-permute-start.2 = (bf16[2,64,512]{2,1,0:T(8,128)(2,1)S(1)}, bf16[2,64,512]{2,1,0:T(8,128)(2,1)S(1)}, u32[]{:S(2)}, u32[]{:S(2)}) collective-permute-start(bf16[2,64,512]{2,1,0:T(8,128)(2,1)S(1)} %get-tuple-element.20), channel_id=1, source_target_pairs={{0,48},{8,56},{16,32},{24,40},{32,16},{40,24},{48,0},{56,8},{64,11... | collective-permute-start | bytes 393224 | tf_op jit(solution)/shard_map/ppermute | solution.py:700
  24.5 7.3 %collective-permute-start.3 = (bf16[2,64,512]{2,1,0:T(8,128)(2,1)S(1)}, bf16[2,64,512]{2,1,0:T(8,128)(2,1)S(1)}, u32[]{:S(2)}, u32[]{:S(2)}) collective-permute-start(bf16[2,64,512]{2,1,0:T(8,128)(2,1)S(1)} %get-tuple-element.21), channel_id=1, source_target_pairs={{0,16},{8,24},{16,0},{24,8},{32,48},{40,56},{48,32},{56,40},{64,80... | collective-permute-start | bytes 393224 | tf_op jit(solution)/shard_map/ppermute | solution.py:700
  26.0 5.8 %collective-permute-start.7 = (bf16[2,64,512]{2,1,0:T(8,128)(2,1)S(1)}, bf16[2,64,512]{2,1,0:T(8,128)(2,1)S(1)}, u32[]{:S(2)}, u32[]{:S(2)}) collective-permute-start(bf16[2,64,512]{2,1,0:T(8,128)(2,1)S(1)} %send_parts.1), channel_id=1, source_target_pairs={{0,64},{8,72},{16,80},{24,88},{32,96},{40,104},{48,112},{56,120},{... | collective-permute-start | bytes 393224 | tf_op jit(solution)/shard_map/ppermute | solution.py:703
  31.9 5.5 %collective-permute-start.12 = (bf16[2,64,512]{2,1,0:T(8,128)(2,1)S(1)}, bf16[2,64,512]{2,1,0:T(8,128)(2,1)S(1)}, u32[]{:S(2)}, u32[]{:S(2)}) collective-permute-start(bf16[2,64,512]{2,1,0:T(8,128)(2,1)S(1)} %get-tuple-element.31.refs_0_), channel_id=1, source_target_pairs={{0,64},{8,72},{16,80},{24,88},{32,96},{40,104},{48,112},{56,120},{... | collective-permute-start | bytes 393224 | tf_op jit(solution)/shard_map/ppermute | solution.py:703
  33.3 10.0 %collective-permute-start.10 = (bf16[2,64,512]{2,1,0:T(8,128)(2,1)S(1)}, bf16[2,64,512]{2,1,0:T(8,128)(2,1)S(1)}, u32[]{:S(2)}, u32[]{:S(2)}) collective-permute-start(bf16[2,64,512]{2,1,0:T(8,128)(2,1)S(1)} %get-tuple-element.31.refs_0_), channel_id=1, source_target_pairs={{0,48},{8,56},{16,32},{24,40},{32,16},{40,24},{48,0},{56,8},{64,11... | collective-permute-start | bytes 393224 | tf_op jit(solution)/shard_map/ppermute | solution.py:700
  35.0 11.5 %collective-permute-start.11 = (bf16[2,64,512]{2,1,0:T(8,128)(2,1)S(1)}, bf16[2,64,512]{2,1,0:T(8,128)(2,1)S(1)}, u32[]{:S(2)}, u32[]{:S(2)}) collective-permute-start(bf16[2,64,512]{2,1,0:T(8,128)(2,1)S(1)} %get-tuple-element.31.refs_0_), channel_id=1, source_target_pairs={{0,32},{8,40},{16,48},{24,56},{32,0},{40,8},{48,16},{56,24},{64,96... | collective-permute-start | bytes 393224 | tf_op jit(solution)/shard_map/ppermute | solution.py:700
  36.2 10.3 %collective-permute-start.9 = (bf16[2,64,512]{2,1,0:T(8,128)(2,1)S(1)}, bf16[2,64,512]{2,1,0:T(8,128)(2,1)S(1)}, u32[]{:S(2)}, u32[]{:S(2)}) collective-permute-start(bf16[2,64,512]{2,1,0:T(8,128)(2,1)S(1)} %get-tuple-element.31.refs_0_), channel_id=1, source_target_pairs={{0,16},{8,24},{16,0},{24,8},{32,48},{40,56},{48,32},{56,40},{64,80... | collective-permute-start | bytes 393224 | tf_op jit(solution)/shard_map/ppermute | solution.py:700
  37.4 10.3 %collective-permute-start.13 = (bf16[2,64,512]{2,1,0:T(8,128)(2,1)S(1)}, bf16[2,64,512]{2,1,0:T(8,128)(2,1)S(1)}, u32[]{:S(2)}, u32[]{:S(2)}) collective-permute-start(bf16[2,64,512]{2,1,0:T(8,128)(2,1)S(1)} %collective-permute-done.12.refs_0_.refs_4_), channel_id=1, source_target_pairs={{0,16},{8,24},{16,0},{24,8},{32,48},{40,56},{48,32},{56,40},{64,80... | collective-permute-start | bytes 393224 | tf_op jit(solution)/shard_map/ppermute | solution.py:700
  38.2 9.5 %collective-permute-start.14 = (bf16[2,64,512]{2,1,0:T(8,128)(2,1)S(1)}, bf16[2,64,512]{2,1,0:T(8,128)(2,1)S(1)}, u32[]{:S(2)}, u32[]{:S(2)}) collective-permute-start(bf16[2,64,512]{2,1,0:T(8,128)(2,1)S(1)} %collective-permute-done.12.refs_0_.refs_4_), channel_id=1, source_target_pairs={{0,48},{8,56},{16,32},{24,40},{32,16},{40,24},{48,0},{56,8},{64,11... | collective-permute-start | bytes 393224 | tf_op jit(solution)/shard_map/ppermute | solution.py:700
  43.3 6.5 %collective-permute-start.15 = (bf16[2,64,512]{2,1,0:T(8,128)(2,1)S(1)}, bf16[2,64,512]{2,1,0:T(8,128)(2,1)S(1)}, u32[]{:S(2)}, u32[]{:S(2)}) collective-permute-start(bf16[2,64,512]{2,1,0:T(8,128)(2,1)S(1)} %collective-permute-done.12.refs_0_.refs_4_), channel_id=1, source_target_pairs={{0,32},{8,40},{16,48},{24,56},{32,0},{40,8},{48,16},{56,24},{64,96... | collective-permute-start | bytes 393224 | tf_op jit(solution)/shard_map/ppermute | solution.py:700
  51.9 22.0 %copy-start.2 = (f32[512,512]{1,0:T(8,128)S(1)}, f32[512,512]{1,0:T(8,128)}, u32[]{:S(2)}) copy-start(f32[512,512]{1,0:T(8,128)} %kernel.1) | copy-start | bytes 3145732
  51.9 22.0 %all-to-all-start = ((bf16[128,16,128]{2,1,0:T(8,128)(2,1)}), bf16[128,16,128]{2,1,0:T(8,128)(2,1)S(1)}, u32[]{:S(2)}, u32[]{:S(2)}) async-start(bf16[128,16,128]{2,1,0:T(8,128)(2,1)} %gradient_parts1.1.refs_8_), calls=%async_computation | async-start | bytes 1048576 | tf_op jit(solution)/shard_map/all_to_all | solution.py:723
  61.4 1.6 %collective-permute-start.16 = (f32[4,32,512]{2,1,0:T(8,128)S(1)}, f32[4,32,512]{2,1,0:T(8,128)S(1)}, u32[]{:S(2)}, u32[]{:S(2)}) collective-permute-start(f32[4,32,512]{2,1,0:T(8,128)S(1)} %get-tuple-element.33), channel_id=1, source_target_pairs={{0,8},{8,0},{16,24},{24,16},{32,40},{40,32},{48,56},{56,48},{64,72... | collective-permute-start | bytes 786440 | tf_op jit(solution)/shard_map/ppermute | solution.py:722
  (4 other events, 19.0 us)

commit v9 on v8

--- a/solution.py
+++ b/solution.py
@@ -712,9 +712,9 @@
     resid, half = residual_parts(parts[0], *near, last, obs, kept, directions0)
     half_z = across_z(half)
     directions1 = direction_parts(1, scaling, own, other, *parts[7:])
-    resids = [
-        array if rel == 0 else across(rel, array) for array in (half, half_z) for rel in range(4)
-    ]
+    one, two = across(1, half), across(2, half)
+    resids = [half, one, two, across(2, one)]
+    resids += [half_z, across(1, half_z), across(2, half_z), across(3, half_z)]
 
     grads = gradient_parts(0, devices, freq_ratio, *resids[:4], directions0, directions1)
     grads = gradient_parts(1, devices, freq_ratio, *resids[4:], directions0, directions1, grads)

time: 75.2 us -> 76.6 us (1.019)
  starting transfers between devices: 32.8 us -> 35.1 us
  waiting for transfers between devices: 16.7 us -> 15.8 us
    ppermute x12, starting transfers between devices: 19.9 us -> 21.4 us  [across(): return lax.ppermute(array, 'dir', dir_perm(rel))]
    ppermute x12, waiting for transfers between devices: 4.59 us -> 3.5 us  [across(): return lax.ppermute(array, 'dir', dir_perm(rel))]
    all_to_all x1, starting transfers between devices: 8.83 us -> 9.71 us  [body(): grads = lax.all_to_all(grads, ('dir', 'freq'), 0, 0, tiled=True)]
  transfers between devices with their start and end apart: 18 -> 18, of which waited for: 5 -> 5; matrix products, arithmetic and copies ran while one was open for 0% -> 0% of each run, Pallas kernels for 17% -> 16%
where the time goes in v9:
time: 76.6 us; the launch traced here: 76.4 us
  starting transfers between devices  35.1 us (46%)
  Pallas kernels  24.5 us (32%)
  waiting for transfers between devices  15.8 us (21%)
  between operations  0.97 us (1%)
    ppermute x12, starting transfers between devices, across(): return lax.ppermute(array, 'dir', dir_perm(rel))  21.4 us
    all_to_all x1, waiting for transfers between devices, body(): grads = lax.all_to_all(grads, ('dir', 'freq'), 0, 0, tiled=True)  9.94 us
    all_to_all x1, starting transfers between devices, body(): grads = lax.all_to_all(grads, ('dir', 'freq'), 0, 0, tiled=True)  9.71 us
    pallas_call x2, Pallas kernels, direction_parts(): pl.pallas_call(functools.partial(direction_kernel, moment, scaling), in_s...  6.27 us
    pallas_call x1, Pallas kernels, phasor_send(): pl.pallas_call(phasor_send_kernel, in_specs=[HBM] * 7, out_specs=HBM, out...  4.72 us
    pallas_call x1, Pallas kernels, model_parts(): pl.pallas_call(functools.partial(model_kernel, scaling), in_specs=[WHOLE,...  3.9 us
    ppermute x2, starting transfers between devices, across_z(): return lax.ppermute(array, 'dir', dir_perm(0, flip_z=True))  3.62 us
    ppermute x12, waiting for transfers between devices, across(): return lax.ppermute(array, 'dir', dir_perm(rel))  3.5 us
  transfers between devices with their start and end apart: 18, of which 5 were waited for; matrix products, arithmetic and copies ran while one was open for 0% of the time, Pallas kernels for 16%

profile of v9, /device:TPU:0, one launch (start us, length us, event | category | flops | bytes accessed | tf_op | source)
XLA Modules:
  0.0 76.4 jit_solution(7103708262082077610)
XLA Ops:
  0.7 4.7 %phasor_send.1 = bf16[2,528,768]{2,1,0:T(8,128)(2,1)} custom-call(f32[2]{0:T(128)} %freq.7, bf16[2,2,2,512,384]{4,3,2,1,0:T(8,128)(2,1)} %gain.3, f32[2,2,512]{2,1,0:T(2,128)} %uv.3, f32[2,512]{1,0:T(2,128)} %screen.5, f32[2,384]{1,0:T(2,128)} %lm.3, f32[384]{0:T(512)} %flux.3, s32[384]{0:T(512)} %direction.3), custom_call_target="tpu_custom_call" | custom-call | flops 15728640 | bytes 3200000 | tf_op jit(solution)/shard_map/phasor_send/pallas_call | solution.py:187
  5.6 2.9 %phasor_own.1.own = bf16[2,528,768]{2,1,0:T(8,128)(2,1)S(1)} custom-call(f32[2]{0:T(128)S(1)} %copy-done.9, bf16[2,2,2,512,384]{4,3,2,1,0:T(8,128)(2,1)S(1)} %copy-done, f32[2,2,512]{2,1,0:T(2,128)S(1)} %copy-done.5, f32[2,512]{1,0:T(2,128)S(1)} %copy-done.4, f32[2,384]{1,0:T(2,128)S(1)} %copy-done.6, f32[384]{0:T(512)S(1)} %copy-done.7, s32[384]{0:T(512)S(1)} %copy-done.8), custom_call_target="tpu_custom_call" | custom-call | flops 15728640 | bytes 3200000 | tf_op jit(solution)/shard_map/phasor_own/pallas_call | solution.py:212
  9.2 3.9 %model_parts.1 = (f32[2,2,64,512]{3,2,1,0:T(8,128)S(1)}, bf16[2,64,512]{2,1,0:T(8,128)(2,1)S(1)}, bf16[2,64,512]{2,1,0:T(8,128)(2,1)S(1)}, bf16[2,64,512]{2,1,0:...) custom-call(bf16[2,528,768]{2,1,0:T(8,128)(2,1)S(1)} %phasor_own.1.o, ...), custom_call_target="tpu_custom_call" | custom-call | flops 3221225472 | bytes 5000000 | tf_op jit(solution)/shard_map/model_parts/pallas_call | solution.py:319
  13.5 3.3 %collective-permute-start.4 = (bf16[2,64,512]{2,1,0:T(8,128)(2,1)S(1)}, bf16[2,64,512]{2,1,0:T(8,128)(2,1)S(1)}, u32[]{:S(2)}, u32[]{:S(2)}) collective-permute-start(bf16[2,64,512]{2,1,0:T(8,128)(2,1)S(1)} %get-tuple-element.22), channel_id=1, source_target_pairs={{0,32},{8,40},{16,48},{24,56},{32,0},{40,8},{48,16},{56,24},{64,96... | collective-permute-start | bytes 393224 | tf_op jit(solution)/shard_map/ppermute | solution.py:700
  16.8 1.1 %collective-permute-start.5 = (bf16[2,64,512]{2,1,0:T(8,128)(2,1)S(1)}, bf16[2,64,512]{2,1,0:T(8,128)(2,1)S(1)}, u32[]{:S(2)}, u32[]{:S(2)}) collective-permute-start(bf16[2,64,512]{2,1,0:T(8,128)(2,1)S(1)} %get-tuple-element.23), channel_id=1, source_target_pairs={{0,48},{8,56},{16,32},{24,40},{32,16},{40,24},{48,0},{56,8},{64,11... | collective-permute-start | bytes 393224 | tf_op jit(solution)/shard_map/ppermute | solution.py:700
  17.9 3.6 %collective-permute-start.1 = (bf16[2,64,512]{2,1,0:T(8,128)(2,1)S(1)}, bf16[2,64,512]{2,1,0:T(8,128)(2,1)S(1)}, u32[]{:S(2)}, u32[]{:S(2)}) collective-permute-start(bf16[2,64,512]{2,1,0:T(8,128)(2,1)S(1)} %get-tuple-element.19._), channel_id=1, source_target_pairs={{0,32},{8,40},{16,48},{24,56},{32,0},{40,8},{48,16},{56,24},{64,96... | collective-permute-start | bytes 393224 | tf_op jit(solution)/shard_map/ppermute | solution.py:700
  21.5 2.9 %collective-permute-start.2 = (bf16[2,64,512]{2,1,0:T(8,128)(2,1)S(1)}, bf16[2,64,512]{2,1,0:T(8,128)(2,1)S(1)}, u32[]{:S(2)}, u32[]{:S(2)}) collective-permute-start(bf16[2,64,512]{2,1,0:T(8,128)(2,1)S(1)} %get-tuple-element.20), channel_id=1, source_target_pairs={{0,48},{8,56},{16,32},{24,40},{32,16},{40,24},{48,0},{56,8},{64,11... | collective-permute-start | bytes 393224 | tf_op jit(solution)/shard_map/ppermute | solution.py:700
  24.5 1.4 %collective-permute-start.3 = (bf16[2,64,512]{2,1,0:T(8,128)(2,1)S(1)}, bf16[2,64,512]{2,1,0:T(8,128)(2,1)S(1)}, u32[]{:S(2)}, u32[]{:S(2)}) collective-permute-start(bf16[2,64,512]{2,1,0:T(8,128)(2,1)S(1)} %get-tuple-element.21), channel_id=1, source_target_pairs={{0,16},{8,24},{16,0},{24,8},{32,48},{40,56},{48,32},{56,40},{64,80... | collective-permute-start | bytes 393224 | tf_op jit(solution)/shard_map/ppermute | solution.py:700
  26.0 2.2 %collective-permute-start.7 = (bf16[2,64,512]{2,1,0:T(8,128)(2,1)S(1)}, bf16[2,64,512]{2,1,0:T(8,128)(2,1)S(1)}, u32[]{:S(2)}, u32[]{:S(2)}) collective-permute-start(bf16[2,64,512]{2,1,0:T(8,128)(2,1)S(1)} %send_parts.1), channel_id=1, source_target_pairs={{0,64},{8,72},{16,80},{24,88},{32,96},{40,104},{48,112},{56,120},{... | collective-permute-start | bytes 393224 | tf_op jit(solution)/shard_map/ppermute | solution.py:703
  28.2 3.1 %direction_parts0.1._.refs_4_ = bf16[4,4,2,64,512]{4,3,2,1,0:T(8,128)(2,1)S(1)} custom-call(bf16[2,528,768]{2,1,0:T(8,128)(2,1)S(1)} %phasor_own.1.own, bf16[2,528,768]{2,1,0:T(8,128)(2,1)S(1)} %collective-permute-done.other_hbm.other, f32[2,2,512,768]{3,2,1,0:T(8,128)S(1)} %get-tuple-element.27.totals, f32[2,2,256,512]{3,2,1,0:T(8,128)S(1)} %get-tuple-element.28.tops, ...), custom_call_target="tpu_custom_call" | custom-call | flops 1610612736 | bytes 5000000 | tf_op jit(solution)/shard_map/direction_parts0/pallas_call | solution.py:363
  31.9 1.4 %collective-permute-start.12 = (bf16[2,64,512]{2,1,0:T(8,128)(2,1)S(1)}, bf16[2,64,512]{2,1,0:T(8,128)(2,1)S(1)}, u32[]{:S(2)}, u32[]{:S(2)}) collective-permute-start(bf16[2,64,512]{2,1,0:T(8,128)(2,1)S(1)} %get-tuple-element.31.refs_0_), channel_id=1, source_target_pairs={{0,64},{8,72},{16,80},{24,88},{32,96},{40,104},{48,112},{56,120},{... | collective-permute-start | bytes 393224 | tf_op jit(solution)/shard_map/ppermute | solution.py:703
  33.9 2.9 %collective-permute-start.10 = (bf16[2,64,512]{2,1,0:T(8,128)(2,1)S(1)}, bf16[2,64,512]{2,1,0:T(8,128)(2,1)S(1)}, u32[]{:S(2)}, u32[]{:S(2)}) collective-permute-start(bf16[2,64,512]{2,1,0:T(8,128)(2,1)S(1)} %get-tuple-element.31.refs_0_), channel_id=1, source_target_pairs={{0,48},{8,56},{16,32},{24,40},{32,16},{40,24},{48,0},{56,8},{64,11... | collective-permute-start | bytes 393224 | tf_op jit(solution)/shard_map/ppermute | solution.py:700
  37.5 2.8 %collective-permute-start.14 = (bf16[2,64,512]{2,1,0:T(8,128)(2,1)S(1)}, bf16[2,64,512]{2,1,0:T(8,128)(2,1)S(1)}, u32[]{:S(2)}, u32[]{:S(2)}) collective-permute-start(bf16[2,64,512]{2,1,0:T(8,128)(2,1)S(1)} %collective-permute-done.12.refs_0_.refs_4_), channel_id=1, source_target_pairs={{0,48},{8,56},{16,32},{24,40},{32,16},{40,24},{48,0},{56,8},{64,11... | collective-permute-start | bytes 393224 | tf_op jit(solution)/shard_map/ppermute | solution.py:700
  40.3 0.7 collective-permute-start.15
  41.0 1.4 %collective-permute-start.11 = (bf16[2,64,512]{2,1,0:T(8,128)(2,1)S(1)}, bf16[2,64,512]{2,1,0:T(8,128)(2,1)S(1)}, u32[]{:S(2)}, u32[]{:S(2)}) collective-permute-start(bf16[2,64,512]{2,1,0:T(8,128)(2,1)S(1)} %collective-permute-done.9.refs_1_), channel_id=1, source_target_pairs={{0,48},{8,56},{16,32},{24,40},{32,16},{40,24},{48,0},{56,8},{64,11... | collective-permute-start | bytes 393224 | tf_op jit(solution)/shard_map/ppermute | solution.py:700
  42.4 3.1 %direction_parts1.1.refs_5_ = bf16[4,4,2,64,512]{4,3,2,1,0:T(8,128)(2,1)S(1)} custom-call(bf16[2,528,768]{2,1,0:T(8,128)(2,1)S(1)} %phasor_own.1.own, bf16[2,528,768]{2,1,0:T(8,128)(2,1)S(1)} %collective-permute-done.other_hbm.other, f32[2,2,512,768]{3,2,1,0:T(8,128)S(1)} %get-tuple-element.27.totals, f32[2,2,256,512]{3,2,1,0:T(8,128)S(1)} %get-tuple-element.28.tops, ...), custom_call_target="tpu_custom_call" | custom-call | flops 1610612736 | bytes 5000000 | tf_op jit(solution)/shard_map/direction_parts1/pallas_call | solution.py:363
  45.6 3.5 %collective-permute-done.11.refs_3_ = bf16[2,64,512]{2,1,0:T(8,128)(2,1)S(1)} collective-permute-done((bf16[2,64,512]{2,1,0:T(8,128)(2,1)S(1)}, bf16[2,64,512]{2,1,0:T(8,128)(2,1)S(1)}, u32[]{:S(2)}, u32[]{:S(2)}) %collective-permute-start.11) | collective-permute-done | bytes 131104 | tf_op jit(solution)/shard_map/ppermute | solution.py:700
  49.1 1.2 %gradient_parts0.1.refs_6_ = f32[16,128]{1,0:T(8,128)S(1)} custom-call(f32[2]{0:T(128)S(1)} %copy-done.9, bf16[2,64,512]{2,1,0:T(8,128)(2,1)S(1)} %get-tuple-element.31.refs_0_, bf16[2,64,512]{2,1,0:T(8,128)(2,1)S(1)} %collective-permute-done.9.refs_1_, bf16[2,64,512]{2,1,0:T(8,128)(2,1)S(1)} %collective-permute-done.10.refs_2_, ...), custom_call_target="tpu_custom_call" | custom-call | flops 5000000 | bytes 3000000 | tf_op jit(solution)/shard_map/gradient_parts0/pallas_call | solution.py:550
  50.3 2.1 %gradient_parts1.1.refs_8_ = bf16[128,16,128]{2,1,0:T(8,128)(2,1)} custom-call(f32[2]{0:T(128)S(1)} %copy-done.9, bf16[2,64,512]{2,1,0:T(8,128)(2,1)S(1)} %collective-permute-done.12.refs_0_.refs_4_, bf16[2,64,512]{2,1,0:T(8,128)(2,1)S(1)} %collective-permute-done.13.refs_1_.refs_5_, bf16[2,64,512]{2,1,0:T(8,128)(2,1)S(1)} %collective-permute-done.14.refs_2_.refs_6_, ...), custom_call_target="tpu_custom_call" | custom-call | flops 5000000 | bytes 3000000 | tf_op jit(solution)/shard_map/gradient_parts1/pallas_call | solution.py:550
  52.4 9.7 %all-to-all-start = ((bf16[128,16,128]{2,1,0:T(8,128)(2,1)}), bf16[128,16,128]{2,1,0:T(8,128)(2,1)S(1)}, u32[]{:S(2)}, u32[]{:S(2)}) async-start(bf16[128,16,128]{2,1,0:T(8,128)(2,1)} %gradient_parts1.1.refs_8_), calls=%async_computation | async-start | bytes 1048576 | tf_op jit(solution)/shard_map/all_to_all | solution.py:723
  62.9 1.5 %collective-permute-done.16.other = f32[4,32,512]{2,1,0:T(8,128)S(1)} collective-permute-done((f32[4,32,512]{2,1,0:T(8,128)S(1)}, f32[4,32,512]{2,1,0:T(8,128)S(1)}, u32[]{:S(2)}, u32[]{:S(2)}) %collective-permute-start.16) | collective-permute-done | bytes 262176 | tf_op jit(solution)/shard_map/ppermute | solution.py:722
  64.4 0.9 %assemble.1 = f32[32,2,2,2,512]{4,3,2,1,0:T(2,128)} custom-call(f32[4,32,512]{2,1,0:T(8,128)S(1)} %get-tuple-element.32.own, f32[4,32,512]{2,1,0:T(8,128)S(1)} %collective-permute-done.16.other), custom_call_target="tpu_custom_call" | custom-call | tf_op jit(solution)/shard_map/assemble/pallas_call | solution.py:623
  65.3 9.9 %all-to-all-done.grads = bf16[128,16,128]{2,1,0:T(8,128)(2,1)S(1)} async-done(((bf16[128,16,128]{2,1,0:T(8,128)(2,1)}), bf16[128,16,128]{2,1,0:T(8,128)(2,1)S(1)}, u32[]{:S(2)}, u32[]{:S(2)}) %all-to-all-start) | async-done | bytes 524320 | tf_op jit(solution)/shard_map/all_to_all | solution.py:723
  75.3 1.1 %updated_rows.1 = f32[2,512]{1,0:T(2,128)} custom-call(bf16[128,16,128]{2,1,0:T(8,128)(2,1)S(1)} %all-to-all-done.grads, f32[512,512]{1,0:T(8,128)S(1)} %copy-done.2, f32[2,512]{1,0:T(2,128)S(1)} %copy-done.4), custom_call_target="tpu_custom_call" | custom-call | flops 200000000 | bytes 1500000 | tf_op jit(solution)/shard_map/updated_rows/pallas_call | solution.py:665
  (46 shorter events, 3.8 us)
Async XLA Ops:
  0.6 4.9 %copy-start.4 = (f32[2,512]{1,0:T(2,128)S(1)}, f32[2,512]{1,0:T(2,128)}, u32[]{:S(2)}) copy-start(f32[2,512]{1,0:T(2,128)} %screen.5) | copy-start | bytes 12292
  0.6 4.9 %copy-start.5 = (f32[2,2,512]{2,1,0:T(2,128)S(1)}, f32[2,2,512]{2,1,0:T(2,128)}, u32[]{:S(2)}) copy-start(f32[2,2,512]{2,1,0:T(2,128)} %uv.3) | copy-start | bytes 24580
  0.7 4.9 %copy-start.6 = (f32[2,384]{1,0:T(2,128)S(1)}, f32[2,384]{1,0:T(2,128)}, u32[]{:S(2)}) copy-start(f32[2,384]{1,0:T(2,128)} %lm.3) | copy-start | bytes 9220
  0.7 4.9 %copy-start.7 = (f32[384]{0:T(512)S(1)}, f32[384]{0:T(512)}, u32[]{:S(2)}) copy-start(f32[384]{0:T(512)} %flux.3) | copy-start | bytes 4612
  0.7 4.9 %copy-start = (bf16[2,2,2,512,384]{4,3,2,1,0:T(8,128)(2,1)S(1)}, bf16[2,2,2,512,384]{4,3,2,1,0:T(8,128)(2,1)}, u32[]{:S(2)}) copy-start(bf16[2,2,2,512,384]{4,3,2,1,0:T(8,128)(2,1)} %gain.3) | copy-start | bytes 9437188
  5.4 3.8 %collective-permute-start = (bf16[2,528,768]{2,1,0:T(8,128)(2,1)}, bf16[2,528,768]{2,1,0:T(8,128)(2,1)S(1)}, u32[]{:S(2)}, u32[]{:S(2)}) collective-permute-start(bf16[2,528,768]{2,1,0:T(8,128)(2,1)} %phasor_send.1), channel_id=1, source_target_pairs={{0,8},{8,0},{16,24},{24,16},{32,40},{40,32},{48,56},{56,48},{64,72... | collective-permute-start | bytes 4866056 | tf_op jit(solution)/shard_map/ppermute | solution.py:696
  13.3 18.0 %collective-permute-start.8 = (f32[32,2,4,512]{3,2,1,0:T(4,128)S(1)}, f32[32,2,4,512]{3,2,1,0:T(4,128)S(1)}, u32[]{:S(2)}, u32[]{:S(2)}) collective-permute-start(f32[32,2,4,512]{3,2,1,0:T(4,128)S(1)} %observed_send.1), channel_id=1, source_target_pairs={{0,8},{8,0},{16,24},{24,16},{32,40},{40,32},{48,56},{56,48},{64,72... | collective-permute-start | bytes 1572872 | tf_op jit(solution)/shard_map/ppermute | solution.py:708
  13.5 8.0 %collective-permute-start.4 = (bf16[2,64,512]{2,1,0:T(8,128)(2,1)S(1)}, bf16[2,64,512]{2,1,0:T(8,128)(2,1)S(1)}, u32[]{:S(2)}, u32[]{:S(2)}) collective-permute-start(bf16[2,64,512]{2,1,0:T(8,128)(2,1)S(1)} %get-tuple-element.22), channel_id=1, source_target_pairs={{0,32},{8,40},{16,48},{24,56},{32,0},{40,8},{48,16},{56,24},{64,96... | collective-permute-start | bytes 393224 | tf_op jit(solution)/shard_map/ppermute | solution.py:700
  16.8 7.7 %collective-permute-start.5 = (bf16[2,64,512]{2,1,0:T(8,128)(2,1)S(1)}, bf16[2,64,512]{2,1,0:T(8,128)(2,1)S(1)}, u32[]{:S(2)}, u32[]{:S(2)}) collective-permute-start(bf16[2,64,512]{2,1,0:T(8,128)(2,1)S(1)} %get-tuple-element.23), channel_id=1, source_target_pairs={{0,48},{8,56},{16,32},{24,40},{32,16},{40,24},{48,0},{56,8},{64,11... | collective-permute-start | bytes 393224 | tf_op jit(solution)/shard_map/ppermute | solution.py:700
  17.9 8.0 %collective-permute-start.6 = (bf16[2,64,512]{2,1,0:T(8,128)(2,1)S(1)}, bf16[2,64,512]{2,1,0:T(8,128)(2,1)S(1)}, u32[]{:S(2)}, u32[]{:S(2)}) collective-permute-start(bf16[2,64,512]{2,1,0:T(8,128)(2,1)S(1)} %get-tuple-element.24), channel_id=1, source_target_pairs={{0,16},{8,24},{16,0},{24,8},{32,48},{40,56},{48,32},{56,40},{64,80... | collective-permute-start | bytes 393224 | tf_op jit(solution)/shard_map/ppermute | solution.py:700
  17.9 13.8 %collective-permute-start.1 = (bf16[2,64,512]{2,1,0:T(8,128)(2,1)S(1)}, bf16[2,64,512]{2,1,0:T(8,128)(2,1)S(1)}, u32[]{:S(2)}, u32[]{:S(2)}) collective-permute-start(bf16[2,64,512]{2,1,0:T(8,128)(2,1)S(1)} %get-tuple-element.19._), channel_id=1, source_target_pairs={{0,32},{8,40},{16,48},{24,56},{32,0},{40,8},{48,16},{56,24},{64,96... | collective-permute-start | bytes 393224 | tf_op jit(solution)/shard_map/ppermute | solution.py:700
  21.5 10.2 %collective-permute-start.2 = (bf16[2,64,512]{2,1,0:T(8,128)(2,1)S(1)}, bf16[2,64,512]{2,1,0:T(8,128)(2,1)S(1)}, u32[]{:S(2)}, u32[]{:S(2)}) collective-permute-start(bf16[2,64,512]{2,1,0:T(8,128)(2,1)S(1)} %get-tuple-element.20), channel_id=1, source_target_pairs={{0,48},{8,56},{16,32},{24,40},{32,16},{40,24},{48,0},{56,8},{64,11... | collective-permute-start | bytes 393224 | tf_op jit(solution)/shard_map/ppermute | solution.py:700
  24.5 7.3 %collective-permute-start.3 = (bf16[2,64,512]{2,1,0:T(8,128)(2,1)S(1)}, bf16[2,64,512]{2,1,0:T(8,128)(2,1)S(1)}, u32[]{:S(2)}, u32[]{:S(2)}) collective-permute-start(bf16[2,64,512]{2,1,0:T(8,128)(2,1)S(1)} %get-tuple-element.21), channel_id=1, source_target_pairs={{0,16},{8,24},{16,0},{24,8},{32,48},{40,56},{48,32},{56,40},{64,80... | collective-permute-start | bytes 393224 | tf_op jit(solution)/shard_map/ppermute | solution.py:700
  26.0 5.8 %collective-permute-start.7 = (bf16[2,64,512]{2,1,0:T(8,128)(2,1)S(1)}, bf16[2,64,512]{2,1,0:T(8,128)(2,1)S(1)}, u32[]{:S(2)}, u32[]{:S(2)}) collective-permute-start(bf16[2,64,512]{2,1,0:T(8,128)(2,1)S(1)} %send_parts.1), channel_id=1, source_target_pairs={{0,64},{8,72},{16,80},{24,88},{32,96},{40,104},{48,112},{56,120},{... | collective-permute-start | bytes 393224 | tf_op jit(solution)/shard_map/ppermute | solution.py:703
  31.9 5.0 %collective-permute-start.12 = (bf16[2,64,512]{2,1,0:T(8,128)(2,1)S(1)}, bf16[2,64,512]{2,1,0:T(8,128)(2,1)S(1)}, u32[]{:S(2)}, u32[]{:S(2)}) collective-permute-start(bf16[2,64,512]{2,1,0:T(8,128)(2,1)S(1)} %get-tuple-element.31.refs_0_), channel_id=1, source_target_pairs={{0,64},{8,72},{16,80},{24,88},{32,96},{40,104},{48,112},{56,120},{... | collective-permute-start | bytes 393224 | tf_op jit(solution)/shard_map/ppermute | solution.py:703
  33.3 7.7 %collective-permute-start.9 = (bf16[2,64,512]{2,1,0:T(8,128)(2,1)S(1)}, bf16[2,64,512]{2,1,0:T(8,128)(2,1)S(1)}, u32[]{:S(2)}, u32[]{:S(2)}) collective-permute-start(bf16[2,64,512]{2,1,0:T(8,128)(2,1)S(1)} %get-tuple-element.31.refs_0_), channel_id=1, source_target_pairs={{0,16},{8,24},{16,0},{24,8},{32,48},{40,56},{48,32},{56,40},{64,80... | collective-permute-start | bytes 393224 | tf_op jit(solution)/shard_map/ppermute | solution.py:700
  33.9 11.7 %collective-permute-start.10 = (bf16[2,64,512]{2,1,0:T(8,128)(2,1)S(1)}, bf16[2,64,512]{2,1,0:T(8,128)(2,1)S(1)}, u32[]{:S(2)}, u32[]{:S(2)}) collective-permute-start(bf16[2,64,512]{2,1,0:T(8,128)(2,1)S(1)} %get-tuple-element.31.refs_0_), channel_id=1, source_target_pairs={{0,48},{8,56},{16,32},{24,40},{32,16},{40,24},{48,0},{56,8},{64,11... | collective-permute-start | bytes 393224 | tf_op jit(solution)/shard_map/ppermute | solution.py:700
  36.9 13.4 %collective-permute-start.13 = (bf16[2,64,512]{2,1,0:T(8,128)(2,1)S(1)}, bf16[2,64,512]{2,1,0:T(8,128)(2,1)S(1)}, u32[]{:S(2)}, u32[]{:S(2)}) collective-permute-start(bf16[2,64,512]{2,1,0:T(8,128)(2,1)S(1)} %collective-permute-done.12.refs_0_.refs_4_), channel_id=1, source_target_pairs={{0,16},{8,24},{16,0},{24,8},{32,48},{40,56},{48,32},{56,40},{64,80... | collective-permute-start | bytes 393224 | tf_op jit(solution)/shard_map/ppermute | solution.py:700
  37.5 12.8 %collective-permute-start.14 = (bf16[2,64,512]{2,1,0:T(8,128)(2,1)S(1)}, bf16[2,64,512]{2,1,0:T(8,128)(2,1)S(1)}, u32[]{:S(2)}, u32[]{:S(2)}) collective-permute-start(bf16[2,64,512]{2,1,0:T(8,128)(2,1)S(1)} %collective-permute-done.12.refs_0_.refs_4_), channel_id=1, source_target_pairs={{0,48},{8,56},{16,32},{24,40},{32,16},{40,24},{48,0},{56,8},{64,11... | collective-permute-start | bytes 393224 | tf_op jit(solution)/shard_map/ppermute | solution.py:700
  40.3 10.0 %collective-permute-start.15 = (bf16[2,64,512]{2,1,0:T(8,128)(2,1)S(1)}, bf16[2,64,512]{2,1,0:T(8,128)(2,1)S(1)}, u32[]{:S(2)}, u32[]{:S(2)}) collective-permute-start(bf16[2,64,512]{2,1,0:T(8,128)(2,1)S(1)} %collective-permute-done.12.refs_0_.refs_4_), channel_id=1, source_target_pairs={{0,32},{8,40},{16,48},{24,56},{32,0},{40,8},{48,16},{56,24},{64,96... | collective-permute-start | bytes 393224 | tf_op jit(solution)/shard_map/ppermute | solution.py:700
  41.0 8.1 %collective-permute-start.11 = (bf16[2,64,512]{2,1,0:T(8,128)(2,1)S(1)}, bf16[2,64,512]{2,1,0:T(8,128)(2,1)S(1)}, u32[]{:S(2)}, u32[]{:S(2)}) collective-permute-start(bf16[2,64,512]{2,1,0:T(8,128)(2,1)S(1)} %collective-permute-done.9.refs_1_), channel_id=1, source_target_pairs={{0,48},{8,56},{16,32},{24,40},{32,16},{40,24},{48,0},{56,8},{64,11... | collective-permute-start | bytes 393224 | tf_op jit(solution)/shard_map/ppermute | solution.py:700
  52.4 22.9 %copy-start.2 = (f32[512,512]{1,0:T(8,128)S(1)}, f32[512,512]{1,0:T(8,128)}, u32[]{:S(2)}) copy-start(f32[512,512]{1,0:T(8,128)} %kernel.1) | copy-start | bytes 3145732
  52.4 22.9 %all-to-all-start = ((bf16[128,16,128]{2,1,0:T(8,128)(2,1)}), bf16[128,16,128]{2,1,0:T(8,128)(2,1)S(1)}, u32[]{:S(2)}, u32[]{:S(2)}) async-start(bf16[128,16,128]{2,1,0:T(8,128)(2,1)} %gradient_parts1.1.refs_8_), calls=%async_computation | async-start | bytes 1048576 | tf_op jit(solution)/shard_map/all_to_all | solution.py:723
  62.8 1.6 %collective-permute-start.16 = (f32[4,32,512]{2,1,0:T(8,128)S(1)}, f32[4,32,512]{2,1,0:T(8,128)S(1)}, u32[]{:S(2)}, u32[]{:S(2)}) collective-permute-start(f32[4,32,512]{2,1,0:T(8,128)S(1)} %get-tuple-element.33), channel_id=1, source_target_pairs={{0,8},{8,0},{16,24},{24,16},{32,40},{40,32},{48,56},{56,48},{64,72... | collective-permute-start | bytes 786440 | tf_op jit(solution)/shard_map/ppermute | solution.py:722
  (4 other events, 19.0 us)

commit v10 on v9

--- a/solution.py
+++ b/solution.py
@@ -712,9 +712,10 @@
     resid, half = residual_parts(parts[0], *near, last, obs, kept, directions0)
     half_z = across_z(half)
     directions1 = direction_parts(1, scaling, own, other, *parts[7:])
-    one, two = across(1, half), across(2, half)
-    resids = [half, one, two, across(2, one)]
-    resids += [half_z, across(1, half_z), across(2, half_z), across(3, half_z)]
+    resids = []
+    for array in (half, half_z):
+        three, two, one = (across(rel, array) for rel in (3, 2, 1))
+        resids += [array, one, two, three]
 
     grads = gradient_parts(0, devices, freq_ratio, *resids[:4], directions0, directions1)
     grads = gradient_parts(1, devices, freq_ratio, *resids[4:], directions0, directions1, grads)

time: 76.6 us -> 75.2 us (0.982)
  starting transfers between devices: 35.1 us -> 32.8 us
  waiting for transfers between devices: 15.8 us -> 16.7 us
    ppermute x12, starting transfers between devices: 21.4 us -> 19.9 us  [across(): return lax.ppermute(array, 'dir', dir_perm(rel))]
    ppermute x12, waiting for transfers between devices: 3.5 us -> 4.59 us  [across(): return lax.ppermute(array, 'dir', dir_perm(rel))]
    all_to_all x1, starting transfers between devices: 9.71 us -> 8.83 us  [body(): grads = lax.all_to_all(grads, ('dir', 'freq'), 0, 0, tiled=True)]
  transfers between devices with their start and end apart: 18 -> 18, of which waited for: 5 -> 5; matrix products, arithmetic and copies ran while one was open for 0% -> 0% of each run, Pallas kernels for 16% -> 17%
where the time goes in v10:
time: 75.2 us; the launch traced here: 75 us
  starting transfers between devices  32.8 us (44%)
  Pallas kernels  24.5 us (33%)
  waiting for transfers between devices  16.7 us (22%)
  between operations  0.97 us (1%)
    ppermute x12, starting transfers between devices, across(): return lax.ppermute(array, 'dir', dir_perm(rel))  19.9 us
    all_to_all x1, waiting for transfers between devices, body(): grads = lax.all_to_all(grads, ('dir', 'freq'), 0, 0, tiled=True)  9.94 us
    all_to_all x1, starting transfers between devices, body(): grads = lax.all_to_all(grads, ('dir', 'freq'), 0, 0, tiled=True)  8.83 us
    pallas_call x2, Pallas kernels, direction_parts(): pl.pallas_call(functools.partial(direction_kernel, moment, scaling), in_s...  6.27 us
    pallas_call x1, Pallas kernels, phasor_send(): pl.pallas_call(phasor_send_kernel, in_specs=[HBM] * 7, out_specs=HBM, out...  4.72 us
    ppermute x12, waiting for transfers between devices, across(): return lax.ppermute(array, 'dir', dir_perm(rel))  4.59 us
    pallas_call x1, Pallas kernels, model_parts(): pl.pallas_call(functools.partial(model_kernel, scaling), in_specs=[WHOLE,...  3.9 us
    ppermute x2, starting transfers between devices, across_z(): return lax.ppermute(array, 'dir', dir_perm(0, flip_z=True))  3.62 us
  transfers between devices with their start and end apart: 18, of which 5 were waited for; matrix products, arithmetic and copies ran while one was open for 0% of the time, Pallas kernels for 17%

profile of v10, /device:TPU:0, one launch (start us, length us, event | category | flops | bytes accessed | tf_op | source)
XLA Modules:
  0.0 75.0 jit_solution(2000592544143872769)
XLA Ops:
  0.7 4.7 %phasor_send.1 = bf16[2,528,768]{2,1,0:T(8,128)(2,1)} custom-call(f32[2]{0:T(128)} %freq.7, bf16[2,2,2,512,384]{4,3,2,1,0:T(8,128)(2,1)} %gain.3, f32[2,2,512]{2,1,0:T(2,128)} %uv.3, f32[2,512]{1,0:T(2,128)} %screen.5, f32[2,384]{1,0:T(2,128)} %lm.3, f32[384]{0:T(512)} %flux.3, s32[384]{0:T(512)} %direction.3), custom_call_target="tpu_custom_call" | custom-call | flops 15728640 | bytes 3200000 | tf_op jit(solution)/shard_map/phasor_send/pallas_call | solution.py:187
  5.6 2.9 %phasor_own.1.own = bf16[2,528,768]{2,1,0:T(8,128)(2,1)S(1)} custom-call(f32[2]{0:T(128)S(1)} %copy-done.9, bf16[2,2,2,512,384]{4,3,2,1,0:T(8,128)(2,1)S(1)} %copy-done, f32[2,2,512]{2,1,0:T(2,128)S(1)} %copy-done.5, f32[2,512]{1,0:T(2,128)S(1)} %copy-done.4, f32[2,384]{1,0:T(2,128)S(1)} %copy-done.6, f32[384]{0:T(512)S(1)} %copy-done.7, s32[384]{0:T(512)S(1)} %copy-done.8), custom_call_target="tpu_custom_call" | custom-call | flops 15728640 | bytes 3200000 | tf_op jit(solution)/shard_map/phasor_own/pallas_call | solution.py:212
  9.2 3.9 %model_parts.1 = (f32[2,2,64,512]{3,2,1,0:T(8,128)S(1)}, bf16[2,64,512]{2,1,0:T(8,128)(2,1)S(1)}, bf16[2,64,512]{2,1,0:T(8,128)(2,1)S(1)}, bf16[2,64,512]{2,1,0:...) custom-call(bf16[2,528,768]{2,1,0:T(8,128)(2,1)S(1)} %phasor_own.1.o, ...), custom_call_target="tpu_custom_call" | custom-call | flops 3221225472 | bytes 5000000 | tf_op jit(solution)/shard_map/model_parts/pallas_call | solution.py:319
  13.5 3.3 %collective-permute-start.4 = (bf16[2,64,512]{2,1,0:T(8,128)(2,1)S(1)}, bf16[2,64,512]{2,1,0:T(8,128)(2,1)S(1)}, u32[]{:S(2)}, u32[]{:S(2)}) collective-permute-start(bf16[2,64,512]{2,1,0:T(8,128)(2,1)S(1)} %get-tuple-element.22), channel_id=1, source_target_pairs={{0,32},{8,40},{16,48},{24,56},{32,0},{40,8},{48,16},{56,24},{64,96... | collective-permute-start | bytes 393224 | tf_op jit(solution)/shard_map/ppermute | solution.py:700
  16.8 1.1 %collective-permute-start.5 = (bf16[2,64,512]{2,1,0:T(8,128)(2,1)S(1)}, bf16[2,64,512]{2,1,0:T(8,128)(2,1)S(1)}, u32[]{:S(2)}, u32[]{:S(2)}) collective-permute-start(bf16[2,64,512]{2,1,0:T(8,128)(2,1)S(1)} %get-tuple-element.23), channel_id=1, source_target_pairs={{0,48},{8,56},{16,32},{24,40},{32,16},{40,24},{48,0},{56,8},{64,11... | collective-permute-start | bytes 393224 | tf_op jit(solution)/shard_map/ppermute | solution.py:700
  17.9 3.6 %collective-permute-start.1 = (bf16[2,64,512]{2,1,0:T(8,128)(2,1)S(1)}, bf16[2,64,512]{2,1,0:T(8,128)(2,1)S(1)}, u32[]{:S(2)}, u32[]{:S(2)}) collective-permute-start(bf16[2,64,512]{2,1,0:T(8,128)(2,1)S(1)} %get-tuple-element.19._), channel_id=1, source_target_pairs={{0,32},{8,40},{16,48},{24,56},{32,0},{40,8},{48,16},{56,24},{64,96... | collective-permute-start | bytes 393224 | tf_op jit(solution)/shard_map/ppermute | solution.py:700
  21.5 2.9 %collective-permute-start.2 = (bf16[2,64,512]{2,1,0:T(8,128)(2,1)S(1)}, bf16[2,64,512]{2,1,0:T(8,128)(2,1)S(1)}, u32[]{:S(2)}, u32[]{:S(2)}) collective-permute-start(bf16[2,64,512]{2,1,0:T(8,128)(2,1)S(1)} %get-tuple-element.20), channel_id=1, source_target_pairs={{0,48},{8,56},{16,32},{24,40},{32,16},{40,24},{48,0},{56,8},{64,11... | collective-permute-start | bytes 393224 | tf_op jit(solution)/shard_map/ppermute | solution.py:700
  24.5 1.4 %collective-permute-start.3 = (bf16[2,64,512]{2,1,0:T(8,128)(2,1)S(1)}, bf16[2,64,512]{2,1,0:T(8,128)(2,1)S(1)}, u32[]{:S(2)}, u32[]{:S(2)}) collective-permute-start(bf16[2,64,512]{2,1,0:T(8,128)(2,1)S(1)} %get-tuple-element.21), channel_id=1, source_target_pairs={{0,16},{8,24},{16,0},{24,8},{32,48},{40,56},{48,32},{56,40},{64,80... | collective-permute-start | bytes 393224 | tf_op jit(solution)/shard_map/ppermute | solution.py:700
  26.0 2.2 %collective-permute-start.7 = (bf16[2,64,512]{2,1,0:T(8,128)(2,1)S(1)}, bf16[2,64,512]{2,1,0:T(8,128)(2,1)S(1)}, u32[]{:S(2)}, u32[]{:S(2)}) collective-permute-start(bf16[2,64,512]{2,1,0:T(8,128)(2,1)S(1)} %send_parts.1), channel_id=1, source_target_pairs={{0,64},{8,72},{16,80},{24,88},{32,96},{40,104},{48,112},{56,120},{... | collective-permute-start | bytes 393224 | tf_op jit(solution)/shard_map/ppermute | solution.py:703
  28.2 3.1 %direction_parts0.1._.refs_4_ = bf16[4,4,2,64,512]{4,3,2,1,0:T(8,128)(2,1)S(1)} custom-call(bf16[2,528,768]{2,1,0:T(8,128)(2,1)S(1)} %phasor_own.1.own, bf16[2,528,768]{2,1,0:T(8,128)(2,1)S(1)} %collective-permute-done.other_hbm.other, f32[2,2,512,768]{3,2,1,0:T(8,128)S(1)} %get-tuple-element.27.totals, f32[2,2,256,512]{3,2,1,0:T(8,128)S(1)} %get-tuple-element.28.tops, ...), custom_call_target="tpu_custom_call" | custom-call | flops 1610612736 | bytes 5000000 | tf_op jit(solution)/shard_map/direction_parts0/pallas_call | solution.py:363
  31.9 1.4 %collective-permute-start.12 = (bf16[2,64,512]{2,1,0:T(8,128)(2,1)S(1)}, bf16[2,64,512]{2,1,0:T(8,128)(2,1)S(1)}, u32[]{:S(2)}, u32[]{:S(2)}) collective-permute-start(bf16[2,64,512]{2,1,0:T(8,128)(2,1)S(1)} %get-tuple-element.31.refs_0_), channel_id=1, source_target_pairs={{0,64},{8,72},{16,80},{24,88},{32,96},{40,104},{48,112},{56,120},{... | collective-permute-start | bytes 393224 | tf_op jit(solution)/shard_map/ppermute | solution.py:703
  33.3 1.7 %collective-permute-start.10 = (bf16[2,64,512]{2,1,0:T(8,128)(2,1)S(1)}, bf16[2,64,512]{2,1,0:T(8,128)(2,1)S(1)}, u32[]{:S(2)}, u32[]{:S(2)}) collective-permute-start(bf16[2,64,512]{2,1,0:T(8,128)(2,1)S(1)} %get-tuple-element.31.refs_0_), channel_id=1, source_target_pairs={{0,48},{8,56},{16,32},{24,40},{32,16},{40,24},{48,0},{56,8},{64,11... | collective-permute-start | bytes 393224 | tf_op jit(solution)/shard_map/ppermute | solution.py:700
  35.0 1.2 %collective-permute-start.11 = (bf16[2,64,512]{2,1,0:T(8,128)(2,1)S(1)}, bf16[2,64,512]{2,1,0:T(8,128)(2,1)S(1)}, u32[]{:S(2)}, u32[]{:S(2)}) collective-permute-start(bf16[2,64,512]{2,1,0:T(8,128)(2,1)S(1)} %get-tuple-element.31.refs_0_), channel_id=1, source_target_pairs={{0,32},{8,40},{16,48},{24,56},{32,0},{40,8},{48,16},{56,24},{64,96... | collective-permute-start | bytes 393224 | tf_op jit(solution)/shard_map/ppermute | solution.py:700
  36.2 1.2 %collective-permute-start.9 = (bf16[2,64,512]{2,1,0:T(8,128)(2,1)S(1)}, bf16[2,64,512]{2,1,0:T(8,128)(2,1)S(1)}, u32[]{:S(2)}, u32[]{:S(2)}) collective-permute-start(bf16[2,64,512]{2,1,0:T(8,128)(2,1)S(1)} %get-tuple-element.31.refs_0_), channel_id=1, source_target_pairs={{0,16},{8,24},{16,0},{24,8},{32,48},{40,56},{48,32},{56,40},{64,80... | collective-permute-start | bytes 393224 | tf_op jit(solution)/shard_map/ppermute | solution.py:700
  38.2 2.6 %collective-permute-start.14 = (bf16[2,64,512]{2,1,0:T(8,128)(2,1)S(1)}, bf16[2,64,512]{2,1,0:T(8,128)(2,1)S(1)}, u32[]{:S(2)}, u32[]{:S(2)}) collective-permute-start(bf16[2,64,512]{2,1,0:T(8,128)(2,1)S(1)} %collective-permute-done.12.refs_0_.refs_4_), channel_id=1, source_target_pairs={{0,48},{8,56},{16,32},{24,40},{32,16},{40,24},{48,0},{56,8},{64,11... | collective-permute-start | bytes 393224 | tf_op jit(solution)/shard_map/ppermute | solution.py:700
  40.9 2.5 %collective-permute-done.10.refs_2_ = bf16[2,64,512]{2,1,0:T(8,128)(2,1)S(1)} collective-permute-done((bf16[2,64,512]{2,1,0:T(8,128)(2,1)S(1)}, bf16[2,64,512]{2,1,0:T(8,128)(2,1)S(1)}, u32[]{:S(2)}, u32[]{:S(2)}) %collective-permute-start.10) | collective-permute-done | bytes 131104 | tf_op jit(solution)/shard_map/ppermute | solution.py:700
  43.3 3.1 %direction_parts1.1.refs_5_ = bf16[4,4,2,64,512]{4,3,2,1,0:T(8,128)(2,1)S(1)} custom-call(bf16[2,528,768]{2,1,0:T(8,128)(2,1)S(1)} %phasor_own.1.own, bf16[2,528,768]{2,1,0:T(8,128)(2,1)S(1)} %collective-permute-done.other_hbm.other, f32[2,2,512,768]{3,2,1,0:T(8,128)S(1)} %get-tuple-element.27.totals, f32[2,2,256,512]{3,2,1,0:T(8,128)S(1)} %get-tuple-element.28.tops, ...), custom_call_target="tpu_custom_call" | custom-call | flops 1610612736 | bytes 5000000 | tf_op jit(solution)/shard_map/direction_parts1/pallas_call | solution.py:363
  46.5 1.2 %gradient_parts0.1.refs_6_ = f32[16,128]{1,0:T(8,128)S(1)} custom-call(f32[2]{0:T(128)S(1)} %copy-done.9, bf16[2,64,512]{2,1,0:T(8,128)(2,1)S(1)} %get-tuple-element.31.refs_0_, bf16[2,64,512]{2,1,0:T(8,128)(2,1)S(1)} %collective-permute-done.9.refs_1_, bf16[2,64,512]{2,1,0:T(8,128)(2,1)S(1)} %collective-permute-done.10.refs_2_, ...), custom_call_target="tpu_custom_call" | custom-call | flops 5000000 | bytes 3000000 | tf_op jit(solution)/shard_map/gradient_parts0/pallas_call | solution.py:550
  47.7 2.1 %collective-permute-done.15.refs_3_.refs_7_ = bf16[2,64,512]{2,1,0:T(8,128)(2,1)S(1)} collective-permute-done((bf16[2,64,512]{2,1,0:T(8,128)(2,1)S(1)}, bf16[2,64,512]{2,1,0:T(8,128)(2,1)S(1)}, u32[]{:S(2)}, u32[]{:S(2)}) %collective-permute-start.15) | collective-permute-done | bytes 131104 | tf_op jit(solution)/shard_map/ppermute | solution.py:700
  49.8 2.1 %gradient_parts1.1.refs_8_ = bf16[128,16,128]{2,1,0:T(8,128)(2,1)} custom-call(f32[2]{0:T(128)S(1)} %copy-done.9, bf16[2,64,512]{2,1,0:T(8,128)(2,1)S(1)} %collective-permute-done.12.refs_0_.refs_4_, bf16[2,64,512]{2,1,0:T(8,128)(2,1)S(1)} %collective-permute-done.13.refs_1_.refs_5_, bf16[2,64,512]{2,1,0:T(8,128)(2,1)S(1)} %collective-permute-done.14.refs_2_.refs_6_, ...), custom_call_target="tpu_custom_call" | custom-call | flops 5000000 | bytes 3000000 | tf_op jit(solution)/shard_map/gradient_parts1/pallas_call | solution.py:550
  51.9 8.8 %all-to-all-start = ((bf16[128,16,128]{2,1,0:T(8,128)(2,1)}), bf16[128,16,128]{2,1,0:T(8,128)(2,1)S(1)}, u32[]{:S(2)}, u32[]{:S(2)}) async-start(bf16[128,16,128]{2,1,0:T(8,128)(2,1)} %gradient_parts1.1.refs_8_), calls=%async_computation | async-start | bytes 1048576 | tf_op jit(solution)/shard_map/all_to_all | solution.py:724
  61.5 1.5 %collective-permute-done.16.other = f32[4,32,512]{2,1,0:T(8,128)S(1)} collective-permute-done((f32[4,32,512]{2,1,0:T(8,128)S(1)}, f32[4,32,512]{2,1,0:T(8,128)S(1)}, u32[]{:S(2)}, u32[]{:S(2)}) %collective-permute-start.16) | collective-permute-done | bytes 262176 | tf_op jit(solution)/shard_map/ppermute | solution.py:723
  63.9 9.9 %all-to-all-done.grads = bf16[128,16,128]{2,1,0:T(8,128)(2,1)S(1)} async-done(((bf16[128,16,128]{2,1,0:T(8,128)(2,1)}), bf16[128,16,128]{2,1,0:T(8,128)(2,1)S(1)}, u32[]{:S(2)}, u32[]{:S(2)}) %all-to-all-start) | async-done | bytes 524320 | tf_op jit(solution)/shard_map/all_to_all | solution.py:724
  73.9 1.1 %updated_rows.1 = f32[2,512]{1,0:T(2,128)} custom-call(bf16[128,16,128]{2,1,0:T(8,128)(2,1)S(1)} %all-to-all-done.grads, f32[512,512]{1,0:T(8,128)S(1)} %copy-done.2, f32[2,512]{1,0:T(2,128)S(1)} %copy-done.4), custom_call_target="tpu_custom_call" | custom-call | flops 200000000 | bytes 1500000 | tf_op jit(solution)/shard_map/updated_rows/pallas_call | solution.py:665
  (46 shorter events, 4.2 us)
Async XLA Ops:
  0.6 4.9 %copy-start.4 = (f32[2,512]{1,0:T(2,128)S(1)}, f32[2,512]{1,0:T(2,128)}, u32[]{:S(2)}) copy-start(f32[2,512]{1,0:T(2,128)} %screen.5) | copy-start | bytes 12292
  0.6 4.9 %copy-start.5 = (f32[2,2,512]{2,1,0:T(2,128)S(1)}, f32[2,2,512]{2,1,0:T(2,128)}, u32[]{:S(2)}) copy-start(f32[2,2,512]{2,1,0:T(2,128)} %uv.3) | copy-start | bytes 24580
  0.7 4.9 %copy-start.6 = (f32[2,384]{1,0:T(2,128)S(1)}, f32[2,384]{1,0:T(2,128)}, u32[]{:S(2)}) copy-start(f32[2,384]{1,0:T(2,128)} %lm.3) | copy-start | bytes 9220
  0.7 4.9 %copy-start.7 = (f32[384]{0:T(512)S(1)}, f32[384]{0:T(512)}, u32[]{:S(2)}) copy-start(f32[384]{0:T(512)} %flux.3) | copy-start | bytes 4612
  0.7 4.9 %copy-start = (bf16[2,2,2,512,384]{4,3,2,1,0:T(8,128)(2,1)S(1)}, bf16[2,2,2,512,384]{4,3,2,1,0:T(8,128)(2,1)}, u32[]{:S(2)}) copy-start(bf16[2,2,2,512,384]{4,3,2,1,0:T(8,128)(2,1)} %gain.3) | copy-start | bytes 9437188
  5.4 3.8 %collective-permute-start = (bf16[2,528,768]{2,1,0:T(8,128)(2,1)}, bf16[2,528,768]{2,1,0:T(8,128)(2,1)S(1)}, u32[]{:S(2)}, u32[]{:S(2)}) collective-permute-start(bf16[2,528,768]{2,1,0:T(8,128)(2,1)} %phasor_send.1), channel_id=1, source_target_pairs={{0,8},{8,0},{16,24},{24,16},{32,40},{40,32},{48,56},{56,48},{64,72... | collective-permute-start | bytes 4866056 | tf_op jit(solution)/shard_map/ppermute | solution.py:696
  13.3 18.0 %collective-permute-start.8 = (f32[32,2,4,512]{3,2,1,0:T(4,128)S(1)}, f32[32,2,4,512]{3,2,1,0:T(4,128)S(1)}, u32[]{:S(2)}, u32[]{:S(2)}) collective-permute-start(f32[32,2,4,512]{3,2,1,0:T(4,128)S(1)} %observed_send.1), channel_id=1, source_target_pairs={{0,8},{8,0},{16,24},{24,16},{32,40},{40,32},{48,56},{56,48},{64,72... | collective-permute-start | bytes 1572872 | tf_op jit(solution)/shard_map/ppermute | solution.py:708
  13.5 8.0 %collective-permute-start.4 = (bf16[2,64,512]{2,1,0:T(8,128)(2,1)S(1)}, bf16[2,64,512]{2,1,0:T(8,128)(2,1)S(1)}, u32[]{:S(2)}, u32[]{:S(2)}) collective-permute-start(bf16[2,64,512]{2,1,0:T(8,128)(2,1)S(1)} %get-tuple-element.22), channel_id=1, source_target_pairs={{0,32},{8,40},{16,48},{24,56},{32,0},{40,8},{48,16},{56,24},{64,96... | collective-permute-start | bytes 393224 | tf_op jit(solution)/shard_map/ppermute | solution.py:700
  16.8 7.7 %collective-permute-start.5 = (bf16[2,64,512]{2,1,0:T(8,128)(2,1)S(1)}, bf16[2,64,512]{2,1,0:T(8,128)(2,1)S(1)}, u32[]{:S(2)}, u32[]{:S(2)}) collective-permute-start(bf16[2,64,512]{2,1,0:T(8,128)(2,1)S(1)} %get-tuple-element.23), channel_id=1, source_target_pairs={{0,48},{8,56},{16,32},{24,40},{32,16},{40,24},{48,0},{56,8},{64,11... | collective-permute-start | bytes 393224 | tf_op jit(solution)/shard_map/ppermute | solution.py:700
  17.9 8.0 %collective-permute-start.6 = (bf16[2,64,512]{2,1,0:T(8,128)(2,1)S(1)}, bf16[2,64,512]{2,1,0:T(8,128)(2,1)S(1)}, u32[]{:S(2)}, u32[]{:S(2)}) collective-permute-start(bf16[2,64,512]{2,1,0:T(8,128)(2,1)S(1)} %get-tuple-element.24), channel_id=1, source_target_pairs={{0,16},{8,24},{16,0},{24,8},{32,48},{40,56},{48,32},{56,40},{64,80... | collective-permute-start | bytes 393224 | tf_op jit(solution)/shard_map/ppermute | solution.py:700
  17.9 13.8 %collective-permute-start.1 = (bf16[2,64,512]{2,1,0:T(8,128)(2,1)S(1)}, bf16[2,64,512]{2,1,0:T(8,128)(2,1)S(1)}, u32[]{:S(2)}, u32[]{:S(2)}) collective-permute-start(bf16[2,64,512]{2,1,0:T(8,128)(2,1)S(1)} %get-tuple-element.19._), channel_id=1, source_target_pairs={{0,32},{8,40},{16,48},{24,56},{32,0},{40,8},{48,16},{56,24},{64,96... | collective-permute-start | bytes 393224 | tf_op jit(solution)/shard_map/ppermute | solution.py:700
  21.5 10.2 %collective-permute-start.2 = (bf16[2,64,512]{2,1,0:T(8,128)(2,1)S(1)}, bf16[2,64,512]{2,1,0:T(8,128)(2,1)S(1)}, u32[]{:S(2)}, u32[]{:S(2)}) collective-permute-start(bf16[2,64,512]{2,1,0:T(8,128)(2,1)S(1)} %get-tuple-element.20), channel_id=1, source_target_pairs={{0,48},{8,56},{16,32},{24,40},{32,16},{40,24},{48,0},{56,8},{64,11... | collective-permute-start | bytes 393224 | tf_op jit(solution)/shard_map/ppermute | solution.py:700
  24.5 7.3 %collective-permute-start.3 = (bf16[2,64,512]{2,1,0:T(8,128)(2,1)S(1)}, bf16[2,64,512]{2,1,0:T(8,128)(2,1)S(1)}, u32[]{:S(2)}, u32[]{:S(2)}) collective-permute-start(bf16[2,64,512]{2,1,0:T(8,128)(2,1)S(1)} %get-tuple-element.21), channel_id=1, source_target_pairs={{0,16},{8,24},{16,0},{24,8},{32,48},{40,56},{48,32},{56,40},{64,80... | collective-permute-start | bytes 393224 | tf_op jit(solution)/shard_map/ppermute | solution.py:700
  26.0 5.8 %collective-permute-start.7 = (bf16[2,64,512]{2,1,0:T(8,128)(2,1)S(1)}, bf16[2,64,512]{2,1,0:T(8,128)(2,1)S(1)}, u32[]{:S(2)}, u32[]{:S(2)}) collective-permute-start(bf16[2,64,512]{2,1,0:T(8,128)(2,1)S(1)} %send_parts.1), channel_id=1, source_target_pairs={{0,64},{8,72},{16,80},{24,88},{32,96},{40,104},{48,112},{56,120},{... | collective-permute-start | bytes 393224 | tf_op jit(solution)/shard_map/ppermute | solution.py:703
  31.9 5.5 %collective-permute-start.12 = (bf16[2,64,512]{2,1,0:T(8,128)(2,1)S(1)}, bf16[2,64,512]{2,1,0:T(8,128)(2,1)S(1)}, u32[]{:S(2)}, u32[]{:S(2)}) collective-permute-start(bf16[2,64,512]{2,1,0:T(8,128)(2,1)S(1)} %get-tuple-element.31.refs_0_), channel_id=1, source_target_pairs={{0,64},{8,72},{16,80},{24,88},{32,96},{40,104},{48,112},{56,120},{... | collective-permute-start | bytes 393224 | tf_op jit(solution)/shard_map/ppermute | solution.py:703
  33.3 10.0 %collective-permute-start.10 = (bf16[2,64,512]{2,1,0:T(8,128)(2,1)S(1)}, bf16[2,64,512]{2,1,0:T(8,128)(2,1)S(1)}, u32[]{:S(2)}, u32[]{:S(2)}) collective-permute-start(bf16[2,64,512]{2,1,0:T(8,128)(2,1)S(1)} %get-tuple-element.31.refs_0_), channel_id=1, source_target_pairs={{0,48},{8,56},{16,32},{24,40},{32,16},{40,24},{48,0},{56,8},{64,11... | collective-permute-start | bytes 393224 | tf_op jit(solution)/shard_map/ppermute | solution.py:700
  35.0 11.5 %collective-permute-start.11 = (bf16[2,64,512]{2,1,0:T(8,128)(2,1)S(1)}, bf16[2,64,512]{2,1,0:T(8,128)(2,1)S(1)}, u32[]{:S(2)}, u32[]{:S(2)}) collective-permute-start(bf16[2,64,512]{2,1,0:T(8,128)(2,1)S(1)} %get-tuple-element.31.refs_0_), channel_id=1, source_target_pairs={{0,32},{8,40},{16,48},{24,56},{32,0},{40,8},{48,16},{56,24},{64,96... | collective-permute-start | bytes 393224 | tf_op jit(solution)/shard_map/ppermute | solution.py:700
  36.2 10.3 %collective-permute-start.9 = (bf16[2,64,512]{2,1,0:T(8,128)(2,1)S(1)}, bf16[2,64,512]{2,1,0:T(8,128)(2,1)S(1)}, u32[]{:S(2)}, u32[]{:S(2)}) collective-permute-start(bf16[2,64,512]{2,1,0:T(8,128)(2,1)S(1)} %get-tuple-element.31.refs_0_), channel_id=1, source_target_pairs={{0,16},{8,24},{16,0},{24,8},{32,48},{40,56},{48,32},{56,40},{64,80... | collective-permute-start | bytes 393224 | tf_op jit(solution)/shard_map/ppermute | solution.py:700
  37.4 10.3 %collective-permute-start.13 = (bf16[2,64,512]{2,1,0:T(8,128)(2,1)S(1)}, bf16[2,64,512]{2,1,0:T(8,128)(2,1)S(1)}, u32[]{:S(2)}, u32[]{:S(2)}) collective-permute-start(bf16[2,64,512]{2,1,0:T(8,128)(2,1)S(1)} %collective-permute-done.12.refs_0_.refs_4_), channel_id=1, source_target_pairs={{0,16},{8,24},{16,0},{24,8},{32,48},{40,56},{48,32},{56,40},{64,80... | collective-permute-start | bytes 393224 | tf_op jit(solution)/shard_map/ppermute | solution.py:700
  38.2 9.5 %collective-permute-start.14 = (bf16[2,64,512]{2,1,0:T(8,128)(2,1)S(1)}, bf16[2,64,512]{2,1,0:T(8,128)(2,1)S(1)}, u32[]{:S(2)}, u32[]{:S(2)}) collective-permute-start(bf16[2,64,512]{2,1,0:T(8,128)(2,1)S(1)} %collective-permute-done.12.refs_0_.refs_4_), channel_id=1, source_target_pairs={{0,48},{8,56},{16,32},{24,40},{32,16},{40,24},{48,0},{56,8},{64,11... | collective-permute-start | bytes 393224 | tf_op jit(solution)/shard_map/ppermute | solution.py:700
  43.3 6.5 %collective-permute-start.15 = (bf16[2,64,512]{2,1,0:T(8,128)(2,1)S(1)}, bf16[2,64,512]{2,1,0:T(8,128)(2,1)S(1)}, u32[]{:S(2)}, u32[]{:S(2)}) collective-permute-start(bf16[2,64,512]{2,1,0:T(8,128)(2,1)S(1)} %collective-permute-done.12.refs_0_.refs_4_), channel_id=1, source_target_pairs={{0,32},{8,40},{16,48},{24,56},{32,0},{40,8},{48,16},{56,24},{64,96... | collective-permute-start | bytes 393224 | tf_op jit(solution)/shard_map/ppermute | solution.py:700
  51.9 22.0 %copy-start.2 = (f32[512,512]{1,0:T(8,128)S(1)}, f32[512,512]{1,0:T(8,128)}, u32[]{:S(2)}) copy-start(f32[512,512]{1,0:T(8,128)} %kernel.1) | copy-start | bytes 3145732
  51.9 22.0 %all-to-all-start = ((bf16[128,16,128]{2,1,0:T(8,128)(2,1)}), bf16[128,16,128]{2,1,0:T(8,128)(2,1)S(1)}, u32[]{:S(2)}, u32[]{:S(2)}) async-start(bf16[128,16,128]{2,1,0:T(8,128)(2,1)} %gradient_parts1.1.refs_8_), calls=%async_computation | async-start | bytes 1048576 | tf_op jit(solution)/shard_map/all_to_all | solution.py:724
  61.4 1.6 %collective-permute-start.16 = (f32[4,32,512]{2,1,0:T(8,128)S(1)}, f32[4,32,512]{2,1,0:T(8,128)S(1)}, u32[]{:S(2)}, u32[]{:S(2)}) collective-permute-start(f32[4,32,512]{2,1,0:T(8,128)S(1)} %get-tuple-element.33), channel_id=1, source_target_pairs={{0,8},{8,0},{16,24},{24,16},{32,40},{40,32},{48,56},{56,48},{64,72... | collective-permute-start | bytes 786440 | tf_op jit(solution)/shard_map/ppermute | solution.py:723
  (4 other events, 19.0 us)
